TPU v7x, 32 devices: a whole 2x2x4 slice. The times are simulated.
32 devices in a mesh: section: 4 (over y, core), dp: 8 (over z, x).
Axes of the slice: x: 2, y: 2, z: 4, core: 2. Of those that a mesh axis runs over, the one named last changes fastest.
Arguments:
- block_input: bfloat16 [6144, 768], P('dp', 'section'), may hold values from -6 to 6
- cotangent: bfloat16 [6144, 768], P('dp', 'section'), may hold values from -6 to 6
- grid_sizes: int32 [16, 2, 2], P('dp'), may hold values from 8 to 13
- section_weight: bfloat16 [4, 768, 4608], P('section'), may hold values from -4 to 4
- norm_gain: float32 [4, 768], P('section'), may hold values from 0.5 to 1.5
- norm_bias: float32 [4, 768], P('section'), may hold values from -1 to 1
- first_vector: float32 [4, 3072], P('section'), may hold values from -2 to 2
- second_vector: float32 [4, 768], P('section'), may hold values from -1.5 to 1.5
Outputs:
- activations: bfloat16 [4, 6144, 768], P('section', 'dp')
- input_grads: bfloat16 [4, 6144, 768], P('section', 'dp')
- section_weight_grad: float32 [4, 768, 4608], P('section')
- norm_gain_grad: float32 [4, 768], P('section')
- norm_bias_grad: float32 [4, 768], P('section')
- first_vector_grad: float32 [4, 3072], P('section')
- second_vector_grad: float32 [4, 768], P('section')
Inputs may be any that keep to these rules, and one draw needn't show every extreme that they name: `grid_sizes`: each packed row holds two images laid out from slot 0; the rest of the row is padding.
All inputs are finite; a program needn't handle non-finite values.
Results may differ from a plain program's by a relative error of at most 0.015.
Values may be sent and summed in bfloat16 or wider, within the bound.
No kernel may reach another device: no remote copies, remote signals or barrier semaphores. Data moves between devices by JAX's collectives and lax.ppermute only.
A program may use at most 192 MiB of HBM per device.

v0:
```python
import jax
import jax.numpy as jnp
from jax import lax
from jax.experimental import pallas as pl
from jax.experimental.pallas import tpu as pltpu
from jax.sharding import PartitionSpec as P

D = 768
HEADS = 12
HEAD_DIM = 64
FF = 3072
L = 384
HALF = D // 2
F32 = jnp.float32
BF = jnp.bfloat16
I32 = jnp.int32
NT = (((1,), (1,)), ((), ()))
TN = (((0,), (0,)), ((), ()))
VM = pltpu.VMEM
DMA = pltpu.SemaphoreType.DMA
MIB = 1024 * 1024
LN2 = 0.6931471805599453
GAIN, SHIFT = slice(0, D), slice(D, 2 * D)
FIRST, SECOND = 2 * D, 2 * D + FF
VECTOR = 3 * D + FF


def dot(a, b):
    return jnp.dot(a, b, preferred_element_type=F32)


def dot_nt(a, b):
    return lax.dot_general(a, b, NT, preferred_element_type=F32)


def dot_tn(a, b):
    return lax.dot_general(a, b, TN, preferred_element_type=F32)


def norm_parts(x):
    center = x - jnp.mean(x, axis=-1, keepdims=True)
    inv = lax.rsqrt(jnp.mean(center * center, axis=-1, keepdims=True) + 1e-06)
    return center * inv, inv


def swap_halves(a):
    lane = lax.broadcasted_iota(I32, (1, 128), 1)
    first = (lane % HEAD_DIM) < HEAD_DIM // 2
    out = []
    for i in range(a.shape[1] // 128):
        s = a[:, 128 * i : 128 * (i + 1)]
        out.append(jnp.where(first, pltpu.roll(s, 96, 1), pltpu.roll(s, 32, 1)))
    return jnp.concatenate(out, axis=1) if len(out) > 1 else out[0]


def lanes(start, size):
    if isinstance(start, int):
        return slice(start, start + size)
    return pl.ds(pl.multiple_of(start, 128), size)


def rows_at(start, size):
    if isinstance(start, int):
        return slice(start, start + size)
    return pl.ds(pl.multiple_of(start, size), size)


def cols(start, size):
    return (slice(None), pl.ds(start, size))


def pick(flag, want, own, oth, src, dst, sem):
    @pl.when(flag == want)
    def _():
        pltpu.make_async_copy(own.at[src], dst, sem).start()

    @pl.when(flag != want)
    def _():
        pltpu.make_async_copy(oth.at[src], dst, sem).start()


def load(src, dst, sem):
    pltpu.make_async_copy(src, dst, sem).start()


def arrived(src, dst, sem):
    pltpu.make_async_copy(src, dst, sem).wait()


def load_attn(core, own, oth, wa, sems):
    for i in range(4):
        pick(core, 0, own, oth, cols(D * i, D), wa.at[i], sems.at[i])


def wait_attn(own, wa, sems, i):
    arrived(own.at[cols(D * i, D)], wa.at[i], sems.at[i])


def hidden_start(core, j):
    return pl.multiple_of(FF // 2 * ((core + j // 2) % 2) + D * (j % 2), 128)


def load_mlp(core, own, oth, w1, wd, sems):
    for j in range(4):
        pick(core, 1, own, oth, (slice(None), pl.ds(hidden_start(core, j), D)), w1.at[j], sems.at[j])
        load((own if j < 2 else oth).at[cols(FF + D * (j % 2), D)], wd.at[j], sems.at[4 + j])


def wait_mlp(own, w1, wd, sems, j):
    if w1 is not None:
        arrived(own.at[cols(0, D)], w1.at[j], sems.at[j])
    arrived(own.at[cols(0, D)], wd.at[j], sems.at[4 + j])


def vectors(core, own, oth):
    a, b = own[...], oth[...]
    return jnp.where(core == 0, a, b), jnp.where(core == 0, b, a)


def attention(x, vec, wa, wait, cosf, sinf, segc, segr, qkv, pt, rec, ml, mlt, vt, n_ref):
    xh, inv = norm_parts(x)
    n = (xh * vec[:, GAIN] + vec[:, SHIFT]).astype(BF)
    n_ref[...] = n
    for i in range(3):
        wait(i)
        part = dot(n, wa[i]) + vec[:, FIRST + D * i : FIRST + D * (i + 1)]
        if i < 2:
            part = part * cosf[...] + swap_halves(part) * sinf[...]
        if i == 0:
            part = part * (HEAD_DIM**-0.5 / LN2)
        qkv[:, D * i : D * (i + 1)] = part.astype(BF)
    vt[...] = qkv[:, 2 * D : 3 * D].T
    same = segc == segr
    lane = lax.broadcasted_iota(I32, (1, 128), 1)

    def score(h):
        p = 128 * (h // 2)
        keys = jnp.where((lane // HEAD_DIM) == h % 2, qkv[:, D + p : D + p + 128], BF(0))
        return dot_nt(keys, qkv[:, p : p + 128])

    ahead = score(0)
    for h in range(HEADS):
        st = ahead
        if h + 1 < HEADS:
            ahead = score(h + 1)
        st = jnp.where(same, st, -1e30)
        e = jnp.exp2(st - jnp.max(st, axis=0, keepdims=True))
        r = 1.0 / jnp.sum(e, axis=0, keepdims=True)
        rec[h : h + 1, :] = r
        e = e.astype(BF)
        pt[h] = e
        here = slice(HEAD_DIM * h, HEAD_DIM * (h + 1))
        mlt[here, :] = (dot(vt[here, :], e) * r).astype(BF)
    ml[...] = mlt[...].T
    wait(3)
    out = x + dot(ml[...], wa[3]) + vec[:, SECOND : SECOND + D]
    return out.astype(BF), xh, inv


C0 = 0.7978845608028654
C1 = 0.044715


def gelu(h):
    h2 = h * h
    t = jnp.tanh(C0 * (h + C1 * h * h2))
    half = 0.5 * (1.0 + t)
    return h * half, half + (0.5 * C0) * h * (1.0 - t * t) * (1.0 + (3.0 * C1) * h2)


def norm_back(gn, xh, inv, gain, c):
    u = gn * gain
    gx = inv * (
        u - jnp.mean(u, axis=-1, keepdims=True) - xh * jnp.mean(u * xh, axis=-1, keepdims=True)
    )
    return (c.astype(F32) + gx).astype(BF)


def head_select():
    head = lax.broadcasted_iota(I32, (16, D), 0)
    lane = lax.broadcasted_iota(I32, (16, D), 1)
    return jnp.where(lane // HEAD_DIM == head, 1.0, 0.0).astype(BF)


def split_two(a):
    hi = a.astype(BF)
    return hi, (a - hi.astype(F32)).astype(BF)


def attention_back(c, wo, cosf, sinf, qkv, pt, rec, ml, kt, gm, gqt, dsum, pair_of, emit):
    kt[...] = qkv[:, D : 2 * D].T
    gm_wide = dot_nt(c, wo[...])
    sel = head_select()
    hi, lo = split_two(gm_wide * ml[...].astype(F32))
    row = lax.broadcasted_iota(I32, (16, L), 0)
    recs = jnp.where(row < HEADS, rec[...], 0.0)
    dsum[...] = (dot_nt(sel, hi) + dot_nt(sel, lo)) * recs
    hi, lo = split_two(recs)
    gm[...] = (gm_wide * (dot_tn(hi, sel) + dot_tn(lo, sel))).astype(BF)
    lane = lax.broadcasted_iota(I32, (1, 128), 1)

    def spot(h):
        return lanes(128 * pair_of(h // 2), 128), (lane // HEAD_DIM) == h % 2

    def from_values(h):
        sl, here = spot(h)
        values = qkv[:, lanes(2 * D + 128 * pair_of(h // 2), 128)]
        return dot_nt(jnp.where(here, values, BF(0)), gm[:, sl])

    ahead = from_values(0)
    for h in range(HEADS):
        gpt = ahead
        if h + 1 < HEADS:
            ahead = from_values(h + 1)
        sl, here = spot(h)
        head = 2 * pair_of(h // 2) + h % 2
        e = pt[head]
        gvh = dot(e, jnp.where(here, gm[:, sl], BF(0)))
        gst = (e.astype(F32) * (gpt - dsum[rows_at(head, 1), :])).astype(BF)
        gkh = dot(gst, jnp.where(here, qkv[:, sl], BF(0)))
        kth = kt[rows_at(HEAD_DIM * head, HEAD_DIM), :]
        gqt[h // 2 % 2, HEAD_DIM * (h % 2) : HEAD_DIM * (h % 2 + 1), :] = dot(kth, gst)
        gv = gvh if h % 2 == 0 else gv + gvh
        gk = gkh if h % 2 == 0 else gk + gkh
        if h % 2 == 1:
            gq = gqt[h // 2 % 2].T * (HEAD_DIM**-0.5)
            gk = gk * LN2
            cs, sn = cosf[:, sl], sinf[:, sl]
            sq, sk = swap_halves(gq), swap_halves(gk)
            emit(
                h // 2, sl, sq, sk,
                ((gq * cs - sq * sn).astype(BF), (gk * cs - sk * sn).astype(BF), gv.astype(BF)),
            )


def positions_kernel(flags, grid, vown, voth, cosf, sinf, pos, segr):
    core = flags[0]
    vec = vectors(core, vown, voth)[0]
    h0, w0, h1, w1 = (grid[core, k // 2, k % 2] for k in range(4))
    e1 = h0 * w0
    e2 = e1 + h1 * w1

    def place(t):
        segment = (t >= e1).astype(I32) + (t >= e2).astype(I32)
        width = jnp.where(segment == 0, w0, w1).astype(F32)
        inside = (t - jnp.where(segment == 0, 0, e1)).astype(F32)
        row = jnp.floor((inside + 0.5) / width)
        column = inside - row * width
        return segment, jnp.where(segment < 2, row, 0.0), jnp.where(segment < 2, column, 0.0)

    segment, row, column = place(lax.broadcasted_iota(I32, (L, 128), 0))
    lane = lax.broadcasted_iota(I32, (L, 128), 1)
    pos[...] = jnp.where(lane == 0, column, jnp.where(lane == 1, row, segment.astype(F32)))
    t = lax.broadcasted_iota(I32, (8, L), 1)
    segr[...] = (t >= e1).astype(F32) + (t >= e2).astype(F32)

    def by_lane(start):
        parts = []
        for h in range(HEADS):
            f = vec[:, start + 32 * h : start + 32 * (h + 1)]
            parts += [f, f]
        return jnp.concatenate(parts, axis=1)

    number = lax.broadcasted_iota(I32, (16, D), 0).astype(F32)

    def look_up(which, table):
        hi, rest = split_two(table)
        mid, low = split_two(table - hi.astype(F32))
        tables = jnp.concatenate([hi, mid, low], axis=0)
        hit = (lax.broadcasted_iota(I32, (L, 48), 1) % 16).astype(F32) == which[:, :48]
        return dot(jnp.where(hit, 1.0, 0.0).astype(BF), tables)

    ax = number * by_lane(FIRST + 3 * D)
    ay = number * by_lane(FIRST + 3 * D + HALF)
    cx, sx = look_up(column, jnp.cos(ax)), look_up(column, jnp.sin(ax))
    cy, sy = look_up(row, jnp.cos(ay)), look_up(row, jnp.sin(ay))
    cosf[...] = cx * cy - sx * sy
    lane = lax.broadcasted_iota(I32, (1, D), 1)
    sign = jnp.where(lane % HEAD_DIM < HEAD_DIM // 2, -1.0, 1.0)
    sinf[...] = (sx * cy + cx * sy) * sign


def split_kernel(flags, x, cot, got, keep, send):
    core, layer = flags[0], flags[1]
    mine = jnp.where(layer == 0, x[...].astype(F32), cot[...].astype(F32)).astype(BF)
    other = got[...]
    w = mine.shape[1]
    for k in range(2):
        rows = slice(L * k, L * (k + 1))

        for at in range(2):
            first, second = (mine, other) if at == 0 else (other, mine)

            @pl.when((core == k) & (layer == at))
            def _(first=first, second=second, rows=rows):
                keep[:, :w] = first[rows]
                keep[:, w:] = second[rows]

            @pl.when((core != k) & (layer == at))
            def _(first=first, second=second, rows=rows):
                send[:, :w] = first[rows]
                send[:, w:] = second[rows]


def first_kernel(
    flags, keep, got, vown, voth, cos_in, sin_in, pos, segr, own, oth,
    field, out, wa, w1, wd, cosf, sinf, qkv, pt, rec, ml, mlt, vt, n_ref, sems,
):
    core = flags[0]
    load_attn(core, own, oth, wa, sems)
    load(cos_in, cosf, sems.at[12])
    load(sin_in, sinf, sems.at[13])
    load_mlp(core, own, oth, w1, wd, sems.at[pl.ds(4, 8)])
    w = keep.shape[1] // 2
    for k in range(2):

        @pl.when(core == k)
        def _(k=k):
            parts = (keep, got) if k == 0 else (got, keep)
            for s in range(4):
                field[:, w * s : w * (s + 1)] = parts[s % 2][:, w * (s // 2) : w * (s // 2 + 1)]

    va, vm = vectors(core, vown, voth)

    def wait(i):
        wait_attn(own, wa, sems, i)
        if i == 0:
            arrived(cos_in, cosf, sems.at[12])
            arrived(sin_in, sinf, sems.at[13])

    x_mid, _, _ = attention(
        field[...].astype(F32), va, wa, wait, cosf, sinf, pos[:, 2:3], segr[0:1, :],
        qkv, pt, rec, ml, mlt, vt, n_ref,
    )
    x = x_mid.astype(F32)
    xh, _ = norm_parts(x)
    n = (xh * vm[:, GAIN] + vm[:, SHIFT]).astype(BF)
    for j in range(4):
        wait_mlp(own, w1, wd, sems.at[pl.ds(4, 8)], j)
    acc = x + vm[:, SECOND : SECOND + D]
    first = jnp.where(core == 0, vm[:, FIRST:SECOND], jnp.concatenate(
        [vm[:, FIRST + FF // 2 : SECOND], vm[:, FIRST : FIRST + FF // 2]], axis=1))
    ahead = dot(n, w1[0])
    for j in range(4):
        h = ahead + first[:, D * j : D * (j + 1)]
        if j < 3:
            ahead = dot(n, w1[j + 1])
        acc = acc + dot_nt(gelu(h)[0].astype(BF), wd[j])
    out[...] = acc.astype(BF)


def second_kernel(
    flags, field, got, vown, voth, cos_in, sin_in, pos, segr, own, oth,
    cx, xm_out, qkv_out, pt_out, rec_out, ml_out, mlt_out, na_out, nm_out, actm_out, acts_out, dg_out,
    wa, w1, wd, cosf, sinf, qkv, pt, rec, ml, mlt, vt, na, nm, xm, actm, acts, dg, xha, xhm,
    kt, gm, gqt, dsum, gp, sems, outs,
):
    core, layer = flags[0], flags[1]
    load_attn(core, own, oth, wa, sems)
    load(cos_in, cosf, sems.at[12])
    load(sin_in, sinf, sems.at[13])
    mlp_sems = sems.at[pl.ds(4, 8)]
    load_mlp(core, own, oth, w1, wd, mlp_sems)
    va, vm = vectors(core, vown, voth)
    sent = []

    def send(src, dst):
        copy = pltpu.make_async_copy(src, dst, outs.at[len(sent)])
        copy.start()
        sent.append(copy)

    def wait(i):
        wait_attn(own, wa, sems, i)
        if i == 0:
            arrived(cos_in, cosf, sems.at[12])
            arrived(sin_in, sinf, sems.at[13])

    x = jnp.where(layer == 0, field[...].astype(F32), got[...].astype(F32))
    x_mid, xh, inv_a = attention(
        x, va, wa, wait, cosf, sinf, pos[:, 2:3], segr[0:1, :], qkv, pt, rec, ml, mlt, vt, na
    )
    xha[...] = xh
    xm[...] = x_mid
    send(qkv, qkv_out)
    send(pt, pt_out)
    send(rec, rec_out)
    send(ml, ml_out)
    send(mlt, mlt_out)
    send(na, na_out)
    send(xm, xm_out)
    xh, inv_m = norm_parts(x_mid.astype(F32))
    xhm[...] = xh
    n = (xh * vm[:, GAIN] + vm[:, SHIFT]).astype(BF)
    nm[...] = n
    send(nm, nm_out)
    for j in range(4):
        wait_mlp(own, w1, wd, mlp_sems, j)
    first = jnp.where(core == 0, vm[:, FIRST:SECOND], jnp.concatenate(
        [vm[:, FIRST + FF // 2 : SECOND], vm[:, FIRST : FIRST + FF // 2]], axis=1))
    c = field[...]
    ahead = dot(n, w1[0]), dot(c, wd[0])
    gn = None
    for j in range(4):
        h, ga = ahead
        h = h + first[:, D * j : D * (j + 1)]
        if j < 3:
            ahead = dot(n, w1[j + 1]), dot(c, wd[j + 1])
        act, slope = gelu(h)
        (actm, acts)[j // 2][:, D * (j % 2) : D * (j % 2 + 1)] = act.astype(BF)
        slope = slope.astype(BF)
        dg[:, D * j : D * (j + 1)] = slope
        part = dot_nt((ga * slope.astype(F32)).astype(BF), w1[j])
        gn = part if gn is None else gn + part
    send(actm, actm_out)
    send(acts, acts_out)
    send(dg, dg_out)
    c = norm_back(gn, xhm[...], inv_m, vm[:, GAIN], c)

    def emit(p, sl, sq, sk, grads):
        for i in range(3):
            gp[:, D * i + 128 * p : D * i + 128 * (p + 1)] = grads[i]

    attention_back(
        c, wa.at[3], cosf, sinf, qkv, pt, rec, ml, kt, gm, gqt, dsum, lambda p: p, emit
    )
    gn = None
    for i in range(3):
        part = dot_nt(gp[:, D * i : D * (i + 1)], wa[i])
        gn = part if gn is None else gn + part
    cx[...] = norm_back(gn, xha[...], inv_a, va[:, GAIN], c)
    for copy in sent:
        copy.wait()


def late_kernel(flags, xm, nm, na, actm, acts, vown, voth, own, oth, out, nmt, nat, wd, sems):
    for j in range(4):
        load((own if j < 2 else oth).at[cols(FF + D * (j % 2), D)], wd.at[j], sems.at[4 + j])
    vm = vectors(flags[0], vown, voth)[1]
    nmt[...] = nm[...].T
    nat[...] = na[...].T
    acc = xm[...].astype(F32) + vm[:, SECOND : SECOND + D]
    for j in range(4):
        wait_mlp(own, None, wd, sems, j)
        acc = acc + dot_nt((actm, acts)[j // 2][:, D * (j % 2) : D * (j % 2 + 1)], wd[j])
    out[...] = acc.astype(BF)


def norm_stats(gn, x, ggain, gshift):
    xh, inv = norm_parts(x)
    ggain[...] = jnp.sum(gn * xh, axis=0, keepdims=True)
    gshift[...] = jnp.sum(gn, axis=0, keepdims=True)
    return xh, inv


def mlp_back_kernel(
    flags, field, got, xm, vown, voth, dg_in, own, oth,
    cm, cmm, cms, ghm, ghs, ggain, gshift, gbias, gsec, w1, wd, dg, sems,
):
    core, layer = flags[0], flags[1]
    for j in range(4):
        load(dg_in.at[cols(D * j, D)], dg.at[j], sems.at[8 + j])
        pick(core, 1, own, oth, (slice(None), pl.ds(hidden_start(core, j), D)), w1.at[j], sems.at[j])
        load((own if j < 2 else oth).at[cols(FF + D * (j % 2), D)], wd.at[j], sems.at[4 + j])
    vm = vectors(core, vown, voth)[1]
    wide = jnp.where(layer == 0, got[...].astype(F32), field[...].astype(F32))
    c = wide.astype(BF)
    gsec[...] = jnp.sum(wide, axis=0, keepdims=True)

    def back(j):
        wait_mlp(own, w1, wd, sems, j)
        arrived(dg_in.at[cols(0, D)], dg.at[j], sems.at[8 + j])
        return dot(c, wd[j])

    ahead = back(0)
    gn = None
    for j in range(4):
        ga = ahead
        if j < 3:
            ahead = back(j + 1)
        gh = (ga * dg[j].astype(F32)).astype(BF)
        (ghm, ghs)[j // 2][:, D * (j % 2) : D * (j % 2 + 1)] = gh
        gbias[:, pl.ds(hidden_start(core, j), D)] = jnp.sum(gh.astype(F32), axis=0, keepdims=True)
        part = dot_nt(gh, w1[j])
        gn = part if gn is None else gn + part
    xh, inv = norm_stats(gn, xm[...].astype(F32), ggain, gshift)
    cm[...] = norm_back(gn, xh, inv, vm[:, GAIN], c)
    cmm[...] = cm[:, lanes(HALF * core, HALF)]
    cms[...] = cm[:, lanes(HALF * (1 - core), HALF)]


def attn_back_kernel(
    flags, field, got, c_ref, vown, voth, pos, rec, cos_in, sin_in, qkv_in, pt_in, ml_in, own, oth,
    cx, gpm, gps, ggain, gshift, gbias, gfx, gfy, gsec,
    wo, wbuf, cosf, sinf, qkv, pt, ml, kt, gm, gqt, dsum, sems,
):
    core, layer = flags[0], flags[1]
    pick(core, 0, own, oth, cols(3 * D, D), wo, sems.at[0])
    loads = [(qkv_in, qkv), (ml_in, ml), (pt_in, pt), (cos_in, cosf), (sin_in, sinf)]
    for k, (src, dst) in enumerate(loads):
        load(src, dst, sems.at[7 + k])
    for m in range(2):
        for i in range(3):
            start = pl.multiple_of(D * i + HALF * ((core + m) % 2), 128)
            pick(
                core, 0, own, oth, (slice(None), pl.ds(start, HALF)),
                wbuf.at[m, :, pl.ds(HALF * i, HALF)], sems.at[1 + 3 * m + i],
            )
    va = vectors(core, vown, voth)[0]
    c = c_ref[...]
    gsec[...] = jnp.sum(c.astype(F32), axis=0, keepdims=True)
    colp, rowp = pos[:, 0:1], pos[:, 1:2]
    arrived(own.at[cols(3 * D, D)], wo, sems.at[0])
    for k, (src, dst) in enumerate(loads):
        arrived(src, dst, sems.at[7 + k])

    def pair_of(p):
        return 3 * ((core + p // 3) % 2) + p % 3

    def emit(p, sl, sq, sk, grads):
        pair = pair_of(p)
        qr = qkv[:, sl].astype(F32) * (LN2 * HEAD_DIM**0.5)
        th = sq * qr + sk * qkv[:, lanes(D + 128 * pair, 128)].astype(F32)
        gfx[:, sl] = jnp.sum(th * colp, axis=0, keepdims=True)
        gfy[:, sl] = jnp.sum(th * rowp, axis=0, keepdims=True)
        at = p % 3
        for i, g in enumerate(grads):
            (gpm, gps)[p // 3][:, HALF * i + 128 * at : HALF * i + 128 * (at + 1)] = g
            gbias[:, lanes(D * i + 128 * pair, 128)] = jnp.sum(g.astype(F32), axis=0, keepdims=True)

    attention_back(c, wo, cosf, sinf, qkv, pt, rec, ml, kt, gm, gqt, dsum, pair_of, emit)
    for m in range(2):
        for i in range(3):
            arrived(own.at[cols(0, HALF)], wbuf.at[m, :, pl.ds(HALF * i, HALF)], sems.at[1 + 3 * m + i])
    gn = dot_nt(gpm[...], wbuf[0]) + dot_nt(gps[...], wbuf[1])
    x = jnp.where(layer == 0, field[...].astype(F32), got[...].astype(F32))
    xh, inv = norm_stats(gn, x, ggain, gshift)
    cx[...] = norm_back(gn, xh, inv, va[:, GAIN], c)


def gram_down_kernel(flags, f0, f1, g0, g1, a0, a1, out):
    first = flags[1] == 0
    c0 = jnp.where(first, g0[...].astype(F32), f0[...].astype(F32)).astype(BF)
    c1 = jnp.where(first, g1[...].astype(F32), f1[...].astype(F32)).astype(BF)
    out[...] = (dot_tn(c0, a0[...]) + dot_tn(c1, a1[...])).astype(BF)


def gram_up_kernel(n0, n1, h0, h1, out):
    out[...] = (dot(n0[...], h0[...]) + dot(n1[...], h1[...])).astype(BF)


def gram_attn_kernel(n0, n1, g0, g1, l0, l1, c0, c1, out):
    out[:, : 3 * HALF] = (dot(n0[...], g0[...]) + dot(n1[...], g1[...])).astype(BF)
    out[:, 3 * HALF :] = (dot(l0[...], c0[...]) + dot(l1[...], c1[...])).astype(BF)


def collect_kernel(flags, *refs):
    out = refs[-1]
    shards = refs[:-1]
    r = shards[0].shape[0]

    @pl.when(flags[0] == 0)
    def _():
        for k in range(len(shards) // 2):
            out[r * k : r * (k + 1), :D] = shards[2 * k][:, 2 * D :]
            out[r * k : r * (k + 1), D:] = shards[2 * k + 1][:, :D]

    @pl.when(flags[0] == 1)
    def _():
        for k in range(len(shards) // 2):
            out[r * k : r * (k + 1), :] = shards[2 * k + 1][:, D:]


def place_kernel(flags, rows, *refs):
    out, buf, sems = refs[-3:]
    count = sems.shape[0]
    shards, got = refs[: 2 * count], refs[2 * count]
    r = shards[0].shape[0]

    @pl.when(flags[0] == 0)
    def _():
        for k in range(count):
            one, two, there = shards[2 * k], shards[2 * k + 1], pl.ds(r * k, r)
            for g in range(4):
                sl = slice(HALF * g, HALF * (g + 1))
                buf[there, D * g : D * g + HALF] = two[:, D + HALF * g : D + HALF * (g + 1)].astype(F32)
                buf[there, D * g + HALF : D * (g + 1)] = got[there, sl].astype(F32)
            buf[there, 4 * D :] = one[:, : 2 * D].astype(F32)

    @pl.when(flags[0] == 1)
    def _():
        for k in range(count):
            one, two, there = shards[2 * k], shards[2 * k + 1], pl.ds(r * k, r)
            buf[there, : 2 * D] = got[there, :].astype(F32)
            buf[there, 2 * D : 3 * D] = one[:, 2 * D :].astype(F32)
            buf[there, 3 * D : 4 * D] = two[:, :D].astype(F32)
            buf[there, 4 * D :] = one[:, : 2 * D].astype(F32)

    copies = []
    for k in range(count):
        start = pl.multiple_of(rows[k], 8)
        copies.append(
            pltpu.make_async_copy(buf.at[pl.ds(r * k, r), :], out.at[pl.ds(start, r), :], sems.at[k])
        )
    for copy in copies:
        copy.start()
    for copy in copies:
        copy.wait()


SMEM = pl.BlockSpec(memory_space=pltpu.SMEM)
VS = pl.BlockSpec(memory_space=pltpu.VMEM)
HBM = pl.BlockSpec(memory_space=pltpu.HBM)


def sds(shape, dtype=BF):
    return jax.ShapeDtypeStruct(shape, dtype)


def call(kernel, name, in_specs, outs, scratch, flops, nbytes, limit=58, out_specs=None, aliases=None):
    return pl.pallas_call(
        kernel,
        name=name,
        in_specs=in_specs,
        out_specs=[VS] * len(outs) if out_specs is None else out_specs,
        out_shape=outs,
        scratch_shapes=scratch,
        input_output_aliases={} if aliases is None else aliases,
        compiler_params=pltpu.CompilerParams(vmem_limit_bytes=limit * MIB),
        cost_estimate=pl.CostEstimate(flops=flops, bytes_accessed=nbytes, transcendentals=0),
    )


ATTN_W = [VM((4, D, D), BF)]
MLP_W = [VM((4, D, D), BF), VM((4, D, D), BF)]
ANGLES = [VM((L, D), F32), VM((L, D), F32)]
ATTN_S = [
    VM((L, 3 * D), BF), VM((HEADS, L, L), BF), VM((16, L), F32), VM((L, D), BF), VM((D, L), BF),
    VM((D, L), BF),
]
BACK_S = [VM((D, L), BF), VM((L, D), BF), VM((2, 128, L), F32), VM((16, L), F32)]


def positions(flags, grid, vown, voth):
    return call(
        positions_kernel, "positions", [SMEM, SMEM, VS, VS],
        [sds((L, D), F32), sds((L, D), F32), sds((L, 128), F32), sds((8, L), F32)],
        [], int(1e8), int(3e6), 30,
    )(flags, grid, vown, voth)


def split_rows(flags, x, cot, got):
    out = sds((L, 2 * x.shape[1]))
    return call(split_kernel, "split", [SMEM, VS, VS, VS], [out, out], [], 1000, int(1e6), 20)(
        flags, x, cot, got
    )


def first_pass(*a):
    return call(
        first_kernel, "first_pass", [SMEM] + [VS] * 4 + [HBM] * 2 + [VS] * 2 + [HBM] * 2,
        [sds((L, D)), sds((L, D))],
        ATTN_W + MLP_W + ANGLES + ATTN_S + [VM((L, D), BF), DMA((14,))],
        int(8e9), int(20e6),
    )(*a)


def second_pass(*a):
    saved = [
        sds((L, D)), sds((L, 3 * D)), sds((HEADS, L, L)), sds((16, L), F32), sds((L, D)), sds((D, L)),
        sds((L, D)), sds((L, D)), sds((L, FF // 2)), sds((L, FF // 2)), sds((L, FF)),
    ]
    return call(
        second_kernel, "second_pass", [SMEM] + [VS] * 4 + [HBM] * 2 + [VS] * 2 + [HBM] * 2,
        [sds((L, D))] + saved,
        ATTN_W + MLP_W + ANGLES + ATTN_S
        + [VM((L, D), BF), VM((L, D), BF), VM((L, D), BF), VM((L, FF // 2), BF), VM((L, FF // 2), BF),
           VM((L, FF), BF), VM((L, D), F32), VM((L, D), F32)]
        + BACK_S + [VM((L, 3 * D), BF), DMA((14,)), DMA((11,))],
        int(18e9), int(35e6), out_specs=[VS] + [HBM] * len(saved),
    )(*a)


def late_pass(*a):
    return call(
        late_kernel, "late_pass", [SMEM] + [VS] * 7 + [HBM] * 2,
        [sds((L, D)), sds((D, L)), sds((D, L))], [VM((4, D, D), BF), DMA((8,))], int(2e9), int(10e6),
    )(*a)


def mlp_back(*a):
    return call(
        mlp_back_kernel, "mlp_back", [SMEM] + [VS] * 5 + [HBM] * 3,
        [sds((L, D)), sds((L, HALF)), sds((L, HALF)), sds((L, FF // 2)), sds((L, FF // 2)),
         sds((1, D), F32), sds((1, D), F32), sds((1, FF), F32), sds((1, D), F32)],
        MLP_W + [VM((4, L, D), BF), DMA((12,))], int(4e9), int(14e6),
    )(*a)


def attn_back(*a):
    return call(
        attn_back_kernel, "attn_back", [SMEM] + [VS] * 7 + [HBM] * 7,
        [sds((L, D)), sds((L, 3 * HALF)), sds((L, 3 * HALF)), sds((1, D), F32), sds((1, D), F32),
         sds((1, 3 * D), F32), sds((1, D), F32), sds((1, D), F32), sds((1, D), F32)],
        [VM((D, D), BF), VM((2, D, 3 * HALF), BF)] + ANGLES
        + [VM((L, 3 * D), BF), VM((HEADS, L, L), BF), VM((L, D), BF)] + BACK_S + [DMA((12,))],
        int(6e9), int(14e6),
    )(*a)


def gram(kernel, name, specs, *a):
    return call(kernel, name, specs, [sds((D, 2 * D))], [], int(2e9), int(6e6))(*a)[0]


def collect(flags, shards):
    r = shards[0].shape[0]
    out = [sds((r * (len(shards) // 2), 2 * D))]
    return call(collect_kernel, "collect", [SMEM] + [VS] * len(shards), out, [], 1000, int(1e6))(
        flags, *shards
    )[0]


def place(flags, rows, shards, got, total):
    r, count = shards[0].shape[0], len(shards) // 2
    into = [] if total is None else [total]
    return call(
        place_kernel, "place", [SMEM, SMEM] + [VS] * (len(shards) + 1) + [HBM] * len(into),
        [sds((D, 6 * D), F32)],
        [VM((r * count, 6 * D), F32), DMA((count,))], 1000, int(2e6),
        out_specs=[HBM], aliases={len(shards) + 3: 0} if into else {},
    )(flags, rows, *shards, got, *into)[0]


def core_swap(a):
    return lax.ppermute(a, "section", [(0, 1), (1, 0), (2, 3), (3, 2)])


class Ring:
    def __init__(self, parts, base, direction, n, where):
        self.parts, self.base, self.n, self.where, self.d = parts, base, n, where, direction
        self.r = D // (2 * n)
        order = list(range(0, n, 2)) + list(range(n - 1, 0, -2))
        self.pairs = [(order[i], order[(i + direction) % n]) for i in range(n)]
        self.cur = self.own(0)
        self.shards = []

    def start(self, t):
        return self.base + ((self.where - self.d * t) % self.n) * self.r

    def own(self, t):
        at = self.start(t)
        return jnp.concatenate(
            [lax.dynamic_slice(a, (at, first), (self.r, size)) for a, first, size in self.parts], axis=1
        )

    def step(self, t):
        got = lax.ppermute(self.cur, "dp", self.pairs)
        if t < self.n - 1:
            self.cur = got + self.own(t + 1)
            if t == self.n - 2:
                self.shards.append((self.start(-1), self.cur))
        else:
            self.cur = got
            self.shards.append((self.start(t - self.n + 1), got))


def summed_weight_grad(flags, one, two):
    n = lax.axis_size("dp")
    if n > 16:
        one, two = lax.psum(
            tuple(
                jnp.concatenate([a[:, first : first + size] for a, first, size in parts], axis=1)
                for parts in (one, two)
            ),
            "dp",
        )
        got = core_swap(collect(flags, [one, two]))
        return place(flags, jnp.zeros((1,), I32), [one, two], got, None)
    i = lax.axis_index("dp")
    where = jnp.where(i % 2 == 0, i // 2, n - 1 - i // 2)
    rings = [Ring(parts, base, d, n, where) for parts in (one, two) for base, d in ((0, 1), (HALF, -1))]
    total = None
    done = 0
    groups = (3, 3, 1, 1)
    marks = [sum(groups[: k + 1]) for k in range(len(groups))]
    for t in range(2 * n - 2):
        for ring in rings:
            ring.step(t)
        have = len(rings[0].shards)
        if have in marks:
            up, down, up_two, down_two = (ring.shards[done:have] for ring in rings)
            shards, rows = [], []
            for a, b in list(zip(up, up_two)) + list(zip(down, down_two)):
                shards += [a[1], b[1]]
                rows.append(a[0])
            got = core_swap(collect(flags, shards))
            total = place(flags, jnp.stack(rows).astype(I32), shards, got, total)
            done = have
    return total


def summed_vector(v):
    n = lax.axis_size("dp")
    if n & (n - 1):
        return lax.psum(v, "dp")
    hop = 1
    while hop < n:
        v = v + lax.ppermute(v, "dp", [(i, i ^ hop) for i in range(n)])
        hop *= 2
    return v


def after(value, first):
    return lax.optimization_barrier((value, first))[0]


def body(
    block_input, cotangent, grid_sizes, section_weight, norm_gain, norm_bias, first_vector, second_vector
):
    section = lax.axis_index("section")
    core = section % 2
    flags = jnp.stack([core, section // 2]).astype(I32)
    first_core = core == 0
    first_layer = section < 2

    away = jnp.where(first_layer, cotangent, block_input)
    got = lax.ppermute(away, "section", [(0, 2), (1, 3), (2, 0), (3, 1)])
    own = section_weight[0]
    oth = core_swap(own)
    vown = jnp.concatenate([norm_gain[0], norm_bias[0], first_vector[0], second_vector[0]])[None]
    voth = core_swap(vown)
    keep, send = split_rows(flags, block_input, cotangent, got)
    angles = positions(flags, grid_sizes, vown, voth)
    cosf, sinf, pos, segr = angles

    field, x_two = first_pass(
        flags, keep, core_swap(send), vown, voth, cosf, sinf, pos, segr, own, oth
    )
    x_got = lax.ppermute(x_two, "section", [(0, 2), (1, 3)])
    c_two, x_mid, qkv, pt, rec, ml, mlt, n_a, n_m, act_mine, act_send, dg = second_pass(
        flags, field, x_got, vown, voth, cosf, sinf, pos, segr, own, oth
    )
    c_got = lax.ppermute(c_two, "section", [(2, 0), (3, 1)])
    x_four, nt_m, nt_a = late_pass(flags, x_mid, n_m, n_a, act_mine, act_send, vown, voth, own, oth)
    x_out = jnp.where(first_layer, x_two, x_four)

    c_mid, c_mid_mine, c_mid_send, gh_mine, gh_send, ggain_m, gshift_m, gbias_m, gsec_m = mlp_back(
        flags, field, c_got, x_mid, vown, voth, dg, own, oth
    )
    gh_oth = core_swap(gh_send)
    down = gram(
        gram_down_kernel, "gram_down", [SMEM] + [VS] * 6, flags, field, core_swap(field), c_got,
        core_swap(c_got), act_mine, core_swap(act_send),
    )
    up = gram(gram_up_kernel, "gram_up", [VS] * 4, nt_m, core_swap(nt_m), gh_mine, gh_oth)
    c_in, gp_mine, gp_send, ggain_a, gshift_a, gbias_a, gfx, gfy, gsec_a = attn_back(
        flags, field, x_got, after(c_mid, up), vown, voth, pos, rec, cosf, sinf, qkv, pt, ml, own, oth
    )
    attn = gram(
        gram_attn_kernel, "gram_attn", [VS] * 8, nt_a, core_swap(nt_a), gp_mine, core_swap(gp_send),
        mlt, core_swap(mlt), c_mid_mine, core_swap(c_mid_send),
    )
    weight_grad = summed_weight_grad(
        flags, [(down, 0, 2 * D), (up, 0, D)], [(up, D, D), (attn, 0, 2 * D)]
    )

    def fold(v):
        pairs = v.reshape(HEADS, 2, HEAD_DIM // 2)
        return (pairs[:, 0] - pairs[:, 1]).reshape(1, -1)

    vg_a = jnp.concatenate([ggain_a, gshift_a, gbias_a, fold(gfx), fold(gfy), gsec_a], axis=1)
    vg_m = jnp.concatenate([ggain_m, gshift_m, gbias_m, gsec_m], axis=1)
    vg = jnp.where(first_core, vg_a, vg_m) + core_swap(jnp.where(first_core, vg_m, vg_a))
    vg = summed_vector(vg)

    def rows_of(attn_row, mlp_row):
        got = core_swap(jnp.where(first_core, mlp_row, attn_row))
        kept = jnp.where(first_core, attn_row, mlp_row)
        above, below = jnp.where(first_core, kept, got), jnp.where(first_core, got, kept)
        return jnp.concatenate([above, below], axis=0)[None]

    return (
        rows_of(x_mid, x_out),
        rows_of(c_in, c_mid),
        weight_grad[None],
        vg[:, GAIN],
        vg[:, SHIFT],
        vg[:, FIRST:SECOND],
        vg[:, SECOND:],
    )


def solution(mesh):
    in_specs = (
        P("dp", "section"),
        P("dp", "section"),
        P("dp", None, None),
        P("section", None, None),
        P("section", None),
        P("section", None),
        P("section", None),
        P("section", None),
    )
    out_specs = (
        P("section", "dp", None),
        P("section", "dp", None),
        P("section", None, None),
        P("section", None),
        P("section", None),
        P("section", None),
        P("section", None),
    )
    return jax.shard_map(body, mesh=mesh, in_specs=in_specs, out_specs=out_specs, check_vma=False)
```

profile of v0, /device:TPU:0, one launch (start us, length us, event | category | flops | bytes accessed | tf_op | source)
XLA Modules:
  0.0 378.9 jit_solution(14892048066391553106)
XLA Ops:
  6.2 9.7 %collective-permute-done.got = bf16[768,192]{1,0:T(8,128)(2,1)S(1)} collective-permute-done((bf16[768,192]{1,0:T(8,128)(2,1)S(1)}, bf16[768,192]{1,0:T(8,128)(2,1)S(1)}, u32[]{:S(2)}, u32[]{:S(2)}) %collective-permute-start) | collective-permute-done | bytes 294944 | tf_op jit(solution)/shard_map/ppermute | solution.py:826
  25.1 15.7 %first_pass.1 = (bf16[384,768]{1,0:T(8,128)(2,1)}, bf16[384,768]{1,0:T(8,128)(2,1)}) custom-call(s32[2]{0:T(128)} %copy-done.5, bf16[384,384]{1,0:T(8,128)(2,1)} %copy-done.6, bf16[384,384]{1,0:T(8,128)(2,1)} %copy-done.77, f32[1,5376]{1,0:T(1,128)} %copy-done.2, f32[1,5376]{1,0:T(1,128)} %copy-done.4, f32[384,768]{1,0:T(8,128)} %copy-done, ...), custom_call_target="tpu_custom_call" | custom-call | flops 8000000000 | bytes 20000000 | tf_op jit(solution)/shard_map/first_pass/pallas_call | solution.py:659
  40.9 3.9 %collective-permute-start.4 = (bf16[384,768]{1,0:T(8,128)(2,1)}, bf16[384,768]{1,0:T(8,128)(2,1)S(1)}, u32[]{:S(2)}, u32[]{:S(2)}) collective-permute-start(bf16[384,768]{1,0:T(8,128)(2,1)} %get-tuple-element.56), channel_id=1, source_target_pairs={{0,16},{8,24},{1,17},{9,25},{2,18},{10,26},{3,19},{11,27},{4,20},{... | collective-permute-start | bytes 1769480 | tf_op jit(solution)/shard_map/ppermute | solution.py:838
  44.8 13.1 %collective-permute-done.4.got = bf16[384,768]{1,0:T(8,128)(2,1)S(1)} collective-permute-done((bf16[384,768]{1,0:T(8,128)(2,1)}, bf16[384,768]{1,0:T(8,128)(2,1)S(1)}, u32[]{:S(2)}, u32[]{:S(2)}) %collective-permute-start.4) | collective-permute-done | bytes 589856 | tf_op jit(solution)/shard_map/ppermute | solution.py:838
  58.7 28.3 %second_pass.1 = (bf16[384,768]{1,0:T(8,128)(2,1)}, bf16[384,768]{1,0:T(8,128)(2,1)}, bf16[384,2304]{1,0:T(8,128)(2,1)}, bf16[12,384,384]{2,1,0:T(8,128)(2,1)}, ...) custom-call(s32[2]{0:T(128)} %copy-done.5, ...), custom_call_target="tpu_custom_call" | custom-call | flops 17999998976 | bytes 35000000 | tf_op jit(solution)/shard_map/second_pass/pallas_call | solution.py:672
  89.4 14.5 %collective-permute-done.6.got.g0 = bf16[384,768]{1,0:T(8,128)(2,1)S(1)} collective-permute-done((bf16[384,768]{1,0:T(8,128)(2,1)}, bf16[384,768]{1,0:T(8,128)(2,1)S(1)}, u32[]{:S(2)}, u32[]{:S(2)}) %collective-permute-start.6) | collective-permute-done | bytes 589856 | tf_op jit(solution)/shard_map/ppermute | solution.py:842
  104.8 10.2 %mlp_back.1 = (bf16[384,768]{1,0:T(8,128)(2,1)}, bf16[384,384]{1,0:T(8,128)(2,1)}, bf16[384,384]{1,0:T(8,128)(2,1)}, bf16[384,1536]{1,0:T(8,128)(2,1)}, bf16[384...) custom-call(s32[2]{0:T(128)} %copy-done.5, ...), custom_call_target="tpu_custom_call" | custom-call | flops 4000000000 | bytes 14000000 | tf_op jit(solution)/shard_map/mlp_back/pallas_call | solution.py:691
  115.1 7.7 %late_pass.1 = (bf16[384,768]{1,0:T(8,128)(2,1)}, bf16[768,384]{1,0:T(8,128)(2,1)}, bf16[768,384]{1,0:T(8,128)(2,1)}) custom-call(s32[2]{0:T(128)} %copy-done.5, bf16[384,768]{1,0:T(8,128)(2,1)} %get-tuple-element.57.xm, bf16[384,768]{1,0:T(8,128)(2,1)} %get-tuple-element.58.nm, bf16[384,768]{1,0:T(8,128)(2,1)} %get-tuple-element.59.na, ...), custom_call_target="tpu_custom_call" | custom-call | flops 2000000000 | bytes 10000000 | tf_op jit(solution)/shard_map/late_pass/pallas_call | solution.py:684
  127.5 6.4 %gram_down.1 = bf16[768,1536]{1,0:T(8,128)(2,1)} custom-call(s32[2]{0:T(128)} %copy-done.5, bf16[384,768]{1,0:T(8,128)(2,1)} %get-tuple-element.55.field.f0, bf16[384,768]{1,0:T(8,128)(2,1)} %copy-done.74, bf16[384,768]{1,0:T(8,128)(2,1)} %copy-done.43, bf16[384,768]{1,0:T(8,128)(2,1)} %copy-done.76, bf16[384,1536]{1,0:T(8,128)(2,1)} %get-tuple-element.60.actm.a0, ...), custom_call_target="tpu_custom_call" | custom-call | flops 2000000000 | bytes 6000000 | tf_op jit(solution)/shard_map/gram_down/pallas_call | solution.py:711
  137.0 6.0 %gram_up.1 = bf16[768,1536]{1,0:T(8,128)(2,1)} custom-call(bf16[768,384]{1,0:T(8,128)(2,1)} %get-tuple-element.66.n0, bf16[768,384]{1,0:T(8,128)(2,1)} %copy-done.75, bf16[384,1536]{1,0:T(8,128)(2,1)} %get-tuple-element.67.h0, bf16[384,1536]{1,0:T(8,128)(2,1)} %copy-done.71), custom_call_target="tpu_custom_call" | custom-call | flops 2000000000 | bytes 6000000 | tf_op jit(solution)/shard_map/gram_up/pallas_call | solution.py:711
  142.9 3.1 constant_dynamic-slice_fusion.48
  146.0 15.2 %attn_back.1 = (bf16[384,768]{1,0:T(8,128)(2,1)}, bf16[384,1152]{1,0:T(8,128)(2,1)}, bf16[384,1152]{1,0:T(8,128)(2,1)}, f32[1,768]{1,0:T(1,128)}, f32[1,768]{1,0...) custom-call(s32[2]{0:T(128)} %copy-done.5, ...), custom_call_target="tpu_custom_call" | custom-call | flops 6000000000 | bytes 14000000 | tf_op jit(solution)/shard_map/attn_back/pallas_call | solution.py:700
  178.0 4.3 %collective-permute-done.13 = bf16[48,2304]{1,0:T(8,128)(2,1)S(1)} collective-permute-done((bf16[48,2304]{1,0:T(8,128)(2,1)S(1)}, bf16[48,2304]{1,0:T(8,128)(2,1)S(1)}, u32[]{:S(2)}, u32[]{:S(2)}) %collective-permute-start.13) | collective-permute-done | bytes 221216 | tf_op jit(solution)/shard_map/ppermute | solution.py:756
  184.8 3.4 collective-permute-done.46
  190.6 3.6 collective-permute-done.14
  195.9 4.2 %collective-permute-done.47 = bf16[48,2304]{1,0:T(8,128)(2,1)S(1)} collective-permute-done((bf16[48,2304]{1,0:T(8,128)(2,1)S(1)}, bf16[48,2304]{1,0:T(8,128)(2,1)S(1)}, u32[]{:S(2)}, u32[]{:S(2)}) %collective-permute-start.47) | collective-permute-done | bytes 221216 | tf_op jit(solution)/shard_map/ppermute | solution.py:756
  201.6 5.7 %collective-permute-done.15 = bf16[48,2304]{1,0:T(8,128)(2,1)S(1)} collective-permute-done((bf16[48,2304]{1,0:T(8,128)(2,1)S(1)}, bf16[48,2304]{1,0:T(8,128)(2,1)S(1)}, u32[]{:S(2)}, u32[]{:S(2)}) %collective-permute-start.15) | collective-permute-done | bytes 221216 | tf_op jit(solution)/shard_map/ppermute | solution.py:756
  211.1 6.5 %gram_attn.1 = bf16[768,1536]{1,0:T(8,128)(2,1)} custom-call(bf16[768,384]{1,0:T(8,128)(2,1)} %get-tuple-element.75.n0, bf16[768,384]{1,0:T(8,128)(2,1)} %collective-permute-done.27.n1, bf16[384,1152]{1,0:T(8,128)(2,1)} %get-tuple-element.76.g0, bf16[384,1152]{1,0:T(8,128)(2,1)} %copy-done.73, bf16[768,384]{1,0:T(8,128)(2,1)} %get-tuple-element.78.l0, ...), custom_call_target="tpu_custom_call" | custom-call | flops 2000000000 | bytes 6000000 | tf_op jit(solution)/shard_map/gram_attn/pallas_call | solution.py:711
  224.1 4.0 %collective-permute-done.59 = bf16[48,2304]{1,0:T(8,128)(2,1)S(1)} collective-permute-done((bf16[48,2304]{1,0:T(8,128)(2,1)S(1)}, bf16[48,2304]{1,0:T(8,128)(2,1)S(1)}, u32[]{:S(2)}, u32[]{:S(2)}) %collective-permute-start.59) | collective-permute-done | bytes 221216 | tf_op jit(solution)/shard_map/ppermute | solution.py:756
  263.4 2.6 collective-permute-done.63
  271.0 3.0 collective-permute-done.64
  276.3 5.8 %collective-permute-done.65 = bf16[48,2304]{1,0:T(8,128)(2,1)S(1)} collective-permute-done((bf16[48,2304]{1,0:T(8,128)(2,1)S(1)}, bf16[48,2304]{1,0:T(8,128)(2,1)S(1)}, u32[]{:S(2)}, u32[]{:S(2)}) %collective-permute-start.65) | collective-permute-done | bytes 221216 | tf_op jit(solution)/shard_map/ppermute | solution.py:756
  284.5 3.8 collective-permute-done.66.refs_9_
  292.5 4.1 %collective-permute-done.67.refs_11_ = bf16[48,2304]{1,0:T(8,128)(2,1)S(1)} collective-permute-done((bf16[48,2304]{1,0:T(8,128)(2,1)S(1)}, bf16[48,2304]{1,0:T(8,128)(2,1)S(1)}, u32[]{:S(2)}, u32[]{:S(2)}) %collective-permute-start.67) | collective-permute-done | bytes 221216 | tf_op jit(solution)/shard_map/ppermute | solution.py:756
  298.7 5.4 %collective-permute-done.78 = f32[1,5376]{1,0:T(1,128)S(1)} collective-permute-done((f32[1,5376]{1,0:T(1,128)S(1)}, f32[1,5376]{1,0:T(1,128)S(1)}, u32[]{:S(2)}, u32[]{:S(2)}) %collective-permute-start.78) | collective-permute-done | bytes 21536 | tf_op jit(solution)/shard_map/ppermute | solution.py:807
  315.1 3.1 collective-permute-done.40.refs_1_
  331.4 2.8 collect.7
  337.1 2.8 collect.6
  360.8 4.9 %place.4.refs_13_ = f32[768,4608]{1,0:T(8,128)} custom-call(s32[2]{0:T(128)} %copy-done.5, s32[6]{0:T(128)} %stack.91.rows, bf16[48,2304]{1,0:T(8,128)(2,1)} %copy-done.14, bf16[48,2304]{1,0:T(8,128)(2,1)} %copy-done.16, bf16[48,2304]{1,0:T(8,128)(2,1)} %copy-done.19, bf16[48,2304]{1,0:T(8,128)(2,1)} %copy-done.25, bf16[48,2304]{1,0:T(8,128)(2,1)} %copy-done.21, ...), custom_call_target="tpu_custom_call" | custom-call | flops 1000 | bytes 2000000 | tf_op jit(solution)/shard_map/place/pallas_call | solution.py:725
  366.6 4.9 %place.5.refs_5_ = f32[768,4608]{1,0:T(8,128)} custom-call(s32[2]{0:T(128)} %copy-done.5, s32[6]{0:T(128)} %stack.84.rows, bf16[48,2304]{1,0:T(8,128)(2,1)} %copy-done.23, bf16[48,2304]{1,0:T(8,128)(2,1)} %collective-permute-done.40.refs_1_, bf16[48,2304]{1,0:T(8,128)(2,1)} %collective-permute-done.23.refs_2_, ...), custom_call_target="tpu_custom_call", output_to_operand_aliasing={{}: (15, {})} | custom-call | flops 1000 | bytes 2000000 | tf_op jit(solution)/shard_map/place/pallas_call | solution.py:725
  372.2 2.7 place.6.refs_5_
  375.7 2.7 place.7
  (383 shorter events, 162.2 us)
Async XLA Ops:
  0.7 23.7 %collective-permute-start.3 = (bf16[768,4608]{1,0:T(8,128)(2,1)}, bf16[768,4608]{1,0:T(8,128)(2,1)}, u32[]{:S(2)}, u32[]{:S(2)}) collective-permute-start(bf16[768,4608]{1,0:T(8,128)(2,1)} %bitcast.26), channel_id=1, source_target_pairs={{0,8},{8,0},{16,24},{24,16},{1,9},{9,1},{17,25},{25,17},{2,10},{10... | collective-permute-start | bytes 21233672 | tf_op jit(solution)/shard_map/ppermute | solution.py:734
  3.5 12.4 %collective-permute-start = (bf16[768,192]{1,0:T(8,128)(2,1)S(1)}, bf16[768,192]{1,0:T(8,128)(2,1)S(1)}, u32[]{:S(2)}, u32[]{:S(2)}) collective-permute-start(bf16[768,192]{1,0:T(8,128)(2,1)S(1)} %broadcast_select_fusion.9), channel_id=1, source_target_pairs={{0,16},{8,24},{16,0},{24,8},{1,17},{9,25},{17,1},{25,9},{2,18},{10... | collective-permute-start | bytes 884744 | tf_op jit(solution)/shard_map/ppermute | solution.py:826
  40.9 17.0 %collective-permute-start.4 = (bf16[384,768]{1,0:T(8,128)(2,1)}, bf16[384,768]{1,0:T(8,128)(2,1)S(1)}, u32[]{:S(2)}, u32[]{:S(2)}) collective-permute-start(bf16[384,768]{1,0:T(8,128)(2,1)} %get-tuple-element.56), channel_id=1, source_target_pairs={{0,16},{8,24},{1,17},{9,25},{2,18},{10,26},{3,19},{11,27},{4,20},{... | collective-permute-start | bytes 1769480 | tf_op jit(solution)/shard_map/ppermute | solution.py:838
  87.0 16.9 %collective-permute-start.6 = (bf16[384,768]{1,0:T(8,128)(2,1)}, bf16[384,768]{1,0:T(8,128)(2,1)S(1)}, u32[]{:S(2)}, u32[]{:S(2)}) collective-permute-start(bf16[384,768]{1,0:T(8,128)(2,1)} %get-tuple-element.63), channel_id=1, source_target_pairs={{16,0},{24,8},{17,1},{25,9},{18,2},{26,10},{19,3},{27,11},{20,4},{... | collective-permute-start | bytes 1769480 | tf_op jit(solution)/shard_map/ppermute | solution.py:842
  88.8 34.7 %collective-permute-start.10 = (bf16[384,768]{1,0:T(8,128)(2,1)S(1)}, bf16[384,768]{1,0:T(8,128)(2,1)S(1)}, u32[]{:S(2)}, u32[]{:S(2)}) collective-permute-start(bf16[384,768]{1,0:T(8,128)(2,1)S(1)} %copy-done.12), channel_id=1, source_target_pairs={{0,8},{8,0},{16,24},{24,16},{1,9},{9,1},{17,25},{25,17},{2,10},{10... | collective-permute-start | bytes 1769480 | tf_op jit(solution)/shard_map/ppermute | solution.py:734
  88.9 35.1 %collective-permute-start.12 = (bf16[384,1536]{1,0:T(8,128)(2,1)}, bf16[384,1536]{1,0:T(8,128)(2,1)S(1)}, u32[]{:S(2)}, u32[]{:S(2)}) collective-permute-start(bf16[384,1536]{1,0:T(8,128)(2,1)} %get-tuple-element.61.acts), channel_id=1, source_target_pairs={{0,8},{8,0},{16,24},{24,16},{1,9},{9,1},{17,25},{25,17},{2,10},{10... | collective-permute-start | bytes 3538952 | tf_op jit(solution)/shard_map/ppermute | solution.py:734
  115.0 20.8 %collective-permute-start.8 = (bf16[384,1536]{1,0:T(8,128)(2,1)}, bf16[384,1536]{1,0:T(8,128)(2,1)S(1)}, u32[]{:S(2)}, u32[]{:S(2)}) collective-permute-start(bf16[384,1536]{1,0:T(8,128)(2,1)} %get-tuple-element.68), channel_id=1, source_target_pairs={{0,8},{8,0},{16,24},{24,16},{1,9},{9,1},{17,25},{25,17},{2,10},{10... | collective-permute-start | bytes 3538952 | tf_op jit(solution)/shard_map/ppermute | solution.py:734
  122.8 12.9 %collective-permute-start.7 = (bf16[768,384]{1,0:T(8,128)(2,1)}, bf16[768,384]{1,0:T(8,128)(2,1)S(1)}, u32[]{:S(2)}, u32[]{:S(2)}) collective-permute-start(bf16[768,384]{1,0:T(8,128)(2,1)} %get-tuple-element.66.n0), channel_id=1, source_target_pairs={{0,8},{8,0},{16,24},{24,16},{1,9},{9,1},{17,25},{25,17},{2,10},{10... | collective-permute-start | bytes 1769480 | tf_op jit(solution)/shard_map/ppermute | solution.py:734
  123.5 85.6 %collective-permute-start.27 = (bf16[768,384]{1,0:T(8,128)(2,1)}, bf16[768,384]{1,0:T(8,128)(2,1)}, u32[]{:S(2)}, u32[]{:S(2)}) collective-permute-start(bf16[768,384]{1,0:T(8,128)(2,1)} %get-tuple-element.75.n0), channel_id=1, source_target_pairs={{0,8},{8,0},{16,24},{24,16},{1,9},{9,1},{17,25},{25,17},{2,10},{10... | collective-permute-start | bytes 1769480 | tf_op jit(solution)/shard_map/ppermute | solution.py:734
  124.0 86.1 %collective-permute-start.29 = (bf16[768,384]{1,0:T(8,128)(2,1)}, bf16[768,384]{1,0:T(8,128)(2,1)}, u32[]{:S(2)}, u32[]{:S(2)}) collective-permute-start(bf16[768,384]{1,0:T(8,128)(2,1)} %get-tuple-element.78.l0), channel_id=1, source_target_pairs={{0,8},{8,0},{16,24},{24,16},{1,9},{9,1},{17,25},{25,17},{2,10},{10... | collective-permute-start | bytes 1769480 | tf_op jit(solution)/shard_map/ppermute | solution.py:734
  126.7 83.5 %collective-permute-start.30 = (bf16[384,384]{1,0:T(8,128)(2,1)}, bf16[384,384]{1,0:T(8,128)(2,1)}, u32[]{:S(2)}, u32[]{:S(2)}) collective-permute-start(bf16[384,384]{1,0:T(8,128)(2,1)} %get-tuple-element.80), channel_id=1, source_target_pairs={{0,8},{8,0},{16,24},{24,16},{1,9},{9,1},{17,25},{25,17},{2,10},{10... | collective-permute-start | bytes 884744 | tf_op jit(solution)/shard_map/ppermute | solution.py:734
  167.5 42.7 %collective-permute-start.28 = (bf16[384,1152]{1,0:T(8,128)(2,1)}, bf16[384,1152]{1,0:T(8,128)(2,1)S(1)}, u32[]{:S(2)}, u32[]{:S(2)}) collective-permute-start(bf16[384,1152]{1,0:T(8,128)(2,1)} %get-tuple-element.77), channel_id=1, source_target_pairs={{0,8},{8,0},{16,24},{24,16},{1,9},{9,1},{17,25},{25,17},{2,10},{10... | collective-permute-start | bytes 2654216 | tf_op jit(solution)/shard_map/ppermute | solution.py:734
  207.3 14.5 %collective-permute-start.48 = (bf16[48,2304]{1,0:T(8,128)(2,1)S(1)}, bf16[48,2304]{1,0:T(8,128)(2,1)S(1)}, u32[]{:S(2)}, u32[]{:S(2)}) collective-permute-start(bf16[48,2304]{1,0:T(8,128)(2,1)S(1)} %maximum_add_fusion.16), channel_id=1, source_target_pairs={{0,1},{2,0},{4,2},{6,4},{7,6},{5,7},{3,5},{1,3},{8,9},{10,8},{12,1... | collective-permute-start | bytes 663560 | tf_op jit(solution)/shard_map/ppermute | solution.py:756
  209.1 14.1 %collective-permute-start.16 = (bf16[48,2304]{1,0:T(8,128)(2,1)S(1)}, bf16[48,2304]{1,0:T(8,128)(2,1)S(1)}, u32[]{:S(2)}, u32[]{:S(2)}) collective-permute-start(bf16[48,2304]{1,0:T(8,128)(2,1)S(1)} %maximum_add_fusion.2), channel_id=1, source_target_pairs={{0,2},{2,4},{4,6},{6,7},{7,5},{5,3},{3,1},{1,0},{8,10},{10,12},{12... | collective-permute-start | bytes 663560 | tf_op jit(solution)/shard_map/ppermute | solution.py:756
  221.9 10.9 %collective-permute-start.49 = (bf16[48,2304]{1,0:T(8,128)(2,1)S(1)}, bf16[48,2304]{1,0:T(8,128)(2,1)S(1)}, u32[]{:S(2)}, u32[]{:S(2)}) collective-permute-start(bf16[48,2304]{1,0:T(8,128)(2,1)S(1)} %maximum_add_fusion.17), channel_id=1, source_target_pairs={{0,1},{2,0},{4,2},{6,4},{7,6},{5,7},{3,5},{1,3},{8,9},{10,8},{12,1... | collective-permute-start | bytes 663560 | tf_op jit(solution)/shard_map/ppermute | solution.py:756
  269.0 19.5 %collective-permute-start.54 = (bf16[48,2304]{1,0:T(8,128)(2,1)S(1)}, bf16[48,2304]{1,0:T(8,128)(2,1)S(1)}, u32[]{:S(2)}, u32[]{:S(2)}) collective-permute-start(bf16[48,2304]{1,0:T(8,128)(2,1)S(1)} %collective-permute-done.53.refs_10_), channel_id=1, source_target_pairs={{0,1},{2,0},{4,2},{6,4},{7,6},{5,7},{3,5},{1,3},{8,9},{10,8},{12,1... | collective-permute-start | bytes 663560 | tf_op jit(solution)/shard_map/ppermute | solution.py:756
  270.7 20.4 %collective-permute-start.22 = (bf16[48,2304]{1,0:T(8,128)(2,1)S(1)}, bf16[48,2304]{1,0:T(8,128)(2,1)S(1)}, u32[]{:S(2)}, u32[]{:S(2)}) collective-permute-start(bf16[48,2304]{1,0:T(8,128)(2,1)S(1)} %collective-permute-done.21.refs_4_), channel_id=1, source_target_pairs={{0,2},{2,4},{4,6},{6,7},{7,5},{5,3},{3,1},{1,0},{8,10},{10,12},{12... | collective-permute-start | bytes 663560 | tf_op jit(solution)/shard_map/ppermute | solution.py:756
  288.5 15.7 %collective-permute-start.55 = (bf16[48,2304]{1,0:T(8,128)(2,1)S(1)}, bf16[48,2304]{1,0:T(8,128)(2,1)}, u32[]{:S(2)}, u32[]{:S(2)}) collective-permute-start(bf16[48,2304]{1,0:T(8,128)(2,1)S(1)} %collective-permute-done.54.refs_6_), channel_id=1, source_target_pairs={{0,1},{2,0},{4,2},{6,4},{7,6},{5,7},{3,5},{1,3},{8,9},{10,8},{12,1... | collective-permute-start | bytes 663560 | tf_op jit(solution)/shard_map/ppermute | solution.py:756
  291.1 14.0 %collective-permute-start.23 = (bf16[48,2304]{1,0:T(8,128)(2,1)S(1)}, bf16[48,2304]{1,0:T(8,128)(2,1)}, u32[]{:S(2)}, u32[]{:S(2)}) collective-permute-start(bf16[48,2304]{1,0:T(8,128)(2,1)S(1)} %collective-permute-done.22.refs_0_), channel_id=1, source_target_pairs={{0,2},{2,4},{4,6},{6,7},{7,5},{5,3},{3,1},{1,0},{8,10},{10,12},{12... | collective-permute-start | bytes 663560 | tf_op jit(solution)/shard_map/ppermute | solution.py:756
  291.1 15.2 %collective-permute-start.39 = (bf16[48,2304]{1,0:T(8,128)(2,1)S(1)}, bf16[48,2304]{1,0:T(8,128)(2,1)}, u32[]{:S(2)}, u32[]{:S(2)}) collective-permute-start(bf16[48,2304]{1,0:T(8,128)(2,1)S(1)} %collective-permute-done.38.refs_3_), channel_id=1, source_target_pairs={{0,2},{2,4},{4,6},{6,7},{7,5},{5,3},{3,1},{1,0},{8,10},{10,12},{12... | collective-permute-start | bytes 663560 | tf_op jit(solution)/shard_map/ppermute | solution.py:756
  296.6 11.7 %collective-permute-start.68 = (bf16[48,2304]{1,0:T(8,128)(2,1)S(1)}, bf16[48,2304]{1,0:T(8,128)(2,1)}, u32[]{:S(2)}, u32[]{:S(2)}) collective-permute-start(bf16[48,2304]{1,0:T(8,128)(2,1)S(1)} %collective-permute-done.67.refs_11_), channel_id=1, source_target_pairs={{0,1},{2,0},{4,2},{6,4},{7,6},{5,7},{3,5},{1,3},{8,9},{10,8},{12,1... | collective-permute-start | bytes 663560 | tf_op jit(solution)/shard_map/ppermute | solution.py:756
  306.3 11.9 %collective-permute-start.40 = (bf16[48,2304]{1,0:T(8,128)(2,1)}, bf16[48,2304]{1,0:T(8,128)(2,1)}, u32[]{:S(2)}, u32[]{:S(2)}) collective-permute-start(bf16[48,2304]{1,0:T(8,128)(2,1)} %collective-permute-done.39.refs_5_), channel_id=1, source_target_pairs={{0,2},{2,4},{4,6},{6,7},{7,5},{5,3},{3,1},{1,0},{8,10},{10,12},{12... | collective-permute-start | bytes 663560 | tf_op jit(solution)/shard_map/ppermute | solution.py:756
  308.3 11.5 %collective-permute-start.69 = (bf16[48,2304]{1,0:T(8,128)(2,1)}, bf16[48,2304]{1,0:T(8,128)(2,1)}, u32[]{:S(2)}, u32[]{:S(2)}) collective-permute-start(bf16[48,2304]{1,0:T(8,128)(2,1)} %collective-permute-done.68.refs_7_), channel_id=1, source_target_pairs={{0,1},{2,0},{4,2},{6,4},{7,6},{5,7},{3,5},{1,3},{8,9},{10,8},{12,1... | collective-permute-start | bytes 663560 | tf_op jit(solution)/shard_map/ppermute | solution.py:756
  309.4 30.5 %collective-permute-start.5 = (bf16[384,768]{1,0:T(8,128)(2,1)}, bf16[384,768]{1,0:T(8,128)(2,1)}, u32[]{:S(2)}, u32[]{:S(2)}) collective-permute-start(bf16[384,768]{1,0:T(8,128)(2,1)} %get-tuple-element.91), channel_id=1, source_target_pairs={{0,8},{8,0},{16,24},{24,16},{1,9},{9,1},{17,25},{25,17},{2,10},{10... | collective-permute-start | bytes 1769480 | tf_op jit(solution)/shard_map/ppermute | solution.py:734
  322.4 17.5 %collective-permute-start.80 = (f32[1,5376]{1,0:T(1,128)S(1)}, f32[1,5376]{1,0:T(1,128)S(1)}, u32[]{:S(2)}, u32[]{:S(2)}) collective-permute-start(f32[1,5376]{1,0:T(1,128)S(1)} %add.423), channel_id=1, source_target_pairs={{0,4},{1,5},{2,6},{3,7},{4,0},{5,1},{6,2},{7,3},{8,12},{9,13},{10,... | collective-permute-start | bytes 64520 | tf_op jit(solution)/shard_map/ppermute | solution.py:807
  324.6 15.9 %collective-permute-start.58 = (bf16[48,2304]{1,0:T(8,128)(2,1)S(1)}, bf16[48,2304]{1,0:T(8,128)(2,1)S(1)}, u32[]{:S(2)}, u32[]{:S(2)}) collective-permute-start(bf16[48,2304]{1,0:T(8,128)(2,1)S(1)} %collective-permute-done.57.refs_2_), channel_id=1, source_target_pairs={{0,1},{2,0},{4,2},{6,4},{7,6},{5,7},{3,5},{1,3},{8,9},{10,8},{12,1... | collective-permute-start | bytes 663560 | tf_op jit(solution)/shard_map/ppermute | solution.py:756
  325.9 16.2 %collective-permute-start.26 = (bf16[48,2304]{1,0:T(8,128)(2,1)S(1)}, bf16[48,2304]{1,0:T(8,128)(2,1)S(1)}, u32[]{:S(2)}, u32[]{:S(2)}) collective-permute-start(bf16[48,2304]{1,0:T(8,128)(2,1)S(1)} %collective-permute-done.25.refs_0_), channel_id=1, source_target_pairs={{0,2},{2,4},{4,6},{6,7},{7,5},{5,3},{3,1},{1,0},{8,10},{10,12},{12... | collective-permute-start | bytes 663560 | tf_op jit(solution)/shard_map/ppermute | solution.py:756
  336.4 22.1 %collective-permute-start.9 = (bf16[384,768]{1,0:T(8,128)(2,1)}, bf16[384,768]{1,0:T(8,128)(2,1)}, u32[]{:S(2)}, u32[]{:S(2)}) collective-permute-start(bf16[384,768]{1,0:T(8,128)(2,1)} %broadcast_select_fusion.3), channel_id=1, source_target_pairs={{0,8},{8,0},{16,24},{24,16},{1,9},{9,1},{17,25},{25,17},{2,10},{10... | collective-permute-start | bytes 1769480 | tf_op jit(solution)/shard_map/ppermute | solution.py:734
  339.9 20.9 %collective-permute-start.76 = (bf16[288,1536]{1,0:T(8,128)(2,1)S(1)}, bf16[288,1536]{1,0:T(8,128)(2,1)}, u32[]{:S(2)}, u32[]{:S(2)}) collective-permute-start(bf16[288,1536]{1,0:T(8,128)(2,1)S(1)} %copy-done.39), channel_id=1, source_target_pairs={{0,8},{8,0},{16,24},{24,16},{1,9},{9,1},{17,25},{25,17},{2,10},{10... | collective-permute-start | bytes 2654216 | tf_op jit(solution)/shard_map/ppermute | solution.py:734
  340.0 25.7 %collective-permute-start.75 = (bf16[288,1536]{1,0:T(8,128)(2,1)}, bf16[288,1536]{1,0:T(8,128)(2,1)S(1)}, u32[]{:S(2)}, u32[]{:S(2)}) collective-permute-start(bf16[288,1536]{1,0:T(8,128)(2,1)} %collect.6), channel_id=1, source_target_pairs={{0,8},{8,0},{16,24},{24,16},{1,9},{9,1},{17,25},{25,17},{2,10},{10... | collective-permute-start | bytes 2654216 | tf_op jit(solution)/shard_map/ppermute | solution.py:734
  354.7 16.8 %collective-permute-start.74 = (bf16[96,1536]{1,0:T(8,128)(2,1)}, bf16[96,1536]{1,0:T(8,128)(2,1)S(1)}, u32[]{:S(2)}, u32[]{:S(2)}) collective-permute-start(bf16[96,1536]{1,0:T(8,128)(2,1)} %collect.5), channel_id=1, source_target_pairs={{0,8},{8,0},{16,24},{24,16},{1,9},{9,1},{17,25},{25,17},{2,10},{10... | collective-permute-start | bytes 884744 | tf_op jit(solution)/shard_map/ppermute | solution.py:734
  358.5 16.5 %collective-permute-start.73 = (bf16[96,1536]{1,0:T(8,128)(2,1)}, bf16[96,1536]{1,0:T(8,128)(2,1)S(1)}, u32[]{:S(2)}, u32[]{:S(2)}) collective-permute-start(bf16[96,1536]{1,0:T(8,128)(2,1)} %collect.4), channel_id=1, source_target_pairs={{0,8},{8,0},{16,24},{24,16},{1,9},{9,1},{17,25},{25,17},{2,10},{10... | collective-permute-start | bytes 884744 | tf_op jit(solution)/shard_map/ppermute | solution.py:734
  (127 other events, 1671.9 us)
where the time goes:
time: 383 us; the launch traced here: 379 us
  waiting for transfers between devices  126 us (33%)
  Pallas kernels  124 us (32%)
  starting transfers between devices  78.2 us (20%)
  local copies, waits for them, and re-layouts  33.8 us (9%)
  other arithmetic  14.9 us (4%)
    ppermute x56, waiting for transfers between devices, step(): got = lax.ppermute(self.cur, 'dp', self.pairs)  79.5 us
    ppermute x56, starting transfers between devices, step(): got = lax.ppermute(self.cur, 'dp', self.pairs)  61.5 us
    pallas_call x1, Pallas kernels, second_pass(): call(second_kernel, 'second_pass', [SMEM] + [VS] * 4 + [HBM] * 2 + [VS] *...  28.3 us
    unnamed x166, local copies, waits for them, and re-layouts  20.8 us
    pallas_call x3, Pallas kernels, gram(): call(kernel, name, specs, [sds((D, 2 * D))], [], int(2000000000.0), int(6...  18.9 us
    pallas_call x1, Pallas kernels, first_pass(): call(first_kernel, 'first_pass', [SMEM] + [VS] * 4 + [HBM] * 2 + [VS] * 2...  15.7 us
    pallas_call x1, Pallas kernels, attn_back(): call(attn_back_kernel, 'attn_back', [SMEM] + [VS] * 7 + [HBM] * 7, [sds((...  15.2 us
    pallas_call x4, Pallas kernels, place(): call(place_kernel, 'place', [SMEM, SMEM] + [VS] * (len(shards) + 1) + [HB...  15.2 us
  transfers between devices with their start and end apart: 81, of which 37 were waited for; matrix products, arithmetic and copies ran while one was open for 9% of the time, Pallas kernels for 20%

commit v1 on v0

v1 whole, which is shorter than its diff:
```python
import jax
import jax.numpy as jnp
from jax import lax
from jax.experimental import pallas as pl
from jax.experimental.pallas import tpu as pltpu
from jax.sharding import PartitionSpec as P

D = 768
HEADS = 12
HEAD_DIM = 64
FF = 3072
L = 384
HALF = D // 2
F32 = jnp.float32
BF = jnp.bfloat16
I32 = jnp.int32
NT = (((1,), (1,)), ((), ()))
TN = (((0,), (0,)), ((), ()))
VM = pltpu.VMEM
DMA = pltpu.SemaphoreType.DMA
MIB = 1024 * 1024
LN2 = 0.6931471805599453
GAIN, SHIFT = slice(0, D), slice(D, 2 * D)
FIRST, SECOND = 2 * D, 2 * D + FF
VECTOR = 3 * D + FF


def dot(a, b):
    return jnp.dot(a, b, preferred_element_type=F32)


def dot_nt(a, b):
    return lax.dot_general(a, b, NT, preferred_element_type=F32)


def dot_tn(a, b):
    return lax.dot_general(a, b, TN, preferred_element_type=F32)


def norm_parts(x):
    center = x - jnp.mean(x, axis=-1, keepdims=True)
    inv = lax.rsqrt(jnp.mean(center * center, axis=-1, keepdims=True) + 1e-06)
    return center * inv, inv


def swap_halves(a):
    lane = lax.broadcasted_iota(I32, (1, 128), 1)
    first = (lane % HEAD_DIM) < HEAD_DIM // 2
    out = []
    for i in range(a.shape[1] // 128):
        s = a[:, 128 * i : 128 * (i + 1)]
        out.append(jnp.where(first, pltpu.roll(s, 96, 1), pltpu.roll(s, 32, 1)))
    return jnp.concatenate(out, axis=1) if len(out) > 1 else out[0]


def lanes(start, size):
    if isinstance(start, int):
        return slice(start, start + size)
    return pl.ds(pl.multiple_of(start, 128), size)


def rows_at(start, size):
    if isinstance(start, int):
        return slice(start, start + size)
    return pl.ds(pl.multiple_of(start, size), size)


def cols(start, size):
    return (slice(None), pl.ds(start, size))


def pick(flag, want, own, oth, src, dst, sem):
    @pl.when(flag == want)
    def _():
        pltpu.make_async_copy(own.at[src], dst, sem).start()

    @pl.when(flag != want)
    def _():
        pltpu.make_async_copy(oth.at[src], dst, sem).start()


def load(src, dst, sem):
    pltpu.make_async_copy(src, dst, sem).start()


def arrived(src, dst, sem):
    pltpu.make_async_copy(src, dst, sem).wait()


def load_attn(core, own, oth, wa, sems, i):
    pick(core, 0, own, oth, cols(D * i, D), wa.at[i], sems.at[i])


def wait_attn(own, wa, sems, i):
    arrived(own.at[cols(D * i, D)], wa.at[i], sems.at[i])


def hidden_start(core, j):
    return pl.multiple_of(FF // 2 * ((core + j // 2) % 2) + D * (j % 2), 128)


def load_mlp(core, own, oth, w1, wd, sems, j):
    pick(core, 1, own, oth, (slice(None), pl.ds(hidden_start(core, j), D)), w1.at[j], sems.at[j])
    load((own if j < 2 else oth).at[cols(FF + D * (j % 2), D)], wd.at[j], sems.at[4 + j])


class Forward:
    def __init__(self, core, own, oth, wa, w1, wd, cos_in, sin_in, cosf, sinf, sems, angle_sems):
        self.attn = core, own, oth, wa, sems
        self.mlp = core, own, oth, w1, wd, sems.at[pl.ds(4, 8)]
        self.angles = cos_in, sin_in, cosf, sinf, angle_sems
        self.own, self.wa, self.sems = own, wa, sems
        load_attn(*self.attn, 0)
        load_angles(*self.angles)
        load_attn(*self.attn, 1)

    def wait(self, what):
        if what == "angles":
            wait_angles(*self.angles)
            return
        wait_attn(self.own, self.wa, self.sems, what)
        if what < 2:
            load_attn(*self.attn, what + 2)
        elif what == 2:
            for j in range(4):
                load_mlp(*self.mlp, j)

    def wait_mlp(self):
        core, own, oth, w1, wd, sems = self.mlp
        for j in range(4):
            wait_mlp(own, w1, wd, sems, j)


def wait_mlp(own, w1, wd, sems, j):
    if w1 is not None:
        arrived(own.at[cols(0, D)], w1.at[j], sems.at[j])
    arrived(own.at[cols(0, D)], wd.at[j], sems.at[4 + j])


def vectors(core, own, oth):
    a, b = own[...], oth[...]
    return jnp.where(core == 0, a, b), jnp.where(core == 0, b, a)


def attention(x, vec, wa, wait, cosf, sinf, segc, segr, qkv, pt, rec, ml, mlt, vt, n_ref):
    xh, inv = norm_parts(x)
    n = (xh * vec[:, GAIN] + vec[:, SHIFT]).astype(BF)
    n_ref[...] = n
    for i in range(3):
        wait(i)
        part = dot(n, wa[i]) + vec[:, FIRST + D * i : FIRST + D * (i + 1)]
        if i == 0:
            wait("angles")
        if i < 2:
            part = part * cosf[...] + swap_halves(part) * sinf[...]
        if i == 0:
            part = part * (HEAD_DIM**-0.5 / LN2)
        qkv[:, D * i : D * (i + 1)] = part.astype(BF)
    vt[...] = qkv[:, 2 * D : 3 * D].T
    same = segc == segr
    lane = lax.broadcasted_iota(I32, (1, 128), 1)

    def score(h):
        p = 128 * (h // 2)
        keys = jnp.where((lane // HEAD_DIM) == h % 2, qkv[:, D + p : D + p + 128], BF(0))
        return dot_nt(keys, qkv[:, p : p + 128])

    ahead = score(0)
    for h in range(HEADS):
        st = ahead
        if h + 1 < HEADS:
            ahead = score(h + 1)
        st = jnp.where(same, st, -1e30)
        e = jnp.exp2(st - jnp.max(st, axis=0, keepdims=True))
        r = 1.0 / jnp.sum(e, axis=0, keepdims=True)
        rec[h : h + 1, :] = r
        e = e.astype(BF)
        pt[h] = e
        here = slice(HEAD_DIM * h, HEAD_DIM * (h + 1))
        mlt[here, :] = (dot(vt[here, :], e) * r).astype(BF)
    ml[...] = mlt[...].T
    wait(3)
    out = x + dot(ml[...], wa[3]) + vec[:, SECOND : SECOND + D]
    return out.astype(BF), xh, inv


C0 = 0.7978845608028654
C1 = 0.044715


def gelu(h):
    h2 = h * h
    t = jnp.tanh(C0 * (h + C1 * h * h2))
    half = 0.5 * (1.0 + t)
    return h * half, half + (0.5 * C0) * h * (1.0 - t * t) * (1.0 + (3.0 * C1) * h2)


def norm_back(gn, xh, inv, gain, c):
    u = gn * gain
    gx = inv * (
        u - jnp.mean(u, axis=-1, keepdims=True) - xh * jnp.mean(u * xh, axis=-1, keepdims=True)
    )
    return (c.astype(F32) + gx).astype(BF)


def head_select():
    head = lax.broadcasted_iota(I32, (16, D), 0)
    lane = lax.broadcasted_iota(I32, (16, D), 1)
    return jnp.where(lane // HEAD_DIM == head, 1.0, 0.0).astype(BF)


def split_two(a):
    hi = a.astype(BF)
    return hi, (a - hi.astype(F32)).astype(BF)


def attention_back(c, wo, cosf, sinf, qkv, pt, rec, ml, kt, gm, gqt, dsum, pair_of, emit):
    kt[...] = qkv[:, D : 2 * D].T
    gm_wide = dot_nt(c, wo[...])
    sel = head_select()
    hi, lo = split_two(gm_wide * ml[...].astype(F32))
    row = lax.broadcasted_iota(I32, (16, L), 0)
    recs = jnp.where(row < HEADS, rec[...], 0.0)
    dsum[...] = (dot_nt(sel, hi) + dot_nt(sel, lo)) * recs
    hi, lo = split_two(recs)
    gm[...] = (gm_wide * (dot_tn(hi, sel) + dot_tn(lo, sel))).astype(BF)
    lane = lax.broadcasted_iota(I32, (1, 128), 1)

    def spot(h):
        return lanes(128 * pair_of(h // 2), 128), (lane // HEAD_DIM) == h % 2

    def from_values(h):
        sl, here = spot(h)
        values = qkv[:, lanes(2 * D + 128 * pair_of(h // 2), 128)]
        return dot_nt(jnp.where(here, values, BF(0)), gm[:, sl])

    ahead = from_values(0)
    for h in range(HEADS):
        gpt = ahead
        if h + 1 < HEADS:
            ahead = from_values(h + 1)
        sl, here = spot(h)
        head = 2 * pair_of(h // 2) + h % 2
        e = pt[head]
        gvh = dot(e, jnp.where(here, gm[:, sl], BF(0)))
        gst = (e.astype(F32) * (gpt - dsum[rows_at(head, 1), :])).astype(BF)
        gkh = dot(gst, jnp.where(here, qkv[:, sl], BF(0)))
        kth = kt[rows_at(HEAD_DIM * head, HEAD_DIM), :]
        gqt[h // 2 % 2, HEAD_DIM * (h % 2) : HEAD_DIM * (h % 2 + 1), :] = dot(kth, gst)
        gv = gvh if h % 2 == 0 else gv + gvh
        gk = gkh if h % 2 == 0 else gk + gkh
        if h % 2 == 1:
            gq = gqt[h // 2 % 2].T * (HEAD_DIM**-0.5)
            gk = gk * LN2
            cs, sn = cosf[:, sl], sinf[:, sl]
            sq, sk = swap_halves(gq), swap_halves(gk)
            emit(
                h // 2, sl, sq, sk,
                ((gq * cs - sq * sn).astype(BF), (gk * cs - sk * sn).astype(BF), gv.astype(BF)),
            )


def positions_kernel(flags, grid, vown, voth, cosf, sinf, pos, segr):
    core = flags[0]
    vec = vectors(core, vown, voth)[0]
    h0, w0, h1, w1 = (grid[core, k // 2, k % 2] for k in range(4))
    e1 = h0 * w0
    e2 = e1 + h1 * w1

    def place(t):
        segment = (t >= e1).astype(I32) + (t >= e2).astype(I32)
        width = jnp.where(segment == 0, w0, w1).astype(F32)
        inside = (t - jnp.where(segment == 0, 0, e1)).astype(F32)
        row = jnp.floor((inside + 0.5) / width)
        column = inside - row * width
        return segment, jnp.where(segment < 2, row, 0.0), jnp.where(segment < 2, column, 0.0)

    segment, row, column = place(lax.broadcasted_iota(I32, (L, 128), 0))
    lane = lax.broadcasted_iota(I32, (L, 128), 1)
    pos[...] = jnp.where(lane == 0, column, jnp.where(lane == 1, row, segment.astype(F32)))
    t = lax.broadcasted_iota(I32, (8, L), 1)
    segr[...] = (t >= e1).astype(F32) + (t >= e2).astype(F32)

    def by_lane(start):
        parts = []
        for h in range(HEADS):
            f = vec[:, start + 32 * h : start + 32 * (h + 1)]
            parts += [f, f]
        return jnp.concatenate(parts, axis=1)

    number = lax.broadcasted_iota(I32, (16, D), 0).astype(F32)

    def look_up(which, table):
        hi, rest = split_two(table)
        mid, low = split_two(table - hi.astype(F32))
        tables = jnp.concatenate([hi, mid, low], axis=0)
        hit = (lax.broadcasted_iota(I32, (L, 48), 1) % 16).astype(F32) == which[:, :48]
        return dot(jnp.where(hit, 1.0, 0.0).astype(BF), tables)

    ax = number * by_lane(FIRST + 3 * D)
    ay = number * by_lane(FIRST + 3 * D + HALF)
    cx, sx = look_up(column, jnp.cos(ax)), look_up(column, jnp.sin(ax))
    cy, sy = look_up(row, jnp.cos(ay)), look_up(row, jnp.sin(ay))
    cosf[...] = cx * cy - sx * sy
    lane = lax.broadcasted_iota(I32, (1, D), 1)
    sign = jnp.where(lane % HEAD_DIM < HEAD_DIM // 2, -1.0, 1.0)
    sinf[...] = (sx * cy + cx * sy) * sign


def prepare_kernel(
    flags, x, cot, gain, shift, first, second, keep, send, away, across, vec
):
    core, layer = flags[0], flags[1]
    for at, (mine, other) in enumerate(((x, cot), (cot, x))):

        @pl.when(layer == at)
        def _(mine=mine, other=other):
            keep[...] = mine[:, lanes(L * core, L)]
            send[...] = mine[:, lanes(L * (1 - core), L)]
            away[...] = other[:, lanes(L * core, L)]
            across[...] = other[:, lanes(L * (1 - core), L)]

    vec[:, GAIN] = gain[...]
    vec[:, SHIFT] = shift[...]
    vec[:, FIRST:SECOND] = first[...]
    vec[:, SECOND:] = second[...]


def load_angles(cos_in, sin_in, cosf, sinf, sems):
    load(cos_in, cosf, sems.at[0])
    load(sin_in, sinf, sems.at[1])


def wait_angles(cos_in, sin_in, cosf, sinf, sems):
    arrived(cos_in, cosf, sems.at[0])
    arrived(sin_in, sinf, sems.at[1])


def first_kernel(
    flags, keep, got, away, across, vown, voth, pos, segr, cos_in, sin_in, own, oth,
    out, field_out, wa, w1, wd, cosf, sinf, field, turned, qkv, pt, rec, ml, mlt, vt, n_ref, sems, angle_sems,
):
    core, layer = flags[0], flags[1]
    w = keep.shape[0]
    for k in range(2):
        for at in range(2):

            @pl.when((core == k) & (layer == at))
            def _(k=k, at=at):
                parts = {(at, k): keep, (at, 1 - k): got, (1 - at, k): away, (1 - at, 1 - k): across}
                for s in range(4):
                    turned[w * s : w * (s + 1), :] = parts[s // 2, s % 2][...]

    field[...] = turned[...].T
    keeping = pltpu.make_async_copy(field, field_out, sems.at[12])
    keeping.start()
    @pl.when(layer == 0)
    def _():
        loads = Forward(core, own, oth, wa, w1, wd, cos_in, sin_in, cosf, sinf, sems, angle_sems)
        va, vm = vectors(core, vown, voth)
        x_mid, _, _ = attention(
            field[...].astype(F32), va, wa, loads.wait, cosf, sinf, pos[:, 2:3], segr[0:1, :],
            qkv, pt, rec, ml, mlt, vt, n_ref,
        )
        x = x_mid.astype(F32)
        xh, _ = norm_parts(x)
        n = (xh * vm[:, GAIN] + vm[:, SHIFT]).astype(BF)
        loads.wait_mlp()
        acc = x + vm[:, SECOND : SECOND + D]
        first = hidden_bias(core, vm)
        ahead = dot(n, w1[0])
        for j in range(4):
            h = ahead + first[:, D * j : D * (j + 1)]
            if j < 3:
                ahead = dot(n, w1[j + 1])
            acc = acc + dot_nt(gelu(h)[0].astype(BF), wd[j])
        out[...] = acc.astype(BF)

    keeping.wait()


def hidden_bias(core, vm):
    a, b = vm[:, FIRST : FIRST + FF // 2], vm[:, FIRST + FF // 2 : SECOND]
    return jnp.concatenate([jnp.where(core == 0, a, b), jnp.where(core == 0, b, a)], axis=1)


def second_kernel(
    flags, field, got, vown, voth, pos, segr, cos_in, sin_in, own, oth,
    cx, xi_out, xm_out, qkv_out, pt_out, rec_out, ml_out, actm_out, acts_out, dg_out,
    main_out, tail_out, main_send, tail_send,
    wa, w1, wd, cosf, sinf, xi, xm, qkv, pt, rec, ml, na, nm, actm, acts, dg,
    mlt, vt, xha, xhm, kt, gm, gqt, dsum, gp, sems, angle_sems, outs,
):
    core, layer = flags[0], flags[1]
    loads = Forward(core, own, oth, wa, w1, wd, cos_in, sin_in, cosf, sinf, sems, angle_sems)
    va, vm = vectors(core, vown, voth)
    sent = []

    def send(src, dst):
        copy = pltpu.make_async_copy(src, dst, outs.at[len(sent)])
        copy.start()
        sent.append(copy)

    x = jnp.where(layer == 0, field[...].astype(F32), got[...].astype(F32))
    xi[...] = x.astype(BF)
    send(xi, xi_out)
    x_mid, xh, inv_a = attention(
        x, va, wa, loads.wait, cosf, sinf, pos[:, 2:3], segr[0:1, :], qkv, pt, rec, ml, mlt, vt, na
    )
    xha[...] = xh
    xm[...] = x_mid
    for src, dst in ((xm, xm_out), (qkv, qkv_out), (pt, pt_out), (rec, rec_out), (ml, ml_out)):
        send(src, dst)
    xh, inv_m = norm_parts(x_mid.astype(F32))
    xhm[...] = xh
    n = (xh * vm[:, GAIN] + vm[:, SHIFT]).astype(BF)
    nm[...] = n
    for when, sources in ((core == 0, (na, ml, nm, nm)), (core != 0, (nm, nm, na, ml))):

        @pl.when(when)
        def _(sources=sources):
            for k, (src, dst) in enumerate(zip(sources, (main_out, tail_out, main_send, tail_send))):
                load(src, dst, outs.at[9 + k])

    loads.wait_mlp()
    first = hidden_bias(core, vm)
    c = field[...]

    def forward(j):
        return dot(n, w1[j])

    def chunk(j, h):
        act, slope = gelu(h + first[:, D * j : D * (j + 1)])
        (actm, acts)[j // 2][:, D * (j % 2) : D * (j % 2 + 1)] = act.astype(BF)
        slope = slope.astype(BF)
        dg[:, D * j : D * (j + 1)] = slope
        return slope

    def leave():
        for k, (src, dst) in enumerate(((actm, actm_out), (acts, acts_out), (dg, dg_out))):
            load(src, dst, outs.at[6 + k])

    @pl.when(layer == 0)
    def _():
        ahead = forward(0)
        for j in range(4):
            h = ahead
            if j < 3:
                ahead = forward(j + 1)
            chunk(j, h)
        leave()

    @pl.when(layer != 0)
    def _():
        ahead = forward(0), dot(c, wd[0])
        gn = None
        for j in range(4):
            h, ga = ahead
            if j < 3:
                ahead = forward(j + 1), dot(c, wd[j + 1])
            slope = chunk(j, h)
            part = dot_nt((ga * slope.astype(F32)).astype(BF), w1[j])
            gn = part if gn is None else gn + part
        leave()
        c_mid = norm_back(gn, xhm[...], inv_m, vm[:, GAIN], c)

        def emit(p, sl, sq, sk, grads):
            for i in range(3):
                gp[:, D * i + 128 * p : D * i + 128 * (p + 1)] = grads[i]

        attention_back(
            c_mid, wa.at[3], cosf, sinf, qkv, pt, rec, ml, kt, gm, gqt, dsum, lambda p: p, emit
        )
        gn = None
        for i in range(3):
            part = dot_nt(gp[:, D * i : D * (i + 1)], wa[i])
            gn = part if gn is None else gn + part
        cx[...] = norm_back(gn, xha[...], inv_a, va[:, GAIN], c_mid)

    for copy in sent:
        copy.wait()
    for k, (src, dst) in enumerate(
        ((actm, actm_out), (acts, acts_out), (dg, dg_out), (nm, main_out), (nm, tail_out), (nm, main_send),
         (nm, tail_send))
    ):
        arrived(src, dst, outs.at[6 + k])


def late_kernel(flags, xm, x_two, actm, acts, vown, voth, own, oth, keep, send, wd, sems):
    core, layer = flags[0], flags[1]
    for j in range(4):
        load((own if j < 2 else oth).at[cols(FF + D * (j % 2), D)], wd.at[j], sems.at[4 + j])
    vm = vectors(core, vown, voth)[1]
    mid = xm[...].astype(F32)
    acc = mid + vm[:, SECOND : SECOND + D]
    for j in range(4):
        wait_mlp(own, None, wd, sems, j)
        acc = acc + dot_nt((actm, acts)[j // 2][:, D * (j % 2) : D * (j % 2 + 1)], wd[j])
    acc = jnp.where(layer == 0, x_two[...].astype(F32), acc)
    keep[...] = jnp.where(core == 0, mid, acc).astype(BF)
    send[...] = jnp.where(core == 0, acc, mid).astype(BF)


def both_rows_kernel(flags, keep, got, out):
    core = flags[0]
    out[rows_at(L * core, L), :] = keep[...]
    out[rows_at(L * (1 - core), L), :] = got[...]


def norm_stats(gn, x, vec):
    xh, inv = norm_parts(x)
    vec[:, GAIN] = jnp.sum(gn * xh, axis=0, keepdims=True)
    vec[:, SHIFT] = jnp.sum(gn, axis=0, keepdims=True)
    return xh, inv


def back_kernel(
    flags, field, got, vown, voth, pos, xi_in, xm_in, dg_in, qkv_in, pt_in, rec_in, ml_in, cos_in, sin_in,
    own, oth,
    row_keep, row_send, va_grad, vm_grad, c_out, keep_out, send_out,
    wa, w1, wd, cosf, sinf, xi, xm, dg, qkv, pt, rec, ml, gh, gp, c_kept, kt, gm, gqt, dsum,
    sems, angle_sems, ins, outs,
):
    core, layer = flags[0], flags[1]
    mlp_sems = sems.at[pl.ds(4, 8)]
    held = ((xm_in, xm), (ml_in, ml), (rec_in, rec), (qkv_in, qkv), (pt_in, pt), (xi_in, xi))

    def slopes(j):
        sl = (slice(None), pl.ds(D * j, D))
        return dg_in.at[sl], dg.at[sl], ins.at[6 + j]

    def start_chunk(j):
        load_mlp(core, own, oth, w1, wd, mlp_sems, j)
        load(*slopes(j))

    start_chunk(0)
    start_chunk(1)
    va, vm = vectors(core, vown, voth)
    wide = jnp.where(layer == 0, got[...].astype(F32), field[...].astype(F32))
    c = wide.astype(BF)
    c_kept[...] = c
    leaving = [pltpu.make_async_copy(c_kept, c_out, outs.at[0])]
    leaving[0].start()
    vm_grad[:, SECOND:] = jnp.sum(wide, axis=0, keepdims=True)

    def from_output(j):
        wait_mlp(own, w1, wd, mlp_sems, j)
        arrived(*slopes(j))
        if j < 2:
            start_chunk(j + 2)
        elif j == 2:
            load_attn(core, own, oth, wa, sems, 3)
            for k in range(4):
                load(*held[k], ins.at[k])
        else:
            for k in range(4, len(held)):
                load(*held[k], ins.at[k])
            load_angles(cos_in, sin_in, cosf, sinf, angle_sems)
            for i in range(3):
                load_attn(core, own, oth, wa, sems, i)
        return dot(c, wd[j])

    ahead = from_output(0)
    gn = None
    for j in range(4):
        ga = ahead
        if j < 3:
            ahead = from_output(j + 1)
        part = (ga * dg[:, D * j : D * (j + 1)].astype(F32)).astype(BF)
        start = hidden_start(core, j)
        gh[:, pl.ds(start, D)] = part
        vm_grad[:, pl.ds(pl.multiple_of(FIRST + start, 128), D)] = jnp.sum(
            part.astype(F32), axis=0, keepdims=True
        )
        part = dot_nt(part, w1[j])
        gn = part if gn is None else gn + part
    for when, dst in ((core == 0, send_out), (core != 0, keep_out)):

        @pl.when(when)
        def _(dst=dst):
            load(gh, dst, outs.at[1])

    arrived(xm_in, xm, ins.at[0])
    xh, inv = norm_stats(gn, xm[...].astype(F32), vm_grad)
    c = norm_back(gn, xh, inv, vm[:, GAIN], c)
    gp[:, 3 * D :] = c
    va_grad[:, FIRST + 5 * D :] = jnp.sum(c.astype(F32), axis=0, keepdims=True)
    colp, rowp = pos[:, 0:1], pos[:, 1:2]

    def emit(p, sl, sq, sk, grads):
        qr = qkv[:, sl].astype(F32) * (LN2 * HEAD_DIM**0.5)
        th = sq * qr + sk * qkv[:, D + 128 * p : D + 128 * (p + 1)].astype(F32)
        at = FIRST + 3 * D + 128 * p
        va_grad[:, at : at + 128] = jnp.sum(th * colp, axis=0, keepdims=True)
        va_grad[:, at + D : at + D + 128] = jnp.sum(th * rowp, axis=0, keepdims=True)
        for i, g in enumerate(grads):
            gp[:, D * i + 128 * p : D * i + 128 * (p + 1)] = g
            va_grad[:, FIRST + D * i + 128 * p : FIRST + D * i + 128 * (p + 1)] = jnp.sum(
                g.astype(F32), axis=0, keepdims=True
            )

    for k in range(1, len(held)):
        arrived(*held[k], ins.at[k])
    for i in range(4):
        wait_attn(own, wa, sems, i)
    wait_angles(cos_in, sin_in, cosf, sinf, angle_sems)
    attention_back(
        c, wa.at[3], cosf, sinf, qkv, pt, rec, ml, kt, gm, gqt, dsum, lambda p: p, emit
    )
    for when, dst in ((core == 0, keep_out), (core != 0, send_out)):

        @pl.when(when)
        def _(dst=dst):
            load(gp, dst, outs.at[2])

    gn = None
    for i in range(3):
        part = dot_nt(gp[:, D * i : D * (i + 1)], wa[i])
        gn = part if gn is None else gn + part
    xh, inv = norm_stats(gn, xi[...].astype(F32), va_grad)
    cx = norm_back(gn, xh, inv, va[:, GAIN], c).astype(F32)
    wide = c.astype(F32)
    row_keep[...] = jnp.where(core == 0, cx, wide).astype(BF)
    row_send[...] = jnp.where(core == 0, wide, cx).astype(BF)
    leaving[0].wait()
    arrived(gh, send_out, outs.at[1])
    arrived(gp, keep_out, outs.at[2])


def put(stage, value, out, first, sem):
    stage[...] = value.astype(BF)
    copy = pltpu.make_async_copy(stage, out.at[:, pl.ds(first, stage.shape[1])], sem)
    copy.start()
    return copy


def gram_down_kernel(flags, c, c_oth, field_oth, a0, a1, out, c0, c1, left, right, stages, sems):
    load(c, c0, sems.at[0])
    for at, src in enumerate((c_oth, field_oth)):

        @pl.when(flags[1] == at)
        def _(src=src):
            load(src, c1, sems.at[1])

    load(a0, right.at[pl.ds(0, L), :], sems.at[2])
    load(a1, right.at[pl.ds(L, L), :], sems.at[3])
    arrived(c, c0, sems.at[0])
    arrived(c, c1, sems.at[1])
    left[:, :L] = c0[...].T
    left[:, L:] = c1[...].T
    arrived(a0, right.at[pl.ds(0, L), :], sems.at[2])
    arrived(a1, right.at[pl.ds(L, L), :], sems.at[3])
    copies = [
        put(stages.at[k], dot(left[...], right[:, D * k : D * (k + 1)]), out, D * (k + 1), sems.at[4 + k])
        for k in range(2)
    ]
    for copy in copies:
        copy.wait()


def gram_main_kernel(
    flags, main0, main1, tail0, tail1, b0, b1, tail_in, main_out, tail_out,
    m0, m1, t0, t1, left, right, stages, sems,
):
    sides = ((tail0, t0), (tail1, t1), (main0, m0), (main1, m1))

    def chunk(k, row):
        sl = pl.ds(D * k, D)
        return (b0, b1)[row].at[:, sl], right.at[k, pl.ds(L * row, L), :], sems.at[4 + 2 * k + row]

    order = (3, 0, 1, 2)
    for k in range(2):
        load(*sides[k], sems.at[k])
        load(*chunk(3, k))
    for k in range(2, 4):
        load(*sides[k], sems.at[k])
        load(*chunk(0, k - 2))
    copies = []
    for at, k in enumerate(order):
        if at < 2:
            for row in range(2):
                arrived(*sides[2 * at + row], sems.at[2 * at + row])
                load(*chunk(order[at + 2], row))
                left[at, :, L * row : L * (row + 1)] = (t0, t1, m0, m1)[2 * at + row][...].T
        for row in range(2):
            arrived(*chunk(k, row))
        out, first = (tail_out, 0) if k == 3 else (main_out, D * k)
        copies.append(put(stages.at[at], dot(left[min(at, 1)], right[k]), out, first, sems.at[12 + at]))
    for copy in copies:
        copy.wait()


def vector_grads_kernel(flags, va, vm, mine, send):
    def fold(start):
        v = va[:, start : start + D]
        w = HEAD_DIM // 2
        return jnp.concatenate(
            [v[:, 2 * w * h : 2 * w * h + w] - v[:, 2 * w * h + w : 2 * w * (h + 1)] for h in range(HEADS)],
            axis=1,
        )

    def attn(out):
        at = FIRST + 3 * D
        out[:, :at] = va[:, :at]
        out[:, at : at + HALF] = fold(at)
        out[:, at + HALF : SECOND] = fold(at + D)
        out[:, SECOND:] = va[:, at + 2 * D :]

    @pl.when(flags[0] == 0)
    def _():
        attn(mine)
        send[...] = vm[...]

    @pl.when(flags[0] != 0)
    def _():
        mine[...] = vm[...]
        attn(send)


def place_kernel(flags, rows, *refs):
    out, buf, sems = refs[-3:]
    count = sems.shape[0]
    shards = refs[: 2 * count]
    r = shards[0].shape[0]
    copies = []
    for k in range(count):
        there = pl.ds(r * k, r)
        buf[there, : 3 * D] = shards[2 * k][...].astype(F32)
        buf[there, 3 * D :] = shards[2 * k + 1][...].astype(F32)
        copy = pltpu.make_async_copy(
            buf.at[there, :], out.at[pl.ds(pl.multiple_of(rows[k], 8), r), :], sems.at[k]
        )
        copy.start()
        copies.append(copy)
    for copy in copies:
        copy.wait()


SMEM = pl.BlockSpec(memory_space=pltpu.SMEM)
VS = pl.BlockSpec(memory_space=pltpu.VMEM)
HBM = pl.BlockSpec(memory_space=pltpu.HBM)


def sds(shape, dtype=BF):
    return jax.ShapeDtypeStruct(shape, dtype)


def call(kernel, name, in_specs, outs, scratch, flops, nbytes, limit=58, out_specs=None, aliases=None):
    return pl.pallas_call(
        kernel,
        name=name,
        in_specs=in_specs,
        out_specs=[VS] * len(outs) if out_specs is None else out_specs,
        out_shape=outs,
        scratch_shapes=scratch,
        input_output_aliases={} if aliases is None else aliases,
        compiler_params=pltpu.CompilerParams(vmem_limit_bytes=limit * MIB),
        cost_estimate=pl.CostEstimate(flops=flops, bytes_accessed=nbytes, transcendentals=0),
    )


ATTN_W = [VM((4, D, D), BF)]
ANGLES = [VM((L, D), F32), VM((L, D), F32)]
MLP_W = [VM((4, D, D), BF), VM((4, D, D), BF)]
BACK_S = [VM((D, L), BF), VM((L, D), BF), VM((2, 128, L), F32), VM((16, L), F32)]


def in_hbm(a):
    return pltpu.with_memory_space_constraint(a, pltpu.HBM)


def row(width=D):
    return VM((L, width), BF)


def row_out(width=D):
    return pltpu.HBM((L, width), BF)


def prepare(flags, x, cot, *vecs):
    out = VM((x.shape[0], L), BF)
    return call(
        prepare_kernel, "prepare", [SMEM] + [VS] * 6, [out] * 4 + [VM((1, VECTOR), F32)], [], 1000,
        int(1e6), 8,
    )(flags, *(in_hbm(a) for a in (x, cot) + vecs))


def positions(flags, grid, own, oth):
    hbm = pltpu.HBM
    return call(
        positions_kernel, "positions", [SMEM, SMEM, VS, VS],
        [hbm((L, D), F32), hbm((L, D), F32), hbm((L, 128), F32), hbm((8, L), F32)],
        [], int(1e8), int(3e6), 58,
    )(flags, grid, own, oth)


def first_pass(*a):
    return call(
        first_kernel, "first_pass", [SMEM] + [VS] * 8 + [HBM] * 4, [row(), row_out()],
        ATTN_W + MLP_W + ANGLES
        + [row(), VM((D, L), BF), row(3 * D), VM((HEADS, L, L), BF), VM((16, L), F32), row(), VM((D, L), BF),
           VM((D, L), BF), row(), DMA((13,)), DMA((2,))],
        int(8e9), int(20e6), 40, out_specs=[VS, HBM],
    )(*a)


def second_pass(*a):
    saved = [
        row_out(), row_out(), row_out(3 * D), pltpu.HBM((HEADS, L, L), BF), pltpu.HBM((16, L), F32), row_out(),
        row_out(FF // 2), row_out(FF // 2), row_out(FF), row_out(), row_out(), row_out(), row_out(),
    ]
    return call(
        second_kernel, "second_pass", [SMEM] + [VS] * 6 + [HBM] * 4, [row()] + saved,
        ATTN_W + MLP_W + ANGLES
        + [row(), row(), row(3 * D), VM((HEADS, L, L), BF), VM((16, L), F32), row(), row(), row(),
           row(FF // 2), row(FF // 2), row(FF), VM((D, L), BF), VM((D, L), BF), VM((L, D), F32),
           VM((L, D), F32)]
        + BACK_S + [row(3 * D), DMA((12,)), DMA((2,)), DMA((13,))],
        int(18e9), int(35e6), 48, out_specs=[VS] + [HBM] * len(saved),
    )(*a)


def late_pass(*a):
    return call(
        late_kernel, "late_pass", [SMEM] + [VS] * 6 + [HBM] * 2, [sds((L, D))] * 2,
        [VM((4, D, D), BF), DMA((8,))], int(2e9), int(10e6), 16,
    )(*a)


def back_pass(*a):
    return call(
        back_kernel, "back_pass", [SMEM] + [VS] * 5 + [HBM] * 11,
        [sds((L, D)), sds((L, D)), VM((1, FIRST + 6 * D), F32), VM((1, VECTOR), F32), row_out(),
         row_out(FF), row_out(FF)],
        ATTN_W + MLP_W + ANGLES
        + [row(), row(), row(FF), row(3 * D), VM((HEADS, L, L), BF), VM((16, L), F32), row(), row(FF),
           row(FF), row()]
        + BACK_S + [DMA((12,)), DMA((2,)), DMA((10,)), DMA((3,))],
        int(10e9), int(30e6), 52, out_specs=[VS] * 4 + [HBM] * 3,
    )(*a)


def gram_down(flags, *a):
    return call(
        gram_down_kernel, "gram_down", [SMEM] + [HBM] * 5, [pltpu.HBM((D, 3 * D), BF)],
        [row(), row(), VM((D, 2 * L), BF), VM((2 * L, 2 * D), BF), VM((2, D, D), BF), DMA((6,))],
        int(2e9), int(8e6), 24, out_specs=[HBM],
    )(flags, *(in_hbm(x) for x in a))[0]


def gram_main(flags, *a):
    return call(
        gram_main_kernel, "gram_main", [SMEM] + [HBM] * 7, [pltpu.HBM((D, 3 * D), BF)] * 2,
        [row()] * 4 + [VM((2, D, 2 * L), BF), VM((4, 2 * L, D), BF), VM((4, D, D), BF), DMA((16,))],
        int(4e9), int(12e6), 32, out_specs=[HBM, HBM], aliases={7: 1},
    )(flags, *(in_hbm(x) for x in a))


def both_rows(flags, keep, got):
    return call(
        both_rows_kernel, "both_rows", [SMEM, VS, VS], [sds((2 * L, D))], [], 1000, int(2e6), 6
    )(flags, keep, got)[0]


def mlp_back(flags, *a):
    return call(
        mlp_back_kernel, "mlp_back", [SMEM] + [VS] * 6 + [HBM] * 2,
        [row(), row(FF), row(), row(), VM((1, VECTOR), F32)],
        MLP_W + [DMA((8,))], int(4e9), int(14e6), 22,
    )(*resident(flags, 6, a))


def attn_back(flags, *a):
    return call(
        attn_back_kernel, "attn_back", [SMEM] + [VS] * 13 + [HBM] * 2,
        [row(), row(), row(3 * D), row(3 * D), VM((1, FIRST + 6 * D), F32)],
        ATTN_W + BACK_S + [row(3 * D), DMA((4,))],
        int(6e9), int(14e6), 20,
    )(*resident(flags, 13, a))


def vector_grads(flags, va, vm):
    out = VM((1, VECTOR), F32)
    return call(vector_grads_kernel, "vector_grads", [SMEM, VS, VS], [out, out], [], 1000, 100000, 4)(
        flags, va, vm
    )


def place(flags, rows, shards, total):
    r, count = shards[0].shape[0], len(shards) // 2
    into = [] if total is None else [total]
    return call(
        place_kernel, "place", [SMEM, SMEM] + [VS] * len(shards) + [HBM] * len(into),
        [pltpu.HBM((D, 6 * D), F32)],
        [VM((r * count, 6 * D), F32), DMA((count,))], 1000, int(2e6), 24,
        out_specs=[HBM], aliases={len(shards) + 2: 0} if into else {},
    )(flags, rows, *shards, *into)[0]


def core_swap(a):
    return lax.ppermute(a, "section", [(0, 1), (1, 0), (2, 3), (3, 2)])


def after(value, first):
    return lax.optimization_barrier((value, first))[0]


class Chain:
    def __init__(self, array):
        self.array = array
        self.n = n = lax.axis_size("dp")
        self.r = array.shape[0] // (2 * n)
        i = lax.axis_index("dp")
        self.where = jnp.where(i % 2 == 0, i // 2, n - 1 - i // 2)
        order = list(range(0, n, 2)) + list(range(n - 1, 0, -2))
        self.pairs = [[(order[k], order[(k + d) % n]) for k in range(n)] for d in (1, -1)]
        self.t = 0
        self.shards = []
        self.cur = self.own(0)

    def rows(self, t):
        return [
            base + ((self.where - d * t) % self.n) * self.r
            for base, d in ((0, 1), (self.array.shape[0] // 2, -1))
        ]

    def own(self, t):
        return [lax.dynamic_slice_in_dim(self.array, at, self.r, 0) for at in self.rows(t)]

    def step(self, token):
        got = [lax.ppermute(c, "dp", p) for c, p in zip(self.cur, self.pairs)]
        got = after(got, token)
        if self.t < self.n - 1:
            self.cur = [g + o for g, o in zip(got, self.own(self.t + 1))]
            if self.t == self.n - 2:
                self.shards.append((self.rows(-1), self.cur))
        else:
            self.cur = got
            self.shards.append((self.rows(self.t - self.n + 1), got))
        self.t += 1
        return self.cur


def small_ring():
    return lax.axis_size("dp") <= 16


def summed_weight_grad(flags, main, tail, token, beside):
    if not small_ring():
        for f in beside:
            token = f(token)
        return place(flags, jnp.zeros((1,), I32), lax.psum([main, tail], "dp"), None)
    n = main.n
    total = None
    beside = list(beside)
    while main.t < 2 * n - 2:
        token = tail.step(token)
        if total is not None:
            token = (token, total)
        token = main.step(token)
        if main.shards:
            (rows, a), (_, b) = main.shards[-1], tail.shards[len(main.shards) - 1]
            total = place(flags, jnp.stack(rows).astype(I32), [a[0], b[0], a[1], b[1]], total)
            if beside and len(main.shards) > 1:
                token = (token, beside.pop(0)(token))
    for f in beside:
        token = f(token)
    return total


class VectorSum:
    def __init__(self, mine, send):
        self.value, self.coming = mine, core_swap(send)
        n = lax.axis_size("dp")
        self.hops = [1 << k for k in range(n.bit_length() - 1)]
        self.whole = n & (n - 1) == 0

    def step(self, token):
        self.value = self.value + after(self.coming, token)
        if self.whole and self.hops:
            hop = self.hops.pop(0)
            self.coming = lax.ppermute(
                self.value, "dp", [(i, i ^ hop) for i in range(lax.axis_size("dp"))]
            )
        else:
            self.coming = None
        return self.value

    def steps(self):
        return [self.step] * (len(self.hops) + 1 if self.whole else 1)

    def total(self):
        return self.value if self.whole else lax.psum(self.value, "dp")


def body(
    block_input, cotangent, grid_sizes, section_weight, norm_gain, norm_bias, first_vector, second_vector
):
    section = lax.axis_index("section")
    core = section % 2
    flags = jnp.stack([core, section // 2]).astype(I32)
    first_layer = section < 2

    keep, send, away, across, vown = prepare(
        flags, block_input.T, cotangent.T, norm_gain, norm_bias, first_vector, second_vector
    )
    got, voth = core_swap(send), core_swap(vown)
    away = lax.ppermute(away, "section", [(0, 2), (1, 3), (2, 0), (3, 1)])
    across = lax.ppermute(across, "section", [(0, 3), (1, 2), (2, 1), (3, 0)])
    own = in_hbm(section_weight[0])
    oth = in_hbm(core_swap(after(section_weight[0], (got, voth))))
    cosf, sinf, pos, segr = (in_hbm(a) for a in positions(flags, grid_sizes, vown, voth))

    x_two, field = first_pass(
        flags, keep, got, away, across, vown, voth, pos, segr, cosf, sinf, own, oth
    )
    field = in_hbm(field)
    x_got = lax.ppermute(x_two, "section", [(0, 2), (1, 3)])
    (
        c_two, x_in, x_mid, qkv, pt, rec, ml, act_mine, act_send, dg, main_left, tail_left, main_send,
        tail_send,
    ) = (in_hbm(a) if k else a for k, a in enumerate(
        second_pass(flags, field, x_got, vown, voth, pos, segr, cosf, sinf, own, oth)
    ))
    c_got = lax.ppermute(c_two, "section", [(2, 0), (3, 1)])
    act_oth, main_oth, tail_oth, field_oth = (
        core_swap(a) for a in (act_send, main_send, tail_send, field)
    )
    x_keep, x_send = late_pass(
        flags, after(x_mid, (act_oth, main_oth, tail_oth, field_oth)), x_two, act_mine, act_send, vown, voth,
        own, oth,
    )
    c_got = after(c_got, x_keep)
    activations = both_rows(flags, x_keep, core_swap(x_send))

    c_keep, c_send, va, vm, c_out, right, right_send = back_pass(
        flags, field, c_got, vown, voth, pos, x_in, x_mid, dg, qkv, pt, rec, ml, cosf, sinf, own, oth
    )
    tail = gram_down(
        flags, c_out, core_swap(c_got), field_oth, act_mine, act_oth
    )
    main, tail = gram_main(
        flags, main_left, main_oth, tail_left, tail_oth, right, core_swap(right_send), tail
    )
    token = main
    if small_ring():
        main, tail = Chain(main), Chain(tail)
        token = main.cur
    vector = VectorSum(*vector_grads(flags, va, vm))
    rows = {}

    def send_rows(token):
        rows["got"] = core_swap(after(c_send, token))
        return c_send

    def join_rows(token):
        rows["out"] = both_rows(flags, c_keep, after(rows["got"], token))
        return rows["out"]

    weight_grad = summed_weight_grad(flags, main, tail, token, vector.steps() + [send_rows, join_rows])
    vg = vector.total()
    input_grads = rows["out"]
    return (
        activations[None],
        input_grads[None],
        weight_grad[None],
        vg[:, GAIN],
        vg[:, SHIFT],
        vg[:, FIRST:SECOND],
        vg[:, SECOND:],
    )


def solution(mesh):
    in_specs = (
        P("dp", "section"),
        P("dp", "section"),
        P("dp", None, None),
        P("section", None, None),
        P("section", None),
        P("section", None),
        P("section", None),
        P("section", None),
    )
    out_specs = (
        P("section", "dp", None),
        P("section", "dp", None),
        P("section", None, None),
        P("section", None),
        P("section", None),
        P("section", None),
        P("section", None),
    )
    return jax.shard_map(body, mesh=mesh, in_specs=in_specs, out_specs=out_specs, check_vma=False)
```

time: 383 us -> 294 us (0.77)
  waiting for transfers between devices: 126 us -> 100 us
  local copies, waits for them, and re-layouts: 33.8 us -> 8.51 us
  Pallas kernels: 124 us -> 103 us
  other arithmetic: 14.9 us -> 5.43 us
  starting transfers between devices: 78.2 us -> 71.9 us
    ppermute x60 -> x61, waiting for transfers between devices: 94.6 us -> 68.1 us  [the longest x56 58.9 us: step(): got = [lax.ppermute(c, 'dp', p) for c, p in zip(self.cur, self.pairs)]]
    pallas_call x18 -> x19, Pallas kernels: 124 us -> 103 us  [the longest x1 24 us: second_pass(): call(second_kernel, 'second_pass', [SMEM] + [VS] * 6 + [HBM] * 4, [row()]...]
    unnamed x166 -> x42, local copies, waits for them, and re-layouts: 20.8 us -> 5.03 us
    ppermute x19 -> x12, waiting for transfers between devices: 3.49 us -> 11.7 us  [core_swap(): return lax.ppermute(a, 'section', [(0, 1), (1, 0), (2, 3), (3, 2)])]
    ppermute x1, waiting for transfers between devices: 14.5 us -> 7.81 us  [body(): c_got = lax.ppermute(c_two, 'section', [(2, 0), (3, 1)])]
    dynamic_slice x3 -> x2, local copies, waits for them, and re-layouts: 6.97 us -> 2.3 us  [own(): lax.dynamic_slice_in_dim(self.array, at, self.r, 0)]
    select_n x6 -> x0, other arithmetic: 4.26 us -> none  [the longest x2 2.35 us: rows_of(): jnp.where(first_core, kept, got)]
    ppermute x60 -> x61, starting transfers between devices: 68.4 us -> 66.5 us  [the longest x56 59.4 us: step(): got = [lax.ppermute(c, 'dp', p) for c, p in zip(self.cur, self.pairs)]]
  transfers between devices with their start and end apart: 81 -> 75, of which waited for: 37 -> 49; matrix products, arithmetic and copies ran while one was open for 9% -> 3% of each run, Pallas kernels for 20% -> 11%
where the time goes in v1:
time: 294 us; the launch traced here: 291 us
  Pallas kernels  103 us (35%)
  waiting for transfers between devices  100 us (34%)
  starting transfers between devices  71.9 us (24%)
  local copies, waits for them, and re-layouts  8.51 us (3%)
  other arithmetic  5.43 us (2%)
    ppermute x56, starting transfers between devices, step(): got = [lax.ppermute(c, 'dp', p) for c, p in zip(self.cur, self.pairs)]  59.4 us
    ppermute x56, waiting for transfers between devices, step(): got = [lax.ppermute(c, 'dp', p) for c, p in zip(self.cur, self.pairs)]  58.9 us
    pallas_call x1, Pallas kernels, second_pass(): call(second_kernel, 'second_pass', [SMEM] + [VS] * 6 + [HBM] * 4, [row()]...  24 us
    pallas_call x1, Pallas kernels, back_pass(): call(back_kernel, 'back_pass', [SMEM] + [VS] * 5 + [HBM] * 11, [sds((L, D...  20.4 us
    pallas_call x8, Pallas kernels, place(): call(place_kernel, 'place', [SMEM, SMEM] + [VS] * len(shards) + [HBM] * l...  14.5 us
    pallas_call x1, Pallas kernels, first_pass(): call(first_kernel, 'first_pass', [SMEM] + [VS] * 8 + [HBM] * 4, [row(), r...  14.4 us
    ppermute x1, waiting for transfers between devices, body(): x_got = lax.ppermute(x_two, 'section', [(0, 2), (1, 3)])  12.7 us
    ppermute x12, waiting for transfers between devices, core_swap(): return lax.ppermute(a, 'section', [(0, 1), (1, 0), (2, 3), (3, 2)])  11.7 us
  transfers between devices with their start and end apart: 75, of which 49 were waited for; matrix products, arithmetic and copies ran while one was open for 3% of the time, Pallas kernels for 11%

profile of v1, /device:TPU:0, one launch (start us, length us, event | category | flops | bytes accessed | tf_op | source)
XLA Modules:
  0.0 290.9 jit_solution(9346695645652882266)
XLA Ops:
  3.8 2.8 collective-permute-start.1
  6.7 3.5 %positions.1 = (f32[384,768]{1,0:T(8,128)}, f32[384,768]{1,0:T(8,128)}, f32[384,128]{1,0:T(8,128)}, f32[8,384]{1,0:T(8,128)}) custom-call(s32[2]{0:T(128)} %copy-done, s32[2,2,2]{2,1,0:T(2,128)} %grid.1, f32[1,5376]{1,0:T(1,128)} %copy-done.3, f32[1,5376]{1,0:T(1,128)} %copy-done.6), custom_call_target="tpu_custom_call" | custom-call | flops 100000000 | bytes 3000000 | tf_op jit(solution)/shard_map/positions/pallas_call | solution.py:790
  11.3 2.4 collective-permute-done.2.across
  17.4 14.4 %first_pass.1 = (bf16[384,768]{1,0:T(8,128)(2,1)S(1)}, bf16[384,768]{1,0:T(8,128)(2,1)}) custom-call(s32[2]{0:T(128)S(1)} %copy-done.1, bf16[192,384]{1,0:T(8,128)(2,1)S(1)} %get-tuple-element.110.keep, bf16[192,384]{1,0:T(8,128)(2,1)S(1)} %collective-permute-done.got, bf16[192,384]{1,0:T(8,128)(2,1)S(1)} %collective-permute-done.1.away, ...), custom_call_target="tpu_custom_call" | custom-call | flops 8000000000 | bytes 20000000 | tf_op jit(solution)/shard_map/first_pass/pallas_call | solution.py:798
  33.3 12.7 %collective-permute-done.5.got = bf16[384,768]{1,0:T(8,128)(2,1)S(1)} collective-permute-done((bf16[384,768]{1,0:T(8,128)(2,1)S(1)}, bf16[384,768]{1,0:T(8,128)(2,1)S(1)}, u32[]{:S(2)}, u32[]{:S(2)}) %collective-permute-start.5) | collective-permute-done | bytes 589856 | tf_op jit(solution)/shard_map/ppermute | solution.py:1018
  46.0 24.0 %second_pass.1 = (bf16[384,768]{1,0:T(8,128)(2,1)S(1)}, bf16[384,768]{1,0:T(8,128)(2,1)}, bf16[384,768]{1,0:T(8,128)(2,1)}, bf16[384,2304]{1,0:T(8,128)(2,1)}, b...) custom-call(s32[2]{0:T(128)S(1)} %copy-done.2, ...), custom_call_target="tpu_custom_call" | custom-call | flops 17999998976 | bytes 35000000 | tf_op jit(solution)/shard_map/second_pass/pallas_call | solution.py:812
  72.4 1.9 collective-permute-done.9.field_oth
  76.9 6.5 %late_pass.1 = (bf16[384,768]{1,0:T(8,128)(2,1)S(1)}, bf16[384,768]{1,0:T(8,128)(2,1)S(1)}) custom-call(s32[2]{0:T(128)S(1)} %copy-done.2, bf16[384,768]{1,0:T(8,128)(2,1)} %get-tuple-element.126.xm.xm_in, bf16[384,768]{1,0:T(8,128)(2,1)S(1)} %get-tuple-element.121.x_two, bf16[384,1536]{1,0:T(8,128)(2,1)} %get-tuple-element.127.actm.a0, ...), custom_call_target="tpu_custom_call" | custom-call | flops 2000000000 | bytes 10000000 | tf_op jit(solution)/shard_map/late_pass/pallas_call | solution.py:824
  84.2 7.8 %collective-permute-done.11.got = bf16[384,768]{1,0:T(8,128)(2,1)S(1)} collective-permute-done((bf16[384,768]{1,0:T(8,128)(2,1)S(1)}, bf16[384,768]{1,0:T(8,128)(2,1)S(1)}, u32[]{:S(2)}, u32[]{:S(2)}) %collective-permute-start.11) | collective-permute-done | bytes 589856 | tf_op jit(solution)/shard_map/ppermute | solution.py:1025
  92.0 20.4 %back_pass.1 = (bf16[384,768]{1,0:T(8,128)(2,1)S(1)}, bf16[384,768]{1,0:T(8,128)(2,1)S(1)}, f32[1,6144]{1,0:T(1,128)S(1)}, f32[1,5376]{1,0:T(1,128)S(1)}, bf16[3...) custom-call(s32[2]{0:T(128)S(1)} %copy-done.2, ...), custom_call_target="tpu_custom_call" | custom-call | flops 10000000000 | bytes 30000000 | tf_op jit(solution)/shard_map/back_pass/pallas_call | solution.py:831
  113.0 4.5 %collective-permute-done.13.c_oth = bf16[384,768]{1,0:T(8,128)(2,1)S(1)} collective-permute-done((bf16[384,768]{1,0:T(8,128)(2,1)S(1)}, bf16[384,768]{1,0:T(8,128)(2,1)S(1)}, u32[]{:S(2)}, u32[]{:S(2)}) %collective-permute-start.13) | collective-permute-done | bytes 589856 | tf_op jit(solution)/shard_map/ppermute | solution.py:901
  118.3 5.6 %gram_down.1.tail_in = bf16[768,2304]{1,0:T(8,128)(2,1)} custom-call(s32[2]{0:T(128)S(1)} %copy-done.2, bf16[384,768]{1,0:T(8,128)(2,1)} %get-tuple-element.144.c, bf16[384,768]{1,0:T(8,128)(2,1)} %copy-done.17, bf16[384,768]{1,0:T(8,128)(2,1)} %copy-done.16, bf16[384,1536]{1,0:T(8,128)(2,1)} %get-tuple-element.127.actm.a0, bf16[384,1536]{1,0:T(8,128)(2,1)} %copy-done.15), custom_call_target="tpu_custom_call" | custom-call | flops 2000000000 | bytes 8000000 | tf_op jit(solution)/shard_map/gram_down/pallas_call | solution.py:844
  124.0 9.3 %gram_main.1 = (bf16[768,2304]{1,0:T(8,128)(2,1)}, bf16[768,2304]{1,0:T(8,128)(2,1)}) custom-call(s32[2]{0:T(128)S(1)} %copy-done.2, bf16[384,768]{1,0:T(8,128)(2,1)} %get-tuple-element.140.main0, bf16[384,768]{1,0:T(8,128)(2,1)} %copy-done.18, bf16[384,768]{1,0:T(8,128)(2,1)} %get-tuple-element.141.tail0, ...), custom_call_target="tpu_custom_call", output_to_operand_aliasing={{1}: (7, {})} | custom-call | flops 4000000000 | bytes 12000000 | tf_op jit(solution)/shard_map/gram_main/pallas_call | solution.py:852
  134.5 2.9 %collective-permute-start.16 = (bf16[48,2304]{1,0:T(8,128)(2,1)S(1)}, bf16[48,2304]{1,0:T(8,128)(2,1)S(1)}, u32[]{:S(2)}, u32[]{:S(2)}) collective-permute-start(bf16[48,2304]{1,0:T(8,128)(2,1)S(1)} %get-tuple-element.242), channel_id=1, source_target_pairs={{0,2},{2,4},{4,6},{6,7},{7,5},{5,3},{3,1},{1,0},{8,10},{10,12},{12... | collective-permute-start | bytes 663560 | tf_op jit(solution)/shard_map/ppermute | solution.py:931
  138.6 2.1 collective-permute-start.14
  140.7 3.0 %collective-permute-done.16 = bf16[48,2304]{1,0:T(8,128)(2,1)S(1)} collective-permute-done((bf16[48,2304]{1,0:T(8,128)(2,1)S(1)}, bf16[48,2304]{1,0:T(8,128)(2,1)S(1)}, u32[]{:S(2)}, u32[]{:S(2)}) %collective-permute-start.16) | collective-permute-done | bytes 221216 | tf_op jit(solution)/shard_map/ppermute | solution.py:931
  143.7 2.1 collective-permute-done.17
  157.1 2.4 collective-permute-done.18
  167.6 2.5 collective-permute-done.22
  230.5 5.7 %collective-permute-done.55 = f32[1,5376]{1,0:T(1,128)S(1)} collective-permute-done((f32[1,5376]{1,0:T(1,128)S(1)}, f32[1,5376]{1,0:T(1,128)S(1)}, u32[]{:S(2)}, u32[]{:S(2)}) %collective-permute-start.55) | collective-permute-done | bytes 21536 | tf_op jit(solution)/shard_map/ppermute | solution.py:982
  236.3 2.0 collective-permute-start.58
  240.3 2.0 collective-permute-start.56
  242.4 2.2 collective-permute-done.58.refs_1_
  244.6 3.3 %collective-permute-start.65 = (f32[1,5376]{1,0:T(1,128)S(1)}, f32[1,5376]{1,0:T(1,128)S(1)}, u32[]{:S(2)}, u32[]{:S(2)}) collective-permute-start(f32[1,5376]{1,0:T(1,128)S(1)} %add.392), channel_id=1, source_target_pairs={{0,4},{1,5},{2,6},{3,7},{4,0},{5,1},{6,2},{7,3},{8,12},{9,13},{10,... | collective-permute-start | bytes 64520 | tf_op jit(solution)/shard_map/ppermute | solution.py:982
  253.4 2.3 collective-permute-start.61
  255.7 1.8 place.12.refs_4_
  260.5 1.9 collective-permute-done.62.refs_2_
  262.5 2.2 collective-permute-start.67
  264.7 2.0 collective-permute-start.69
  270.3 4.7 %collective-permute-done.69.refs_1_ = bf16[48,2304]{1,0:T(8,128)(2,1)S(1)} collective-permute-done((bf16[48,2304]{1,0:T(8,128)(2,1)S(1)}, bf16[48,2304]{1,0:T(8,128)(2,1)S(1)}, u32[]{:S(2)}, u32[]{:S(2)}) %collective-permute-start.69) | collective-permute-done | bytes 221216 | tf_op jit(solution)/shard_map/ppermute | solution.py:931
  275.0 1.9 collective-permute-done.70.refs_3_
  285.7 2.8 collective-permute-done.71.refs_0_
  (210 shorter events, 124.0 us)
Async XLA Ops:
  3.6 11.6 %collective-permute-start.4 = (bf16[768,4608]{1,0:T(8,128)(2,1)}, bf16[768,4608]{1,0:T(8,128)(2,1)}, u32[]{:S(2)}, u32[]{:S(2)}) collective-permute-start(bf16[768,4608]{1,0:T(8,128)(2,1)} %bitcast.25), channel_id=1, source_target_pairs={{0,8},{8,0},{16,24},{24,16},{1,9},{9,1},{17,25},{25,17},{2,10},{10... | collective-permute-start | bytes 21233672 | tf_op jit(solution)/shard_map/ppermute | solution.py:901
  31.8 14.2 %collective-permute-start.5 = (bf16[384,768]{1,0:T(8,128)(2,1)S(1)}, bf16[384,768]{1,0:T(8,128)(2,1)S(1)}, u32[]{:S(2)}, u32[]{:S(2)}) collective-permute-start(bf16[384,768]{1,0:T(8,128)(2,1)S(1)} %get-tuple-element.121.x_two), channel_id=1, source_target_pairs={{0,16},{8,24},{1,17},{9,25},{2,18},{10,26},{3,19},{11,27},{4,20},{... | collective-permute-start | bytes 1769480 | tf_op jit(solution)/shard_map/ppermute | solution.py:1018
  71.1 20.9 %collective-permute-start.11 = (bf16[384,768]{1,0:T(8,128)(2,1)S(1)}, bf16[384,768]{1,0:T(8,128)(2,1)S(1)}, u32[]{:S(2)}, u32[]{:S(2)}) collective-permute-start(bf16[384,768]{1,0:T(8,128)(2,1)S(1)} %get-tuple-element.130), channel_id=1, source_target_pairs={{16,0},{24,8},{17,1},{25,9},{18,2},{26,10},{19,3},{27,11},{20,4},{... | collective-permute-start | bytes 1769480 | tf_op jit(solution)/shard_map/ppermute | solution.py:1025
  112.4 11.5 %collective-permute-start.12 = (bf16[384,3072]{1,0:T(8,128)(2,1)}, bf16[384,3072]{1,0:T(8,128)(2,1)}, u32[]{:S(2)}, u32[]{:S(2)}) collective-permute-start(bf16[384,3072]{1,0:T(8,128)(2,1)} %get-tuple-element.143), channel_id=1, source_target_pairs={{0,8},{8,0},{16,24},{24,16},{1,9},{9,1},{17,25},{25,17},{2,10},{10... | collective-permute-start | bytes 7077896 | tf_op jit(solution)/shard_map/ppermute | solution.py:901
  134.5 9.1 %collective-permute-start.16 = (bf16[48,2304]{1,0:T(8,128)(2,1)S(1)}, bf16[48,2304]{1,0:T(8,128)(2,1)S(1)}, u32[]{:S(2)}, u32[]{:S(2)}) collective-permute-start(bf16[48,2304]{1,0:T(8,128)(2,1)S(1)} %get-tuple-element.242), channel_id=1, source_target_pairs={{0,2},{2,4},{4,6},{6,7},{7,5},{5,3},{3,1},{1,0},{8,10},{10,12},{12... | collective-permute-start | bytes 663560 | tf_op jit(solution)/shard_map/ppermute | solution.py:931
  138.6 10.4 %collective-permute-start.14 = (bf16[48,2304]{1,0:T(8,128)(2,1)S(1)}, bf16[48,2304]{1,0:T(8,128)(2,1)S(1)}, u32[]{:S(2)}, u32[]{:S(2)}) collective-permute-start(bf16[48,2304]{1,0:T(8,128)(2,1)S(1)} %get-tuple-element.244), channel_id=1, source_target_pairs={{0,2},{2,4},{4,6},{6,7},{7,5},{5,3},{3,1},{1,0},{8,10},{10,12},{12... | collective-permute-start | bytes 663560 | tf_op jit(solution)/shard_map/ppermute | solution.py:931
  140.7 9.3 %collective-permute-start.15 = (bf16[48,2304]{1,0:T(8,128)(2,1)S(1)}, bf16[48,2304]{1,0:T(8,128)(2,1)S(1)}, u32[]{:S(2)}, u32[]{:S(2)}) collective-permute-start(bf16[48,2304]{1,0:T(8,128)(2,1)S(1)} %get-tuple-element.243), channel_id=1, source_target_pairs={{0,1},{2,0},{4,2},{6,4},{7,6},{5,7},{3,5},{1,3},{8,9},{10,8},{12,1... | collective-permute-start | bytes 663560 | tf_op jit(solution)/shard_map/ppermute | solution.py:931
  155.1 9.3 %collective-permute-start.24 = (bf16[48,2304]{1,0:T(8,128)(2,1)S(1)}, bf16[48,2304]{1,0:T(8,128)(2,1)S(1)}, u32[]{:S(2)}, u32[]{:S(2)}) collective-permute-start(bf16[48,2304]{1,0:T(8,128)(2,1)S(1)} %get-tuple-element.236), channel_id=1, source_target_pairs={{0,2},{2,4},{4,6},{6,7},{7,5},{5,3},{3,1},{1,0},{8,10},{10,12},{12... | collective-permute-start | bytes 663560 | tf_op jit(solution)/shard_map/ppermute | solution.py:931
  156.7 8.7 %collective-permute-start.25 = (bf16[48,2304]{1,0:T(8,128)(2,1)S(1)}, bf16[48,2304]{1,0:T(8,128)(2,1)S(1)}, u32[]{:S(2)}, u32[]{:S(2)}) collective-permute-start(bf16[48,2304]{1,0:T(8,128)(2,1)S(1)} %get-tuple-element.235), channel_id=1, source_target_pairs={{0,1},{2,0},{4,2},{6,4},{7,6},{5,7},{3,5},{1,3},{8,9},{10,8},{12,1... | collective-permute-start | bytes 663560 | tf_op jit(solution)/shard_map/ppermute | solution.py:931
  165.5 9.3 %collective-permute-start.28 = (bf16[48,2304]{1,0:T(8,128)(2,1)S(1)}, bf16[48,2304]{1,0:T(8,128)(2,1)S(1)}, u32[]{:S(2)}, u32[]{:S(2)}) collective-permute-start(bf16[48,2304]{1,0:T(8,128)(2,1)S(1)} %get-tuple-element.232), channel_id=1, source_target_pairs={{0,2},{2,4},{4,6},{6,7},{7,5},{5,3},{3,1},{1,0},{8,10},{10,12},{12... | collective-permute-start | bytes 663560 | tf_op jit(solution)/shard_map/ppermute | solution.py:931
  167.0 9.4 %collective-permute-start.29 = (bf16[48,2304]{1,0:T(8,128)(2,1)S(1)}, bf16[48,2304]{1,0:T(8,128)(2,1)S(1)}, u32[]{:S(2)}, u32[]{:S(2)}) collective-permute-start(bf16[48,2304]{1,0:T(8,128)(2,1)S(1)} %get-tuple-element.231), channel_id=1, source_target_pairs={{0,1},{2,0},{4,2},{6,4},{7,6},{5,7},{3,5},{1,3},{8,9},{10,8},{12,1... | collective-permute-start | bytes 663560 | tf_op jit(solution)/shard_map/ppermute | solution.py:931
  186.0 8.7 %collective-permute-start.36 = (bf16[48,2304]{1,0:T(8,128)(2,1)S(1)}, bf16[48,2304]{1,0:T(8,128)(2,1)S(1)}, u32[]{:S(2)}, u32[]{:S(2)}) collective-permute-start(bf16[48,2304]{1,0:T(8,128)(2,1)S(1)} %get-tuple-element.224), channel_id=1, source_target_pairs={{0,2},{2,4},{4,6},{6,7},{7,5},{5,3},{3,1},{1,0},{8,10},{10,12},{12... | collective-permute-start | bytes 663560 | tf_op jit(solution)/shard_map/ppermute | solution.py:931
  209.8 8.7 %collective-permute-start.42 = (bf16[48,2304]{1,0:T(8,128)(2,1)S(1)}, bf16[48,2304]{1,0:T(8,128)(2,1)S(1)}, u32[]{:S(2)}, u32[]{:S(2)}) collective-permute-start(bf16[48,2304]{1,0:T(8,128)(2,1)S(1)} %get-tuple-element.214.refs_0_), channel_id=1, source_target_pairs={{0,2},{2,4},{4,6},{6,7},{7,5},{5,3},{3,1},{1,0},{8,10},{10,12},{12... | collective-permute-start | bytes 663560 | tf_op jit(solution)/shard_map/ppermute | solution.py:931
  214.6 8.8 %collective-permute-start.48 = (bf16[48,2304]{1,0:T(8,128)(2,1)S(1)}, bf16[48,2304]{1,0:T(8,128)(2,1)S(1)}, u32[]{:S(2)}, u32[]{:S(2)}) collective-permute-start(bf16[48,2304]{1,0:T(8,128)(2,1)S(1)} %collective-permute-done.44.refs_1_), channel_id=1, source_target_pairs={{0,2},{2,4},{4,6},{6,7},{7,5},{5,3},{3,1},{1,0},{8,10},{10,12},{12... | collective-permute-start | bytes 663560 | tf_op jit(solution)/shard_map/ppermute | solution.py:931
  223.4 12.8 %collective-permute-start.53 = (bf16[48,2304]{1,0:T(8,128)(2,1)S(1)}, bf16[48,2304]{1,0:T(8,128)(2,1)S(1)}, u32[]{:S(2)}, u32[]{:S(2)}) collective-permute-start(bf16[48,2304]{1,0:T(8,128)(2,1)S(1)} %collective-permute-done.48.refs_1_), channel_id=1, source_target_pairs={{0,2},{2,4},{4,6},{6,7},{7,5},{5,3},{3,1},{1,0},{8,10},{10,12},{12... | collective-permute-start | bytes 663560 | tf_op jit(solution)/shard_map/ppermute | solution.py:931
  224.8 11.5 %collective-permute-start.54 = (bf16[48,2304]{1,0:T(8,128)(2,1)S(1)}, bf16[48,2304]{1,0:T(8,128)(2,1)S(1)}, u32[]{:S(2)}, u32[]{:S(2)}) collective-permute-start(bf16[48,2304]{1,0:T(8,128)(2,1)S(1)} %collective-permute-done.49.refs_3_), channel_id=1, source_target_pairs={{0,1},{2,0},{4,2},{6,4},{7,6},{5,7},{3,5},{1,3},{8,9},{10,8},{12,1... | collective-permute-start | bytes 663560 | tf_op jit(solution)/shard_map/ppermute | solution.py:931
  227.4 12.8 %collective-permute-start.51 = (bf16[48,2304]{1,0:T(8,128)(2,1)S(1)}, bf16[48,2304]{1,0:T(8,128)(2,1)S(1)}, u32[]{:S(2)}, u32[]{:S(2)}) collective-permute-start(bf16[48,2304]{1,0:T(8,128)(2,1)S(1)} %collective-permute-done.46.refs_0_), channel_id=1, source_target_pairs={{0,2},{2,4},{4,6},{6,7},{7,5},{5,3},{3,1},{1,0},{8,10},{10,12},{12... | collective-permute-start | bytes 663560 | tf_op jit(solution)/shard_map/ppermute | solution.py:931
  228.8 11.5 %collective-permute-start.52 = (bf16[48,2304]{1,0:T(8,128)(2,1)S(1)}, bf16[48,2304]{1,0:T(8,128)(2,1)S(1)}, u32[]{:S(2)}, u32[]{:S(2)}) collective-permute-start(bf16[48,2304]{1,0:T(8,128)(2,1)S(1)} %collective-permute-done.47.refs_2_), channel_id=1, source_target_pairs={{0,1},{2,0},{4,2},{6,4},{7,6},{5,7},{3,5},{1,3},{8,9},{10,8},{12,1... | collective-permute-start | bytes 663560 | tf_op jit(solution)/shard_map/ppermute | solution.py:931
  236.2 30.5 %collective-permute-start.10 = (bf16[384,768]{1,0:T(8,128)(2,1)S(1)}, bf16[384,768]{1,0:T(8,128)(2,1)S(1)}, u32[]{:S(2)}, u32[]{:S(2)}) collective-permute-start(bf16[384,768]{1,0:T(8,128)(2,1)S(1)} %copy-done.12), channel_id=1, source_target_pairs={{0,8},{8,0},{16,24},{24,16},{1,9},{9,1},{17,25},{25,17},{2,10},{10... | collective-permute-start | bytes 1769480 | tf_op jit(solution)/shard_map/ppermute | solution.py:901
  240.2 9.6 %collective-permute-start.59 = (bf16[48,2304]{1,0:T(8,128)(2,1)S(1)}, bf16[48,2304]{1,0:T(8,128)(2,1)S(1)}, u32[]{:S(2)}, u32[]{:S(2)}) collective-permute-start(bf16[48,2304]{1,0:T(8,128)(2,1)S(1)} %collective-permute-done.54.refs_3_), channel_id=1, source_target_pairs={{0,1},{2,0},{4,2},{6,4},{7,6},{5,7},{3,5},{1,3},{8,9},{10,8},{12,1... | collective-permute-start | bytes 663560 | tf_op jit(solution)/shard_map/ppermute | solution.py:931
  240.3 10.1 %collective-permute-start.56 = (bf16[48,2304]{1,0:T(8,128)(2,1)S(1)}, bf16[48,2304]{1,0:T(8,128)(2,1)S(1)}, u32[]{:S(2)}, u32[]{:S(2)}) collective-permute-start(bf16[48,2304]{1,0:T(8,128)(2,1)S(1)} %collective-permute-done.51.refs_0_), channel_id=1, source_target_pairs={{0,2},{2,4},{4,6},{6,7},{7,5},{5,3},{3,1},{1,0},{8,10},{10,12},{12... | collective-permute-start | bytes 663560 | tf_op jit(solution)/shard_map/ppermute | solution.py:931
  242.3 11.1 %collective-permute-start.57 = (bf16[48,2304]{1,0:T(8,128)(2,1)S(1)}, bf16[48,2304]{1,0:T(8,128)(2,1)S(1)}, u32[]{:S(2)}, u32[]{:S(2)}) collective-permute-start(bf16[48,2304]{1,0:T(8,128)(2,1)S(1)} %collective-permute-done.52.refs_2_), channel_id=1, source_target_pairs={{0,1},{2,0},{4,2},{6,4},{7,6},{5,7},{3,5},{1,3},{8,9},{10,8},{12,1... | collective-permute-start | bytes 663560 | tf_op jit(solution)/shard_map/ppermute | solution.py:931
  244.6 11.1 %collective-permute-start.65 = (f32[1,5376]{1,0:T(1,128)S(1)}, f32[1,5376]{1,0:T(1,128)S(1)}, u32[]{:S(2)}, u32[]{:S(2)}) collective-permute-start(f32[1,5376]{1,0:T(1,128)S(1)} %add.392), channel_id=1, source_target_pairs={{0,4},{1,5},{2,6},{3,7},{4,0},{5,1},{6,2},{7,3},{8,12},{9,13},{10,... | collective-permute-start | bytes 64520 | tf_op jit(solution)/shard_map/ppermute | solution.py:982
  250.4 8.6 %collective-permute-start.64 = (bf16[48,2304]{1,0:T(8,128)(2,1)S(1)}, bf16[48,2304]{1,0:T(8,128)(2,1)S(1)}, u32[]{:S(2)}, u32[]{:S(2)}) collective-permute-start(bf16[48,2304]{1,0:T(8,128)(2,1)S(1)} %collective-permute-done.59.refs_3_), channel_id=1, source_target_pairs={{0,1},{2,0},{4,2},{6,4},{7,6},{5,7},{3,5},{1,3},{8,9},{10,8},{12,1... | collective-permute-start | bytes 663560 | tf_op jit(solution)/shard_map/ppermute | solution.py:931
  262.4 21.7 %collective-permute-start.66 = (bf16[384,768]{1,0:T(8,128)(2,1)S(1)}, bf16[384,768]{1,0:T(8,128)(2,1)S(1)}, u32[]{:S(2)}, u32[]{:S(2)}) collective-permute-start(bf16[384,768]{1,0:T(8,128)(2,1)S(1)} %copy-done.10), channel_id=1, source_target_pairs={{0,8},{8,0},{16,24},{24,16},{1,9},{9,1},{17,25},{25,17},{2,10},{10... | collective-permute-start | bytes 1769480 | tf_op jit(solution)/shard_map/ppermute | solution.py:901
  262.5 16.5 %collective-permute-start.67 = (bf16[48,2304]{1,0:T(8,128)(2,1)S(1)}, bf16[48,2304]{1,0:T(8,128)(2,1)S(1)}, u32[]{:S(2)}, u32[]{:S(2)}) collective-permute-start(bf16[48,2304]{1,0:T(8,128)(2,1)S(1)} %collective-permute-done.61.refs_0_), channel_id=1, source_target_pairs={{0,2},{2,4},{4,6},{6,7},{7,5},{5,3},{3,1},{1,0},{8,10},{10,12},{12... | collective-permute-start | bytes 663560 | tf_op jit(solution)/shard_map/ppermute | solution.py:931
  264.7 14.3 %collective-permute-start.68 = (bf16[48,2304]{1,0:T(8,128)(2,1)S(1)}, bf16[48,2304]{1,0:T(8,128)(2,1)S(1)}, u32[]{:S(2)}, u32[]{:S(2)}) collective-permute-start(bf16[48,2304]{1,0:T(8,128)(2,1)S(1)} %collective-permute-done.62.refs_2_), channel_id=1, source_target_pairs={{0,1},{2,0},{4,2},{6,4},{7,6},{5,7},{3,5},{1,3},{8,9},{10,8},{12,1... | collective-permute-start | bytes 663560 | tf_op jit(solution)/shard_map/ppermute | solution.py:931
  264.7 10.4 %collective-permute-start.69 = (bf16[48,2304]{1,0:T(8,128)(2,1)S(1)}, bf16[48,2304]{1,0:T(8,128)(2,1)S(1)}, u32[]{:S(2)}, u32[]{:S(2)}) collective-permute-start(bf16[48,2304]{1,0:T(8,128)(2,1)S(1)} %collective-permute-done.63.refs_1_), channel_id=1, source_target_pairs={{0,2},{2,4},{4,6},{6,7},{7,5},{5,3},{3,1},{1,0},{8,10},{10,12},{12... | collective-permute-start | bytes 663560 | tf_op jit(solution)/shard_map/ppermute | solution.py:931
  266.7 10.3 %collective-permute-start.70 = (bf16[48,2304]{1,0:T(8,128)(2,1)S(1)}, bf16[48,2304]{1,0:T(8,128)(2,1)S(1)}, u32[]{:S(2)}, u32[]{:S(2)}) collective-permute-start(bf16[48,2304]{1,0:T(8,128)(2,1)S(1)} %collective-permute-done.64.refs_3_), channel_id=1, source_target_pairs={{0,1},{2,0},{4,2},{6,4},{7,6},{5,7},{3,5},{1,3},{8,9},{10,8},{12,1... | collective-permute-start | bytes 663560 | tf_op jit(solution)/shard_map/ppermute | solution.py:931
  277.0 8.7 %collective-permute-start.73 = (bf16[48,2304]{1,0:T(8,128)(2,1)S(1)}, bf16[48,2304]{1,0:T(8,128)(2,1)S(1)}, u32[]{:S(2)}, u32[]{:S(2)}) collective-permute-start(bf16[48,2304]{1,0:T(8,128)(2,1)S(1)} %collective-permute-done.69.refs_1_), channel_id=1, source_target_pairs={{0,2},{2,4},{4,6},{6,7},{7,5},{5,3},{3,1},{1,0},{8,10},{10,12},{12... | collective-permute-start | bytes 663560 | tf_op jit(solution)/shard_map/ppermute | solution.py:931
  279.0 9.4 %collective-permute-start.71 = (bf16[48,2304]{1,0:T(8,128)(2,1)S(1)}, bf16[48,2304]{1,0:T(8,128)(2,1)S(1)}, u32[]{:S(2)}, u32[]{:S(2)}) collective-permute-start(bf16[48,2304]{1,0:T(8,128)(2,1)S(1)} %collective-permute-done.67.refs_0_), channel_id=1, source_target_pairs={{0,2},{2,4},{4,6},{6,7},{7,5},{5,3},{3,1},{1,0},{8,10},{10,12},{12... | collective-permute-start | bytes 663560 | tf_op jit(solution)/shard_map/ppermute | solution.py:931
  279.3 9.5 %collective-permute-start.72 = (bf16[48,2304]{1,0:T(8,128)(2,1)S(1)}, bf16[48,2304]{1,0:T(8,128)(2,1)S(1)}, u32[]{:S(2)}, u32[]{:S(2)}) collective-permute-start(bf16[48,2304]{1,0:T(8,128)(2,1)S(1)} %collective-permute-done.68.refs_2_), channel_id=1, source_target_pairs={{0,1},{2,0},{4,2},{6,4},{7,6},{5,7},{3,5},{1,3},{8,9},{10,8},{12,1... | collective-permute-start | bytes 663560 | tf_op jit(solution)/shard_map/ppermute | solution.py:931
  (64 other events, 568.7 us)

commit v2 on v1

--- a/solution.py
+++ b/solution.py
@@ -23,6 +23,7 @@
 GAIN, SHIFT = slice(0, D), slice(D, 2 * D)
 FIRST, SECOND = 2 * D, 2 * D + FF
 VECTOR = 3 * D + FF
+PACKED = (48, 128)
 
 
 def dot(a, b):
@@ -384,15 +385,24 @@
     return jnp.concatenate([jnp.where(core == 0, a, b), jnp.where(core == 0, b, a)], axis=1)
 
 
+def fetch_kernel(flags, cos_in, sin_in, own, oth, cosf, sinf, wa, w1, wd, sems):
+    core = flags[0]
+    for i in range(4):
+        load_attn(core, own, oth, wa, sems, i)
+        load_mlp(core, own, oth, w1, wd, sems.at[pl.ds(4, 8)], i)
+    load_angles(cos_in, sin_in, cosf, sinf, sems.at[pl.ds(12, 2)])
+    for i in range(4):
+        wait_attn(own, wa, sems, i)
+        wait_mlp(own, w1, wd, sems.at[pl.ds(4, 8)], i)
+    wait_angles(cos_in, sin_in, cosf, sinf, sems.at[pl.ds(12, 2)])
+
+
 def second_kernel(
-    flags, field, got, vown, voth, pos, segr, cos_in, sin_in, own, oth,
-    cx, xi_out, xm_out, qkv_out, pt_out, rec_out, ml_out, actm_out, acts_out, dg_out,
-    main_out, tail_out, main_send, tail_send,
-    wa, w1, wd, cosf, sinf, xi, xm, qkv, pt, rec, ml, na, nm, actm, acts, dg,
-    mlt, vt, xha, xhm, kt, gm, gqt, dsum, gp, sems, angle_sems, outs,
+    flags, field, got, vown, voth, pos, segr, cosf, sinf, wa, w1, wd,
+    cx, xi_out, xm_out, qkv_out, pt_out, rec_out, ml_out, actm_out, acts_out, dg_out, main_out, tail_out, bundle,
+    xi, xm, qkv, pt, rec, ml, na, nm, actm, acts, dg, mlt, vt, xha, xhm, kt, gm, gqt, dsum, gp, outs,
 ):
     core, layer = flags[0], flags[1]
-    loads = Forward(core, own, oth, wa, w1, wd, cos_in, sin_in, cosf, sinf, sems, angle_sems)
     va, vm = vectors(core, vown, voth)
     sent = []
 
@@ -405,7 +415,7 @@
     xi[...] = x.astype(BF)
     send(xi, xi_out)
     x_mid, xh, inv_a = attention(
-        x, va, wa, loads.wait, cosf, sinf, pos[:, 2:3], segr[0:1, :], qkv, pt, rec, ml, mlt, vt, na
+        x, va, wa, lambda what: None, cosf, sinf, pos[:, 2:3], segr[0:1, :], qkv, pt, rec, ml, mlt, vt, na
     )
     xha[...] = xh
     xm[...] = x_mid
@@ -415,14 +425,17 @@
     xhm[...] = xh
     n = (xh * vm[:, GAIN] + vm[:, SHIFT]).astype(BF)
     nm[...] = n
+    sides = (
+        main_out, tail_out, bundle.at[:, pl.ds(2 * D, D)], bundle.at[:, pl.ds(3 * D, D)],
+    )
+    load(field, bundle.at[:, pl.ds(4 * D, D)], outs.at[13])
     for when, sources in ((core == 0, (na, ml, nm, nm)), (core != 0, (nm, nm, na, ml))):
 
         @pl.when(when)
         def _(sources=sources):
-            for k, (src, dst) in enumerate(zip(sources, (main_out, tail_out, main_send, tail_send))):
+            for k, (src, dst) in enumerate(zip(sources, sides)):
                 load(src, dst, outs.at[9 + k])
 
-    loads.wait_mlp()
     first = hidden_bias(core, vm)
     c = field[...]
 
@@ -437,6 +450,7 @@
         return slope
 
     def leave():
+        load(acts, bundle.at[:, pl.ds(0, 2 * D)], outs.at[14])
         for k, (src, dst) in enumerate(((actm, actm_out), (acts, acts_out), (dg, dg_out))):
             load(src, dst, outs.at[6 + k])
 
@@ -480,25 +494,39 @@
     for copy in sent:
         copy.wait()
     for k, (src, dst) in enumerate(
-        ((actm, actm_out), (acts, acts_out), (dg, dg_out), (nm, main_out), (nm, tail_out), (nm, main_send),
-         (nm, tail_send))
+        ((actm, actm_out), (acts, acts_out), (dg, dg_out)) + tuple((nm, side) for side in sides)
+        + ((field, sides[2]), (acts, bundle.at[:, pl.ds(0, 2 * D)]))
     ):
         arrived(src, dst, outs.at[6 + k])
 
 
-def late_kernel(flags, xm, x_two, actm, acts, vown, voth, own, oth, keep, send, wd, sems):
+def late_kernel(
+    flags, x_two, vown, voth, xm_in, dg_in, actm_in, acts_in, own, oth,
+    keep, send, xm, dg, wa, w1, wd, actm, acts, sems, ins,
+):
     core, layer = flags[0], flags[1]
+    held = ((xm_in, xm), (actm_in, actm), (acts_in, acts), (dg_in, dg))
     for j in range(4):
-        load((own if j < 2 else oth).at[cols(FF + D * (j % 2), D)], wd.at[j], sems.at[4 + j])
+        load((own if j < 2 else oth).at[cols(FF + D * (j % 2), D)], wd.at[j], sems.at[8 + j])
+    for k, (src, dst) in enumerate(held):
+        load(src, dst, ins.at[k])
+    for j in range(4):
+        pick(core, 1, own, oth, (slice(None), pl.ds(hidden_start(core, j), D)), w1.at[j], sems.at[4 + j])
+        load_attn(core, own, oth, wa, sems, j)
     vm = vectors(core, vown, voth)[1]
+    for k, (src, dst) in enumerate(held):
+        arrived(src, dst, ins.at[k])
     mid = xm[...].astype(F32)
     acc = mid + vm[:, SECOND : SECOND + D]
     for j in range(4):
-        wait_mlp(own, None, wd, sems, j)
+        arrived(own.at[cols(0, D)], wd.at[j], sems.at[8 + j])
         acc = acc + dot_nt((actm, acts)[j // 2][:, D * (j % 2) : D * (j % 2 + 1)], wd[j])
     acc = jnp.where(layer == 0, x_two[...].astype(F32), acc)
     keep[...] = jnp.where(core == 0, mid, acc).astype(BF)
     send[...] = jnp.where(core == 0, acc, mid).astype(BF)
+    for j in range(4):
+        arrived(own.at[cols(0, D)], w1.at[j], sems.at[4 + j])
+        wait_attn(own, wa, sems, j)
 
 
 def both_rows_kernel(flags, keep, got, out):
@@ -515,49 +543,23 @@
 
 
 def back_kernel(
-    flags, field, got, vown, voth, pos, xi_in, xm_in, dg_in, qkv_in, pt_in, rec_in, ml_in, cos_in, sin_in,
-    own, oth,
-    row_keep, row_send, va_grad, vm_grad, c_out, keep_out, send_out,
-    wa, w1, wd, cosf, sinf, xi, xm, dg, qkv, pt, rec, ml, gh, gp, c_kept, kt, gm, gqt, dsum,
-    sems, angle_sems, ins, outs,
+    flags, field, got, vown, voth, pos, xm, dg, wa, w1, wd, xi_in, qkv_in, pt_in, rec_in, ml_in, cos_in, sin_in,
+    row_keep, row_send, c_out, vec_keep, keep_out, send_out,
+    cosf, sinf, xi, qkv, pt, rec, ml, gh, gp, va_grad, vm_grad, folded, vec_send, kt, gm, gqt, dsum,
+    angle_sems, ins, outs,
 ):
     core, layer = flags[0], flags[1]
-    mlp_sems = sems.at[pl.ds(4, 8)]
-    held = ((xm_in, xm), (ml_in, ml), (rec_in, rec), (qkv_in, qkv), (pt_in, pt), (xi_in, xi))
-
-    def slopes(j):
-        sl = (slice(None), pl.ds(D * j, D))
-        return dg_in.at[sl], dg.at[sl], ins.at[6 + j]
-
-    def start_chunk(j):
-        load_mlp(core, own, oth, w1, wd, mlp_sems, j)
-        load(*slopes(j))
-
-    start_chunk(0)
-    start_chunk(1)
+    held = ((ml_in, ml), (rec_in, rec), (qkv_in, qkv), (pt_in, pt), (xi_in, xi))
+    for k, (src, dst) in enumerate(held):
+        load(src, dst, ins.at[k])
+    load_angles(cos_in, sin_in, cosf, sinf, angle_sems)
     va, vm = vectors(core, vown, voth)
     wide = jnp.where(layer == 0, got[...].astype(F32), field[...].astype(F32))
     c = wide.astype(BF)
-    c_kept[...] = c
-    leaving = [pltpu.make_async_copy(c_kept, c_out, outs.at[0])]
-    leaving[0].start()
+    c_out[...] = c
     vm_grad[:, SECOND:] = jnp.sum(wide, axis=0, keepdims=True)
 
     def from_output(j):
-        wait_mlp(own, w1, wd, mlp_sems, j)
-        arrived(*slopes(j))
-        if j < 2:
-            start_chunk(j + 2)
-        elif j == 2:
-            load_attn(core, own, oth, wa, sems, 3)
-            for k in range(4):
-                load(*held[k], ins.at[k])
-        else:
-            for k in range(4, len(held)):
-                load(*held[k], ins.at[k])
-            load_angles(cos_in, sin_in, cosf, sinf, angle_sems)
-            for i in range(3):
-                load_attn(core, own, oth, wa, sems, i)
         return dot(c, wd[j])
 
     ahead = from_output(0)
@@ -574,13 +576,12 @@
         )
         part = dot_nt(part, w1[j])
         gn = part if gn is None else gn + part
-    for when, dst in ((core == 0, send_out), (core != 0, keep_out)):
+    for when, dst in ((core == 0, send_out.at[pl.ds(0, L), :]), (core != 0, keep_out)):
 
         @pl.when(when)
         def _(dst=dst):
             load(gh, dst, outs.at[1])
 
-    arrived(xm_in, xm, ins.at[0])
     xh, inv = norm_stats(gn, xm[...].astype(F32), vm_grad)
     c = norm_back(gn, xh, inv, vm[:, GAIN], c)
     gp[:, 3 * D :] = c
@@ -599,15 +600,13 @@
                 g.astype(F32), axis=0, keepdims=True
             )
 
-    for k in range(1, len(held)):
-        arrived(*held[k], ins.at[k])
-    for i in range(4):
-        wait_attn(own, wa, sems, i)
+    for k, (src, dst) in enumerate(held):
+        arrived(src, dst, ins.at[k])
     wait_angles(cos_in, sin_in, cosf, sinf, angle_sems)
     attention_back(
         c, wa.at[3], cosf, sinf, qkv, pt, rec, ml, kt, gm, gqt, dsum, lambda p: p, emit
     )
-    for when, dst in ((core == 0, keep_out), (core != 0, send_out)):
+    for when, dst in ((core == 0, keep_out), (core != 0, send_out.at[pl.ds(0, L), :])):
 
         @pl.when(when)
         def _(dst=dst):
@@ -622,9 +621,18 @@
     wide = c.astype(F32)
     row_keep[...] = jnp.where(core == 0, cx, wide).astype(BF)
     row_send[...] = jnp.where(core == 0, wide, cx).astype(BF)
-    leaving[0].wait()
-    arrived(gh, send_out, outs.at[1])
+    fold_vector(va_grad, folded)
+    a, m = packed_vector(folded), packed_vector(vm_grad)
+    vec_keep[...] = jnp.where(core == 0, a, m)
+    for k, part in enumerate(split_two(jnp.where(core == 0, m, a))):
+        for b in range(3):
+            vec_send[:, 128 * (3 * k + b) : 128 * (3 * k + b + 1)] = part[16 * b : 16 * (b + 1), :]
+    vec_out = send_out.at[pl.ds(L, 16), pl.ds(0, D)]
+    load(vec_send, vec_out, outs.at[0])
+    main_rows = pl.ds(0, L)
+    arrived(gh, send_out.at[main_rows, :], outs.at[1])
     arrived(gp, keep_out, outs.at[2])
+    arrived(vec_send, vec_out, outs.at[0])
 
 
 def put(stage, value, out, first, sem):
@@ -634,63 +642,85 @@
     return copy
 
 
-def gram_down_kernel(flags, c, c_oth, field_oth, a0, a1, out, c0, c1, left, right, stages, sems):
-    load(c, c0, sems.at[0])
-    for at, src in enumerate((c_oth, field_oth)):
-
-        @pl.when(flags[1] == at)
-        def _(src=src):
-            load(src, c1, sems.at[1])
-
-    load(a0, right.at[pl.ds(0, L), :], sems.at[2])
-    load(a1, right.at[pl.ds(L, L), :], sems.at[3])
-    arrived(c, c0, sems.at[0])
-    arrived(c, c1, sems.at[1])
-    left[:, :L] = c0[...].T
-    left[:, L:] = c1[...].T
-    arrived(a0, right.at[pl.ds(0, L), :], sems.at[2])
-    arrived(a1, right.at[pl.ds(L, L), :], sems.at[3])
-    copies = [
-        put(stages.at[k], dot(left[...], right[:, D * k : D * (k + 1)]), out, D * (k + 1), sems.at[4 + k])
+def gram_down_kernel(
+    flags, c, c_oth, act, bundle, main0, tail0, right0, down, left_main, left_tail, right_out,
+    c1, sides, left, right, sems,
+):
+    loads = (
+        (bundle.at[:, pl.ds(4 * D, D)], c1), (act, right.at[pl.ds(0, L), :]),
+        (bundle.at[:, pl.ds(0, 2 * D)], right.at[pl.ds(L, L), :]),
+        (tail0, sides.at[0]), (bundle.at[:, pl.ds(3 * D, D)], sides.at[1]),
+        (main0, sides.at[2]), (bundle.at[:, pl.ds(2 * D, D)], sides.at[3]),
+        (right0, right_out.at[pl.ds(0, L), :]),
+    )
+    for k, (src, dst) in enumerate(loads):
+        load(src, dst, sems.at[k])
+    left[:, :L] = c[...].T
+    arrived(*loads[0], sems.at[0])
+
+    @pl.when(flags[1] == 0)
+    def _():
+        left[:, L:] = c_oth[...].T
+
+    @pl.when(flags[1] != 0)
+    def _():
+        left[:, L:] = c1[...].T
+
+    for k in range(1, 3):
+        arrived(*loads[k], sems.at[k])
+    down[...] = dot(left[...], right[...]).astype(BF)
+    for k in range(4):
+        arrived(*loads[3 + k], sems.at[3 + k])
+        (left_tail, left_main)[k // 2][:, L * (k % 2) : L * (k % 2 + 1)] = sides[k].T
+    arrived(*loads[7], sems.at[7])
+
+
+def gram_main_kernel(
+    rows, right1, down, left_main, left_tail, vec, right_in,
+    right, main, head, main_up, main_down, tail_up, tail_down, vec_out,
+):
+    right[L:, :] = right1[:L, :]
+    head[...] = dot(left_tail[...], right[:, 3 * D :]).astype(BF)
+    main[...] = dot(left_main[...], right[:, : 3 * D]).astype(BF)
+    other = [
+        jnp.concatenate(
+            [right1[L : L + 16, 128 * (3 * k + b) : 128 * (3 * k + b + 1)].astype(F32) for b in range(3)], axis=0
+        )
         for k in range(2)
     ]
-    for copy in copies:
-        copy.wait()
-
-
-def gram_main_kernel(
-    flags, main0, main1, tail0, tail1, b0, b1, tail_in, main_out, tail_out,
-    m0, m1, t0, t1, left, right, stages, sems,
-):
-    sides = ((tail0, t0), (tail1, t1), (main0, m0), (main1, m1))
-
-    def chunk(k, row):
-        sl = pl.ds(D * k, D)
-        return (b0, b1)[row].at[:, sl], right.at[k, pl.ds(L * row, L), :], sems.at[4 + 2 * k + row]
-
-    order = (3, 0, 1, 2)
-    for k in range(2):
-        load(*sides[k], sems.at[k])
-        load(*chunk(3, k))
-    for k in range(2, 4):
-        load(*sides[k], sems.at[k])
-        load(*chunk(0, k - 2))
-    copies = []
-    for at, k in enumerate(order):
-        if at < 2:
-            for row in range(2):
-                arrived(*sides[2 * at + row], sems.at[2 * at + row])
-                load(*chunk(order[at + 2], row))
-                left[at, :, L * row : L * (row + 1)] = (t0, t1, m0, m1)[2 * at + row][...].T
-        for row in range(2):
-            arrived(*chunk(k, row))
-        out, first = (tail_out, 0) if k == 3 else (main_out, D * k)
-        copies.append(put(stages.at[at], dot(left[min(at, 1)], right[k]), out, first, sems.at[12 + at]))
-    for copy in copies:
-        copy.wait()
-
-
-def vector_grads_kernel(flags, va, vm, mine, send):
+    total = vec[...] + (other[0] + other[1])
+    hi, lo = split_two(total)
+    vec_out[...] = hi.astype(F32) + lo.astype(F32)
+    r = main_up.shape[0]
+    for k, (m, t) in enumerate(((main_up, tail_up), (main_down, tail_down))):
+        here = own_rows(rows, 0, k, r)
+        m[:, : 3 * D] = main[here, :]
+        m[:, 3 * D :] = hi
+        t[:, :D] = head[here, :]
+        t[:, D : 3 * D] = down[here, :]
+        t[:, 3 * D :] = lo
+
+
+def own_rows(rows, t, way, r):
+    return pl.ds(pl.multiple_of(rows[t, way], 16), r)
+
+
+def add_kernel(t, rows, up, down, *refs, count, vector):
+    parts, outs, vectors = refs[:count], refs[count : count + 2], refs[count + 2 :]
+    for k, (got, out) in enumerate(zip((up, down), outs)):
+        here = own_rows(rows, t, k, got.shape[0])
+        at = 0
+        for part in parts:
+            sl = slice(at, at + part.shape[1])
+            out[:, sl] = (got[:, sl].astype(F32) + part[here, :].astype(F32)).astype(BF)
+            at += part.shape[1]
+        if out.shape[1] > at:
+            out[:, at:] = got[:, at:]
+        if k < vector:
+            vectors[k][...] = got[:, at : at + 128].astype(F32)
+
+
+def fold_vector(va, out):
     def fold(start):
         v = va[:, start : start + D]
         w = HEAD_DIM // 2
@@ -699,25 +729,34 @@
             axis=1,
         )
 
-    def attn(out):
-        at = FIRST + 3 * D
-        out[:, :at] = va[:, :at]
-        out[:, at : at + HALF] = fold(at)
-        out[:, at + HALF : SECOND] = fold(at + D)
-        out[:, SECOND:] = va[:, at + 2 * D :]
-
-    @pl.when(flags[0] == 0)
-    def _():
-        attn(mine)
-        send[...] = vm[...]
-
-    @pl.when(flags[0] != 0)
-    def _():
-        mine[...] = vm[...]
-        attn(send)
-
-
-def place_kernel(flags, rows, *refs):
+    at = FIRST + 3 * D
+    out[:, :at] = va[:, :at]
+    out[:, at : at + HALF] = fold(at)
+    out[:, at + HALF : SECOND] = fold(at + D)
+    out[:, SECOND:] = va[:, at + 2 * D :]
+
+
+def packed_vector(ref):
+    rows = [ref[:, 128 * k : 128 * (k + 1)] for k in range(VECTOR // 128)]
+    rows += [jnp.zeros((1, 128), F32)] * (PACKED[0] - len(rows))
+    return jnp.concatenate(rows, axis=0)
+
+
+def vector_sum_kernel(table, *refs):
+    out, slots = refs[-2:]
+    own, pieces = refs[0], refs[1:-2]
+    n = len(pieces) // 2 + 1
+    slots[table[0, 2]] = own[...]
+    for k in range(1, n):
+        t, way = (k + 1) // 2, (k + 1) % 2
+        slots[table[t, 2 + way]] = pieces[k - 1][...] + pieces[n + k - 2][...]
+    total = slots[0]
+    for k in range(1, n):
+        total = total + slots[k]
+    out[...] = total
+
+
+def place_kernel(t, rows, *refs):
     out, buf, sems = refs[-3:]
     count = sems.shape[0]
     shards = refs[: 2 * count]
@@ -728,7 +767,7 @@
         buf[there, : 3 * D] = shards[2 * k][...].astype(F32)
         buf[there, 3 * D :] = shards[2 * k + 1][...].astype(F32)
         copy = pltpu.make_async_copy(
-            buf.at[there, :], out.at[pl.ds(pl.multiple_of(rows[k], 8), r), :], sems.at[k]
+            buf.at[there, :], out.at[own_rows(rows, t, k, r), :], sems.at[k]
         )
         copy.start()
         copies.append(copy)
@@ -765,6 +804,10 @@
 BACK_S = [VM((D, L), BF), VM((L, D), BF), VM((2, 128, L), F32), VM((16, L), F32)]
 
 
+def in_vmem(a):
+    return pltpu.with_memory_space_constraint(a, pltpu.VMEM)
+
+
 def in_hbm(a):
     return pltpu.with_memory_space_constraint(a, pltpu.HBM)
 
@@ -780,7 +823,7 @@
 def prepare(flags, x, cot, *vecs):
     out = VM((x.shape[0], L), BF)
     return call(
-        prepare_kernel, "prepare", [SMEM] + [VS] * 6, [out] * 4 + [VM((1, VECTOR), F32)], [], 1000,
+        prepare_kernel, "prepare", [SMEM] + [VS] * 6, [out] * 4 + [pltpu.HBM((1, VECTOR), F32)], [], 1000,
         int(1e6), 8,
     )(flags, *(in_hbm(a) for a in (x, cot) + vecs))
 
@@ -790,7 +833,7 @@
     return call(
         positions_kernel, "positions", [SMEM, SMEM, VS, VS],
         [hbm((L, D), F32), hbm((L, D), F32), hbm((L, 128), F32), hbm((8, L), F32)],
-        [], int(1e8), int(3e6), 58,
+        [], int(1e8), int(3e6), 56,
     )(flags, grid, own, oth)
 
 
@@ -804,56 +847,78 @@
     )(*a)
 
 
+def fetch(*a):
+    return call(
+        fetch_kernel, "fetch", [SMEM] + [HBM] * 4, ANGLES + ATTN_W + MLP_W, [DMA((14,))], int(1e8), int(17e6), 8
+    )(*a)
+
+
 def second_pass(*a):
     saved = [
         row_out(), row_out(), row_out(3 * D), pltpu.HBM((HEADS, L, L), BF), pltpu.HBM((16, L), F32), row_out(),
-        row_out(FF // 2), row_out(FF // 2), row_out(FF), row_out(), row_out(), row_out(), row_out(),
+        row_out(FF // 2), row_out(FF // 2), row_out(FF), row_out(), row_out(), row_out(5 * D),
     ]
     return call(
-        second_kernel, "second_pass", [SMEM] + [VS] * 6 + [HBM] * 4, [row()] + saved,
-        ATTN_W + MLP_W + ANGLES
-        + [row(), row(), row(3 * D), VM((HEADS, L, L), BF), VM((16, L), F32), row(), row(), row(),
-           row(FF // 2), row(FF // 2), row(FF), VM((D, L), BF), VM((D, L), BF), VM((L, D), F32),
-           VM((L, D), F32)]
-        + BACK_S + [row(3 * D), DMA((12,)), DMA((2,)), DMA((13,))],
-        int(18e9), int(35e6), 48, out_specs=[VS] + [HBM] * len(saved),
+        second_kernel, "second_pass", [SMEM] + [VS] * 11, [row()] + saved,
+        [row(), row(), row(3 * D), VM((HEADS, L, L), BF), VM((16, L), F32), row(), row(), row(),
+         row(FF // 2), row(FF // 2), row(FF), VM((D, L), BF), VM((D, L), BF), VM((L, D), F32),
+         VM((L, D), F32)]
+        + BACK_S + [row(3 * D), DMA((15,))],
+        int(18e9), int(20e6), 32, out_specs=[VS] + [HBM] * len(saved),
     )(*a)
 
 
 def late_pass(*a):
     return call(
-        late_kernel, "late_pass", [SMEM] + [VS] * 6 + [HBM] * 2, [sds((L, D))] * 2,
-        [VM((4, D, D), BF), DMA((8,))], int(2e9), int(10e6), 16,
+        late_kernel, "late_pass", [SMEM] + [VS] * 3 + [HBM] * 6,
+        [sds((L, D))] * 2 + [row(), row(FF)] + ATTN_W + MLP_W,
+        [row(FF // 2), row(FF // 2), DMA((12,)), DMA((4,))], int(2e9), int(20e6), 14,
     )(*a)
 
 
 def back_pass(*a):
     return call(
-        back_kernel, "back_pass", [SMEM] + [VS] * 5 + [HBM] * 11,
-        [sds((L, D)), sds((L, D)), VM((1, FIRST + 6 * D), F32), VM((1, VECTOR), F32), row_out(),
-         row_out(FF), row_out(FF)],
-        ATTN_W + MLP_W + ANGLES
-        + [row(), row(), row(FF), row(3 * D), VM((HEADS, L, L), BF), VM((16, L), F32), row(), row(FF),
-           row(FF), row()]
-        + BACK_S + [DMA((12,)), DMA((2,)), DMA((10,)), DMA((3,))],
-        int(10e9), int(30e6), 52, out_specs=[VS] * 4 + [HBM] * 3,
+        back_kernel, "back_pass", [SMEM] + [VS] * 10 + [HBM] * 7,
+        [sds((L, D)), sds((L, D)), row(), VM(PACKED, F32), row_out(FF), pltpu.HBM((L + 16, FF), BF)],
+        ANGLES
+        + [row(), row(3 * D), VM((HEADS, L, L), BF), VM((16, L), F32), row(), row(FF), row(FF),
+           VM((1, FIRST + 6 * D), F32), VM((1, VECTOR), F32), VM((1, VECTOR), F32), VM((16, D), BF)]
+        + BACK_S + [DMA((2,)), DMA((5,)), DMA((3,))],
+        int(10e9), int(15e6), 30, out_specs=[VS] * 4 + [HBM] * 2,
     )(*a)
 
 
-def gram_down(flags, *a):
-    return call(
-        gram_down_kernel, "gram_down", [SMEM] + [HBM] * 5, [pltpu.HBM((D, 3 * D), BF)],
-        [row(), row(), VM((D, 2 * L), BF), VM((2 * L, 2 * D), BF), VM((2, D, D), BF), DMA((6,))],
-        int(2e9), int(8e6), 24, out_specs=[HBM],
-    )(flags, *(in_hbm(x) for x in a))[0]
-
-
-def gram_main(flags, *a):
-    return call(
-        gram_main_kernel, "gram_main", [SMEM] + [HBM] * 7, [pltpu.HBM((D, 3 * D), BF)] * 2,
-        [row()] * 4 + [VM((2, D, 2 * L), BF), VM((4, 2 * L, D), BF), VM((4, D, D), BF), DMA((16,))],
-        int(4e9), int(12e6), 32, out_specs=[HBM, HBM], aliases={7: 1},
-    )(flags, *(in_hbm(x) for x in a))
+def gram_down(*a):
+    square = VM((D, 2 * L), BF)
+    return call(
+        gram_down_kernel, "gram_down", [SMEM] + [VS] * 2 + [HBM] * 5,
+        [VM((D, 2 * D), BF), square, square, VM((2 * L, FF), BF)],
+        [row(), VM((4, L, D), BF), square, VM((2 * L, 2 * D), BF), DMA((8,))], int(2e9), int(8e6), 18,
+    )(*a)
+
+
+def gram_main(rows, r, *a):
+    wide = VM((r, 3 * D + 128), BF)
+    return call(
+        gram_main_kernel, "gram_main", [SMEM] + [VS] * 6,
+        [VM((2 * L, FF), BF), VM((D, 3 * D), BF), VM((D, D), BF)] + [wide] * 4 + [VM(PACKED, F32)],
+        [], int(4e9), int(12e6), 20, aliases={6: 0},
+    )(rows, *a)
+
+
+def add(t, rows, up, down, parts, vector, wide):
+    count = len(parts)
+
+    def kernel(*refs):
+        add_kernel(t, *refs, count=count, vector=vector)
+
+    width = sum(p.shape[1] for p in parts)
+    out = VM((up.shape[0], width + (128 if wide else 0)), BF)
+    results = call(
+        kernel, "add", [SMEM] + [VS] * (2 + count), [out, out] + [pltpu.HBM(PACKED, F32)] * vector, [], 1000,
+        int(1e6), 4,
+    )(rows, in_vmem(up), in_vmem(down), *(in_vmem(p) for p in parts))
+    return results[:2], results[2:]
 
 
 def both_rows(flags, keep, got):
@@ -879,22 +944,26 @@
     )(*resident(flags, 13, a))
 
 
-def vector_grads(flags, va, vm):
-    out = VM((1, VECTOR), F32)
-    return call(vector_grads_kernel, "vector_grads", [SMEM, VS, VS], [out, out], [], 1000, 100000, 4)(
-        flags, va, vm
-    )
-
-
-def place(flags, rows, shards, total):
+def vector_sum(table, own, pieces):
+    n = len(pieces) // 2 + 1
+    return call(
+        vector_sum_kernel, "vector_sum", [SMEM] + [VS] * (2 * n - 1), [sds(PACKED, F32)],
+        [VM((n,) + PACKED, F32)], 1000, 100000, 4,
+    )(table, own, *pieces)[0]
+
+
+def place(t, rows, shards, total):
+    def kernel(*refs):
+        place_kernel(t, *refs)
+
     r, count = shards[0].shape[0], len(shards) // 2
     into = [] if total is None else [total]
     return call(
-        place_kernel, "place", [SMEM, SMEM] + [VS] * len(shards) + [HBM] * len(into),
+        kernel, "place", [SMEM] + [VS] * len(shards) + [HBM] * len(into),
         [pltpu.HBM((D, 6 * D), F32)],
         [VM((r * count, 6 * D), F32), DMA((count,))], 1000, int(2e6), 24,
-        out_specs=[HBM], aliases={len(shards) + 2: 0} if into else {},
-    )(flags, rows, *shards, *into)[0]
+        out_specs=[HBM], aliases={len(shards) + 1: 0} if into else {},
+    )(rows, *shards, *into)[0]
 
 
 def core_swap(a):
@@ -905,39 +974,46 @@
     return lax.optimization_barrier((value, first))[0]
 
 
-class Chain:
-    def __init__(self, array):
-        self.array = array
+class Cycle:
+    def __init__(self):
         self.n = n = lax.axis_size("dp")
-        self.r = array.shape[0] // (2 * n)
+        self.r = D // (2 * n)
         i = lax.axis_index("dp")
-        self.where = jnp.where(i % 2 == 0, i // 2, n - 1 - i // 2)
+        where = jnp.where(i % 2 == 0, i // 2, n - 1 - i // 2)
         order = list(range(0, n, 2)) + list(range(n - 1, 0, -2))
         self.pairs = [[(order[k], order[(k + d) % n]) for k in range(n)] for d in (1, -1)]
+        t = jnp.arange(2 * n, dtype=I32)[:, None]
+        way = jnp.array([[1, -1]], I32)
+        step = jnp.where(t < n, t, t - n)
+        at = (where - way * step) % n
+        whose = jnp.where(2 * at < n, 2 * at, 2 * (n - at) - 1)
+        self.rows = in_hbm(jnp.concatenate([at * self.r + jnp.array([[0, HALF]], I32), whose], axis=1))
+
+    def placed(self, k):
+        return 2 * self.n - 1 if k == 0 else self.n + k - 1
+
+
+class Chain:
+    def __init__(self, cycle, parts, cur):
+        self.cycle, self.parts, self.cur = cycle, parts, cur
         self.t = 0
         self.shards = []
-        self.cur = self.own(0)
-
-    def rows(self, t):
-        return [
-            base + ((self.where - d * t) % self.n) * self.r
-            for base, d in ((0, 1), (self.array.shape[0] // 2, -1))
-        ]
-
-    def own(self, t):
-        return [lax.dynamic_slice_in_dim(self.array, at, self.r, 0) for at in self.rows(t)]
+        self.vectors = []
 
     def step(self, token):
-        got = [lax.ppermute(c, "dp", p) for c, p in zip(self.cur, self.pairs)]
+        c = self.cycle
+        got = [lax.ppermute(a, "dp", p) for a, p in zip(self.cur, c.pairs)]
         got = after(got, token)
-        if self.t < self.n - 1:
-            self.cur = [g + o for g, o in zip(got, self.own(self.t + 1))]
-            if self.t == self.n - 2:
-                self.shards.append((self.rows(-1), self.cur))
+        self.t += 1
+        if self.t < c.n:
+            t = self.t
+            ways = int(t <= c.n // 2) + int(t <= (c.n - 1) // 2)
+            self.cur, came = add(t, c.rows, *got, self.parts, ways, t < c.n // 2)
+            self.vectors += came
         else:
             self.cur = got
-            self.shards.append((self.rows(self.t - self.n + 1), got))
-        self.t += 1
+        if self.t >= c.n - 1:
+            self.shards.append(self.cur)
         return self.cur
 
 
@@ -945,12 +1021,13 @@
     return lax.axis_size("dp") <= 16
 
 
-def summed_weight_grad(flags, main, tail, token, beside):
+def summed_weight_grad(main, tail, token, beside):
     if not small_ring():
         for f in beside:
             token = f(token)
-        return place(flags, jnp.zeros((1,), I32), lax.psum([main, tail], "dp"), None)
-    n = main.n
+        return place(0, jnp.zeros((1, 1), I32), lax.psum([main, tail], "dp"), None)
+    cycle = main.cycle
+    n = cycle.n
     total = None
     beside = list(beside)
     while main.t < 2 * n - 2:
@@ -959,38 +1036,14 @@
             token = (token, total)
         token = main.step(token)
         if main.shards:
-            (rows, a), (_, b) = main.shards[-1], tail.shards[len(main.shards) - 1]
-            total = place(flags, jnp.stack(rows).astype(I32), [a[0], b[0], a[1], b[1]], total)
-            if beside and len(main.shards) > 1:
-                token = (token, beside.pop(0)(token))
+            k = len(main.shards) - 1
+            a, b = main.shards[k], tail.shards[k]
+            total = place(cycle.placed(k), cycle.rows, [a[0], b[0], a[1], b[1]], total)
+        if beside and main.t >= n:
+            token = (token, beside.pop(0)(token))
     for f in beside:
         token = f(token)
     return total
-
-
-class VectorSum:
-    def __init__(self, mine, send):
-        self.value, self.coming = mine, core_swap(send)
-        n = lax.axis_size("dp")
-        self.hops = [1 << k for k in range(n.bit_length() - 1)]
-        self.whole = n & (n - 1) == 0
-
-    def step(self, token):
-        self.value = self.value + after(self.coming, token)
-        if self.whole and self.hops:
-            hop = self.hops.pop(0)
-            self.coming = lax.ppermute(
-                self.value, "dp", [(i, i ^ hop) for i in range(lax.axis_size("dp"))]
-            )
-        else:
-            self.coming = None
-        return self.value
-
-    def steps(self):
-        return [self.step] * (len(self.hops) + 1 if self.whole else 1)
-
-    def total(self):
-        return self.value if self.whole else lax.psum(self.value, "dp")
 
 
 def body(
@@ -998,68 +1051,89 @@
 ):
     section = lax.axis_index("section")
     core = section % 2
-    flags = jnp.stack([core, section // 2]).astype(I32)
+    flags = in_hbm(jnp.stack([core, section // 2]).astype(I32))
     first_layer = section < 2
 
     keep, send, away, across, vown = prepare(
         flags, block_input.T, cotangent.T, norm_gain, norm_bias, first_vector, second_vector
     )
-    got, voth = core_swap(send), core_swap(vown)
+    n = lax.axis_size("dp")
+    if n % 2 == 0:
+        voth = lax.ppermute(
+            vown, ("section", "dp"), [(n * s + d, n * (s ^ 1) + (d ^ 1)) for s in range(4) for d in range(n)]
+        )
+    else:
+        voth = core_swap(vown)
+    vown, voth = in_hbm(vown), in_hbm(voth)
+    got = core_swap(send)
     away = lax.ppermute(away, "section", [(0, 2), (1, 3), (2, 0), (3, 1)])
     across = lax.ppermute(across, "section", [(0, 3), (1, 2), (2, 1), (3, 0)])
     own = in_hbm(section_weight[0])
-    oth = in_hbm(core_swap(after(section_weight[0], (got, voth))))
+    oth = in_hbm(core_swap(section_weight[0]))
     cosf, sinf, pos, segr = (in_hbm(a) for a in positions(flags, grid_sizes, vown, voth))
 
     x_two, field = first_pass(
         flags, keep, got, away, across, vown, voth, pos, segr, cosf, sinf, own, oth
     )
     field = in_hbm(field)
-    x_got = lax.ppermute(x_two, "section", [(0, 2), (1, 3)])
+    fetched = fetch(flags, cosf, sinf, own, after(oth, x_two))
+    x_got = after(lax.ppermute(x_two, "section", [(0, 2), (1, 3)]), fetched)
     (
-        c_two, x_in, x_mid, qkv, pt, rec, ml, act_mine, act_send, dg, main_left, tail_left, main_send,
-        tail_send,
-    ) = (in_hbm(a) if k else a for k, a in enumerate(
-        second_pass(flags, field, x_got, vown, voth, pos, segr, cosf, sinf, own, oth)
-    ))
+        c_two, x_in, x_mid, qkv, pt, rec, ml, act_mine, act_send, dg, main_left, tail_left, bundle,
+    ) = second_pass(flags, field, x_got, vown, voth, pos, segr, *(in_vmem(a) for a in fetched))
+    x_in, qkv, pt, rec, ml = (in_hbm(a) for a in (x_in, qkv, pt, rec, ml))
+    act_mine, main_left, tail_left = (in_hbm(a) for a in (act_mine, main_left, tail_left))
     c_got = lax.ppermute(c_two, "section", [(2, 0), (3, 1)])
-    act_oth, main_oth, tail_oth, field_oth = (
-        core_swap(a) for a in (act_send, main_send, tail_send, field)
-    )
-    x_keep, x_send = late_pass(
-        flags, after(x_mid, (act_oth, main_oth, tail_oth, field_oth)), x_two, act_mine, act_send, vown, voth,
-        own, oth,
+    bundle = in_hbm(core_swap(bundle))
+    x_keep, x_send, *held = late_pass(
+        flags, x_two, vown, voth, in_hbm(after(x_mid, bundle)), in_hbm(dg), act_mine, in_hbm(act_send), own, oth
     )
     c_got = after(c_got, x_keep)
-    activations = both_rows(flags, x_keep, core_swap(x_send))
-
-    c_keep, c_send, va, vm, c_out, right, right_send = back_pass(
-        flags, field, c_got, vown, voth, pos, x_in, x_mid, dg, qkv, pt, rec, ml, cosf, sinf, own, oth
-    )
-    tail = gram_down(
-        flags, c_out, core_swap(c_got), field_oth, act_mine, act_oth
-    )
-    main, tail = gram_main(
-        flags, main_left, main_oth, tail_left, tail_oth, right, core_swap(right_send), tail
+
+    c_keep, c_send, c_out, vec, right, right_send = back_pass(
+        flags, field, c_got, vown, voth, pos,
+        *(in_vmem(a) for a in held), x_in, qkv, pt, rec, ml, cosf, sinf,
+    )
+    c_oth = core_swap(c_got)
+    right_oth = core_swap(after(right_send, c_oth))
+    down, left_main, left_tail, right = gram_down(
+        flags, c_out, c_oth, act_mine, bundle, main_left, tail_left, in_hbm(right)
+    )
+    if small_ring():
+        cycle = Cycle()
+        rows, r = cycle.rows, cycle.r
+    else:
+        rows, r = jnp.zeros((1, 2), I32), PACKED[0]
+    right, main, head, *first, vec = gram_main(
+        rows, r, right_oth, down, left_main, left_tail, vec, right
     )
     token = main
     if small_ring():
-        main, tail = Chain(main), Chain(tail)
-        token = main.cur
-    vector = VectorSum(*vector_grads(flags, va, vm))
-    rows = {}
+        main, tail = Chain(cycle, [main], first[:2]), Chain(cycle, [head, down], first[2:])
+    else:
+        tail = jnp.concatenate([head, down], axis=1)
+    swapped = {}
 
     def send_rows(token):
-        rows["got"] = core_swap(after(c_send, token))
-        return c_send
-
-    def join_rows(token):
-        rows["out"] = both_rows(flags, c_keep, after(rows["got"], token))
-        return rows["out"]
-
-    weight_grad = summed_weight_grad(flags, main, tail, token, vector.steps() + [send_rows, join_rows])
-    vg = vector.total()
-    input_grads = rows["out"]
+        swapped["x"], swapped["c"] = core_swap(after(x_send, token)), core_swap(after(c_send, token))
+        return x_keep
+
+    def join(name, keep):
+        def f(token):
+            swapped[name] = both_rows(flags, keep, after(swapped[name], token))
+            return swapped[name]
+
+        return f
+
+    weight_grad = summed_weight_grad(
+        main, tail, token, [send_rows, join("x", x_keep), join("c", c_keep)]
+    )
+    if small_ring():
+        vec = vector_sum(cycle.rows, vec, main.vectors + tail.vectors)
+    else:
+        vec = lax.psum(vec, "dp")
+    vg = vec.reshape(1, -1)[:, :VECTOR]
+    activations, input_grads = swapped["x"], swapped["c"]
     return (
         activations[None],
         input_grads[None],

time: 294 us -> 271 us (0.922)
  waiting for transfers between devices: 100 us -> 74.5 us
  Pallas kernels: 103 us -> 117 us
  other arithmetic: 5.43 us -> 0.69 us
  local copies, waits for them, and re-layouts: 8.51 us -> 4.76 us
  starting transfers between devices: 71.9 us -> 68.6 us
    ppermute x60 -> x58, waiting for transfers between devices: 77.3 us -> 60.5 us  [the longest x56 53.7 us: step(): got = [lax.ppermute(a, 'dp', p) for a, p in zip(self.cur, c.pairs)]]
    pallas_call x15 -> x30, Pallas kernels: 82.2 us -> 96.1 us  [the longest x1 17.7 us: back_pass(): call(back_kernel, 'back_pass', [SMEM] + [VS] * 10 + [HBM] * 7, [sds((L, D...]
    ppermute x12 -> x7, waiting for transfers between devices: 11.7 us -> 4.29 us  [core_swap(): return lax.ppermute(a, 'section', [(0, 1), (1, 0), (2, 3), (3, 2)])]
    add x18 -> x2, other arithmetic: 4.75 us -> 0.09 us  [__init__(): at * self.r + jnp.array([[0, HALF]], I32)]
    ppermute x60 -> x58, starting transfers between devices: 65.3 us -> 63.1 us  [the longest x56 58.6 us: step(): got = [lax.ppermute(a, 'dp', p) for a, p in zip(self.cur, c.pairs)]]
  transfers between devices with their start and end apart: 75 -> 68, of which waited for: 49 -> 46; matrix products, arithmetic and copies ran while one was open for 3% -> 1% of each run, Pallas kernels for 11% -> 30%
where the time goes in v2:
time: 271 us; the launch traced here: 267 us
  Pallas kernels  117 us (43%)
  waiting for transfers between devices  74.5 us (27%)
  starting transfers between devices  68.6 us (25%)
  local copies, waits for them, and re-layouts  4.76 us (2%)
    ppermute x56, starting transfers between devices, step(): got = [lax.ppermute(a, 'dp', p) for a, p in zip(self.cur, c.pairs)]  58.6 us
    ppermute x56, waiting for transfers between devices, step(): got = [lax.ppermute(a, 'dp', p) for a, p in zip(self.cur, c.pairs)]  53.7 us
    pallas_call x1, Pallas kernels, back_pass(): call(back_kernel, 'back_pass', [SMEM] + [VS] * 10 + [HBM] * 7, [sds((L, D...  17.7 us
    pallas_call x14, Pallas kernels, add(): call(kernel, 'add', [SMEM] + [VS] * (2 + count), [out, out] + [pltpu.HBM(...  16.6 us
    pallas_call x8, Pallas kernels, place(): call(kernel, 'place', [SMEM] + [VS] * len(shards) + [HBM] * len(into), [p...  16.5 us
    pallas_call x1, Pallas kernels, first_pass(): call(first_kernel, 'first_pass', [SMEM] + [VS] * 8 + [HBM] * 4, [row(), r...  14.4 us
    pallas_call x1, Pallas kernels, second_pass(): call(second_kernel, 'second_pass', [SMEM] + [VS] * 11, [row()] + saved, [...  13.9 us
    pallas_call x1, Pallas kernels, late_pass(): call(late_kernel, 'late_pass', [SMEM] + [VS] * 3 + [HBM] * 6, [sds((L, D)...  11.1 us
  transfers between devices with their start and end apart: 68, of which 46 were waited for; matrix products, arithmetic and copies ran while one was open for 1% of the time, Pallas kernels for 30%

profile of v2, /device:TPU:0, one launch (start us, length us, event | category | flops | bytes accessed | tf_op | source)
XLA Modules:
  0.0 267.4 jit_solution(9089453412566038465)
XLA Ops:
  3.5 3.0 %collective-permute-start.1 = (bf16[192,384]{1,0:T(8,128)(2,1)S(1)}, bf16[192,384]{1,0:T(8,128)(2,1)S(1)}, u32[]{:S(2)}, u32[]{:S(2)}) collective-permute-start(bf16[192,384]{1,0:T(8,128)(2,1)S(1)} %get-tuple-element.169), channel_id=1, source_target_pairs={{0,16},{8,24},{16,0},{24,8},{1,17},{9,25},{17,1},{25,9},{2,18},{10... | collective-permute-start | bytes 442376 | tf_op jit(solution)/shard_map/ppermute | solution.py:1069
  10.5 3.5 %positions.1 = (f32[384,768]{1,0:T(8,128)}, f32[384,768]{1,0:T(8,128)}, f32[384,128]{1,0:T(8,128)}, f32[8,384]{1,0:T(8,128)}) custom-call(s32[2]{0:T(128)} %pad_add_fusion.1.flags, s32[2,2,2]{2,1,0:T(2,128)} %grid.1, f32[1,5376]{1,0:T(1,128)} %get-tuple-element.171.vown, f32[1,5376]{1,0:T(1,128)} %copy-done.17), custom_call_target="tpu_custom_call" | custom-call | flops 100000000 | bytes 3000000 | tf_op jit(solution)/shard_map/positions/pallas_call | solution.py:833
  14.1 14.4 %first_pass.1 = (bf16[384,768]{1,0:T(8,128)(2,1)S(1)}, bf16[384,768]{1,0:T(8,128)(2,1)}) custom-call(s32[2]{0:T(128)} %pad_add_fusion.1.flags, bf16[192,384]{1,0:T(8,128)(2,1)S(1)} %get-tuple-element.167.keep, bf16[192,384]{1,0:T(8,128)(2,1)S(1)} %collective-permute-done.got, bf16[192,384]{1,0:T(8,128)(2,1)S(1)} %collective-permute-done.1.away, ...), custom_call_target="tpu_custom_call" | custom-call | flops 8000000000 | bytes 20000000 | tf_op jit(solution)/shard_map/first_pass/pallas_call | solution.py:841
  28.5 2.8 %collective-permute-start.5 = (bf16[384,768]{1,0:T(8,128)(2,1)S(1)}, bf16[384,768]{1,0:T(8,128)(2,1)S(1)}, u32[]{:S(2)}, u32[]{:S(2)}) collective-permute-start(bf16[384,768]{1,0:T(8,128)(2,1)S(1)} %get-tuple-element.176.x_two), channel_id=1, source_target_pairs={{0,16},{8,24},{1,17},{9,25},{2,18},{10,26},{3,19},{11,27},{4,20},{... | collective-permute-start | bytes 1769480 | tf_op jit(solution)/shard_map/ppermute | solution.py:1080
  31.3 6.6 %fetch.1 = (f32[384,768]{1,0:T(8,128)S(1)}, f32[384,768]{1,0:T(8,128)S(1)}, bf16[4,768,768]{2,1,0:T(8,128)(2,1)S(1)}, bf16[4,768,768]{2,1,0:T(8,128)(2,1)S(1)}, bf16[4,768,768]{2,1,0:T(8,128)(2,1)S(1)}) custom-call(s32[2]{0:T(128)} %pad_add_fusion.1.flags, f32[384,768]{1,0:T(8,128)} %get-tuple-element.174.cos_in, f32[384,768]{1,0:T(8,128)} %get-tuple-element.175.sin_in, ...), custom_call_target="tpu_custom_call" | custom-call | flops 100000000 | bytes 17000000 | tf_op jit(solution)/shard_map/fetch/pallas_call | solution.py:851
  37.9 5.0 %collective-permute-done.5.got = bf16[384,768]{1,0:T(8,128)(2,1)S(1)} collective-permute-done((bf16[384,768]{1,0:T(8,128)(2,1)S(1)}, bf16[384,768]{1,0:T(8,128)(2,1)S(1)}, u32[]{:S(2)}, u32[]{:S(2)}) %collective-permute-start.5) | collective-permute-done | bytes 589856 | tf_op jit(solution)/shard_map/ppermute | solution.py:1080
  42.9 13.9 %second_pass.1 = (bf16[384,768]{1,0:T(8,128)(2,1)S(1)}, bf16[384,768]{1,0:T(8,128)(2,1)}, bf16[384,768]{1,0:T(8,128)(2,1)}, bf16[384,2304]{1,0:T(8,128)(2,1)}, b...) custom-call(s32[2]{0:T(128)} %pad_add_fusion.1.flags, ...), custom_call_target="tpu_custom_call" | custom-call | flops 17999998976 | bytes 20000000 | tf_op jit(solution)/shard_map/second_pass/pallas_call | solution.py:861
  58.2 4.3 %collective-permute-done.6.bundle = bf16[384,3840]{1,0:T(8,128)(2,1)S(1)} collective-permute-done((bf16[384,3840]{1,0:T(8,128)(2,1)}, bf16[384,3840]{1,0:T(8,128)(2,1)S(1)}, u32[]{:S(2)}, u32[]{:S(2)}) %collective-permute-start.6) | collective-permute-done | bytes 2949152 | tf_op jit(solution)/shard_map/ppermute | solution.py:970
  64.1 11.1 %late_pass.1 = (bf16[384,768]{1,0:T(8,128)(2,1)S(1)}, bf16[384,768]{1,0:T(8,128)(2,1)S(1)}, bf16[384,768]{1,0:T(8,128)(2,1)S(1)}, bf16[384,3072]{1,0:T(8,128)(2,...) custom-call(s32[2]{0:T(128)} %pad_add_fusion.1.flags, ...), custom_call_target="tpu_custom_call" | custom-call | flops 2000000000 | bytes 20000000 | tf_op jit(solution)/shard_map/late_pass/pallas_call | solution.py:872
  75.2 9.7 %collective-permute-done.7.got = bf16[384,768]{1,0:T(8,128)(2,1)S(1)} collective-permute-done((bf16[384,768]{1,0:T(8,128)(2,1)S(1)}, bf16[384,768]{1,0:T(8,128)(2,1)S(1)}, u32[]{:S(2)}, u32[]{:S(2)}) %collective-permute-start.7) | collective-permute-done | bytes 589856 | tf_op jit(solution)/shard_map/ppermute | solution.py:1086
  84.9 17.7 %back_pass.1 = (bf16[384,768]{1,0:T(8,128)(2,1)S(1)}, bf16[384,768]{1,0:T(8,128)(2,1)S(1)}, bf16[384,768]{1,0:T(8,128)(2,1)S(1)}, f32[48,128]{1,0:T(8,128)S(1)},...) custom-call(s32[2]{0:T(128)} %pad_add_fusion.1.flags, bf16[384,768]{1,0:T(8,128)(2,1)} %get-tuple-element.177.field, ...), custom_call_target="tpu_custom_call" | custom-call | flops 10000000000 | bytes 15000000 | tf_op jit(solution)/shard_map/back_pass/pallas_call | solution.py:880
  104.5 5.5 %gram_down.1 = (bf16[768,1536]{1,0:T(8,128)(2,1)S(1)}, bf16[768,768]{1,0:T(8,128)(2,1)S(1)}, bf16[768,768]{1,0:T(8,128)(2,1)S(1)}, bf16[768,3072]{1,0:T(8,128)(2,1)S(1)}) custom-call(s32[2]{0:T(128)} %pad_add_fusion.1.flags, bf16[384,768]{1,0:T(8,128)(2,1)S(1)} %get-tuple-element.207.c, bf16[384,768]{1,0:T(8,128)(2,1)S(1)} %collective-permute-done.8.c_oth, ...), custom_call_target="tpu_custom_call" | custom-call | flops 2000000000 | bytes 8000000 | tf_op jit(solution)/shard_map/gram_down/pallas_call | solution.py:893
  110.1 5.6 %gram_main.1 = (bf16[768,3072]{1,0:T(8,128)(2,1)S(1)}, bf16[768,2304]{1,0:T(8,128)(2,1)S(1)}, bf16[768,768]{1,0:T(8,128)(2,1)S(1)}, bf16[48,2432]{1,0:T(8,128)(2...) custom-call(s32[16,4]{1,0:T(8,128)} %copy.39.rows.refs_0_.table, ...), custom_call_target="tpu_custom_call", output_to_operand_aliasing={{0}: (6, {})} | custom-call | flops 4000000000 | bytes 12000000 | tf_op jit(solution)/shard_map/gram_main/pallas_call | solution.py:902
  115.7 2.1 collective-permute-start.12
  117.8 2.0 collective-permute-start.10
  119.8 4.4 %collective-permute-done.12.refs_1_ = bf16[48,2432]{1,0:T(8,128)(2,1)S(1)} collective-permute-done((bf16[48,2432]{1,0:T(8,128)(2,1)S(1)}, bf16[48,2432]{1,0:T(8,128)(2,1)S(1)}, u32[]{:S(2)}, u32[]{:S(2)}) %collective-permute-start.12) | collective-permute-done | bytes 233504 | tf_op jit(solution)/shard_map/ppermute | solution.py:1005
  124.3 2.1 collective-permute-done.13.refs_2_
  134.7 1.9 collective-permute-done.17.refs_2_
  165.0 2.0 collective-permute-start.26
  175.1 1.8 collective-permute-start.30
  180.1 1.9 collective-permute-start.36
  197.8 2.1 place.8.refs_5_
  206.3 4.2 %collective-permute-done.45.refs_2_ = bf16[48,2304]{1,0:T(8,128)(2,1)S(1)} collective-permute-done((bf16[48,2304]{1,0:T(8,128)(2,1)S(1)}, bf16[48,2304]{1,0:T(8,128)(2,1)S(1)}, u32[]{:S(2)}, u32[]{:S(2)}) %collective-permute-start.45) | collective-permute-done | bytes 221216 | tf_op jit(solution)/shard_map/ppermute | solution.py:1005
  210.4 2.1 place.9.refs_5_
  214.8 1.8 collective-permute-start.51
  218.6 2.1 place.10.refs_5_
  225.5 2.6 collective-permute-done.49.refs_3_
  230.1 2.1 place.11.refs_5_
  239.5 2.1 place.12.refs_5_
  252.3 2.1 place.13.refs_5_
  260.6 2.1 place.14.refs_5_
  265.1 2.1 place.15
  (184 shorter events, 119.5 us)
Async XLA Ops:
  0.6 13.4 %collective-permute-start.4 = (bf16[768,4608]{1,0:T(8,128)(2,1)}, bf16[768,4608]{1,0:T(8,128)(2,1)}, u32[]{:S(2)}, u32[]{:S(2)}) collective-permute-start(bf16[768,4608]{1,0:T(8,128)(2,1)} %bitcast.12), channel_id=1, source_target_pairs={{0,8},{8,0},{16,24},{24,16},{1,9},{9,1},{17,25},{25,17},{2,10},{10... | collective-permute-start | bytes 21233672 | tf_op jit(solution)/shard_map/ppermute | solution.py:970
  3.5 10.6 %collective-permute-start = (bf16[192,384]{1,0:T(8,128)(2,1)S(1)}, bf16[192,384]{1,0:T(8,128)(2,1)S(1)}, u32[]{:S(2)}, u32[]{:S(2)}) collective-permute-start(bf16[192,384]{1,0:T(8,128)(2,1)S(1)} %get-tuple-element.168), channel_id=1, source_target_pairs={{0,8},{8,0},{16,24},{24,16},{1,9},{9,1},{17,25},{25,17},{2,10},{10... | collective-permute-start | bytes 442376 | tf_op jit(solution)/shard_map/ppermute | solution.py:970
  3.5 10.5 %collective-permute-start.1 = (bf16[192,384]{1,0:T(8,128)(2,1)S(1)}, bf16[192,384]{1,0:T(8,128)(2,1)S(1)}, u32[]{:S(2)}, u32[]{:S(2)}) collective-permute-start(bf16[192,384]{1,0:T(8,128)(2,1)S(1)} %get-tuple-element.169), channel_id=1, source_target_pairs={{0,16},{8,24},{16,0},{24,8},{1,17},{9,25},{17,1},{25,9},{2,18},{10... | collective-permute-start | bytes 442376 | tf_op jit(solution)/shard_map/ppermute | solution.py:1069
  28.5 14.5 %collective-permute-start.5 = (bf16[384,768]{1,0:T(8,128)(2,1)S(1)}, bf16[384,768]{1,0:T(8,128)(2,1)S(1)}, u32[]{:S(2)}, u32[]{:S(2)}) collective-permute-start(bf16[384,768]{1,0:T(8,128)(2,1)S(1)} %get-tuple-element.176.x_two), channel_id=1, source_target_pairs={{0,16},{8,24},{1,17},{9,25},{2,18},{10,26},{3,19},{11,27},{4,20},{... | collective-permute-start | bytes 1769480 | tf_op jit(solution)/shard_map/ppermute | solution.py:1080
  56.9 28.0 %collective-permute-start.7 = (bf16[384,768]{1,0:T(8,128)(2,1)S(1)}, bf16[384,768]{1,0:T(8,128)(2,1)S(1)}, u32[]{:S(2)}, u32[]{:S(2)}) collective-permute-start(bf16[384,768]{1,0:T(8,128)(2,1)S(1)} %get-tuple-element.193), channel_id=1, source_target_pairs={{16,0},{24,8},{17,1},{25,9},{18,2},{26,10},{19,3},{27,11},{20,4},{... | collective-permute-start | bytes 1769480 | tf_op jit(solution)/shard_map/ppermute | solution.py:1086
  84.9 18.3 %collective-permute-start.8 = (bf16[384,768]{1,0:T(8,128)(2,1)S(1)}, bf16[384,768]{1,0:T(8,128)(2,1)S(1)}, u32[]{:S(2)}, u32[]{:S(2)}) collective-permute-start(bf16[384,768]{1,0:T(8,128)(2,1)S(1)} %collective-permute-done.7.got), channel_id=1, source_target_pairs={{0,8},{8,0},{16,24},{24,16},{1,9},{9,1},{17,25},{25,17},{2,10},{10... | collective-permute-start | bytes 1769480 | tf_op jit(solution)/shard_map/ppermute | solution.py:970
  115.7 8.6 %collective-permute-start.12 = (bf16[48,2432]{1,0:T(8,128)(2,1)S(1)}, bf16[48,2432]{1,0:T(8,128)(2,1)S(1)}, u32[]{:S(2)}, u32[]{:S(2)}) collective-permute-start(bf16[48,2432]{1,0:T(8,128)(2,1)S(1)} %get-tuple-element.218), channel_id=1, source_target_pairs={{0,2},{2,4},{4,6},{6,7},{7,5},{5,3},{3,1},{1,0},{8,10},{10,12},{12... | collective-permute-start | bytes 700424 | tf_op jit(solution)/shard_map/ppermute | solution.py:1005
  117.8 8.6 %collective-permute-start.13 = (bf16[48,2432]{1,0:T(8,128)(2,1)S(1)}, bf16[48,2432]{1,0:T(8,128)(2,1)S(1)}, u32[]{:S(2)}, u32[]{:S(2)}) collective-permute-start(bf16[48,2432]{1,0:T(8,128)(2,1)S(1)} %get-tuple-element.219), channel_id=1, source_target_pairs={{0,1},{2,0},{4,2},{6,4},{7,6},{5,7},{3,5},{1,3},{8,9},{10,8},{12,1... | collective-permute-start | bytes 700424 | tf_op jit(solution)/shard_map/ppermute | solution.py:1005
  117.8 12.0 %collective-permute-start.10 = (bf16[48,2432]{1,0:T(8,128)(2,1)S(1)}, bf16[48,2432]{1,0:T(8,128)(2,1)S(1)}, u32[]{:S(2)}, u32[]{:S(2)}) collective-permute-start(bf16[48,2432]{1,0:T(8,128)(2,1)S(1)} %get-tuple-element.216), channel_id=1, source_target_pairs={{0,2},{2,4},{4,6},{6,7},{7,5},{5,3},{3,1},{1,0},{8,10},{10,12},{12... | collective-permute-start | bytes 700424 | tf_op jit(solution)/shard_map/ppermute | solution.py:1005
  119.8 11.1 %collective-permute-start.11 = (bf16[48,2432]{1,0:T(8,128)(2,1)S(1)}, bf16[48,2432]{1,0:T(8,128)(2,1)S(1)}, u32[]{:S(2)}, u32[]{:S(2)}) collective-permute-start(bf16[48,2432]{1,0:T(8,128)(2,1)S(1)} %get-tuple-element.217), channel_id=1, source_target_pairs={{0,1},{2,0},{4,2},{6,4},{7,6},{5,7},{3,5},{1,3},{8,9},{10,8},{12,1... | collective-permute-start | bytes 700424 | tf_op jit(solution)/shard_map/ppermute | solution.py:1005
  132.3 8.6 %collective-permute-start.14 = (bf16[48,2432]{1,0:T(8,128)(2,1)S(1)}, bf16[48,2432]{1,0:T(8,128)(2,1)S(1)}, u32[]{:S(2)}, u32[]{:S(2)}) collective-permute-start(bf16[48,2432]{1,0:T(8,128)(2,1)S(1)} %get-tuple-element.228), channel_id=1, source_target_pairs={{0,2},{2,4},{4,6},{6,7},{7,5},{5,3},{3,1},{1,0},{8,10},{10,12},{12... | collective-permute-start | bytes 700424 | tf_op jit(solution)/shard_map/ppermute | solution.py:1005
  133.9 8.6 %collective-permute-start.15 = (bf16[48,2432]{1,0:T(8,128)(2,1)S(1)}, bf16[48,2432]{1,0:T(8,128)(2,1)S(1)}, u32[]{:S(2)}, u32[]{:S(2)}) collective-permute-start(bf16[48,2432]{1,0:T(8,128)(2,1)S(1)} %get-tuple-element.229), channel_id=1, source_target_pairs={{0,1},{2,0},{4,2},{6,4},{7,6},{5,7},{3,5},{1,3},{8,9},{10,8},{12,1... | collective-permute-start | bytes 700424 | tf_op jit(solution)/shard_map/ppermute | solution.py:1005
  169.9 8.4 %collective-permute-start.32 = (bf16[48,2304]{1,0:T(8,128)(2,1)S(1)}, bf16[48,2304]{1,0:T(8,128)(2,1)S(1)}, u32[]{:S(2)}, u32[]{:S(2)}) collective-permute-start(bf16[48,2304]{1,0:T(8,128)(2,1)S(1)} %get-tuple-element.256), channel_id=1, source_target_pairs={{0,2},{2,4},{4,6},{6,7},{7,5},{5,3},{3,1},{1,0},{8,10},{10,12},{12... | collective-permute-start | bytes 663560 | tf_op jit(solution)/shard_map/ppermute | solution.py:1005
  186.4 8.5 %collective-permute-start.35 = (bf16[48,2304]{1,0:T(8,128)(2,1)S(1)}, bf16[48,2304]{1,0:T(8,128)(2,1)S(1)}, u32[]{:S(2)}, u32[]{:S(2)}) collective-permute-start(bf16[48,2304]{1,0:T(8,128)(2,1)S(1)} %get-tuple-element.269), channel_id=1, source_target_pairs={{0,1},{2,0},{4,2},{6,4},{7,6},{5,7},{3,5},{1,3},{8,9},{10,8},{12,1... | collective-permute-start | bytes 663560 | tf_op jit(solution)/shard_map/ppermute | solution.py:1005
  191.0 8.9 %collective-permute-start.40 = (bf16[48,2304]{1,0:T(8,128)(2,1)S(1)}, bf16[48,2304]{1,0:T(8,128)(2,1)S(1)}, u32[]{:S(2)}, u32[]{:S(2)}) collective-permute-start(bf16[48,2304]{1,0:T(8,128)(2,1)S(1)} %get-tuple-element.272.refs_2_), channel_id=1, source_target_pairs={{0,2},{2,4},{4,6},{6,7},{7,5},{5,3},{3,1},{1,0},{8,10},{10,12},{12... | collective-permute-start | bytes 663560 | tf_op jit(solution)/shard_map/ppermute | solution.py:1005
  191.4 8.6 %collective-permute-start.41 = (bf16[48,2304]{1,0:T(8,128)(2,1)S(1)}, bf16[48,2304]{1,0:T(8,128)(2,1)S(1)}, u32[]{:S(2)}, u32[]{:S(2)}) collective-permute-start(bf16[48,2304]{1,0:T(8,128)(2,1)S(1)} %get-tuple-element.273.refs_4_), channel_id=1, source_target_pairs={{0,1},{2,0},{4,2},{6,4},{7,6},{5,7},{3,5},{1,3},{8,9},{10,8},{12,1... | collective-permute-start | bytes 663560 | tf_op jit(solution)/shard_map/ppermute | solution.py:1005
  202.2 14.9 %collective-permute-start.42 = (bf16[384,768]{1,0:T(8,128)(2,1)S(1)}, bf16[384,768]{1,0:T(8,128)(2,1)S(1)}, u32[]{:S(2)}, u32[]{:S(2)}) collective-permute-start(bf16[384,768]{1,0:T(8,128)(2,1)S(1)} %get-tuple-element.282), channel_id=1, source_target_pairs={{0,8},{8,0},{16,24},{24,16},{1,9},{9,1},{17,25},{25,17},{2,10},{10... | collective-permute-start | bytes 1769480 | tf_op jit(solution)/shard_map/ppermute | solution.py:970
  203.8 8.7 %collective-permute-start.46 = (bf16[48,2304]{1,0:T(8,128)(2,1)S(1)}, bf16[48,2304]{1,0:T(8,128)(2,1)S(1)}, u32[]{:S(2)}, u32[]{:S(2)}) collective-permute-start(bf16[48,2304]{1,0:T(8,128)(2,1)S(1)} %collective-permute-done.41.refs_4_), channel_id=1, source_target_pairs={{0,1},{2,0},{4,2},{6,4},{7,6},{5,7},{3,5},{1,3},{8,9},{10,8},{12,1... | collective-permute-start | bytes 663560 | tf_op jit(solution)/shard_map/ppermute | solution.py:1005
  204.2 10.6 %collective-permute-start.43 = (bf16[48,2304]{1,0:T(8,128)(2,1)S(1)}, bf16[48,2304]{1,0:T(8,128)(2,1)S(1)}, u32[]{:S(2)}, u32[]{:S(2)}) collective-permute-start(bf16[48,2304]{1,0:T(8,128)(2,1)S(1)} %collective-permute-done.38.refs_1_), channel_id=1, source_target_pairs={{0,2},{2,4},{4,6},{6,7},{7,5},{5,3},{3,1},{1,0},{8,10},{10,12},{12... | collective-permute-start | bytes 663560 | tf_op jit(solution)/shard_map/ppermute | solution.py:1005
  205.8 10.8 %collective-permute-start.44 = (bf16[48,2304]{1,0:T(8,128)(2,1)S(1)}, bf16[48,2304]{1,0:T(8,128)(2,1)S(1)}, u32[]{:S(2)}, u32[]{:S(2)}) collective-permute-start(bf16[48,2304]{1,0:T(8,128)(2,1)S(1)} %collective-permute-done.39.refs_3_), channel_id=1, source_target_pairs={{0,1},{2,0},{4,2},{6,4},{7,6},{5,7},{3,5},{1,3},{8,9},{10,8},{12,1... | collective-permute-start | bytes 663560 | tf_op jit(solution)/shard_map/ppermute | solution.py:1005
  210.4 21.8 %collective-permute-start.47 = (bf16[384,768]{1,0:T(8,128)(2,1)S(1)}, bf16[384,768]{1,0:T(8,128)(2,1)S(1)}, u32[]{:S(2)}, u32[]{:S(2)}) collective-permute-start(bf16[384,768]{1,0:T(8,128)(2,1)S(1)} %get-tuple-element.290), channel_id=1, source_target_pairs={{0,8},{8,0},{16,24},{24,16},{1,9},{9,1},{17,25},{25,17},{2,10},{10... | collective-permute-start | bytes 1769480 | tf_op jit(solution)/shard_map/ppermute | solution.py:970
  212.5 10.0 %collective-permute-start.50 = (bf16[48,2304]{1,0:T(8,128)(2,1)S(1)}, bf16[48,2304]{1,0:T(8,128)(2,1)S(1)}, u32[]{:S(2)}, u32[]{:S(2)}) collective-permute-start(bf16[48,2304]{1,0:T(8,128)(2,1)S(1)} %collective-permute-done.45.refs_2_), channel_id=1, source_target_pairs={{0,2},{2,4},{4,6},{6,7},{7,5},{5,3},{3,1},{1,0},{8,10},{10,12},{12... | collective-permute-start | bytes 663560 | tf_op jit(solution)/shard_map/ppermute | solution.py:1005
  214.8 8.6 %collective-permute-start.51 = (bf16[48,2304]{1,0:T(8,128)(2,1)S(1)}, bf16[48,2304]{1,0:T(8,128)(2,1)S(1)}, u32[]{:S(2)}, u32[]{:S(2)}) collective-permute-start(bf16[48,2304]{1,0:T(8,128)(2,1)S(1)} %collective-permute-done.46.refs_4_), channel_id=1, source_target_pairs={{0,1},{2,0},{4,2},{6,4},{7,6},{5,7},{3,5},{1,3},{8,9},{10,8},{12,1... | collective-permute-start | bytes 663560 | tf_op jit(solution)/shard_map/ppermute | solution.py:1005
  216.6 8.9 %collective-permute-start.48 = (bf16[48,2304]{1,0:T(8,128)(2,1)S(1)}, bf16[48,2304]{1,0:T(8,128)(2,1)S(1)}, u32[]{:S(2)}, u32[]{:S(2)}) collective-permute-start(bf16[48,2304]{1,0:T(8,128)(2,1)S(1)} %collective-permute-done.43.refs_1_), channel_id=1, source_target_pairs={{0,2},{2,4},{4,6},{6,7},{7,5},{5,3},{3,1},{1,0},{8,10},{10,12},{12... | collective-permute-start | bytes 663560 | tf_op jit(solution)/shard_map/ppermute | solution.py:1005
  217.1 11.0 %collective-permute-start.49 = (bf16[48,2304]{1,0:T(8,128)(2,1)S(1)}, bf16[48,2304]{1,0:T(8,128)(2,1)S(1)}, u32[]{:S(2)}, u32[]{:S(2)}) collective-permute-start(bf16[48,2304]{1,0:T(8,128)(2,1)S(1)} %collective-permute-done.44.refs_3_), channel_id=1, source_target_pairs={{0,1},{2,0},{4,2},{6,4},{7,6},{5,7},{3,5},{1,3},{8,9},{10,8},{12,1... | collective-permute-start | bytes 663560 | tf_op jit(solution)/shard_map/ppermute | solution.py:1005
  223.3 10.7 %collective-permute-start.54 = (bf16[48,2304]{1,0:T(8,128)(2,1)S(1)}, bf16[48,2304]{1,0:T(8,128)(2,1)S(1)}, u32[]{:S(2)}, u32[]{:S(2)}) collective-permute-start(bf16[48,2304]{1,0:T(8,128)(2,1)S(1)} %collective-permute-done.50.refs_2_), channel_id=1, source_target_pairs={{0,2},{2,4},{4,6},{6,7},{7,5},{5,3},{3,1},{1,0},{8,10},{10,12},{12... | collective-permute-start | bytes 663560 | tf_op jit(solution)/shard_map/ppermute | solution.py:1005
  224.9 9.2 %collective-permute-start.55 = (bf16[48,2304]{1,0:T(8,128)(2,1)S(1)}, bf16[48,2304]{1,0:T(8,128)(2,1)S(1)}, u32[]{:S(2)}, u32[]{:S(2)}) collective-permute-start(bf16[48,2304]{1,0:T(8,128)(2,1)S(1)} %collective-permute-done.51.refs_4_), channel_id=1, source_target_pairs={{0,1},{2,0},{4,2},{6,4},{7,6},{5,7},{3,5},{1,3},{8,9},{10,8},{12,1... | collective-permute-start | bytes 663560 | tf_op jit(solution)/shard_map/ppermute | solution.py:1005
  237.5 9.7 %collective-permute-start.56 = (bf16[48,2304]{1,0:T(8,128)(2,1)S(1)}, bf16[48,2304]{1,0:T(8,128)(2,1)S(1)}, u32[]{:S(2)}, u32[]{:S(2)}) collective-permute-start(bf16[48,2304]{1,0:T(8,128)(2,1)S(1)} %collective-permute-done.52.refs_1_), channel_id=1, source_target_pairs={{0,2},{2,4},{4,6},{6,7},{7,5},{5,3},{3,1},{1,0},{8,10},{10,12},{12... | collective-permute-start | bytes 663560 | tf_op jit(solution)/shard_map/ppermute | solution.py:1005
  239.1 9.6 %collective-permute-start.57 = (bf16[48,2304]{1,0:T(8,128)(2,1)S(1)}, bf16[48,2304]{1,0:T(8,128)(2,1)S(1)}, u32[]{:S(2)}, u32[]{:S(2)}) collective-permute-start(bf16[48,2304]{1,0:T(8,128)(2,1)S(1)} %collective-permute-done.53.refs_3_), channel_id=1, source_target_pairs={{0,1},{2,0},{4,2},{6,4},{7,6},{5,7},{3,5},{1,3},{8,9},{10,8},{12,1... | collective-permute-start | bytes 663560 | tf_op jit(solution)/shard_map/ppermute | solution.py:1005
  244.0 10.4 %collective-permute-start.62 = (bf16[48,2304]{1,0:T(8,128)(2,1)S(1)}, bf16[48,2304]{1,0:T(8,128)(2,1)S(1)}, u32[]{:S(2)}, u32[]{:S(2)}) collective-permute-start(bf16[48,2304]{1,0:T(8,128)(2,1)S(1)} %collective-permute-done.58.refs_2_), channel_id=1, source_target_pairs={{0,2},{2,4},{4,6},{6,7},{7,5},{5,3},{3,1},{1,0},{8,10},{10,12},{12... | collective-permute-start | bytes 663560 | tf_op jit(solution)/shard_map/ppermute | solution.py:1005
  244.4 10.0 %collective-permute-start.63 = (bf16[48,2304]{1,0:T(8,128)(2,1)S(1)}, bf16[48,2304]{1,0:T(8,128)(2,1)S(1)}, u32[]{:S(2)}, u32[]{:S(2)}) collective-permute-start(bf16[48,2304]{1,0:T(8,128)(2,1)S(1)} %collective-permute-done.59.refs_4_), channel_id=1, source_target_pairs={{0,1},{2,0},{4,2},{6,4},{7,6},{5,7},{3,5},{1,3},{8,9},{10,8},{12,1... | collective-permute-start | bytes 663560 | tf_op jit(solution)/shard_map/ppermute | solution.py:1005
  249.1 8.9 %collective-permute-start.61 = (bf16[48,2304]{1,0:T(8,128)(2,1)S(1)}, bf16[48,2304]{1,0:T(8,128)(2,1)S(1)}, u32[]{:S(2)}, u32[]{:S(2)}) collective-permute-start(bf16[48,2304]{1,0:T(8,128)(2,1)S(1)} %collective-permute-done.57.refs_3_), channel_id=1, source_target_pairs={{0,1},{2,0},{4,2},{6,4},{7,6},{5,7},{3,5},{1,3},{8,9},{10,8},{12,1... | collective-permute-start | bytes 663560 | tf_op jit(solution)/shard_map/ppermute | solution.py:1005
  (55 other events, 531.4 us)

commit v3 on v2

--- a/solution.py
+++ b/solution.py
@@ -106,30 +106,38 @@
 
 
 class Forward:
-    def __init__(self, core, own, oth, wa, w1, wd, cos_in, sin_in, cosf, sinf, sems, angle_sems):
+    def __init__(self, when, core, own, oth, wa, w1, wd, cos_in, sin_in, cosf, sinf, sems):
         self.attn = core, own, oth, wa, sems
         self.mlp = core, own, oth, w1, wd, sems.at[pl.ds(4, 8)]
-        self.angles = cos_in, sin_in, cosf, sinf, angle_sems
-        self.own, self.wa, self.sems = own, wa, sems
-        load_attn(*self.attn, 0)
-        load_angles(*self.angles)
-        load_attn(*self.attn, 1)
+        self.angles = cos_in, sin_in, cosf, sinf, sems.at[pl.ds(12, 2)]
+        self.own, self.wa, self.sems, self.when = own, wa, sems, when
+
+        @pl.when(when)
+        def _():
+            load_attn(*self.attn, 0)
+            load_angles(*self.angles)
+            load_attn(*self.attn, 1)
 
     def wait(self, what):
-        if what == "angles":
-            wait_angles(*self.angles)
-            return
-        wait_attn(self.own, self.wa, self.sems, what)
-        if what < 2:
-            load_attn(*self.attn, what + 2)
-        elif what == 2:
-            for j in range(4):
-                load_mlp(*self.mlp, j)
+        @pl.when(self.when)
+        def _():
+            if what == "angles":
+                wait_angles(*self.angles)
+                return
+            wait_attn(self.own, self.wa, self.sems, what)
+            if what < 2:
+                load_attn(*self.attn, what + 2)
+            elif what == 2:
+                for j in range(4):
+                    load_mlp(*self.mlp, j)
 
     def wait_mlp(self):
         core, own, oth, w1, wd, sems = self.mlp
-        for j in range(4):
-            wait_mlp(own, w1, wd, sems, j)
+
+        @pl.when(self.when)
+        def _():
+            for j in range(4):
+                wait_mlp(own, w1, wd, sems, j)
 
 
 def wait_mlp(own, w1, wd, sems, j):
@@ -337,10 +345,13 @@
     arrived(sin_in, sinf, sems.at[1])
 
 
+HELD = 5
+
+
 def first_kernel(
-    flags, keep, got, away, across, vown, voth, pos, segr, cos_in, sin_in, own, oth,
-    out, field_out, wa, w1, wd, cosf, sinf, field, turned, qkv, pt, rec, ml, mlt, vt, n_ref, sems, angle_sems,
+    flags, keep, got, away, across, vown, voth, pos, segr, cos_in, sin_in, own, oth, *refs,
 ):
+    out, field_out, cosf, sinf, wa, w1, wd, field, turned, qkv, pt, rec, ml, mlt, vt, n_ref, sems = refs[HELD:]
     core, layer = flags[0], flags[1]
     w = keep.shape[0]
     for k in range(2):
@@ -353,11 +364,11 @@
                     turned[w * s : w * (s + 1), :] = parts[s // 2, s % 2][...]
 
     field[...] = turned[...].T
-    keeping = pltpu.make_async_copy(field, field_out, sems.at[12])
+    keeping = pltpu.make_async_copy(field, field_out, sems.at[14])
     keeping.start()
     @pl.when(layer == 0)
     def _():
-        loads = Forward(core, own, oth, wa, w1, wd, cos_in, sin_in, cosf, sinf, sems, angle_sems)
+        loads = Forward(core == 0, core, own, oth, wa, w1, wd, cos_in, sin_in, cosf, sinf, sems)
         va, vm = vectors(core, vown, voth)
         x_mid, _, _ = attention(
             field[...].astype(F32), va, wa, loads.wait, cosf, sinf, pos[:, 2:3], segr[0:1, :],
@@ -387,40 +398,38 @@
 
 def fetch_kernel(flags, cos_in, sin_in, own, oth, cosf, sinf, wa, w1, wd, sems):
     core = flags[0]
-    for i in range(4):
-        load_attn(core, own, oth, wa, sems, i)
-        load_mlp(core, own, oth, w1, wd, sems.at[pl.ds(4, 8)], i)
-    load_angles(cos_in, sin_in, cosf, sinf, sems.at[pl.ds(12, 2)])
-    for i in range(4):
-        wait_attn(own, wa, sems, i)
-        wait_mlp(own, w1, wd, sems.at[pl.ds(4, 8)], i)
-    wait_angles(cos_in, sin_in, cosf, sinf, sems.at[pl.ds(12, 2)])
+
+    @pl.when((core != 0) | (flags[1] != 0))
+    def _():
+        for i in range(4):
+            load_attn(core, own, oth, wa, sems, i)
+            load_mlp(core, own, oth, w1, wd, sems.at[pl.ds(4, 8)], i)
+        load_angles(cos_in, sin_in, cosf, sinf, sems.at[pl.ds(12, 2)])
+        for i in range(4):
+            wait_attn(own, wa, sems, i)
+            wait_mlp(own, w1, wd, sems.at[pl.ds(4, 8)], i)
+        wait_angles(cos_in, sin_in, cosf, sinf, sems.at[pl.ds(12, 2)])
 
 
 def second_kernel(
-    flags, field, got, vown, voth, pos, segr, cosf, sinf, wa, w1, wd,
-    cx, xi_out, xm_out, qkv_out, pt_out, rec_out, ml_out, actm_out, acts_out, dg_out, main_out, tail_out, bundle,
-    xi, xm, qkv, pt, rec, ml, na, nm, actm, acts, dg, mlt, vt, xha, xhm, kt, gm, gqt, dsum, gp, outs,
+    flags, field, got, got_late, vown, voth, pos, segr, *refs,
 ):
+    (
+        cosf, sinf, wa, w1, wd, xi, xm, rec, ml, dg, actm, acts, cx, act_out, main_out, tail_out, bundle,
+        qkv_out, pt_out, qkv, pt, na, nm, mlt, vt, xha, xhm, kt, gm, gqt, dsum, gp, outs,
+    ) = refs[HELD:]
     core, layer = flags[0], flags[1]
     va, vm = vectors(core, vown, voth)
-    sent = []
-
-    def send(src, dst):
-        copy = pltpu.make_async_copy(src, dst, outs.at[len(sent)])
-        copy.start()
-        sent.append(copy)
-
-    x = jnp.where(layer == 0, field[...].astype(F32), got[...].astype(F32))
+    x = jnp.where(core == 0, got[...].astype(F32), got_late[...].astype(F32))
+    x = jnp.where(layer == 0, field[...].astype(F32), x)
     xi[...] = x.astype(BF)
-    send(xi, xi_out)
     x_mid, xh, inv_a = attention(
         x, va, wa, lambda what: None, cosf, sinf, pos[:, 2:3], segr[0:1, :], qkv, pt, rec, ml, mlt, vt, na
     )
     xha[...] = xh
     xm[...] = x_mid
-    for src, dst in ((xm, xm_out), (qkv, qkv_out), (pt, pt_out), (rec, rec_out), (ml, ml_out)):
-        send(src, dst)
+    load(qkv, qkv_out, outs.at[7])
+    load(pt, pt_out, outs.at[8])
     xh, inv_m = norm_parts(x_mid.astype(F32))
     xhm[...] = xh
     n = (xh * vm[:, GAIN] + vm[:, SHIFT]).astype(BF)
@@ -428,13 +437,13 @@
     sides = (
         main_out, tail_out, bundle.at[:, pl.ds(2 * D, D)], bundle.at[:, pl.ds(3 * D, D)],
     )
-    load(field, bundle.at[:, pl.ds(4 * D, D)], outs.at[13])
+    load(field, bundle.at[:, pl.ds(4 * D, D)], outs.at[4])
     for when, sources in ((core == 0, (na, ml, nm, nm)), (core != 0, (nm, nm, na, ml))):
 
         @pl.when(when)
         def _(sources=sources):
             for k, (src, dst) in enumerate(zip(sources, sides)):
-                load(src, dst, outs.at[9 + k])
+                load(src, dst, outs.at[k])
 
     first = hidden_bias(core, vm)
     c = field[...]
@@ -450,21 +459,10 @@
         return slope
 
     def leave():
-        load(acts, bundle.at[:, pl.ds(0, 2 * D)], outs.at[14])
-        for k, (src, dst) in enumerate(((actm, actm_out), (acts, acts_out), (dg, dg_out))):
-            load(src, dst, outs.at[6 + k])
-
-    @pl.when(layer == 0)
-    def _():
-        ahead = forward(0)
-        for j in range(4):
-            h = ahead
-            if j < 3:
-                ahead = forward(j + 1)
-            chunk(j, h)
-        leave()
-
-    @pl.when(layer != 0)
+        load(acts, bundle.at[:, pl.ds(0, 2 * D)], outs.at[5])
+        load(actm, act_out, outs.at[6])
+
+    @pl.when(layer >= 0)
     def _():
         ahead = forward(0), dot(c, wd[0])
         gn = None
@@ -491,48 +489,32 @@
             gn = part if gn is None else gn + part
         cx[...] = norm_back(gn, xha[...], inv_a, va[:, GAIN], c_mid)
 
-    for copy in sent:
-        copy.wait()
     for k, (src, dst) in enumerate(
-        ((actm, actm_out), (acts, acts_out), (dg, dg_out)) + tuple((nm, side) for side in sides)
-        + ((field, sides[2]), (acts, bundle.at[:, pl.ds(0, 2 * D)]))
+        tuple((nm, side) for side in sides)
+        + ((field, sides[2]), (acts, bundle.at[:, pl.ds(0, 2 * D)]), (actm, act_out), (qkv, qkv_out), (pt, pt_out))
     ):
-        arrived(src, dst, outs.at[6 + k])
-
-
-def late_kernel(
-    flags, x_two, vown, voth, xm_in, dg_in, actm_in, acts_in, own, oth,
-    keep, send, xm, dg, wa, w1, wd, actm, acts, sems, ins,
-):
+        arrived(src, dst, outs.at[k])
+
+
+def late_kernel(flags, x_two, vown, voth, actm, acts, *refs):
+    xm, wd = refs[HELD + 1], refs[HELD - 1]
+    keep, send = refs[-2:]
     core, layer = flags[0], flags[1]
-    held = ((xm_in, xm), (actm_in, actm), (acts_in, acts), (dg_in, dg))
-    for j in range(4):
-        load((own if j < 2 else oth).at[cols(FF + D * (j % 2), D)], wd.at[j], sems.at[8 + j])
-    for k, (src, dst) in enumerate(held):
-        load(src, dst, ins.at[k])
-    for j in range(4):
-        pick(core, 1, own, oth, (slice(None), pl.ds(hidden_start(core, j), D)), w1.at[j], sems.at[4 + j])
-        load_attn(core, own, oth, wa, sems, j)
     vm = vectors(core, vown, voth)[1]
-    for k, (src, dst) in enumerate(held):
-        arrived(src, dst, ins.at[k])
     mid = xm[...].astype(F32)
     acc = mid + vm[:, SECOND : SECOND + D]
     for j in range(4):
-        arrived(own.at[cols(0, D)], wd.at[j], sems.at[8 + j])
         acc = acc + dot_nt((actm, acts)[j // 2][:, D * (j % 2) : D * (j % 2 + 1)], wd[j])
     acc = jnp.where(layer == 0, x_two[...].astype(F32), acc)
     keep[...] = jnp.where(core == 0, mid, acc).astype(BF)
     send[...] = jnp.where(core == 0, acc, mid).astype(BF)
-    for j in range(4):
-        arrived(own.at[cols(0, D)], w1.at[j], sems.at[4 + j])
-        wait_attn(own, wa, sems, j)
-
-
-def both_rows_kernel(flags, keep, got, out):
-    core = flags[0]
-    out[rows_at(L * core, L), :] = keep[...]
-    out[rows_at(L * (1 - core), L), :] = got[...]
+
+
+def both_rows(core, keep, got, out, sems):
+    return [
+        pltpu.make_async_copy(src, out.at[rows_at(L * at, L), :], sems.at[k])
+        for k, (src, at) in enumerate(((keep, core), (got, 1 - core)))
+    ]
 
 
 def norm_stats(gn, x, vec):
@@ -543,16 +525,13 @@
 
 
 def back_kernel(
-    flags, field, got, vown, voth, pos, xm, dg, wa, w1, wd, xi_in, qkv_in, pt_in, rec_in, ml_in, cos_in, sin_in,
+    flags, field, got, vown, voth, pos, qkv_in, pt_in, cosf, sinf, wa, w1, wd, xi, xm, rec, ml, dg,
     row_keep, row_send, c_out, vec_keep, keep_out, send_out,
-    cosf, sinf, xi, qkv, pt, rec, ml, gh, gp, va_grad, vm_grad, folded, vec_send, kt, gm, gqt, dsum,
-    angle_sems, ins, outs,
+    qkv, pt, gh, gp, va_grad, vm_grad, folded, vec_send, kt, gm, gqt, dsum, outs,
 ):
     core, layer = flags[0], flags[1]
-    held = ((ml_in, ml), (rec_in, rec), (qkv_in, qkv), (pt_in, pt), (xi_in, xi))
-    for k, (src, dst) in enumerate(held):
-        load(src, dst, ins.at[k])
-    load_angles(cos_in, sin_in, cosf, sinf, angle_sems)
+    load(qkv_in, qkv, outs.at[3])
+    load(pt_in, pt, outs.at[4])
     va, vm = vectors(core, vown, voth)
     wide = jnp.where(layer == 0, got[...].astype(F32), field[...].astype(F32))
     c = wide.astype(BF)
@@ -600,9 +579,8 @@
                 g.astype(F32), axis=0, keepdims=True
             )
 
-    for k, (src, dst) in enumerate(held):
-        arrived(src, dst, ins.at[k])
-    wait_angles(cos_in, sin_in, cosf, sinf, angle_sems)
+    arrived(qkv_in, qkv, outs.at[3])
+    arrived(pt_in, pt, outs.at[4])
     attention_back(
         c, wa.at[3], cosf, sinf, qkv, pt, rec, ml, kt, gm, gqt, dsum, lambda p: p, emit
     )
@@ -643,9 +621,13 @@
 
 
 def gram_down_kernel(
-    flags, c, c_oth, act, bundle, main0, tail0, right0, down, left_main, left_tail, right_out,
-    c1, sides, left, right, sems,
+    flags, c, c_oth, x_keep, x_oth, act, bundle, main0, tail0, right0,
+    down, left_main, left_tail, right_out, activations,
+    c1, sides, left, right, sems, row_sems,
 ):
+    leaving = both_rows(flags[0], x_keep, x_oth, activations, row_sems)
+    for copy in leaving:
+        copy.start()
     loads = (
         (bundle.at[:, pl.ds(4 * D, D)], c1), (act, right.at[pl.ds(0, L), :]),
         (bundle.at[:, pl.ds(0, 2 * D)], right.at[pl.ds(L, L), :]),
@@ -673,6 +655,8 @@
         arrived(*loads[3 + k], sems.at[3 + k])
         (left_tail, left_main)[k // 2][:, L * (k % 2) : L * (k % 2 + 1)] = sides[k].T
     arrived(*loads[7], sems.at[7])
+    for copy in leaving:
+        copy.wait()
 
 
 def gram_main_kernel(
@@ -689,16 +673,16 @@
         for k in range(2)
     ]
     total = vec[...] + (other[0] + other[1])
-    hi, lo = split_two(total)
-    vec_out[...] = hi.astype(F32) + lo.astype(F32)
+    total = total.astype(BF)
+    vec_out[...] = total.astype(F32)
     r = main_up.shape[0]
     for k, (m, t) in enumerate(((main_up, tail_up), (main_down, tail_down))):
         here = own_rows(rows, 0, k, r)
         m[:, : 3 * D] = main[here, :]
-        m[:, 3 * D :] = hi
+        m[:, 3 * D :] = total
         t[:, :D] = head[here, :]
         t[:, D : 3 * D] = down[here, :]
-        t[:, 3 * D :] = lo
+        t[:, 3 * D :] = total
 
 
 def own_rows(rows, t, way, r):
@@ -742,35 +726,47 @@
     return jnp.concatenate(rows, axis=0)
 
 
-def vector_sum_kernel(table, *refs):
-    out, slots = refs[-2:]
-    own, pieces = refs[0], refs[1:-2]
-    n = len(pieces) // 2 + 1
-    slots[table[0, 2]] = own[...]
-    for k in range(1, n):
-        t, way = (k + 1) // 2, (k + 1) % 2
-        slots[table[t, 2 + way]] = pieces[k - 1][...] + pieces[n + k - 2][...]
-    total = slots[0]
-    for k in range(1, n):
-        total = total + slots[k]
-    out[...] = total
-
-
-def place_kernel(t, rows, *refs):
-    out, buf, sems = refs[-3:]
-    count = sems.shape[0]
-    shards = refs[: 2 * count]
-    r = shards[0].shape[0]
+def sum_vectors(table, vectors, slots, outs):
+    n = len(vectors)
+    if table is None:
+        total = vectors[0][...]
+    else:
+        slots[table[0, 2]] = vectors[0][...]
+        for k in range(1, n):
+            t, way = (k + 1) // 2, (k + 1) % 2
+            slots[table[t, 2 + way]] = vectors[k][...]
+        total = slots[0]
+        for k in range(1, n):
+            total = total + slots[k]
+    at = 0
+    for out in outs:
+        for k in range(out.shape[1] // 128):
+            out[:, 128 * k : 128 * (k + 1)] = total[at + k : at + k + 1, :]
+        at += out.shape[1] // 128
+
+
+def place_kernel(spots, whole, flags, rows, *refs):
+    count, pair, vectors, into = whole
+    ins, refs = refs[: 2 * count + pair + vectors], refs[2 * count + pair + vectors + into :]
+    out, buf, sems = refs[0], refs[-3], refs[-2]
     copies = []
+    if pair:
+        copies += both_rows(flags[0], ins[2 * count], ins[2 * count + 1], refs[1], refs[-1])
+        copies[0].start()
+        copies[1].start()
+    r = ins[0].shape[0]
     for k in range(count):
         there = pl.ds(r * k, r)
-        buf[there, : 3 * D] = shards[2 * k][...].astype(F32)
-        buf[there, 3 * D :] = shards[2 * k + 1][...].astype(F32)
+        buf[there, : 3 * D] = ins[2 * k][...].astype(F32)
+        buf[there, 3 * D :] = ins[2 * k + 1][...].astype(F32)
         copy = pltpu.make_async_copy(
-            buf.at[there, :], out.at[own_rows(rows, t, k, r), :], sems.at[k]
+            buf.at[there, :], out.at[own_rows(rows, *spots[k], r), :], sems.at[k]
         )
         copy.start()
         copies.append(copy)
+    if vectors:
+        outs = refs[1 + pair // 2 : 5 + pair // 2]
+        sum_vectors(rows if vectors > 1 else None, ins[2 * count + pair :], refs[-4], outs)
     for copy in copies:
         copy.wait()
 
@@ -837,63 +833,73 @@
     )(flags, grid, own, oth)
 
 
-def first_pass(*a):
+def fetch(flags, *sources):
     return call(
-        first_kernel, "first_pass", [SMEM] + [VS] * 8 + [HBM] * 4, [row(), row_out()],
-        ATTN_W + MLP_W + ANGLES
-        + [row(), VM((D, L), BF), row(3 * D), VM((HEADS, L, L), BF), VM((16, L), F32), row(), VM((D, L), BF),
-           VM((D, L), BF), row(), DMA((13,)), DMA((2,))],
-        int(8e9), int(20e6), 40, out_specs=[VS, HBM],
-    )(*a)
-
-
-def fetch(*a):
+        fetch_kernel, "fetch", [SMEM] + [HBM] * 4, ANGLES + ATTN_W + MLP_W, [DMA((14,))], int(1e8), int(17e6), 28
+    )(flags, *sources)
+
+
+def first_pass(held, *a):
+    results = call(
+        first_kernel, "first_pass", [SMEM] + [VS] * 8 + [HBM] * 4 + [VS] * HELD,
+        [row(), row_out()] + ANGLES + ATTN_W + MLP_W,
+        [row(), VM((D, L), BF), row(3 * D), VM((HEADS, L, L), BF), VM((16, L), F32), row(), VM((D, L), BF),
+         VM((D, L), BF), row(), DMA((15,))],
+        int(8e9), int(20e6), 28, out_specs=[VS, HBM] + [VS] * HELD,
+        aliases={len(a) + k: 2 + k for k in range(HELD)},
+    )(*a, *(in_vmem(x) for x in held))
+    return results[0], results[1], results[2:]
+
+
+SAVED = [VM((L, D), BF), VM((L, D), BF), VM((16, L), F32), VM((L, D), BF), VM((L, FF), BF)]
+HEAD_S = [VM((L, 3 * D), BF), VM((HEADS, L, L), BF)]
+
+
+def second_pass(held, *a):
+    outs = [
+        row_out(FF // 2), row_out(), row_out(), row_out(5 * D), row_out(3 * D), pltpu.HBM((HEADS, L, L), BF)
+    ]
+    resident = ANGLES + ATTN_W + MLP_W + SAVED
+    results = call(
+        second_kernel, "second_pass", [SMEM] + [VS] * (7 + HELD),
+        resident + [row(FF // 2), row(FF // 2), row()] + outs,
+        HEAD_S + [row(), row(), VM((D, L), BF), VM((D, L), BF), VM((L, D), F32), VM((L, D), F32)]
+        + BACK_S + [row(3 * D), DMA((9,))],
+        int(18e9), int(20e6), 28, out_specs=[VS] * (len(resident) + 3) + [HBM] * len(outs),
+        aliases={len(a) + k: k for k in range(HELD)},
+    )(*a, *(in_vmem(x) for x in held))
+    n = len(resident)
+    return results[:n], results[n : n + 2], results[n + 2], results[n + 3 :]
+
+
+def late_pass(held, *a):
+    results = call(
+        late_kernel, "late_pass", [SMEM] + [VS] * (len(a) - 1 + len(held)),
+        ANGLES + ATTN_W + MLP_W + SAVED + [sds((L, D))] * 2, [], int(2e9), int(5e6), 28,
+        aliases={len(a) + k: k for k in range(len(held))},
+    )(*a, *(in_vmem(x) for x in held))
+    return results[: len(held)], results[len(held) :]
+
+
+def back_pass(held, *a):
     return call(
-        fetch_kernel, "fetch", [SMEM] + [HBM] * 4, ANGLES + ATTN_W + MLP_W, [DMA((14,))], int(1e8), int(17e6), 8
-    )(*a)
-
-
-def second_pass(*a):
-    saved = [
-        row_out(), row_out(), row_out(3 * D), pltpu.HBM((HEADS, L, L), BF), pltpu.HBM((16, L), F32), row_out(),
-        row_out(FF // 2), row_out(FF // 2), row_out(FF), row_out(), row_out(), row_out(5 * D),
-    ]
-    return call(
-        second_kernel, "second_pass", [SMEM] + [VS] * 11, [row()] + saved,
-        [row(), row(), row(3 * D), VM((HEADS, L, L), BF), VM((16, L), F32), row(), row(), row(),
-         row(FF // 2), row(FF // 2), row(FF), VM((D, L), BF), VM((D, L), BF), VM((L, D), F32),
-         VM((L, D), F32)]
-        + BACK_S + [row(3 * D), DMA((15,))],
-        int(18e9), int(20e6), 32, out_specs=[VS] + [HBM] * len(saved),
-    )(*a)
-
-
-def late_pass(*a):
-    return call(
-        late_kernel, "late_pass", [SMEM] + [VS] * 3 + [HBM] * 6,
-        [sds((L, D))] * 2 + [row(), row(FF)] + ATTN_W + MLP_W,
-        [row(FF // 2), row(FF // 2), DMA((12,)), DMA((4,))], int(2e9), int(20e6), 14,
-    )(*a)
-
-
-def back_pass(*a):
-    return call(
-        back_kernel, "back_pass", [SMEM] + [VS] * 10 + [HBM] * 7,
+        back_kernel, "back_pass", [SMEM] + [VS] * 5 + [HBM] * 2 + [VS] * len(held),
         [sds((L, D)), sds((L, D)), row(), VM(PACKED, F32), row_out(FF), pltpu.HBM((L + 16, FF), BF)],
-        ANGLES
-        + [row(), row(3 * D), VM((HEADS, L, L), BF), VM((16, L), F32), row(), row(FF), row(FF),
-           VM((1, FIRST + 6 * D), F32), VM((1, VECTOR), F32), VM((1, VECTOR), F32), VM((16, D), BF)]
-        + BACK_S + [DMA((2,)), DMA((5,)), DMA((3,))],
-        int(10e9), int(15e6), 30, out_specs=[VS] * 4 + [HBM] * 2,
-    )(*a)
+        HEAD_S
+        + [row(FF), row(FF), VM((1, FIRST + 6 * D), F32), VM((1, VECTOR), F32), VM((1, VECTOR), F32),
+           VM((16, D), BF)]
+        + BACK_S + [DMA((5,))],
+        int(10e9), int(15e6), 28, out_specs=[VS] * 4 + [HBM] * 2,
+    )(*a, *(in_vmem(x) for x in held))
 
 
 def gram_down(*a):
     square = VM((D, 2 * L), BF)
     return call(
-        gram_down_kernel, "gram_down", [SMEM] + [VS] * 2 + [HBM] * 5,
-        [VM((D, 2 * D), BF), square, square, VM((2 * L, FF), BF)],
-        [row(), VM((4, L, D), BF), square, VM((2 * L, 2 * D), BF), DMA((8,))], int(2e9), int(8e6), 18,
+        gram_down_kernel, "gram_down", [SMEM] + [VS] * 4 + [HBM] * 5,
+        [VM((D, 2 * D), BF), square, square, VM((2 * L, FF), BF), pltpu.HBM((2 * L, D), BF)],
+        [row(), VM((4, L, D), BF), square, VM((2 * L, 2 * D), BF), DMA((8,)), DMA((2,))], int(2e9), int(8e6), 20,
+        out_specs=[VS] * 4 + [HBM],
     )(*a)
 
 
@@ -921,49 +927,24 @@
     return results[:2], results[2:]
 
 
-def both_rows(flags, keep, got):
-    return call(
-        both_rows_kernel, "both_rows", [SMEM, VS, VS], [sds((2 * L, D))], [], 1000, int(2e6), 6
-    )(flags, keep, got)[0]
-
-
-def mlp_back(flags, *a):
-    return call(
-        mlp_back_kernel, "mlp_back", [SMEM] + [VS] * 6 + [HBM] * 2,
-        [row(), row(FF), row(), row(), VM((1, VECTOR), F32)],
-        MLP_W + [DMA((8,))], int(4e9), int(14e6), 22,
-    )(*resident(flags, 6, a))
-
-
-def attn_back(flags, *a):
-    return call(
-        attn_back_kernel, "attn_back", [SMEM] + [VS] * 13 + [HBM] * 2,
-        [row(), row(), row(3 * D), row(3 * D), VM((1, FIRST + 6 * D), F32)],
-        ATTN_W + BACK_S + [row(3 * D), DMA((4,))],
-        int(6e9), int(14e6), 20,
-    )(*resident(flags, 13, a))
-
-
-def vector_sum(table, own, pieces):
-    n = len(pieces) // 2 + 1
-    return call(
-        vector_sum_kernel, "vector_sum", [SMEM] + [VS] * (2 * n - 1), [sds(PACKED, F32)],
-        [VM((n,) + PACKED, F32)], 1000, 100000, 4,
-    )(table, own, *pieces)[0]
-
-
-def place(t, rows, shards, total):
-    def kernel(*refs):
-        place_kernel(t, *refs)
-
+def place(flags, spots, rows, shards, total, pair=(), vectors=()):
     r, count = shards[0].shape[0], len(shards) // 2
     into = [] if total is None else [total]
+    whole = count, len(pair), len(vectors), len(into)
+
+    def kernel(*refs):
+        place_kernel(spots, whole, *refs)
+
+    outs = [pltpu.HBM((D, 6 * D), F32)]
+    outs += [pltpu.HBM((2 * L, D), BF)] if pair else []
+    outs += [sds((1, w), F32) for w in (D, D, FF, D)] if vectors else []
+    given = len(shards) + len(pair) + len(vectors)
     return call(
-        kernel, "place", [SMEM] + [VS] * len(shards) + [HBM] * len(into),
-        [pltpu.HBM((D, 6 * D), F32)],
-        [VM((r * count, 6 * D), F32), DMA((count,))], 1000, int(2e6), 24,
-        out_specs=[HBM], aliases={len(shards) + 1: 0} if into else {},
-    )(rows, *shards, *into)[0]
+        kernel, "place", [SMEM, SMEM] + [VS] * given + [HBM] * len(into), outs,
+        [VM((max(len(vectors), 1),) + PACKED, F32), VM((r * count, 6 * D), F32), DMA((count,)), DMA((2,))], 1000,
+        int(2e7), 24, out_specs=[HBM] * (2 if pair else 1) + ([VS] * 4 if vectors else []),
+        aliases={given + 2: 0} if into else {},
+    )(flags, rows, *shards, *pair, *vectors, *into)
 
 
 def core_swap(a):
@@ -994,8 +975,8 @@
 
 
 class Chain:
-    def __init__(self, cycle, parts, cur):
-        self.cycle, self.parts, self.cur = cycle, parts, cur
+    def __init__(self, cycle, parts, cur, carries=False):
+        self.cycle, self.parts, self.cur, self.carries = cycle, parts, cur, carries
         self.t = 0
         self.shards = []
         self.vectors = []
@@ -1007,7 +988,7 @@
         self.t += 1
         if self.t < c.n:
             t = self.t
-            ways = int(t <= c.n // 2) + int(t <= (c.n - 1) // 2)
+            ways = int(t <= c.n // 2) + int(t <= (c.n - 1) // 2) if self.carries else 0
             self.cur, came = add(t, c.rows, *got, self.parts, ways, t < c.n // 2)
             self.vectors += came
         else:
@@ -1021,29 +1002,36 @@
     return lax.axis_size("dp") <= 16
 
 
-def summed_weight_grad(main, tail, token, beside):
+def summed(flags, main, tail, token, pair, vector):
     if not small_ring():
-        for f in beside:
-            token = f(token)
-        return place(0, jnp.zeros((1, 1), I32), lax.psum([main, tail], "dp"), None)
+        chains, vector = lax.psum([main, tail], "dp"), lax.psum(vector, "dp")
+        return place(flags, [(0, 0)], jnp.zeros((1, 1), I32), chains, None, pair, [vector])
     cycle = main.cycle
     n = cycle.n
-    total = None
-    beside = list(beside)
+    total, placed = None, 0
+    results = {}
     while main.t < 2 * n - 2:
         token = tail.step(token)
         if total is not None:
             token = (token, total)
         token = main.step(token)
-        if main.shards:
-            k = len(main.shards) - 1
-            a, b = main.shards[k], tail.shards[k]
-            total = place(cycle.placed(k), cycle.rows, [a[0], b[0], a[1], b[1]], total)
-        if beside and main.t >= n:
-            token = (token, beside.pop(0)(token))
-    for f in beside:
-        token = f(token)
-    return total
+        whole = len(main.shards)
+        if whole > placed and (whole % 2 == 0 or whole == n - 1):
+            spots, shards = [], []
+            for k in range(placed, whole):
+                for way in range(2):
+                    spots.append((cycle.placed(k), way))
+                    shards += [main.shards[k][way], tail.shards[k][way]]
+            now, then = placed == 0, "vectors" not in results and whole >= min(4, n)
+            total, *more = place(
+                flags, spots, cycle.rows, shards, total, pair if now else (), [vector] + main.vectors if then else ()
+            )
+            if now:
+                results["rows"] = more[0]
+            if then:
+                results["vectors"] = more
+            placed = whole
+    return total, results["rows"], *results["vectors"]
 
 
 def body(
@@ -1064,7 +1052,12 @@
         )
     else:
         voth = core_swap(vown)
-    vown, voth = in_hbm(vown), in_hbm(voth)
+    if small_ring():
+        cycle = Cycle()
+        rows, r = cycle.rows, cycle.r
+    else:
+        rows, r = jnp.zeros((1, 2), I32), PACKED[0]
+    vown, voth = in_hbm(vown), in_hbm(after(voth, rows))
     got = core_swap(send)
     away = lax.ppermute(away, "section", [(0, 2), (1, 3), (2, 0), (3, 1)])
     across = lax.ppermute(across, "section", [(0, 3), (1, 2), (2, 1), (3, 0)])
@@ -1072,76 +1065,46 @@
     oth = in_hbm(core_swap(section_weight[0]))
     cosf, sinf, pos, segr = (in_hbm(a) for a in positions(flags, grid_sizes, vown, voth))
 
-    x_two, field = first_pass(
-        flags, keep, got, away, across, vown, voth, pos, segr, cosf, sinf, own, oth
+    held = fetch(flags, cosf, sinf, own, oth)
+    x_two, field, held = first_pass(
+        held, flags, keep, got, away, across, vown, voth, pos, segr, cosf, sinf, own, oth
     )
     field = in_hbm(field)
-    fetched = fetch(flags, cosf, sinf, own, after(oth, x_two))
-    x_got = after(lax.ppermute(x_two, "section", [(0, 2), (1, 3)]), fetched)
-    (
-        c_two, x_in, x_mid, qkv, pt, rec, ml, act_mine, act_send, dg, main_left, tail_left, bundle,
-    ) = second_pass(flags, field, x_got, vown, voth, pos, segr, *(in_vmem(a) for a in fetched))
-    x_in, qkv, pt, rec, ml = (in_hbm(a) for a in (x_in, qkv, pt, rec, ml))
+    x_got, x_late = (lax.ppermute(x_two, "section", [pair]) for pair in ((0, 2), (1, 3)))
+    held, active, c_two, (act_mine, main_left, tail_left, bundle, qkv, pt) = second_pass(
+        held, flags, field, x_got, x_late, vown, voth, pos, segr
+    )
     act_mine, main_left, tail_left = (in_hbm(a) for a in (act_mine, main_left, tail_left))
     c_got = lax.ppermute(c_two, "section", [(2, 0), (3, 1)])
-    bundle = in_hbm(core_swap(bundle))
-    x_keep, x_send, *held = late_pass(
-        flags, x_two, vown, voth, in_hbm(after(x_mid, bundle)), in_hbm(dg), act_mine, in_hbm(act_send), own, oth
-    )
+    held, (x_keep, x_send) = late_pass(held, flags, x_two, vown, voth, *(in_vmem(a) for a in active))
     c_got = after(c_got, x_keep)
+    bundle = in_hbm(core_swap(after(bundle, c_got)))
+    x_oth = core_swap(after(x_send, c_got))
 
     c_keep, c_send, c_out, vec, right, right_send = back_pass(
-        flags, field, c_got, vown, voth, pos,
-        *(in_vmem(a) for a in held), x_in, qkv, pt, rec, ml, cosf, sinf,
+        held, flags, field, c_got, vown, voth, pos, in_hbm(qkv), in_hbm(pt)
     )
     c_oth = core_swap(c_got)
-    right_oth = core_swap(after(right_send, c_oth))
-    down, left_main, left_tail, right = gram_down(
-        flags, c_out, c_oth, act_mine, bundle, main_left, tail_left, in_hbm(right)
-    )
-    if small_ring():
-        cycle = Cycle()
-        rows, r = cycle.rows, cycle.r
-    else:
-        rows, r = jnp.zeros((1, 2), I32), PACKED[0]
+    right_oth = core_swap(after(right_send, (c_oth, bundle, x_oth)))
+    down, left_main, left_tail, right, activations = gram_down(
+        flags, c_out, c_oth, x_keep, x_oth, act_mine, bundle, main_left, tail_left, in_hbm(right)
+    )
     right, main, head, *first, vec = gram_main(
         rows, r, right_oth, down, left_main, left_tail, vec, right
     )
     token = main
     if small_ring():
-        main, tail = Chain(cycle, [main], first[:2]), Chain(cycle, [head, down], first[2:])
+        main, tail = Chain(cycle, [main], first[:2], True), Chain(cycle, [head, down], first[2:])
     else:
         tail = jnp.concatenate([head, down], axis=1)
-    swapped = {}
-
-    def send_rows(token):
-        swapped["x"], swapped["c"] = core_swap(after(x_send, token)), core_swap(after(c_send, token))
-        return x_keep
-
-    def join(name, keep):
-        def f(token):
-            swapped[name] = both_rows(flags, keep, after(swapped[name], token))
-            return swapped[name]
-
-        return f
-
-    weight_grad = summed_weight_grad(
-        main, tail, token, [send_rows, join("x", x_keep), join("c", c_keep)]
-    )
-    if small_ring():
-        vec = vector_sum(cycle.rows, vec, main.vectors + tail.vectors)
-    else:
-        vec = lax.psum(vec, "dp")
-    vg = vec.reshape(1, -1)[:, :VECTOR]
-    activations, input_grads = swapped["x"], swapped["c"]
+    weight_grad, input_grads, *vectors = summed(
+        flags, main, tail, token, (c_keep, core_swap(after(c_send, token))), vec
+    )
     return (
         activations[None],
         input_grads[None],
         weight_grad[None],
-        vg[:, GAIN],
-        vg[:, SHIFT],
-        vg[:, FIRST:SECOND],
-        vg[:, SECOND:],
+        *vectors,
     )
 
 

time: 271 us -> 260 us (0.959)
  Pallas kernels: 117 us -> 103 us
  waiting for transfers between devices: 74.5 us -> 78.9 us
    pallas_call x16 -> x10, Pallas kernels: 83.4 us -> 76.7 us  [the longest x1 23.9 us: second_pass(): call(second_kernel, 'second_pass', [SMEM] + [VS] * (7 + HELD), resident +...]
    pallas_call x1, Pallas kernels: 6.6 us -> 0.8 us  [fetch(): call(fetch_kernel, 'fetch', [SMEM] + [HBM] * 4, ANGLES + ATTN_W + MLP_W,...]
    ppermute x7, waiting for transfers between devices: 4.29 us -> 0.02 us  [core_swap(): return lax.ppermute(a, 'section', [(0, 1), (1, 0), (2, 3), (3, 2)])]
    ppermute x56, waiting for transfers between devices: 53.7 us -> 57.7 us  [step(): got = [lax.ppermute(a, 'dp', p) for a, p in zip(self.cur, c.pairs)]]
    ppermute x1 -> x2, waiting for transfers between devices: 5.04 us -> 8.87 us  [body(): lax.ppermute(x_two, 'section', [pair])]
  transfers between devices with their start and end apart: 68 -> 69, of which waited for: 46 -> 47; matrix products, arithmetic and copies ran while one was open for 1% -> 1% of each run, Pallas kernels for 30% -> 22%
where the time goes in v3:
time: 260 us; the launch traced here: 257 us
  Pallas kernels  103 us (40%)
  waiting for transfers between devices  78.9 us (30%)
  starting transfers between devices  70.1 us (27%)
    ppermute x56, starting transfers between devices, step(): got = [lax.ppermute(a, 'dp', p) for a, p in zip(self.cur, c.pairs)]  58.1 us
    ppermute x56, waiting for transfers between devices, step(): got = [lax.ppermute(a, 'dp', p) for a, p in zip(self.cur, c.pairs)]  57.7 us
    pallas_call x1, Pallas kernels, second_pass(): call(second_kernel, 'second_pass', [SMEM] + [VS] * (7 + HELD), resident +...  23.9 us
    pallas_call x1, Pallas kernels, back_pass(): call(back_kernel, 'back_pass', [SMEM] + [VS] * 5 + [HBM] * 2 + [VS] * len...  16.4 us
    pallas_call x14, Pallas kernels, add(): call(kernel, 'add', [SMEM] + [VS] * (2 + count), [out, out] + [pltpu.HBM(...  14.6 us
    pallas_call x1, Pallas kernels, first_pass(): call(first_kernel, 'first_pass', [SMEM] + [VS] * 8 + [HBM] * 4 + [VS] * H...  14.2 us
    pallas_call x5, Pallas kernels, place(): call(kernel, 'place', [SMEM, SMEM] + [VS] * given + [HBM] * len(into), ou...  13.2 us
    ppermute x1, waiting for transfers between devices, body(): c_got = lax.ppermute(c_two, 'section', [(2, 0), (3, 1)])  10.8 us
  transfers between devices with their start and end apart: 69, of which 47 were waited for; matrix products, arithmetic and copies ran while one was open for 1% of the time, Pallas kernels for 22%

profile of v3, /device:TPU:0, one launch (start us, length us, event | category | flops | bytes accessed | tf_op | source)
XLA Modules:
  0.0 256.6 jit_solution(18327881634771276513)
XLA Ops:
  1.8 1.7 prepare.1
  3.5 2.6 %collective-permute-start.3 = (f32[1,5376]{1,0:T(1,128)}, f32[1,5376]{1,0:T(1,128)S(1)}, u32[]{:S(2)}, u32[]{:S(2)}) collective-permute-start(f32[1,5376]{1,0:T(1,128)} %get-tuple-element.185.vown), channel_id=1, source_target_pairs={{0,9},{1,8},{2,11},{3,10},{4,13},{5,12},{6,15},{7,14},{8,1},{9,0},... | collective-permute-start | bytes 64520 | tf_op jit(solution)/shard_map/ppermute | solution.py:1050
  9.4 3.5 %positions.1 = (f32[384,768]{1,0:T(8,128)}, f32[384,768]{1,0:T(8,128)}, f32[384,128]{1,0:T(8,128)}, f32[8,384]{1,0:T(8,128)}) custom-call(s32[2]{0:T(128)} %pad_add_fusion.1.flags.refs_0_, s32[2,2,2]{2,1,0:T(2,128)} %grid.1, f32[1,5376]{1,0:T(1,128)} %get-tuple-element.185.vown, f32[1,5376]{1,0:T(1,128)} %copy-done.9), custom_call_target="tpu_custom_call" | custom-call | flops 100000000 | bytes 3000000 | tf_op jit(solution)/shard_map/positions/pallas_call | solution.py:829
  15.1 14.2 %first_pass.1 = (bf16[384,768]{1,0:T(8,128)(2,1)S(1)}, bf16[384,768]{1,0:T(8,128)(2,1)}, f32[384,768]{1,0:T(8,128)S(1)}, f32[384,768]{1,0:T(8,128)S(1)}, bf16[4,...) custom-call(s32[2]{0:T(128)} %pad_add_fusion.1.flags.refs_0_, ...), custom_call_target="tpu_custom_call", output_to_operand_aliasing={{2}: (13, {}), {3}: (14, {}), {4}: (15, {}), {5}: (16, {}),... | custom-call | flops 8000000000 | bytes 20000000 | tf_op jit(solution)/shard_map/first_pass/pallas_call | solution.py:843
  31.8 8.9 %collective-permute-done.5.got = bf16[384,768]{1,0:T(8,128)(2,1)S(1)} collective-permute-done((bf16[384,768]{1,0:T(8,128)(2,1)S(1)}, bf16[384,768]{1,0:T(8,128)(2,1)S(1)}, u32[]{:S(2)}, u32[]{:S(2)}) %collective-permute-start.5) | collective-permute-done | bytes 589856 | tf_op jit(solution)/shard_map/ppermute | solution.py:1073
  40.7 23.9 %second_pass.1 = (f32[384,768]{1,0:T(8,128)S(1)}, f32[384,768]{1,0:T(8,128)S(1)}, bf16[4,768,768]{2,1,0:T(8,128)(2,1)S(1)}, bf16[4,768,768]{2,1,0:T(8,128)(2,1)S...) custom-call(s32[2]{0:T(128)} %pad_add_fusion.1.flags.refs_0_, ...), custom_call_target="tpu_custom_call", output_to_operand_aliasing={{0}: (8, {}), {1}: (9, {}), {2}: (10, {}), {3}: (11, {}), {... | custom-call | flops 17999998976 | bytes 20000000 | tf_op jit(solution)/shard_map/second_pass/pallas_call | solution.py:863
  65.9 3.1 %late_pass.1 = (f32[384,768]{1,0:T(8,128)S(1)}, f32[384,768]{1,0:T(8,128)S(1)}, bf16[4,768,768]{2,1,0:T(8,128)(2,1)S(1)}, bf16[4,768,768]{2,1,0:T(8,128)(2,1)S(1...) custom-call(s32[2]{0:T(128)} %pad_add_fusion.1.flags.refs_0_, ...), custom_call_target="tpu_custom_call", output_to_operand_aliasing={{0}: (6, {}), {1}: (7, {}), {2}: (8, {}), {3}: (9, {}), {4}... | custom-call | flops 2000000000 | bytes 5000000 | tf_op jit(solution)/shard_map/late_pass/pallas_call | solution.py:876
  69.0 10.8 %collective-permute-done.7.got = bf16[384,768]{1,0:T(8,128)(2,1)S(1)} collective-permute-done((bf16[384,768]{1,0:T(8,128)(2,1)S(1)}, bf16[384,768]{1,0:T(8,128)(2,1)S(1)}, u32[]{:S(2)}, u32[]{:S(2)}) %collective-permute-start.7) | collective-permute-done | bytes 589856 | tf_op jit(solution)/shard_map/ppermute | solution.py:1078
  79.8 2.7 %collective-permute-start.10 = (bf16[384,3840]{1,0:T(8,128)(2,1)S(1)}, bf16[384,3840]{1,0:T(8,128)(2,1)}, u32[]{:S(2)}, u32[]{:S(2)}) collective-permute-start(bf16[384,3840]{1,0:T(8,128)(2,1)S(1)} %copy-done.10), channel_id=1, source_target_pairs={{0,8},{8,0},{16,24},{24,16},{1,9},{9,1},{17,25},{25,17},{2,10},{10... | collective-permute-start | bytes 8847368 | tf_op jit(solution)/shard_map/ppermute | solution.py:951
  83.0 16.4 %back_pass.1 = (bf16[384,768]{1,0:T(8,128)(2,1)S(1)}, bf16[384,768]{1,0:T(8,128)(2,1)S(1)}, bf16[384,768]{1,0:T(8,128)(2,1)S(1)}, f32[48,128]{1,0:T(8,128)S(1)},...) custom-call(s32[2]{0:T(128)} %pad_add_fusion.1.flags.refs_0_, bf16[384,768]{1,0:T(8,128)(2,1)} %get-tuple-element.196.field, ...), custom_call_target="tpu_custom_call" | custom-call | flops 10000000000 | bytes 15000000 | tf_op jit(solution)/shard_map/back_pass/pallas_call | solution.py:885
  101.0 5.8 %gram_down.1 = (bf16[768,1536]{1,0:T(8,128)(2,1)S(1)}, bf16[768,768]{1,0:T(8,128)(2,1)S(1)}, bf16[768,768]{1,0:T(8,128)(2,1)S(1)}, bf16[768,3072]{1,0:T(8,128)(2,1)S(1)}, bf16[768,768]{1,0:T(8,128)(2,1)}) custom-call(s32[2]{0:T(128)} %pad_add_fusion.1.flags.refs_0_, bf16[384,768]{1,0:T(8,128)(2,1)S(1)} %get-tuple-element.230.c, ...), custom_call_target="tpu_custom_call" | custom-call | flops 2000000000 | bytes 8000000 | tf_op jit(solution)/shard_map/gram_down/pallas_call | solution.py:898
  106.9 5.6 %gram_main.1 = (bf16[768,3072]{1,0:T(8,128)(2,1)S(1)}, bf16[768,2304]{1,0:T(8,128)(2,1)S(1)}, bf16[768,768]{1,0:T(8,128)(2,1)S(1)}, bf16[48,2432]{1,0:T(8,128)(2...) custom-call(s32[16,4]{1,0:T(8,128)} %copy.57.rows.refs_0_.refs_1_, ...), custom_call_target="tpu_custom_call", output_to_operand_aliasing={{0}: (6, {})} | custom-call | flops 4000000000 | bytes 12000000 | tf_op jit(solution)/shard_map/gram_main/pallas_call | solution.py:908
  116.5 4.4 %collective-permute-done.14.refs_1_ = bf16[48,2432]{1,0:T(8,128)(2,1)S(1)} collective-permute-done((bf16[48,2432]{1,0:T(8,128)(2,1)S(1)}, bf16[48,2432]{1,0:T(8,128)(2,1)S(1)}, u32[]{:S(2)}, u32[]{:S(2)}) %collective-permute-start.14) | collective-permute-done | bytes 233504 | tf_op jit(solution)/shard_map/ppermute | solution.py:986
  134.4 2.5 collective-permute-done.16.refs_1_
  144.9 2.1 collective-permute-done.20.refs_1_
  148.8 2.0 collective-permute-start.24
  153.4 2.0 collective-permute-start.30
  155.4 2.0 collective-permute-done.24.refs_1_
  157.5 1.7 collective-permute-done.25.refs_2_
  179.6 2.3 collective-permute-start.36
  196.9 1.7 collective-permute-done.41.refs_8_
  200.7 3.0 %place.5 = (f32[768,4608]{1,0:T(8,128)}, bf16[768,768]{1,0:T(8,128)(2,1)}) custom-call(s32[2]{0:T(128)} %pad_add_fusion.1.flags.refs_0_, s32[16,4]{1,0:T(8,128)} %copy.57.rows.refs_0_.refs_1_, bf16[48,2304]{1,0:T(8,128)(2,1)S(1)} %get-tuple-element.307.refs_2_, bf16[48,2304]{1,0:T(8,128)(2,1)S(1)} %get-tuple-element.303.refs_3_, ...), custom_call_target="tpu_custom_call" | custom-call | flops 1000 | bytes 20000000 | tf_op jit(solution)/shard_map/place/pallas_call | solution.py:942
  206.4 1.7 collective-permute-done.46.refs_4_
  211.2 1.8 collective-permute-done.52.refs_9_
  215.8 2.0 collective-permute-done.50.refs_8_
  219.9 3.3 %place.6 = (f32[768,4608]{1,0:T(8,128)}, f32[1,768]{1,0:T(1,128)}, f32[1,768]{1,0:T(1,128)}, f32[1,3072]{1,0:T(1,128)}, f32[1,768]{1,0:T(1,128)}) custom-call(s32[2]{0:T(128)} %pad_add_fusion.1.flags.refs_0_, s32[16,4]{1,0:T(8,128)} %copy.57.rows.refs_0_.refs_1_, ...), custom_call_target="tpu_custom_call", output_to_operand_aliasing={{0}: (18, {})} | custom-call | flops 1000 | bytes 20000000 | tf_op jit(solution)/shard_map/place/pallas_call | solution.py:942
  225.5 1.8 collective-permute-done.54.refs_4_
  229.3 2.0 collective-permute-done.59.refs_7_
  234.4 1.7 collective-permute-done.57.refs_6_
  239.1 2.7 %place.7.refs_6_ = f32[768,4608]{1,0:T(8,128)} custom-call(s32[2]{0:T(128)} %pad_add_fusion.1.flags.refs_0_, s32[16,4]{1,0:T(8,128)} %copy.57.rows.refs_0_.refs_1_, bf16[48,2304]{1,0:T(8,128)(2,1)S(1)} %collective-permute-done.53.refs_2_, bf16[48,2304]{1,0:T(8,128)(2,1)S(1)} %collective-permute-done.55.refs_3_, ...), custom_call_target="tpu_custom_call", output_to_operand_aliasing={{}: (10, {})} | custom-call | flops 1000 | bytes 20000000 | tf_op jit(solution)/shard_map/place/pallas_call | solution.py:942
  248.6 2.1 place.8.refs_6_
  254.2 2.1 place.9
  (162 shorter events, 111.0 us)
Async XLA Ops:
  0.6 12.2 %collective-permute-start.4 = (bf16[768,4608]{1,0:T(8,128)(2,1)}, bf16[768,4608]{1,0:T(8,128)(2,1)}, u32[]{:S(2)}, u32[]{:S(2)}) collective-permute-start(bf16[768,4608]{1,0:T(8,128)(2,1)} %bitcast.9), channel_id=1, source_target_pairs={{0,8},{8,0},{16,24},{24,16},{1,9},{9,1},{17,25},{25,17},{2,10},{10... | collective-permute-start | bytes 21233672 | tf_op jit(solution)/shard_map/ppermute | solution.py:951
  29.4 11.3 %collective-permute-start.5 = (bf16[384,768]{1,0:T(8,128)(2,1)S(1)}, bf16[384,768]{1,0:T(8,128)(2,1)S(1)}, u32[]{:S(2)}, u32[]{:S(2)}) collective-permute-start(bf16[384,768]{1,0:T(8,128)(2,1)S(1)} %get-tuple-element.197.x_two), channel_id=1, source_target_pairs={{0,16},{1,17},{2,18},{3,19},{4,20},{5,21},{6,22},{7,23}} | collective-permute-start | bytes 1769480 | tf_op jit(solution)/shard_map/ppermute | solution.py:1073
  30.7 10.0 %collective-permute-start.6 = (bf16[384,768]{1,0:T(8,128)(2,1)S(1)}, bf16[384,768]{1,0:T(8,128)(2,1)S(1)}, u32[]{:S(2)}, u32[]{:S(2)}) collective-permute-start(bf16[384,768]{1,0:T(8,128)(2,1)S(1)} %get-tuple-element.197.x_two), channel_id=1, source_target_pairs={{8,24},{9,25},{10,26},{11,27},{12,28},{13,29},{14,30},{15,31}} | collective-permute-start | bytes 1769480 | tf_op jit(solution)/shard_map/ppermute | solution.py:1073
  64.6 15.2 %collective-permute-start.7 = (bf16[384,768]{1,0:T(8,128)(2,1)S(1)}, bf16[384,768]{1,0:T(8,128)(2,1)S(1)}, u32[]{:S(2)}, u32[]{:S(2)}) collective-permute-start(bf16[384,768]{1,0:T(8,128)(2,1)S(1)} %get-tuple-element.203), channel_id=1, source_target_pairs={{16,0},{24,8},{17,1},{25,9},{18,2},{26,10},{19,3},{27,11},{20,4},{... | collective-permute-start | bytes 1769480 | tf_op jit(solution)/shard_map/ppermute | solution.py:1078
  79.8 20.5 %collective-permute-start.10 = (bf16[384,3840]{1,0:T(8,128)(2,1)S(1)}, bf16[384,3840]{1,0:T(8,128)(2,1)}, u32[]{:S(2)}, u32[]{:S(2)}) collective-permute-start(bf16[384,3840]{1,0:T(8,128)(2,1)S(1)} %copy-done.10), channel_id=1, source_target_pairs={{0,8},{8,0},{16,24},{24,16},{1,9},{9,1},{17,25},{25,17},{2,10},{10... | collective-permute-start | bytes 8847368 | tf_op jit(solution)/shard_map/ppermute | solution.py:951
  82.5 17.8 %collective-permute-start.8 = (bf16[384,768]{1,0:T(8,128)(2,1)S(1)}, bf16[384,768]{1,0:T(8,128)(2,1)S(1)}, u32[]{:S(2)}, u32[]{:S(2)}) collective-permute-start(bf16[384,768]{1,0:T(8,128)(2,1)S(1)} %collective-permute-done.7.got), channel_id=1, source_target_pairs={{0,8},{8,0},{16,24},{24,16},{1,9},{9,1},{17,25},{25,17},{2,10},{10... | collective-permute-start | bytes 1769480 | tf_op jit(solution)/shard_map/ppermute | solution.py:951
  82.5 17.8 %collective-permute-start.9 = (bf16[384,768]{1,0:T(8,128)(2,1)S(1)}, bf16[384,768]{1,0:T(8,128)(2,1)S(1)}, u32[]{:S(2)}, u32[]{:S(2)}) collective-permute-start(bf16[384,768]{1,0:T(8,128)(2,1)S(1)} %get-tuple-element.232), channel_id=1, source_target_pairs={{0,8},{8,0},{16,24},{24,16},{1,9},{9,1},{17,25},{25,17},{2,10},{10... | collective-permute-start | bytes 1769480 | tf_op jit(solution)/shard_map/ppermute | solution.py:951
  114.5 11.5 %collective-permute-start.12 = (bf16[48,2432]{1,0:T(8,128)(2,1)S(1)}, bf16[48,2432]{1,0:T(8,128)(2,1)S(1)}, u32[]{:S(2)}, u32[]{:S(2)}) collective-permute-start(bf16[48,2432]{1,0:T(8,128)(2,1)S(1)} %get-tuple-element.247), channel_id=1, source_target_pairs={{0,2},{2,4},{4,6},{6,7},{7,5},{5,3},{3,1},{1,0},{8,10},{10,12},{12... | collective-permute-start | bytes 700424 | tf_op jit(solution)/shard_map/ppermute | solution.py:986
  115.3 11.5 %collective-permute-start.13 = (bf16[48,2432]{1,0:T(8,128)(2,1)S(1)}, bf16[48,2432]{1,0:T(8,128)(2,1)S(1)}, u32[]{:S(2)}, u32[]{:S(2)}) collective-permute-start(bf16[48,2432]{1,0:T(8,128)(2,1)S(1)} %get-tuple-element.248), channel_id=1, source_target_pairs={{0,1},{2,0},{4,2},{6,4},{7,6},{5,7},{3,5},{1,3},{8,9},{10,8},{12,1... | collective-permute-start | bytes 700424 | tf_op jit(solution)/shard_map/ppermute | solution.py:986
  122.8 8.7 %collective-permute-start.18 = (bf16[48,2432]{1,0:T(8,128)(2,1)S(1)}, bf16[48,2432]{1,0:T(8,128)(2,1)S(1)}, u32[]{:S(2)}, u32[]{:S(2)}) collective-permute-start(bf16[48,2432]{1,0:T(8,128)(2,1)S(1)} %get-tuple-element.255), channel_id=1, source_target_pairs={{0,2},{2,4},{4,6},{6,7},{7,5},{5,3},{3,1},{1,0},{8,10},{10,12},{12... | collective-permute-start | bytes 700424 | tf_op jit(solution)/shard_map/ppermute | solution.py:986
  128.3 8.6 %collective-permute-start.16 = (bf16[48,2432]{1,0:T(8,128)(2,1)S(1)}, bf16[48,2432]{1,0:T(8,128)(2,1)S(1)}, u32[]{:S(2)}, u32[]{:S(2)}) collective-permute-start(bf16[48,2432]{1,0:T(8,128)(2,1)S(1)} %get-tuple-element.259), channel_id=1, source_target_pairs={{0,2},{2,4},{4,6},{6,7},{7,5},{5,3},{3,1},{1,0},{8,10},{10,12},{12... | collective-permute-start | bytes 700424 | tf_op jit(solution)/shard_map/ppermute | solution.py:986
  132.4 9.5 %collective-permute-start.22 = (bf16[48,2432]{1,0:T(8,128)(2,1)S(1)}, bf16[48,2432]{1,0:T(8,128)(2,1)S(1)}, u32[]{:S(2)}, u32[]{:S(2)}) collective-permute-start(bf16[48,2432]{1,0:T(8,128)(2,1)S(1)} %get-tuple-element.263), channel_id=1, source_target_pairs={{0,2},{2,4},{4,6},{6,7},{7,5},{5,3},{3,1},{1,0},{8,10},{10,12},{12... | collective-permute-start | bytes 700424 | tf_op jit(solution)/shard_map/ppermute | solution.py:986
  138.4 8.6 %collective-permute-start.20 = (bf16[48,2432]{1,0:T(8,128)(2,1)S(1)}, bf16[48,2432]{1,0:T(8,128)(2,1)S(1)}, u32[]{:S(2)}, u32[]{:S(2)}) collective-permute-start(bf16[48,2432]{1,0:T(8,128)(2,1)S(1)} %get-tuple-element.267), channel_id=1, source_target_pairs={{0,2},{2,4},{4,6},{6,7},{7,5},{5,3},{3,1},{1,0},{8,10},{10,12},{12... | collective-permute-start | bytes 700424 | tf_op jit(solution)/shard_map/ppermute | solution.py:986
  142.9 9.2 %collective-permute-start.26 = (bf16[48,2432]{1,0:T(8,128)(2,1)S(1)}, bf16[48,2432]{1,0:T(8,128)(2,1)S(1)}, u32[]{:S(2)}, u32[]{:S(2)}) collective-permute-start(bf16[48,2432]{1,0:T(8,128)(2,1)S(1)} %get-tuple-element.271), channel_id=1, source_target_pairs={{0,2},{2,4},{4,6},{6,7},{7,5},{5,3},{3,1},{1,0},{8,10},{10,12},{12... | collective-permute-start | bytes 700424 | tf_op jit(solution)/shard_map/ppermute | solution.py:986
  148.8 8.6 %collective-permute-start.24 = (bf16[48,2432]{1,0:T(8,128)(2,1)S(1)}, bf16[48,2432]{1,0:T(8,128)(2,1)S(1)}, u32[]{:S(2)}, u32[]{:S(2)}) collective-permute-start(bf16[48,2432]{1,0:T(8,128)(2,1)S(1)} %get-tuple-element.275), channel_id=1, source_target_pairs={{0,2},{2,4},{4,6},{6,7},{7,5},{5,3},{3,1},{1,0},{8,10},{10,12},{12... | collective-permute-start | bytes 700424 | tf_op jit(solution)/shard_map/ppermute | solution.py:986
  153.4 9.2 %collective-permute-start.30 = (bf16[48,2304]{1,0:T(8,128)(2,1)S(1)}, bf16[48,2304]{1,0:T(8,128)(2,1)S(1)}, u32[]{:S(2)}, u32[]{:S(2)}) collective-permute-start(bf16[48,2304]{1,0:T(8,128)(2,1)S(1)} %get-tuple-element.279), channel_id=1, source_target_pairs={{0,2},{2,4},{4,6},{6,7},{7,5},{5,3},{3,1},{1,0},{8,10},{10,12},{12... | collective-permute-start | bytes 663560 | tf_op jit(solution)/shard_map/ppermute | solution.py:986
  182.0 18.7 %collective-permute-start.44 = (bf16[384,768]{1,0:T(8,128)(2,1)S(1)}, bf16[384,768]{1,0:T(8,128)(2,1)S(1)}, u32[]{:S(2)}, u32[]{:S(2)}) collective-permute-start(bf16[384,768]{1,0:T(8,128)(2,1)S(1)} %copy-done.8), channel_id=1, source_target_pairs={{0,8},{8,0},{16,24},{24,16},{1,9},{9,1},{17,25},{25,17},{2,10},{10... | collective-permute-start | bytes 1769480 | tf_op jit(solution)/shard_map/ppermute | solution.py:951
  189.7 8.9 %collective-permute-start.41 = (bf16[48,2304]{1,0:T(8,128)(2,1)S(1)}, bf16[48,2304]{1,0:T(8,128)(2,1)S(1)}, u32[]{:S(2)}, u32[]{:S(2)}) collective-permute-start(bf16[48,2304]{1,0:T(8,128)(2,1)S(1)} %get-tuple-element.308.refs_4_), channel_id=1, source_target_pairs={{0,1},{2,0},{4,2},{6,4},{7,6},{5,7},{3,5},{1,3},{8,9},{10,8},{12,1... | collective-permute-start | bytes 663560 | tf_op jit(solution)/shard_map/ppermute | solution.py:986
  193.9 9.8 %collective-permute-start.47 = (bf16[48,2304]{1,0:T(8,128)(2,1)S(1)}, bf16[48,2304]{1,0:T(8,128)(2,1)S(1)}, u32[]{:S(2)}, u32[]{:S(2)}) collective-permute-start(bf16[48,2304]{1,0:T(8,128)(2,1)S(1)} %collective-permute-done.42.refs_7_), channel_id=1, source_target_pairs={{0,2},{2,4},{4,6},{6,7},{7,5},{5,3},{3,1},{1,0},{8,10},{10,12},{12... | collective-permute-start | bytes 663560 | tf_op jit(solution)/shard_map/ppermute | solution.py:986
  194.8 8.9 %collective-permute-start.48 = (bf16[48,2304]{1,0:T(8,128)(2,1)S(1)}, bf16[48,2304]{1,0:T(8,128)(2,1)S(1)}, u32[]{:S(2)}, u32[]{:S(2)}) collective-permute-start(bf16[48,2304]{1,0:T(8,128)(2,1)S(1)} %collective-permute-done.43.refs_9_), channel_id=1, source_target_pairs={{0,1},{2,0},{4,2},{6,4},{7,6},{5,7},{3,5},{1,3},{8,9},{10,8},{12,1... | collective-permute-start | bytes 663560 | tf_op jit(solution)/shard_map/ppermute | solution.py:986
  199.5 8.6 %collective-permute-start.46 = (bf16[48,2304]{1,0:T(8,128)(2,1)S(1)}, bf16[48,2304]{1,0:T(8,128)(2,1)S(1)}, u32[]{:S(2)}, u32[]{:S(2)}) collective-permute-start(bf16[48,2304]{1,0:T(8,128)(2,1)S(1)} %collective-permute-done.41.refs_8_), channel_id=1, source_target_pairs={{0,1},{2,0},{4,2},{6,4},{7,6},{5,7},{3,5},{1,3},{8,9},{10,8},{12,1... | collective-permute-start | bytes 663560 | tf_op jit(solution)/shard_map/ppermute | solution.py:986
  209.0 8.8 %collective-permute-start.50 = (bf16[48,2304]{1,0:T(8,128)(2,1)S(1)}, bf16[48,2304]{1,0:T(8,128)(2,1)S(1)}, u32[]{:S(2)}, u32[]{:S(2)}) collective-permute-start(bf16[48,2304]{1,0:T(8,128)(2,1)S(1)} %collective-permute-done.46.refs_4_), channel_id=1, source_target_pairs={{0,1},{2,0},{4,2},{6,4},{7,6},{5,7},{3,5},{1,3},{8,9},{10,8},{12,1... | collective-permute-start | bytes 663560 | tf_op jit(solution)/shard_map/ppermute | solution.py:986
  213.0 10.1 %collective-permute-start.55 = (bf16[48,2304]{1,0:T(8,128)(2,1)S(1)}, bf16[48,2304]{1,0:T(8,128)(2,1)S(1)}, u32[]{:S(2)}, u32[]{:S(2)}) collective-permute-start(bf16[48,2304]{1,0:T(8,128)(2,1)S(1)} %collective-permute-done.51.refs_7_), channel_id=1, source_target_pairs={{0,2},{2,4},{4,6},{6,7},{7,5},{5,3},{3,1},{1,0},{8,10},{10,12},{12... | collective-permute-start | bytes 663560 | tf_op jit(solution)/shard_map/ppermute | solution.py:986
  214.0 9.2 %collective-permute-start.56 = (bf16[48,2304]{1,0:T(8,128)(2,1)S(1)}, bf16[48,2304]{1,0:T(8,128)(2,1)S(1)}, u32[]{:S(2)}, u32[]{:S(2)}) collective-permute-start(bf16[48,2304]{1,0:T(8,128)(2,1)S(1)} %collective-permute-done.52.refs_9_), channel_id=1, source_target_pairs={{0,1},{2,0},{4,2},{6,4},{7,6},{5,7},{3,5},{1,3},{8,9},{10,8},{12,1... | collective-permute-start | bytes 663560 | tf_op jit(solution)/shard_map/ppermute | solution.py:986
  218.5 8.8 %collective-permute-start.54 = (bf16[48,2304]{1,0:T(8,128)(2,1)S(1)}, bf16[48,2304]{1,0:T(8,128)(2,1)S(1)}, u32[]{:S(2)}, u32[]{:S(2)}) collective-permute-start(bf16[48,2304]{1,0:T(8,128)(2,1)S(1)} %collective-permute-done.50.refs_8_), channel_id=1, source_target_pairs={{0,1},{2,0},{4,2},{6,4},{7,6},{5,7},{3,5},{1,3},{8,9},{10,8},{12,1... | collective-permute-start | bytes 663560 | tf_op jit(solution)/shard_map/ppermute | solution.py:986
  227.3 8.8 %collective-permute-start.57 = (bf16[48,2304]{1,0:T(8,128)(2,1)S(1)}, bf16[48,2304]{1,0:T(8,128)(2,1)S(1)}, u32[]{:S(2)}, u32[]{:S(2)}) collective-permute-start(bf16[48,2304]{1,0:T(8,128)(2,1)S(1)} %collective-permute-done.53.refs_2_), channel_id=1, source_target_pairs={{0,2},{2,4},{4,6},{6,7},{7,5},{5,3},{3,1},{1,0},{8,10},{10,12},{12... | collective-permute-start | bytes 663560 | tf_op jit(solution)/shard_map/ppermute | solution.py:986
  228.0 9.1 %collective-permute-start.58 = (bf16[48,2304]{1,0:T(8,128)(2,1)S(1)}, bf16[48,2304]{1,0:T(8,128)(2,1)S(1)}, u32[]{:S(2)}, u32[]{:S(2)}) collective-permute-start(bf16[48,2304]{1,0:T(8,128)(2,1)S(1)} %collective-permute-done.54.refs_4_), channel_id=1, source_target_pairs={{0,1},{2,0},{4,2},{6,4},{7,6},{5,7},{3,5},{1,3},{8,9},{10,8},{12,1... | collective-permute-start | bytes 663560 | tf_op jit(solution)/shard_map/ppermute | solution.py:986
  232.3 9.5 %collective-permute-start.63 = (bf16[48,2304]{1,0:T(8,128)(2,1)S(1)}, bf16[48,2304]{1,0:T(8,128)(2,1)S(1)}, u32[]{:S(2)}, u32[]{:S(2)}) collective-permute-start(bf16[48,2304]{1,0:T(8,128)(2,1)S(1)} %collective-permute-done.59.refs_7_), channel_id=1, source_target_pairs={{0,2},{2,4},{4,6},{6,7},{7,5},{5,3},{3,1},{1,0},{8,10},{10,12},{12... | collective-permute-start | bytes 663560 | tf_op jit(solution)/shard_map/ppermute | solution.py:986
  232.7 9.1 %collective-permute-start.64 = (bf16[48,2304]{1,0:T(8,128)(2,1)S(1)}, bf16[48,2304]{1,0:T(8,128)(2,1)S(1)}, u32[]{:S(2)}, u32[]{:S(2)}) collective-permute-start(bf16[48,2304]{1,0:T(8,128)(2,1)S(1)} %collective-permute-done.60.refs_9_), channel_id=1, source_target_pairs={{0,1},{2,0},{4,2},{6,4},{7,6},{5,7},{3,5},{1,3},{8,9},{10,8},{12,1... | collective-permute-start | bytes 663560 | tf_op jit(solution)/shard_map/ppermute | solution.py:986
  237.5 9.1 %collective-permute-start.62 = (bf16[48,2304]{1,0:T(8,128)(2,1)S(1)}, bf16[48,2304]{1,0:T(8,128)(2,1)S(1)}, u32[]{:S(2)}, u32[]{:S(2)}) collective-permute-start(bf16[48,2304]{1,0:T(8,128)(2,1)S(1)} %collective-permute-done.58.refs_8_), channel_id=1, source_target_pairs={{0,1},{2,0},{4,2},{6,4},{7,6},{5,7},{3,5},{1,3},{8,9},{10,8},{12,1... | collective-permute-start | bytes 663560 | tf_op jit(solution)/shard_map/ppermute | solution.py:986
  241.8 8.9 %collective-permute-start.67 = (bf16[48,2304]{1,0:T(8,128)(2,1)S(1)}, bf16[48,2304]{1,0:T(8,128)(2,1)S(1)}, u32[]{:S(2)}, u32[]{:S(2)}) collective-permute-start(bf16[48,2304]{1,0:T(8,128)(2,1)S(1)} %collective-permute-done.63.refs_3_), channel_id=1, source_target_pairs={{0,2},{2,4},{4,6},{6,7},{7,5},{5,3},{3,1},{1,0},{8,10},{10,12},{12... | collective-permute-start | bytes 663560 | tf_op jit(solution)/shard_map/ppermute | solution.py:986
  242.3 9.0 %collective-permute-start.68 = (bf16[48,2304]{1,0:T(8,128)(2,1)S(1)}, bf16[48,2304]{1,0:T(8,128)(2,1)S(1)}, u32[]{:S(2)}, u32[]{:S(2)}) collective-permute-start(bf16[48,2304]{1,0:T(8,128)(2,1)S(1)} %collective-permute-done.64.refs_5_), channel_id=1, source_target_pairs={{0,1},{2,0},{4,2},{6,4},{7,6},{5,7},{3,5},{1,3},{8,9},{10,8},{12,1... | collective-permute-start | bytes 663560 | tf_op jit(solution)/shard_map/ppermute | solution.py:986
  (48 other events, 541.2 us)

commit v4 on v3

--- a/solution.py
+++ b/solution.py
@@ -317,9 +317,14 @@
 
 
 def prepare_kernel(
-    flags, x, cot, gain, shift, first, second, keep, send, away, across, vec
+    flags, x, cot, gain, shift, first, second, keep, send, away, across, vec, table, n
 ):
-    core, layer = flags[0], flags[1]
+    core, layer, where = flags[0], flags[1], flags[2]
+    for t in range(table.shape[0]):
+        for way, d in ((0, 1), (1, -1)):
+            at = lax.rem(where - d * (t % n) + 2 * n, n)
+            table[t, way] = at * (D // (2 * n)) + way * HALF
+            table[t, 2 + way] = jnp.where(2 * at < n, 2 * at, 2 * (n - at) - 1)
     for at, (mine, other) in enumerate(((x, cot), (cot, x))):
 
         @pl.when(layer == at)
@@ -401,13 +406,14 @@
 
     @pl.when((core != 0) | (flags[1] != 0))
     def _():
-        for i in range(4):
-            load_attn(core, own, oth, wa, sems, i)
-            load_mlp(core, own, oth, w1, wd, sems.at[pl.ds(4, 8)], i)
+        for j in range(2):
+            for i in range(2 * j, 2 * j + 2):
+                load_attn(core, own, oth, wa, sems, i)
+                load_mlp(core, own, oth, w1, wd, sems.at[pl.ds(4, 8)], i)
+            for i in range(2 * j, 2 * j + 2):
+                wait_attn(own, wa, sems, i)
+                wait_mlp(own, w1, wd, sems.at[pl.ds(4, 8)], i)
         load_angles(cos_in, sin_in, cosf, sinf, sems.at[pl.ds(12, 2)])
-        for i in range(4):
-            wait_attn(own, wa, sems, i)
-            wait_mlp(own, w1, wd, sems.at[pl.ds(4, 8)], i)
         wait_angles(cos_in, sin_in, cosf, sinf, sems.at[pl.ds(12, 2)])
 
 
@@ -621,11 +627,14 @@
 
 
 def gram_down_kernel(
-    flags, c, c_oth, x_keep, x_oth, act, bundle, main0, tail0, right0,
-    down, left_main, left_tail, right_out, activations,
+    flags, c, c_oth, x_keep, x_oth, c_keep, c_send, act, bundle, main0, tail0, right0,
+    down, left_main, left_tail, right_out, activations, c_kept, c_sent,
     c1, sides, left, right, sems, row_sems,
 ):
-    leaving = both_rows(flags[0], x_keep, x_oth, activations, row_sems)
+    leaving = both_rows(flags[0], x_keep, x_oth, activations, row_sems) + [
+        pltpu.make_async_copy(src, dst, row_sems.at[2 + k])
+        for k, (src, dst) in enumerate(((c_keep, c_kept), (c_send, c_sent)))
+    ]
     for copy in leaving:
         copy.start()
     loads = (
@@ -659,30 +668,31 @@
         copy.wait()
 
 
-def gram_main_kernel(
-    rows, right1, down, left_main, left_tail, vec, right_in,
-    right, main, head, main_up, main_down, tail_up, tail_down, vec_out,
-):
-    right[L:, :] = right1[:L, :]
-    head[...] = dot(left_tail[...], right[:, 3 * D :]).astype(BF)
-    main[...] = dot(left_main[...], right[:, : 3 * D]).astype(BF)
+def gram_head_kernel(rows, right1, down, left, vec, right0, head, tail_up, tail_down, vec_out, right):
+    right[:L, :] = right0[:L, 3 * D :]
+    right[L:, :] = right1[:L, 3 * D :]
+    head[...] = dot(left[...], right[...]).astype(BF)
     other = [
         jnp.concatenate(
             [right1[L : L + 16, 128 * (3 * k + b) : 128 * (3 * k + b + 1)].astype(F32) for b in range(3)], axis=0
         )
         for k in range(2)
     ]
-    total = vec[...] + (other[0] + other[1])
-    total = total.astype(BF)
+    total = (vec[...] + (other[0] + other[1])).astype(BF)
     vec_out[...] = total.astype(F32)
-    r = main_up.shape[0]
-    for k, (m, t) in enumerate(((main_up, tail_up), (main_down, tail_down))):
-        here = own_rows(rows, 0, k, r)
-        m[:, : 3 * D] = main[here, :]
-        m[:, 3 * D :] = total
+    for k, t in enumerate((tail_up, tail_down)):
+        here = own_rows(rows, 0, k, t.shape[0])
         t[:, :D] = head[here, :]
         t[:, D : 3 * D] = down[here, :]
         t[:, 3 * D :] = total
+
+
+def gram_main_kernel(rows, right1, left, vec, right_in, right, main, main_up, main_down):
+    right[L:, :] = right1[:L, :]
+    main[...] = dot(left[...], right[:, : 3 * D]).astype(BF)
+    for k, m in enumerate((main_up, main_down)):
+        m[:, : 3 * D] = main[own_rows(rows, 0, k, m.shape[0]), :]
+        m[:, 3 * D :] = vec[...].astype(BF)
 
 
 def own_rows(rows, t, way, r):
@@ -774,6 +784,7 @@
 SMEM = pl.BlockSpec(memory_space=pltpu.SMEM)
 VS = pl.BlockSpec(memory_space=pltpu.VMEM)
 HBM = pl.BlockSpec(memory_space=pltpu.HBM)
+ANY = pl.BlockSpec(memory_space=pl.ANY)
 
 
 def sds(shape, dtype=BF):
@@ -816,11 +827,16 @@
     return pltpu.HBM((L, width), BF)
 
 
-def prepare(flags, x, cot, *vecs):
+def prepare(flags, n, x, cot, *vecs):
     out = VM((x.shape[0], L), BF)
+
+    def kernel(*refs):
+        prepare_kernel(*refs, n)
+
+    table = pltpu.HBM((2 * n if n <= 16 else 1, 4), I32)
     return call(
-        prepare_kernel, "prepare", [SMEM] + [VS] * 6, [out] * 4 + [pltpu.HBM((1, VECTOR), F32)], [], 1000,
-        int(1e6), 8,
+        kernel, "prepare", [SMEM] + [VS] * 6, [out] * 4 + [pltpu.HBM((1, VECTOR), F32), table], [], 1000,
+        int(1e6), 8, out_specs=[VS] * 5 + [SMEM],
     )(flags, *(in_hbm(a) for a in (x, cot) + vecs))
 
 
@@ -884,7 +900,7 @@
 def back_pass(held, *a):
     return call(
         back_kernel, "back_pass", [SMEM] + [VS] * 5 + [HBM] * 2 + [VS] * len(held),
-        [sds((L, D)), sds((L, D)), row(), VM(PACKED, F32), row_out(FF), pltpu.HBM((L + 16, FF), BF)],
+        [row(), row(), row(), VM(PACKED, F32), row_out(FF), pltpu.HBM((L + 16, FF), BF)],
         HEAD_S
         + [row(FF), row(FF), VM((1, FIRST + 6 * D), F32), VM((1, VECTOR), F32), VM((1, VECTOR), F32),
            VM((16, D), BF)]
@@ -896,20 +912,27 @@
 def gram_down(*a):
     square = VM((D, 2 * L), BF)
     return call(
-        gram_down_kernel, "gram_down", [SMEM] + [VS] * 4 + [HBM] * 5,
-        [VM((D, 2 * D), BF), square, square, VM((2 * L, FF), BF), pltpu.HBM((2 * L, D), BF)],
-        [row(), VM((4, L, D), BF), square, VM((2 * L, 2 * D), BF), DMA((8,)), DMA((2,))], int(2e9), int(8e6), 20,
-        out_specs=[VS] * 4 + [HBM],
+        gram_down_kernel, "gram_down", [SMEM] + [VS] * 6 + [HBM, ANY] + [HBM] * 3,
+        [VM((D, 2 * D), BF), square, square, VM((2 * L, FF), BF), pltpu.HBM((2 * L, D), BF), row_out(), row_out()],
+        [row(), VM((4, L, D), BF), square, VM((2 * L, 2 * D), BF), DMA((8,)), DMA((4,))], int(2e9), int(8e6), 20,
+        out_specs=[VS] * 4 + [HBM] * 3,
     )(*a)
+
+
+def gram_head(rows, r, *a):
+    wide = VM((r, 3 * D + 128), BF)
+    return call(
+        gram_head_kernel, "gram_head", [SMEM] + [VS] * 5, [VM((D, D), BF), wide, wide, VM(PACKED, F32)],
+        [VM((2 * L, D), BF)], int(1e9), int(5e6), 12,
+    )(rows, *a)
 
 
 def gram_main(rows, r, *a):
     wide = VM((r, 3 * D + 128), BF)
     return call(
-        gram_main_kernel, "gram_main", [SMEM] + [VS] * 6,
-        [VM((2 * L, FF), BF), VM((D, 3 * D), BF), VM((D, D), BF)] + [wide] * 4 + [VM(PACKED, F32)],
-        [], int(4e9), int(12e6), 20, aliases={6: 0},
-    )(rows, *a)
+        gram_main_kernel, "gram_main", [SMEM] + [VS] * 4,
+        [VM((2 * L, FF), BF), VM((D, 3 * D), BF), wide, wide], [], int(6e9), int(12e6), 20, aliases={4: 0},
+    )(rows, *a)[1:]
 
 
 def add(t, rows, up, down, parts, vector, wide):
@@ -921,7 +944,7 @@
     width = sum(p.shape[1] for p in parts)
     out = VM((up.shape[0], width + (128 if wide else 0)), BF)
     results = call(
-        kernel, "add", [SMEM] + [VS] * (2 + count), [out, out] + [pltpu.HBM(PACKED, F32)] * vector, [], 1000,
+        kernel, "add", [SMEM] + [VS] * (2 + count), [out, out] + [VM(PACKED, F32)] * vector, [], 1000,
         int(1e6), 4,
     )(rows, in_vmem(up), in_vmem(down), *(in_vmem(p) for p in parts))
     return results[:2], results[2:]
@@ -956,19 +979,12 @@
 
 
 class Cycle:
-    def __init__(self):
+    def __init__(self, rows):
         self.n = n = lax.axis_size("dp")
         self.r = D // (2 * n)
-        i = lax.axis_index("dp")
-        where = jnp.where(i % 2 == 0, i // 2, n - 1 - i // 2)
         order = list(range(0, n, 2)) + list(range(n - 1, 0, -2))
         self.pairs = [[(order[k], order[(k + d) % n]) for k in range(n)] for d in (1, -1)]
-        t = jnp.arange(2 * n, dtype=I32)[:, None]
-        way = jnp.array([[1, -1]], I32)
-        step = jnp.where(t < n, t, t - n)
-        at = (where - way * step) % n
-        whose = jnp.where(2 * at < n, 2 * at, 2 * (n - at) - 1)
-        self.rows = in_hbm(jnp.concatenate([at * self.r + jnp.array([[0, HALF]], I32), whose], axis=1))
+        self.rows = rows
 
     def placed(self, k):
         return 2 * self.n - 1 if k == 0 else self.n + k - 1
@@ -1002,10 +1018,10 @@
     return lax.axis_size("dp") <= 16
 
 
-def summed(flags, main, tail, token, pair, vector):
+def summed(flags, rows, main, tail, token, pair, vector):
     if not small_ring():
         chains, vector = lax.psum([main, tail], "dp"), lax.psum(vector, "dp")
-        return place(flags, [(0, 0)], jnp.zeros((1, 1), I32), chains, None, pair, [vector])
+        return place(flags, [(0, 0)], rows, chains, None, pair, [vector])
     cycle = main.cycle
     n = cycle.n
     total, placed = None, 0
@@ -1039,25 +1055,23 @@
 ):
     section = lax.axis_index("section")
     core = section % 2
-    flags = in_hbm(jnp.stack([core, section // 2]).astype(I32))
+    n = lax.axis_size("dp")
+    i = lax.axis_index("dp")
+    where = jnp.where(i % 2 == 0, i // 2, n - 1 - i // 2)
+    flags = in_hbm(jnp.stack([core, section // 2, where]).astype(I32))
     first_layer = section < 2
 
-    keep, send, away, across, vown = prepare(
-        flags, block_input.T, cotangent.T, norm_gain, norm_bias, first_vector, second_vector
-    )
-    n = lax.axis_size("dp")
+    keep, send, away, across, vown, rows = prepare(
+        flags, n, block_input.T, cotangent.T, norm_gain, norm_bias, first_vector, second_vector
+    )
     if n % 2 == 0:
         voth = lax.ppermute(
             vown, ("section", "dp"), [(n * s + d, n * (s ^ 1) + (d ^ 1)) for s in range(4) for d in range(n)]
         )
     else:
         voth = core_swap(vown)
-    if small_ring():
-        cycle = Cycle()
-        rows, r = cycle.rows, cycle.r
-    else:
-        rows, r = jnp.zeros((1, 2), I32), PACKED[0]
-    vown, voth = in_hbm(vown), in_hbm(after(voth, rows))
+    r = D // (2 * n) if small_ring() else PACKED[0]
+    vown, voth, rows = in_hbm(vown), in_hbm(voth), in_hbm(rows)
     got = core_swap(send)
     away = lax.ppermute(away, "section", [(0, 2), (1, 3), (2, 0), (3, 1)])
     across = lax.ppermute(across, "section", [(0, 3), (1, 2), (2, 1), (3, 0)])
@@ -1078,7 +1092,7 @@
     c_got = lax.ppermute(c_two, "section", [(2, 0), (3, 1)])
     held, (x_keep, x_send) = late_pass(held, flags, x_two, vown, voth, *(in_vmem(a) for a in active))
     c_got = after(c_got, x_keep)
-    bundle = in_hbm(core_swap(after(bundle, c_got)))
+    bundle = core_swap(after(bundle, c_got))
     x_oth = core_swap(after(x_send, c_got))
 
     c_keep, c_send, c_out, vec, right, right_send = back_pass(
@@ -1086,19 +1100,23 @@
     )
     c_oth = core_swap(c_got)
     right_oth = core_swap(after(right_send, (c_oth, bundle, x_oth)))
-    down, left_main, left_tail, right, activations = gram_down(
-        flags, c_out, c_oth, x_keep, x_oth, act_mine, bundle, main_left, tail_left, in_hbm(right)
-    )
-    right, main, head, *first, vec = gram_main(
-        rows, r, right_oth, down, left_main, left_tail, vec, right
-    )
-    token = main
+    down, left_main, left_tail, right, activations, c_keep, c_send = gram_down(
+        flags, c_out, c_oth, x_keep, x_oth, in_vmem(c_keep), in_vmem(c_send), act_mine, bundle, main_left, tail_left, in_hbm(right)
+    )
+    head, *tail_first, vec = gram_head(rows, r, right_oth, down, left_tail, vec, right)
     if small_ring():
-        main, tail = Chain(cycle, [main], first[:2], True), Chain(cycle, [head, down], first[2:])
+        cycle = Cycle(rows)
+        tail = Chain(cycle, [head, down], tail_first)
     else:
         tail = jnp.concatenate([head, down], axis=1)
+    main, *main_first = gram_main(rows, r, right_oth, left_main, vec, right)
+    if small_ring():
+        main = Chain(cycle, [main], main_first, True)
+        token = main.cur
+    else:
+        token = main
     weight_grad, input_grads, *vectors = summed(
-        flags, main, tail, token, (c_keep, core_swap(after(c_send, token))), vec
+        flags, rows, main, tail, token, (c_keep, core_swap(after(c_send, token))), vec
     )
     return (
         activations[None],

time: 260 us -> 253 us (0.973)
  waiting for transfers between devices: 78.9 us -> 74.1 us
  Pallas kernels: 103 us -> 100 us
    pallas_call x17 -> x18, Pallas kernels: 27.7 us -> 25.9 us  [the longest x14 12.6 us: add(): call(kernel, 'add', [SMEM] + [VS] * (2 + count), [out, out] + [VM(PACKED,...]
  transfers between devices with their start and end apart: 69 -> 69, of which waited for: 47 -> 49; matrix products, arithmetic and copies ran while one was open for 1% -> 0% of each run, Pallas kernels for 22% -> 24%
where the time goes in v4:
time: 253 us; the launch traced here: 249 us
  Pallas kernels  100 us (40%)
  waiting for transfers between devices  74.1 us (29%)
  starting transfers between devices  72.4 us (29%)
    ppermute x56, starting transfers between devices, step(): got = [lax.ppermute(a, 'dp', p) for a, p in zip(self.cur, c.pairs)]  58 us
    ppermute x56, waiting for transfers between devices, step(): got = [lax.ppermute(a, 'dp', p) for a, p in zip(self.cur, c.pairs)]  56.1 us
    pallas_call x1, Pallas kernels, second_pass(): call(second_kernel, 'second_pass', [SMEM] + [VS] * (7 + HELD), resident +...  23.4 us
    pallas_call x1, Pallas kernels, back_pass(): call(back_kernel, 'back_pass', [SMEM] + [VS] * 5 + [HBM] * 2 + [VS] * len...  16.2 us
    pallas_call x1, Pallas kernels, first_pass(): call(first_kernel, 'first_pass', [SMEM] + [VS] * 8 + [HBM] * 4 + [VS] * H...  14.2 us
    pallas_call x5, Pallas kernels, place(): call(kernel, 'place', [SMEM, SMEM] + [VS] * given + [HBM] * len(into), ou...  13.2 us
    pallas_call x14, Pallas kernels, add(): call(kernel, 'add', [SMEM] + [VS] * (2 + count), [out, out] + [VM(PACKED,...  12.6 us
    ppermute x1, waiting for transfers between devices, body(): c_got = lax.ppermute(c_two, 'section', [(2, 0), (3, 1)])  8.74 us
  transfers between devices with their start and end apart: 69, of which 49 were waited for; matrix products, arithmetic and copies ran while one was open for 0% of the time, Pallas kernels for 24%

profile of v4, /device:TPU:0, one launch (start us, length us, event | category | flops | bytes accessed | tf_op | source)
XLA Modules:
  0.0 249.3 jit_solution(10678576586200082759)
XLA Ops:
  1.8 1.9 prepare.1
  3.8 3.0 %collective-permute-start.1 = (bf16[192,384]{1,0:T(8,128)(2,1)S(1)}, bf16[192,384]{1,0:T(8,128)(2,1)S(1)}, u32[]{:S(2)}, u32[]{:S(2)}) collective-permute-start(bf16[192,384]{1,0:T(8,128)(2,1)S(1)} %get-tuple-element.185), channel_id=1, source_target_pairs={{0,16},{8,24},{16,0},{24,8},{1,17},{9,25},{17,1},{25,9},{2,18},{10... | collective-permute-start | bytes 442376 | tf_op jit(solution)/shard_map/ppermute | solution.py:1076
  6.8 1.7 collective-permute-start.3
  8.5 1.7 collective-permute-done.3.voth
  10.8 3.5 %positions.1 = (f32[384,768]{1,0:T(8,128)}, f32[384,768]{1,0:T(8,128)}, f32[384,128]{1,0:T(8,128)}, f32[8,384]{1,0:T(8,128)}) custom-call(s32[3]{0:T(128)} %pad_add_fusion.refs_0_.flags, s32[2,2,2]{2,1,0:T(2,128)} %grid.1, f32[1,5376]{1,0:T(1,128)} %get-tuple-element.187.vown, f32[1,5376]{1,0:T(1,128)} %copy-done.1), custom_call_target="tpu_custom_call" | custom-call | flops 100000000 | bytes 3000000 | tf_op jit(solution)/shard_map/positions/pallas_call | solution.py:845
  15.2 14.2 %first_pass.1 = (bf16[384,768]{1,0:T(8,128)(2,1)S(1)}, bf16[384,768]{1,0:T(8,128)(2,1)}, f32[384,768]{1,0:T(8,128)S(1)}, f32[384,768]{1,0:T(8,128)S(1)}, bf16[4,...) custom-call(s32[3]{0:T(128)} %pad_add_fusion.refs_0_.flags, ...), custom_call_target="tpu_custom_call", output_to_operand_aliasing={{2}: (13, {}), {3}: (14, {}), {4}: (15, {}), {5}: (16, {}),... | custom-call | flops 8000000000 | bytes 20000000 | tf_op jit(solution)/shard_map/first_pass/pallas_call | solution.py:859
  30.0 1.7 collective-permute-start.5
  31.8 7.5 %collective-permute-done.5.got = bf16[384,768]{1,0:T(8,128)(2,1)S(1)} collective-permute-done((bf16[384,768]{1,0:T(8,128)(2,1)S(1)}, bf16[384,768]{1,0:T(8,128)(2,1)S(1)}, u32[]{:S(2)}, u32[]{:S(2)}) %collective-permute-start.5) | collective-permute-done | bytes 589856 | tf_op jit(solution)/shard_map/ppermute | solution.py:1087
  39.3 23.4 %second_pass.1 = (f32[384,768]{1,0:T(8,128)S(1)}, f32[384,768]{1,0:T(8,128)S(1)}, bf16[4,768,768]{2,1,0:T(8,128)(2,1)S(1)}, bf16[4,768,768]{2,1,0:T(8,128)(2,1)S...) custom-call(s32[3]{0:T(128)} %pad_add_fusion.refs_0_.flags, ...), custom_call_target="tpu_custom_call", output_to_operand_aliasing={{0}: (8, {}), {1}: (9, {}), {2}: (10, {}), {3}: (11, {}), {... | custom-call | flops 17999998976 | bytes 20000000 | tf_op jit(solution)/shard_map/second_pass/pallas_call | solution.py:879
  64.0 3.1 %late_pass.1 = (f32[384,768]{1,0:T(8,128)S(1)}, f32[384,768]{1,0:T(8,128)S(1)}, bf16[4,768,768]{2,1,0:T(8,128)(2,1)S(1)}, bf16[4,768,768]{2,1,0:T(8,128)(2,1)S(1...) custom-call(s32[3]{0:T(128)} %pad_add_fusion.refs_0_.flags, ...), custom_call_target="tpu_custom_call", output_to_operand_aliasing={{0}: (6, {}), {1}: (7, {}), {2}: (8, {}), {3}: (9, {}), {4}... | custom-call | flops 2000000000 | bytes 5000000 | tf_op jit(solution)/shard_map/late_pass/pallas_call | solution.py:892
  67.0 8.7 %collective-permute-done.7.got = bf16[384,768]{1,0:T(8,128)(2,1)S(1)} collective-permute-done((bf16[384,768]{1,0:T(8,128)(2,1)S(1)}, bf16[384,768]{1,0:T(8,128)(2,1)S(1)}, u32[]{:S(2)}, u32[]{:S(2)}) %collective-permute-start.7) | collective-permute-done | bytes 589856 | tf_op jit(solution)/shard_map/ppermute | solution.py:1092
  75.8 4.8 %collective-permute-start.10 = (bf16[384,3840]{1,0:T(8,128)(2,1)S(1)}, bf16[384,3840]{1,0:T(8,128)(2,1)S(1)}, u32[]{:S(2)}, u32[]{:S(2)}) collective-permute-start(bf16[384,3840]{1,0:T(8,128)(2,1)S(1)} %copy-done.2), channel_id=1, source_target_pairs={{0,8},{8,0},{16,24},{24,16},{1,9},{9,1},{17,25},{25,17},{2,10},{10... | collective-permute-start | bytes 8847368 | tf_op jit(solution)/shard_map/ppermute | solution.py:974
  81.1 16.2 %back_pass.1 = (bf16[384,768]{1,0:T(8,128)(2,1)S(1)}, bf16[384,768]{1,0:T(8,128)(2,1)S(1)}, bf16[384,768]{1,0:T(8,128)(2,1)S(1)}, f32[48,128]{1,0:T(8,128)S(1)},...) custom-call(s32[3]{0:T(128)} %pad_add_fusion.refs_0_.flags, bf16[384,768]{1,0:T(8,128)(2,1)} %get-tuple-element.197.field, ...), custom_call_target="tpu_custom_call" | custom-call | flops 10000000000 | bytes 15000000 | tf_op jit(solution)/shard_map/back_pass/pallas_call | solution.py:901
  97.4 5.8 %gram_down.1 = (bf16[768,1536]{1,0:T(8,128)(2,1)S(1)}, bf16[768,768]{1,0:T(8,128)(2,1)S(1)}, bf16[768,768]{1,0:T(8,128)(2,1)S(1)}, bf16[768,3072]{1,0:T(8,128)(2...) custom-call(s32[3]{0:T(128)} %pad_add_fusion.refs_0_.flags, ...), custom_call_target="tpu_custom_call" | custom-call | flops 2000000000 | bytes 8000000 | tf_op jit(solution)/shard_map/gram_down/pallas_call | solution.py:914
  103.2 1.9 gram_head.1
  107.2 3.8 %gram_main.1 = (bf16[768,3072]{1,0:T(8,128)(2,1)S(1)}, bf16[768,2304]{1,0:T(8,128)(2,1)S(1)}, bf16[48,2432]{1,0:T(8,128)(2,1)S(1)}, bf16[48,2432]{1,0:T(8,128)(2,1)S(1)}) custom-call(s32[16,4]{1,0:T(8,128)} %get-tuple-element.243.rows.refs_0_.refs_1_, bf16[400,3072]{1,0:T(8,128)(2,1)S(1)} %collective-permute-done.11.right1, ...), custom_call_target="tpu_custom_call", output_to_operand_aliasing={{0}: (4, {})} | custom-call | flops 6000000000 | bytes 12000000 | tf_op jit(solution)/shard_map/gram_main/pallas_call | solution.py:932
  117.0 2.6 %collective-permute-done.12.refs_1_ = bf16[48,2432]{1,0:T(8,128)(2,1)S(1)} collective-permute-done((bf16[48,2432]{1,0:T(8,128)(2,1)S(1)}, bf16[48,2432]{1,0:T(8,128)(2,1)S(1)}, u32[]{:S(2)}, u32[]{:S(2)}) %collective-permute-start.12) | collective-permute-done | bytes 233504 | tf_op jit(solution)/shard_map/ppermute | solution.py:1002
  131.2 1.7 collective-permute-start.20
  133.3 1.6 collective-permute-done.22.refs_1_
  140.0 1.7 collective-permute-done.21.refs_2_
  170.0 1.8 collective-permute-done.33.refs_2_
  182.7 3.0 %collective-permute-done.42.refs_7_ = bf16[48,2304]{1,0:T(8,128)(2,1)S(1)} collective-permute-done((bf16[48,2304]{1,0:T(8,128)(2,1)S(1)}, bf16[48,2304]{1,0:T(8,128)(2,1)S(1)}, u32[]{:S(2)}, u32[]{:S(2)}) %collective-permute-start.42) | collective-permute-done | bytes 221216 | tf_op jit(solution)/shard_map/ppermute | solution.py:1002
  193.9 3.0 %place.5 = (f32[768,4608]{1,0:T(8,128)}, bf16[768,768]{1,0:T(8,128)(2,1)}) custom-call(s32[3]{0:T(128)} %pad_add_fusion.refs_0_.flags, s32[16,4]{1,0:T(8,128)} %get-tuple-element.243.rows.refs_0_.refs_1_, bf16[48,2304]{1,0:T(8,128)(2,1)S(1)} %get-tuple-element.312.refs_2_, bf16[48,2304]{1,0:T(8,128)(2,1)S(1)} %get-tuple-element.308.refs_3_, ...), custom_call_target="tpu_custom_call" | custom-call | flops 1000 | bytes 20000000 | tf_op jit(solution)/shard_map/place/pallas_call | solution.py:965
  203.6 1.8 collective-permute-done.51.refs_7_
  213.5 3.3 %place.6 = (f32[768,4608]{1,0:T(8,128)}, f32[1,768]{1,0:T(1,128)}, f32[1,768]{1,0:T(1,128)}, f32[1,3072]{1,0:T(1,128)}, f32[1,768]{1,0:T(1,128)}) custom-call(s32[3]{0:T(128)} %pad_add_fusion.refs_0_.flags, s32[16,4]{1,0:T(8,128)} %get-tuple-element.243.rows.refs_0_.refs_1_, ...), custom_call_target="tpu_custom_call", output_to_operand_aliasing={{0}: (18, {})} | custom-call | flops 1000 | bytes 20000000 | tf_op jit(solution)/shard_map/place/pallas_call | solution.py:965
  223.0 2.3 collective-permute-done.59.refs_7_
  227.7 2.3 collective-permute-done.57.refs_6_
  232.5 2.7 %place.7.refs_6_ = f32[768,4608]{1,0:T(8,128)} custom-call(s32[3]{0:T(128)} %pad_add_fusion.refs_0_.flags, s32[16,4]{1,0:T(8,128)} %get-tuple-element.243.rows.refs_0_.refs_1_, bf16[48,2304]{1,0:T(8,128)(2,1)S(1)} %collective-permute-done.53.refs_2_, bf16[48,2304]{1,0:T(8,128)(2,1)S(1)} %collective-permute-done.55.refs_3_, ...), custom_call_target="tpu_custom_call", output_to_operand_aliasing={{}: (10, {})} | custom-call | flops 1000 | bytes 20000000 | tf_op jit(solution)/shard_map/place/pallas_call | solution.py:965
  237.3 2.2 collective-permute-done.61.refs_2_
  241.9 2.1 place.8.refs_6_
  244.1 1.8 collective-permute-done.65.refs_2_
  247.0 2.1 place.9
  (144 shorter events, 109.3 us)
Async XLA Ops:
  0.6 13.7 %collective-permute-start.4 = (bf16[768,4608]{1,0:T(8,128)(2,1)}, bf16[768,4608]{1,0:T(8,128)(2,1)}, u32[]{:S(2)}, u32[]{:S(2)}) collective-permute-start(bf16[768,4608]{1,0:T(8,128)(2,1)} %bitcast.10), channel_id=1, source_target_pairs={{0,8},{8,0},{16,24},{24,16},{1,9},{9,1},{17,25},{25,17},{2,10},{10... | collective-permute-start | bytes 21233672 | tf_op jit(solution)/shard_map/ppermute | solution.py:974
  3.7 11.5 %collective-permute-start = (bf16[192,384]{1,0:T(8,128)(2,1)S(1)}, bf16[192,384]{1,0:T(8,128)(2,1)S(1)}, u32[]{:S(2)}, u32[]{:S(2)}) collective-permute-start(bf16[192,384]{1,0:T(8,128)(2,1)S(1)} %get-tuple-element.184), channel_id=1, source_target_pairs={{0,8},{8,0},{16,24},{24,16},{1,9},{9,1},{17,25},{25,17},{2,10},{10... | collective-permute-start | bytes 442376 | tf_op jit(solution)/shard_map/ppermute | solution.py:974
  3.8 11.3 %collective-permute-start.1 = (bf16[192,384]{1,0:T(8,128)(2,1)S(1)}, bf16[192,384]{1,0:T(8,128)(2,1)S(1)}, u32[]{:S(2)}, u32[]{:S(2)}) collective-permute-start(bf16[192,384]{1,0:T(8,128)(2,1)S(1)} %get-tuple-element.185), channel_id=1, source_target_pairs={{0,16},{8,24},{16,0},{24,8},{1,17},{9,25},{17,1},{25,9},{2,18},{10... | collective-permute-start | bytes 442376 | tf_op jit(solution)/shard_map/ppermute | solution.py:1076
  30.0 9.2 %collective-permute-start.5 = (bf16[384,768]{1,0:T(8,128)(2,1)S(1)}, bf16[384,768]{1,0:T(8,128)(2,1)S(1)}, u32[]{:S(2)}, u32[]{:S(2)}) collective-permute-start(bf16[384,768]{1,0:T(8,128)(2,1)S(1)} %get-tuple-element.198.x_two), channel_id=1, source_target_pairs={{0,16},{1,17},{2,18},{3,19},{4,20},{5,21},{6,22},{7,23}} | collective-permute-start | bytes 1769480 | tf_op jit(solution)/shard_map/ppermute | solution.py:1087
  62.7 13.1 %collective-permute-start.7 = (bf16[384,768]{1,0:T(8,128)(2,1)S(1)}, bf16[384,768]{1,0:T(8,128)(2,1)S(1)}, u32[]{:S(2)}, u32[]{:S(2)}) collective-permute-start(bf16[384,768]{1,0:T(8,128)(2,1)S(1)} %get-tuple-element.204), channel_id=1, source_target_pairs={{16,0},{24,8},{17,1},{25,9},{18,2},{26,10},{19,3},{27,11},{20,4},{... | collective-permute-start | bytes 1769480 | tf_op jit(solution)/shard_map/ppermute | solution.py:1092
  75.8 21.5 %collective-permute-start.10 = (bf16[384,3840]{1,0:T(8,128)(2,1)S(1)}, bf16[384,3840]{1,0:T(8,128)(2,1)S(1)}, u32[]{:S(2)}, u32[]{:S(2)}) collective-permute-start(bf16[384,3840]{1,0:T(8,128)(2,1)S(1)} %copy-done.2), channel_id=1, source_target_pairs={{0,8},{8,0},{16,24},{24,16},{1,9},{9,1},{17,25},{25,17},{2,10},{10... | collective-permute-start | bytes 8847368 | tf_op jit(solution)/shard_map/ppermute | solution.py:974
  80.6 16.7 %collective-permute-start.8 = (bf16[384,768]{1,0:T(8,128)(2,1)S(1)}, bf16[384,768]{1,0:T(8,128)(2,1)S(1)}, u32[]{:S(2)}, u32[]{:S(2)}) collective-permute-start(bf16[384,768]{1,0:T(8,128)(2,1)S(1)} %collective-permute-done.7.got), channel_id=1, source_target_pairs={{0,8},{8,0},{16,24},{24,16},{1,9},{9,1},{17,25},{25,17},{2,10},{10... | collective-permute-start | bytes 1769480 | tf_op jit(solution)/shard_map/ppermute | solution.py:974
  80.6 16.7 %collective-permute-start.9 = (bf16[384,768]{1,0:T(8,128)(2,1)S(1)}, bf16[384,768]{1,0:T(8,128)(2,1)S(1)}, u32[]{:S(2)}, u32[]{:S(2)}) collective-permute-start(bf16[384,768]{1,0:T(8,128)(2,1)S(1)} %get-tuple-element.233), channel_id=1, source_target_pairs={{0,8},{8,0},{16,24},{24,16},{1,9},{9,1},{17,25},{25,17},{2,10},{10... | collective-permute-start | bytes 1769480 | tf_op jit(solution)/shard_map/ppermute | solution.py:974
  111.0 8.6 %collective-permute-start.12 = (bf16[48,2432]{1,0:T(8,128)(2,1)S(1)}, bf16[48,2432]{1,0:T(8,128)(2,1)S(1)}, u32[]{:S(2)}, u32[]{:S(2)}) collective-permute-start(bf16[48,2432]{1,0:T(8,128)(2,1)S(1)} %get-tuple-element.252), channel_id=1, source_target_pairs={{0,2},{2,4},{4,6},{6,7},{7,5},{5,3},{3,1},{1,0},{8,10},{10,12},{12... | collective-permute-start | bytes 700424 | tf_op jit(solution)/shard_map/ppermute | solution.py:1002
  114.9 9.6 %collective-permute-start.18 = (bf16[48,2432]{1,0:T(8,128)(2,1)S(1)}, bf16[48,2432]{1,0:T(8,128)(2,1)S(1)}, u32[]{:S(2)}, u32[]{:S(2)}) collective-permute-start(bf16[48,2432]{1,0:T(8,128)(2,1)S(1)} %get-tuple-element.259), channel_id=1, source_target_pairs={{0,2},{2,4},{4,6},{6,7},{7,5},{5,3},{3,1},{1,0},{8,10},{10,12},{12... | collective-permute-start | bytes 700424 | tf_op jit(solution)/shard_map/ppermute | solution.py:1002
  116.6 8.8 %collective-permute-start.19 = (bf16[48,2432]{1,0:T(8,128)(2,1)S(1)}, bf16[48,2432]{1,0:T(8,128)(2,1)S(1)}, u32[]{:S(2)}, u32[]{:S(2)}) collective-permute-start(bf16[48,2432]{1,0:T(8,128)(2,1)S(1)} %get-tuple-element.260), channel_id=1, source_target_pairs={{0,1},{2,0},{4,2},{6,4},{7,6},{5,7},{3,5},{1,3},{8,9},{10,8},{12,1... | collective-permute-start | bytes 700424 | tf_op jit(solution)/shard_map/ppermute | solution.py:1002
  121.3 8.7 %collective-permute-start.16 = (bf16[48,2432]{1,0:T(8,128)(2,1)S(1)}, bf16[48,2432]{1,0:T(8,128)(2,1)S(1)}, u32[]{:S(2)}, u32[]{:S(2)}) collective-permute-start(bf16[48,2432]{1,0:T(8,128)(2,1)S(1)} %get-tuple-element.264), channel_id=1, source_target_pairs={{0,2},{2,4},{4,6},{6,7},{7,5},{5,3},{3,1},{1,0},{8,10},{10,12},{12... | collective-permute-start | bytes 700424 | tf_op jit(solution)/shard_map/ppermute | solution.py:1002
  126.3 8.7 %collective-permute-start.22 = (bf16[48,2432]{1,0:T(8,128)(2,1)S(1)}, bf16[48,2432]{1,0:T(8,128)(2,1)S(1)}, u32[]{:S(2)}, u32[]{:S(2)}) collective-permute-start(bf16[48,2432]{1,0:T(8,128)(2,1)S(1)} %get-tuple-element.268), channel_id=1, source_target_pairs={{0,2},{2,4},{4,6},{6,7},{7,5},{5,3},{3,1},{1,0},{8,10},{10,12},{12... | collective-permute-start | bytes 700424 | tf_op jit(solution)/shard_map/ppermute | solution.py:1002
  127.9 8.6 %collective-permute-start.23 = (bf16[48,2432]{1,0:T(8,128)(2,1)S(1)}, bf16[48,2432]{1,0:T(8,128)(2,1)S(1)}, u32[]{:S(2)}, u32[]{:S(2)}) collective-permute-start(bf16[48,2432]{1,0:T(8,128)(2,1)S(1)} %get-tuple-element.269), channel_id=1, source_target_pairs={{0,1},{2,0},{4,2},{6,4},{7,6},{5,7},{3,5},{1,3},{8,9},{10,8},{12,1... | collective-permute-start | bytes 700424 | tf_op jit(solution)/shard_map/ppermute | solution.py:1002
  131.2 8.7 %collective-permute-start.20 = (bf16[48,2432]{1,0:T(8,128)(2,1)S(1)}, bf16[48,2432]{1,0:T(8,128)(2,1)S(1)}, u32[]{:S(2)}, u32[]{:S(2)}) collective-permute-start(bf16[48,2432]{1,0:T(8,128)(2,1)S(1)} %get-tuple-element.272), channel_id=1, source_target_pairs={{0,2},{2,4},{4,6},{6,7},{7,5},{5,3},{3,1},{1,0},{8,10},{10,12},{12... | collective-permute-start | bytes 700424 | tf_op jit(solution)/shard_map/ppermute | solution.py:1002
  133.0 8.6 %collective-permute-start.21 = (bf16[48,2432]{1,0:T(8,128)(2,1)S(1)}, bf16[48,2432]{1,0:T(8,128)(2,1)S(1)}, u32[]{:S(2)}, u32[]{:S(2)}) collective-permute-start(bf16[48,2432]{1,0:T(8,128)(2,1)S(1)} %get-tuple-element.273), channel_id=1, source_target_pairs={{0,1},{2,0},{4,2},{6,4},{7,6},{5,7},{3,5},{1,3},{8,9},{10,8},{12,1... | collective-permute-start | bytes 700424 | tf_op jit(solution)/shard_map/ppermute | solution.py:1002
  137.4 8.7 %collective-permute-start.26 = (bf16[48,2432]{1,0:T(8,128)(2,1)S(1)}, bf16[48,2432]{1,0:T(8,128)(2,1)S(1)}, u32[]{:S(2)}, u32[]{:S(2)}) collective-permute-start(bf16[48,2432]{1,0:T(8,128)(2,1)S(1)} %get-tuple-element.276), channel_id=1, source_target_pairs={{0,2},{2,4},{4,6},{6,7},{7,5},{5,3},{3,1},{1,0},{8,10},{10,12},{12... | collective-permute-start | bytes 700424 | tf_op jit(solution)/shard_map/ppermute | solution.py:1002
  142.5 8.7 %collective-permute-start.24 = (bf16[48,2432]{1,0:T(8,128)(2,1)S(1)}, bf16[48,2432]{1,0:T(8,128)(2,1)S(1)}, u32[]{:S(2)}, u32[]{:S(2)}) collective-permute-start(bf16[48,2432]{1,0:T(8,128)(2,1)S(1)} %get-tuple-element.280), channel_id=1, source_target_pairs={{0,2},{2,4},{4,6},{6,7},{7,5},{5,3},{3,1},{1,0},{8,10},{10,12},{12... | collective-permute-start | bytes 700424 | tf_op jit(solution)/shard_map/ppermute | solution.py:1002
  174.8 19.1 %collective-permute-start.44 = (bf16[384,768]{1,0:T(8,128)(2,1)S(1)}, bf16[384,768]{1,0:T(8,128)(2,1)S(1)}, u32[]{:S(2)}, u32[]{:S(2)}) collective-permute-start(bf16[384,768]{1,0:T(8,128)(2,1)S(1)} %copy-done.3), channel_id=1, source_target_pairs={{0,8},{8,0},{16,24},{24,16},{1,9},{9,1},{17,25},{25,17},{2,10},{10... | collective-permute-start | bytes 1769480 | tf_op jit(solution)/shard_map/ppermute | solution.py:974
  180.6 9.9 %collective-permute-start.40 = (bf16[48,2304]{1,0:T(8,128)(2,1)S(1)}, bf16[48,2304]{1,0:T(8,128)(2,1)S(1)}, u32[]{:S(2)}, u32[]{:S(2)}) collective-permute-start(bf16[48,2304]{1,0:T(8,128)(2,1)S(1)} %get-tuple-element.312.refs_2_), channel_id=1, source_target_pairs={{0,2},{2,4},{4,6},{6,7},{7,5},{5,3},{3,1},{1,0},{8,10},{10,12},{12... | collective-permute-start | bytes 663560 | tf_op jit(solution)/shard_map/ppermute | solution.py:1002
  182.1 9.5 %collective-permute-start.41 = (bf16[48,2304]{1,0:T(8,128)(2,1)S(1)}, bf16[48,2304]{1,0:T(8,128)(2,1)S(1)}, u32[]{:S(2)}, u32[]{:S(2)}) collective-permute-start(bf16[48,2304]{1,0:T(8,128)(2,1)S(1)} %get-tuple-element.313.refs_4_), channel_id=1, source_target_pairs={{0,1},{2,0},{4,2},{6,4},{7,6},{5,7},{3,5},{1,3},{8,9},{10,8},{12,1... | collective-permute-start | bytes 663560 | tf_op jit(solution)/shard_map/ppermute | solution.py:1002
  186.9 10.1 %collective-permute-start.47 = (bf16[48,2304]{1,0:T(8,128)(2,1)S(1)}, bf16[48,2304]{1,0:T(8,128)(2,1)S(1)}, u32[]{:S(2)}, u32[]{:S(2)}) collective-permute-start(bf16[48,2304]{1,0:T(8,128)(2,1)S(1)} %collective-permute-done.42.refs_7_), channel_id=1, source_target_pairs={{0,2},{2,4},{4,6},{6,7},{7,5},{5,3},{3,1},{1,0},{8,10},{10,12},{12... | collective-permute-start | bytes 663560 | tf_op jit(solution)/shard_map/ppermute | solution.py:1002
  188.2 8.7 %collective-permute-start.48 = (bf16[48,2304]{1,0:T(8,128)(2,1)S(1)}, bf16[48,2304]{1,0:T(8,128)(2,1)S(1)}, u32[]{:S(2)}, u32[]{:S(2)}) collective-permute-start(bf16[48,2304]{1,0:T(8,128)(2,1)S(1)} %collective-permute-done.43.refs_9_), channel_id=1, source_target_pairs={{0,1},{2,0},{4,2},{6,4},{7,6},{5,7},{3,5},{1,3},{8,9},{10,8},{12,1... | collective-permute-start | bytes 663560 | tf_op jit(solution)/shard_map/ppermute | solution.py:1002
  191.6 8.6 %collective-permute-start.45 = (bf16[48,2304]{1,0:T(8,128)(2,1)S(1)}, bf16[48,2304]{1,0:T(8,128)(2,1)S(1)}, u32[]{:S(2)}, u32[]{:S(2)}) collective-permute-start(bf16[48,2304]{1,0:T(8,128)(2,1)S(1)} %collective-permute-done.40.refs_6_), channel_id=1, source_target_pairs={{0,2},{2,4},{4,6},{6,7},{7,5},{5,3},{3,1},{1,0},{8,10},{10,12},{12... | collective-permute-start | bytes 663560 | tf_op jit(solution)/shard_map/ppermute | solution.py:1002
  201.6 8.5 %collective-permute-start.49 = (bf16[48,2304]{1,0:T(8,128)(2,1)S(1)}, bf16[48,2304]{1,0:T(8,128)(2,1)S(1)}, u32[]{:S(2)}, u32[]{:S(2)}) collective-permute-start(bf16[48,2304]{1,0:T(8,128)(2,1)S(1)} %collective-permute-done.45.refs_2_), channel_id=1, source_target_pairs={{0,2},{2,4},{4,6},{6,7},{7,5},{5,3},{3,1},{1,0},{8,10},{10,12},{12... | collective-permute-start | bytes 663560 | tf_op jit(solution)/shard_map/ppermute | solution.py:1002
  202.8 8.7 %collective-permute-start.50 = (bf16[48,2304]{1,0:T(8,128)(2,1)S(1)}, bf16[48,2304]{1,0:T(8,128)(2,1)S(1)}, u32[]{:S(2)}, u32[]{:S(2)}) collective-permute-start(bf16[48,2304]{1,0:T(8,128)(2,1)S(1)} %collective-permute-done.46.refs_4_), channel_id=1, source_target_pairs={{0,1},{2,0},{4,2},{6,4},{7,6},{5,7},{3,5},{1,3},{8,9},{10,8},{12,1... | collective-permute-start | bytes 663560 | tf_op jit(solution)/shard_map/ppermute | solution.py:1002
  206.7 10.1 %collective-permute-start.55 = (bf16[48,2304]{1,0:T(8,128)(2,1)S(1)}, bf16[48,2304]{1,0:T(8,128)(2,1)S(1)}, u32[]{:S(2)}, u32[]{:S(2)}) collective-permute-start(bf16[48,2304]{1,0:T(8,128)(2,1)S(1)} %collective-permute-done.51.refs_7_), channel_id=1, source_target_pairs={{0,2},{2,4},{4,6},{6,7},{7,5},{5,3},{3,1},{1,0},{8,10},{10,12},{12... | collective-permute-start | bytes 663560 | tf_op jit(solution)/shard_map/ppermute | solution.py:1002
  207.8 9.0 %collective-permute-start.56 = (bf16[48,2304]{1,0:T(8,128)(2,1)S(1)}, bf16[48,2304]{1,0:T(8,128)(2,1)S(1)}, u32[]{:S(2)}, u32[]{:S(2)}) collective-permute-start(bf16[48,2304]{1,0:T(8,128)(2,1)S(1)} %collective-permute-done.52.refs_9_), channel_id=1, source_target_pairs={{0,1},{2,0},{4,2},{6,4},{7,6},{5,7},{3,5},{1,3},{8,9},{10,8},{12,1... | collective-permute-start | bytes 663560 | tf_op jit(solution)/shard_map/ppermute | solution.py:1002
  220.9 9.0 %collective-permute-start.57 = (bf16[48,2304]{1,0:T(8,128)(2,1)S(1)}, bf16[48,2304]{1,0:T(8,128)(2,1)S(1)}, u32[]{:S(2)}, u32[]{:S(2)}) collective-permute-start(bf16[48,2304]{1,0:T(8,128)(2,1)S(1)} %collective-permute-done.53.refs_2_), channel_id=1, source_target_pairs={{0,2},{2,4},{4,6},{6,7},{7,5},{5,3},{3,1},{1,0},{8,10},{10,12},{12... | collective-permute-start | bytes 663560 | tf_op jit(solution)/shard_map/ppermute | solution.py:1002
  225.7 9.5 %collective-permute-start.63 = (bf16[48,2304]{1,0:T(8,128)(2,1)S(1)}, bf16[48,2304]{1,0:T(8,128)(2,1)S(1)}, u32[]{:S(2)}, u32[]{:S(2)}) collective-permute-start(bf16[48,2304]{1,0:T(8,128)(2,1)S(1)} %collective-permute-done.59.refs_7_), channel_id=1, source_target_pairs={{0,2},{2,4},{4,6},{6,7},{7,5},{5,3},{3,1},{1,0},{8,10},{10,12},{12... | collective-permute-start | bytes 663560 | tf_op jit(solution)/shard_map/ppermute | solution.py:1002
  230.4 9.0 %collective-permute-start.61 = (bf16[48,2304]{1,0:T(8,128)(2,1)S(1)}, bf16[48,2304]{1,0:T(8,128)(2,1)S(1)}, u32[]{:S(2)}, u32[]{:S(2)}) collective-permute-start(bf16[48,2304]{1,0:T(8,128)(2,1)S(1)} %collective-permute-done.57.refs_6_), channel_id=1, source_target_pairs={{0,2},{2,4},{4,6},{6,7},{7,5},{5,3},{3,1},{1,0},{8,10},{10,12},{12... | collective-permute-start | bytes 663560 | tf_op jit(solution)/shard_map/ppermute | solution.py:1002
  235.2 8.9 %collective-permute-start.67 = (bf16[48,2304]{1,0:T(8,128)(2,1)S(1)}, bf16[48,2304]{1,0:T(8,128)(2,1)S(1)}, u32[]{:S(2)}, u32[]{:S(2)}) collective-permute-start(bf16[48,2304]{1,0:T(8,128)(2,1)S(1)} %collective-permute-done.63.refs_3_), channel_id=1, source_target_pairs={{0,2},{2,4},{4,6},{6,7},{7,5},{5,3},{3,1},{1,0},{8,10},{10,12},{12... | collective-permute-start | bytes 663560 | tf_op jit(solution)/shard_map/ppermute | solution.py:1002
  (41 other events, 315.3 us)

commit v5 on v4

--- a/solution.py
+++ b/solution.py
@@ -106,35 +106,38 @@
 
 
 class Forward:
-    def __init__(self, when, core, own, oth, wa, w1, wd, cos_in, sin_in, cosf, sinf, sems):
+    def __init__(self, on_the_way, core, own, oth, wa, w1, wd, sems):
         self.attn = core, own, oth, wa, sems
         self.mlp = core, own, oth, w1, wd, sems.at[pl.ds(4, 8)]
-        self.angles = cos_in, sin_in, cosf, sinf, sems.at[pl.ds(12, 2)]
-        self.own, self.wa, self.sems, self.when = own, wa, sems, when
-
-        @pl.when(when)
+        self.own, self.wa, self.sems, self.on_the_way = own, wa, sems, on_the_way
+
+        @pl.when(on_the_way)
         def _():
             load_attn(*self.attn, 0)
-            load_angles(*self.angles)
             load_attn(*self.attn, 1)
 
-    def wait(self, what):
-        @pl.when(self.when)
+        @pl.when(jnp.logical_not(on_the_way))
         def _():
-            if what == "angles":
-                wait_angles(*self.angles)
-                return
-            wait_attn(self.own, self.wa, self.sems, what)
-            if what < 2:
-                load_attn(*self.attn, what + 2)
-            elif what == 2:
+            for i in range(4):
+                load_attn(*self.attn, i)
+                load_mlp(*self.mlp, i)
+                wait_attn(own, wa, sems, i)
+                wait_mlp(own, w1, wd, self.mlp[-1], i)
+
+    def wait(self, i):
+        @pl.when(self.on_the_way)
+        def _():
+            wait_attn(self.own, self.wa, self.sems, i)
+            if i < 2:
+                load_attn(*self.attn, i + 2)
+            elif i == 2:
                 for j in range(4):
                     load_mlp(*self.mlp, j)
 
     def wait_mlp(self):
         core, own, oth, w1, wd, sems = self.mlp
 
-        @pl.when(self.when)
+        @pl.when(self.on_the_way)
         def _():
             for j in range(4):
                 wait_mlp(own, w1, wd, sems, j)
@@ -158,8 +161,6 @@
     for i in range(3):
         wait(i)
         part = dot(n, wa[i]) + vec[:, FIRST + D * i : FIRST + D * (i + 1)]
-        if i == 0:
-            wait("angles")
         if i < 2:
             part = part * cosf[...] + swap_halves(part) * sinf[...]
         if i == 0:
@@ -340,24 +341,15 @@
     vec[:, SECOND:] = second[...]
 
 
-def load_angles(cos_in, sin_in, cosf, sinf, sems):
-    load(cos_in, cosf, sems.at[0])
-    load(sin_in, sinf, sems.at[1])
-
-
-def wait_angles(cos_in, sin_in, cosf, sinf, sems):
-    arrived(cos_in, cosf, sems.at[0])
-    arrived(sin_in, sinf, sems.at[1])
-
-
 HELD = 5
 
 
 def first_kernel(
-    flags, keep, got, away, across, vown, voth, pos, segr, cos_in, sin_in, own, oth, *refs,
+    flags, keep, got, away, across, vown, voth, pos, segr, own, oth, cos_in, sin_in,
+    out, field_out, cosf, sinf, wa, w1, wd, field, turned, qkv, pt, rec, ml, mlt, vt, n_ref, sems,
 ):
-    out, field_out, cosf, sinf, wa, w1, wd, field, turned, qkv, pt, rec, ml, mlt, vt, n_ref, sems = refs[HELD:]
     core, layer = flags[0], flags[1]
+    loads = Forward((core == 0) & (layer == 0), core, own, oth, wa, w1, wd, sems)
     w = keep.shape[0]
     for k in range(2):
         for at in range(2):
@@ -369,11 +361,10 @@
                     turned[w * s : w * (s + 1), :] = parts[s // 2, s % 2][...]
 
     field[...] = turned[...].T
-    keeping = pltpu.make_async_copy(field, field_out, sems.at[14])
+    keeping = pltpu.make_async_copy(field, field_out, sems.at[12])
     keeping.start()
     @pl.when(layer == 0)
     def _():
-        loads = Forward(core == 0, core, own, oth, wa, w1, wd, cos_in, sin_in, cosf, sinf, sems)
         va, vm = vectors(core, vown, voth)
         x_mid, _, _ = attention(
             field[...].astype(F32), va, wa, loads.wait, cosf, sinf, pos[:, 2:3], segr[0:1, :],
@@ -399,22 +390,6 @@
 def hidden_bias(core, vm):
     a, b = vm[:, FIRST : FIRST + FF // 2], vm[:, FIRST + FF // 2 : SECOND]
     return jnp.concatenate([jnp.where(core == 0, a, b), jnp.where(core == 0, b, a)], axis=1)
-
-
-def fetch_kernel(flags, cos_in, sin_in, own, oth, cosf, sinf, wa, w1, wd, sems):
-    core = flags[0]
-
-    @pl.when((core != 0) | (flags[1] != 0))
-    def _():
-        for j in range(2):
-            for i in range(2 * j, 2 * j + 2):
-                load_attn(core, own, oth, wa, sems, i)
-                load_mlp(core, own, oth, w1, wd, sems.at[pl.ds(4, 8)], i)
-            for i in range(2 * j, 2 * j + 2):
-                wait_attn(own, wa, sems, i)
-                wait_mlp(own, w1, wd, sems.at[pl.ds(4, 8)], i)
-        load_angles(cos_in, sin_in, cosf, sinf, sems.at[pl.ds(12, 2)])
-        wait_angles(cos_in, sin_in, cosf, sinf, sems.at[pl.ds(12, 2)])
 
 
 def second_kernel(
@@ -687,12 +662,11 @@
         t[:, 3 * D :] = total
 
 
-def gram_main_kernel(rows, right1, left, vec, right_in, right, main, main_up, main_down):
+def gram_main_kernel(rows, right1, left, right_in, right, main, main_up, main_down):
     right[L:, :] = right1[:L, :]
     main[...] = dot(left[...], right[:, : 3 * D]).astype(BF)
     for k, m in enumerate((main_up, main_down)):
-        m[:, : 3 * D] = main[own_rows(rows, 0, k, m.shape[0]), :]
-        m[:, 3 * D :] = vec[...].astype(BF)
+        m[...] = main[own_rows(rows, 0, k, m.shape[0]), :]
 
 
 def own_rows(rows, t, way, r):
@@ -844,26 +818,20 @@
     hbm = pltpu.HBM
     return call(
         positions_kernel, "positions", [SMEM, SMEM, VS, VS],
-        [hbm((L, D), F32), hbm((L, D), F32), hbm((L, 128), F32), hbm((8, L), F32)],
+        [VM((L, D), F32), VM((L, D), F32), hbm((L, 128), F32), hbm((8, L), F32)],
         [], int(1e8), int(3e6), 56,
     )(flags, grid, own, oth)
 
 
-def fetch(flags, *sources):
-    return call(
-        fetch_kernel, "fetch", [SMEM] + [HBM] * 4, ANGLES + ATTN_W + MLP_W, [DMA((14,))], int(1e8), int(17e6), 28
-    )(flags, *sources)
-
-
-def first_pass(held, *a):
+def first_pass(*a):
     results = call(
-        first_kernel, "first_pass", [SMEM] + [VS] * 8 + [HBM] * 4 + [VS] * HELD,
+        first_kernel, "first_pass", [SMEM] + [VS] * 8 + [HBM] * 2 + [VS] * 2,
         [row(), row_out()] + ANGLES + ATTN_W + MLP_W,
         [row(), VM((D, L), BF), row(3 * D), VM((HEADS, L, L), BF), VM((16, L), F32), row(), VM((D, L), BF),
-         VM((D, L), BF), row(), DMA((15,))],
-        int(8e9), int(20e6), 28, out_specs=[VS, HBM] + [VS] * HELD,
-        aliases={len(a) + k: 2 + k for k in range(HELD)},
-    )(*a, *(in_vmem(x) for x in held))
+         VM((D, L), BF), row(), DMA((13,))],
+        int(8e9), int(20e6), 26, out_specs=[VS, HBM] + [VS] * HELD,
+        aliases={len(a) - 2: 2, len(a) - 1: 3},
+    )(*a)
     return results[0], results[1], results[2:]
 
 
@@ -881,7 +849,7 @@
         resident + [row(FF // 2), row(FF // 2), row()] + outs,
         HEAD_S + [row(), row(), VM((D, L), BF), VM((D, L), BF), VM((L, D), F32), VM((L, D), F32)]
         + BACK_S + [row(3 * D), DMA((9,))],
-        int(18e9), int(20e6), 28, out_specs=[VS] * (len(resident) + 3) + [HBM] * len(outs),
+        int(18e9), int(20e6), 26, out_specs=[VS] * (len(resident) + 3) + [HBM] * len(outs),
         aliases={len(a) + k: k for k in range(HELD)},
     )(*a, *(in_vmem(x) for x in held))
     n = len(resident)
@@ -891,7 +859,7 @@
 def late_pass(held, *a):
     results = call(
         late_kernel, "late_pass", [SMEM] + [VS] * (len(a) - 1 + len(held)),
-        ANGLES + ATTN_W + MLP_W + SAVED + [sds((L, D))] * 2, [], int(2e9), int(5e6), 28,
+        ANGLES + ATTN_W + MLP_W + SAVED + [sds((L, D))] * 2, [], int(2e9), int(5e6), 26,
         aliases={len(a) + k: k for k in range(len(held))},
     )(*a, *(in_vmem(x) for x in held))
     return results[: len(held)], results[len(held) :]
@@ -905,7 +873,7 @@
         + [row(FF), row(FF), VM((1, FIRST + 6 * D), F32), VM((1, VECTOR), F32), VM((1, VECTOR), F32),
            VM((16, D), BF)]
         + BACK_S + [DMA((5,))],
-        int(10e9), int(15e6), 28, out_specs=[VS] * 4 + [HBM] * 2,
+        int(10e9), int(15e6), 26, out_specs=[VS] * 4 + [HBM] * 2,
     )(*a, *(in_vmem(x) for x in held))
 
 
@@ -928,10 +896,10 @@
 
 
 def gram_main(rows, r, *a):
-    wide = VM((r, 3 * D + 128), BF)
+    shard = VM((r, 3 * D), BF)
     return call(
-        gram_main_kernel, "gram_main", [SMEM] + [VS] * 4,
-        [VM((2 * L, FF), BF), VM((D, 3 * D), BF), wide, wide], [], int(6e9), int(12e6), 20, aliases={4: 0},
+        gram_main_kernel, "gram_main", [SMEM] + [VS] * 3,
+        [VM((2 * L, FF), BF), VM((D, 3 * D), BF), shard, shard], [], int(6e9), int(12e6), 20, aliases={3: 0},
     )(rows, *a)[1:]
 
 
@@ -1005,7 +973,7 @@
         if self.t < c.n:
             t = self.t
             ways = int(t <= c.n // 2) + int(t <= (c.n - 1) // 2) if self.carries else 0
-            self.cur, came = add(t, c.rows, *got, self.parts, ways, t < c.n // 2)
+            self.cur, came = add(t, c.rows, *got, self.parts, ways, self.carries and t < c.n // 2)
             self.vectors += came
         else:
             self.cur = got
@@ -1040,7 +1008,7 @@
                     shards += [main.shards[k][way], tail.shards[k][way]]
             now, then = placed == 0, "vectors" not in results and whole >= min(4, n)
             total, *more = place(
-                flags, spots, cycle.rows, shards, total, pair if now else (), [vector] + main.vectors if then else ()
+                flags, spots, cycle.rows, shards, total, pair if now else (), [vector] + tail.vectors if then else ()
             )
             if now:
                 results["rows"] = more[0]
@@ -1071,17 +1039,16 @@
     else:
         voth = core_swap(vown)
     r = D // (2 * n) if small_ring() else PACKED[0]
-    vown, voth, rows = in_hbm(vown), in_hbm(voth), in_hbm(rows)
+    cosf, sinf, pos, segr = positions(flags, grid_sizes, in_hbm(vown), voth)
+    vown, voth, rows, pos, segr = (in_hbm(a) for a in (vown, voth, rows, pos, segr))
     got = core_swap(send)
     away = lax.ppermute(away, "section", [(0, 2), (1, 3), (2, 0), (3, 1)])
     across = lax.ppermute(across, "section", [(0, 3), (1, 2), (2, 1), (3, 0)])
     own = in_hbm(section_weight[0])
     oth = in_hbm(core_swap(section_weight[0]))
-    cosf, sinf, pos, segr = (in_hbm(a) for a in positions(flags, grid_sizes, vown, voth))
-
-    held = fetch(flags, cosf, sinf, own, oth)
+
     x_two, field, held = first_pass(
-        held, flags, keep, got, away, across, vown, voth, pos, segr, cosf, sinf, own, oth
+        flags, keep, got, away, across, vown, voth, pos, segr, own, oth, in_vmem(cosf), in_vmem(sinf)
     )
     field = in_hbm(field)
     x_got, x_late = (lax.ppermute(x_two, "section", [pair]) for pair in ((0, 2), (1, 3)))
@@ -1106,12 +1073,12 @@
     head, *tail_first, vec = gram_head(rows, r, right_oth, down, left_tail, vec, right)
     if small_ring():
         cycle = Cycle(rows)
-        tail = Chain(cycle, [head, down], tail_first)
+        tail = Chain(cycle, [head, down], tail_first, True)
     else:
         tail = jnp.concatenate([head, down], axis=1)
-    main, *main_first = gram_main(rows, r, right_oth, left_main, vec, right)
+    main, *main_first = gram_main(rows, r, right_oth, left_main, right)
     if small_ring():
-        main = Chain(cycle, [main], main_first, True)
+        main = Chain(cycle, [main], main_first)
         token = main.cur
     else:
         token = main

time: 253 us -> 251 us (level)
    pallas_call x4 -> x3, Pallas kernels: 22.2 us -> 19.6 us  [the longest x1 13.2 us: first_pass(): call(first_kernel, 'first_pass', [SMEM] + [VS] * 8 + [HBM] * 2 + [VS] * 2...]
  transfers between devices with their start and end apart: 69 -> 69, of which waited for: 49 -> 48; matrix products, arithmetic and copies ran while one was open for 0% -> 0% of each run, Pallas kernels for 24% -> 23%
where the time goes in v5:
time: 251 us; the launch traced here: 247 us
  Pallas kernels  98.6 us (39%)
  starting transfers between devices  73.3 us (29%)
  waiting for transfers between devices  72.6 us (29%)
    ppermute x56, starting transfers between devices, step(): got = [lax.ppermute(a, 'dp', p) for a, p in zip(self.cur, c.pairs)]  58.1 us
    ppermute x56, waiting for transfers between devices, step(): got = [lax.ppermute(a, 'dp', p) for a, p in zip(self.cur, c.pairs)]  55.9 us
    pallas_call x1, Pallas kernels, second_pass(): call(second_kernel, 'second_pass', [SMEM] + [VS] * (7 + HELD), resident +...  24.1 us
    pallas_call x1, Pallas kernels, back_pass(): call(back_kernel, 'back_pass', [SMEM] + [VS] * 5 + [HBM] * 2 + [VS] * len...  16.6 us
    pallas_call x5, Pallas kernels, place(): call(kernel, 'place', [SMEM, SMEM] + [VS] * given + [HBM] * len(into), ou...  13.2 us
    pallas_call x1, Pallas kernels, first_pass(): call(first_kernel, 'first_pass', [SMEM] + [VS] * 8 + [HBM] * 2 + [VS] * 2...  13.2 us
    pallas_call x14, Pallas kernels, add(): call(kernel, 'add', [SMEM] + [VS] * (2 + count), [out, out] + [VM(PACKED,...  12.5 us
    ppermute x1, waiting for transfers between devices, body(): c_got = lax.ppermute(c_two, 'section', [(2, 0), (3, 1)])  7.95 us
  transfers between devices with their start and end apart: 69, of which 48 were waited for; matrix products, arithmetic and copies ran while one was open for 0% of the time, Pallas kernels for 23%

profile of v5, /device:TPU:0, one launch (start us, length us, event | category | flops | bytes accessed | tf_op | source)
XLA Modules:
  0.0 247.0 jit_solution(5510810145013457446)
XLA Ops:
  1.8 1.9 prepare.1
  3.8 3.0 %collective-permute-start.1 = (bf16[192,384]{1,0:T(8,128)(2,1)S(1)}, bf16[192,384]{1,0:T(8,128)(2,1)S(1)}, u32[]{:S(2)}, u32[]{:S(2)}) collective-permute-start(bf16[192,384]{1,0:T(8,128)(2,1)S(1)} %get-tuple-element.180), channel_id=1, source_target_pairs={{0,16},{8,24},{16,0},{24,8},{1,17},{9,25},{17,1},{25,9},{2,18},{10... | collective-permute-start | bytes 442376 | tf_op jit(solution)/shard_map/ppermute | solution.py:1045
  6.7 1.7 collective-permute-start.3
  8.4 1.7 collective-permute-done.3.voth
  10.8 2.7 %positions.1 = (f32[384,768]{1,0:T(8,128)S(1)}, f32[384,768]{1,0:T(8,128)S(1)}, f32[384,128]{1,0:T(8,128)}, f32[8,384]{1,0:T(8,128)}) custom-call(s32[3]{0:T(128)} %pad_add_fusion.refs_0_.flags, s32[2,2,2]{2,1,0:T(2,128)} %grid.1, f32[1,5376]{1,0:T(1,128)} %get-tuple-element.182.vown, f32[1,5376]{1,0:T(1,128)} %copy-done.1), custom_call_target="tpu_custom_call" | custom-call | flops 100000000 | bytes 3000000 | tf_op jit(solution)/shard_map/positions/pallas_call | solution.py:819
  13.5 13.2 %first_pass.1 = (bf16[384,768]{1,0:T(8,128)(2,1)S(1)}, bf16[384,768]{1,0:T(8,128)(2,1)}, f32[384,768]{1,0:T(8,128)S(1)}, f32[384,768]{1,0:T(8,128)S(1)}, bf16[4,...) custom-call(s32[3]{0:T(128)} %pad_add_fusion.refs_0_.flags, ...), custom_call_target="tpu_custom_call", output_to_operand_aliasing={{2}: (11, {}), {3}: (12, {})} | custom-call | flops 8000000000 | bytes 20000000 | tf_op jit(solution)/shard_map/first_pass/pallas_call | solution.py:827
  27.3 1.7 collective-permute-start.5
  29.1 6.9 %collective-permute-done.5.got = bf16[384,768]{1,0:T(8,128)(2,1)S(1)} collective-permute-done((bf16[384,768]{1,0:T(8,128)(2,1)S(1)}, bf16[384,768]{1,0:T(8,128)(2,1)S(1)}, u32[]{:S(2)}, u32[]{:S(2)}) %collective-permute-start.5) | collective-permute-done | bytes 589856 | tf_op jit(solution)/shard_map/ppermute | solution.py:1054
  36.0 24.1 %second_pass.1 = (f32[384,768]{1,0:T(8,128)S(1)}, f32[384,768]{1,0:T(8,128)S(1)}, bf16[4,768,768]{2,1,0:T(8,128)(2,1)S(1)}, bf16[4,768,768]{2,1,0:T(8,128)(2,1)S...) custom-call(s32[3]{0:T(128)} %pad_add_fusion.refs_0_.flags, ...), custom_call_target="tpu_custom_call", output_to_operand_aliasing={{0}: (8, {}), {1}: (9, {}), {2}: (10, {}), {3}: (11, {}), {... | custom-call | flops 17999998976 | bytes 20000000 | tf_op jit(solution)/shard_map/second_pass/pallas_call | solution.py:847
  61.4 3.0 %late_pass.1 = (f32[384,768]{1,0:T(8,128)S(1)}, f32[384,768]{1,0:T(8,128)S(1)}, bf16[4,768,768]{2,1,0:T(8,128)(2,1)S(1)}, bf16[4,768,768]{2,1,0:T(8,128)(2,1)S(1...) custom-call(s32[3]{0:T(128)} %pad_add_fusion.refs_0_.flags, ...), custom_call_target="tpu_custom_call", output_to_operand_aliasing={{0}: (6, {}), {1}: (7, {}), {2}: (8, {}), {3}: (9, {}), {4}... | custom-call | flops 2000000000 | bytes 5000000 | tf_op jit(solution)/shard_map/late_pass/pallas_call | solution.py:860
  64.5 7.9 %collective-permute-done.7.got = bf16[384,768]{1,0:T(8,128)(2,1)S(1)} collective-permute-done((bf16[384,768]{1,0:T(8,128)(2,1)S(1)}, bf16[384,768]{1,0:T(8,128)(2,1)S(1)}, u32[]{:S(2)}, u32[]{:S(2)}) %collective-permute-start.7) | collective-permute-done | bytes 589856 | tf_op jit(solution)/shard_map/ppermute | solution.py:1059
  72.4 5.6 %collective-permute-start.10 = (bf16[384,3840]{1,0:T(8,128)(2,1)S(1)}, bf16[384,3840]{1,0:T(8,128)(2,1)S(1)}, u32[]{:S(2)}, u32[]{:S(2)}) collective-permute-start(bf16[384,3840]{1,0:T(8,128)(2,1)S(1)} %copy-done.2), channel_id=1, source_target_pairs={{0,8},{8,0},{16,24},{24,16},{1,9},{9,1},{17,25},{25,17},{2,10},{10... | collective-permute-start | bytes 8847368 | tf_op jit(solution)/shard_map/ppermute | solution.py:942
  78.6 16.6 %back_pass.1 = (bf16[384,768]{1,0:T(8,128)(2,1)S(1)}, bf16[384,768]{1,0:T(8,128)(2,1)S(1)}, bf16[384,768]{1,0:T(8,128)(2,1)S(1)}, f32[48,128]{1,0:T(8,128)S(1)},...) custom-call(s32[3]{0:T(128)} %pad_add_fusion.refs_0_.flags, bf16[384,768]{1,0:T(8,128)(2,1)} %get-tuple-element.187.field, ...), custom_call_target="tpu_custom_call" | custom-call | flops 10000000000 | bytes 15000000 | tf_op jit(solution)/shard_map/back_pass/pallas_call | solution.py:869
  95.2 5.8 %gram_down.1 = (bf16[768,1536]{1,0:T(8,128)(2,1)S(1)}, bf16[768,768]{1,0:T(8,128)(2,1)S(1)}, bf16[768,768]{1,0:T(8,128)(2,1)S(1)}, bf16[768,3072]{1,0:T(8,128)(2...) custom-call(s32[3]{0:T(128)} %pad_add_fusion.refs_0_.flags, ...), custom_call_target="tpu_custom_call" | custom-call | flops 2000000000 | bytes 8000000 | tf_op jit(solution)/shard_map/gram_down/pallas_call | solution.py:882
  101.0 1.9 gram_head.1
  102.9 1.9 collective-permute-start.14
  105.0 3.8 %gram_main.1 = (bf16[768,3072]{1,0:T(8,128)(2,1)S(1)}, bf16[768,2304]{1,0:T(8,128)(2,1)S(1)}, bf16[48,2304]{1,0:T(8,128)(2,1)S(1)}, bf16[48,2304]{1,0:T(8,128)(2,1)S(1)}) custom-call(s32[16,4]{1,0:T(8,128)} %get-tuple-element.233.rows.refs_0_.refs_1_, bf16[400,3072]{1,0:T(8,128)(2,1)S(1)} %collective-permute-done.11.right1, ...), custom_call_target="tpu_custom_call", output_to_operand_aliasing={{0}: (3, {})} | custom-call | flops 6000000000 | bytes 12000000 | tf_op jit(solution)/shard_map/gram_main/pallas_call | solution.py:900
  108.8 1.9 collective-permute-start.12
  132.8 1.8 collective-permute-done.23.refs_2_
  137.6 1.7 collective-permute-done.21.refs_2_
  145.6 2.1 collective-permute-start.30
  150.3 2.0 collective-permute-start.28
  155.5 1.8 collective-permute-start.34
  180.9 2.1 collective-permute-done.42.refs_7_
  191.7 3.0 %place.5 = (f32[768,4608]{1,0:T(8,128)}, bf16[768,768]{1,0:T(8,128)(2,1)}) custom-call(s32[3]{0:T(128)} %pad_add_fusion.refs_0_.flags, s32[16,4]{1,0:T(8,128)} %get-tuple-element.233.rows.refs_0_.refs_1_, bf16[48,2304]{1,0:T(8,128)(2,1)S(1)} %get-tuple-element.301.refs_2_, bf16[48,2304]{1,0:T(8,128)(2,1)S(1)} %get-tuple-element.297.refs_3_, ...), custom_call_target="tpu_custom_call" | custom-call | flops 1000 | bytes 20000000 | tf_op jit(solution)/shard_map/place/pallas_call | solution.py:933
  201.4 1.7 collective-permute-done.51.refs_7_
  211.3 3.3 %place.6 = (f32[768,4608]{1,0:T(8,128)}, f32[1,768]{1,0:T(1,128)}, f32[1,768]{1,0:T(1,128)}, f32[1,3072]{1,0:T(1,128)}, f32[1,768]{1,0:T(1,128)}) custom-call(s32[3]{0:T(128)} %pad_add_fusion.refs_0_.flags, s32[16,4]{1,0:T(8,128)} %get-tuple-element.233.rows.refs_0_.refs_1_, ...), custom_call_target="tpu_custom_call", output_to_operand_aliasing={{0}: (18, {})} | custom-call | flops 1000 | bytes 20000000 | tf_op jit(solution)/shard_map/place/pallas_call | solution.py:933
  220.8 2.0 collective-permute-done.59.refs_7_
  230.8 2.7 %place.7.refs_6_ = f32[768,4608]{1,0:T(8,128)} custom-call(s32[3]{0:T(128)} %pad_add_fusion.refs_0_.flags, s32[16,4]{1,0:T(8,128)} %get-tuple-element.233.rows.refs_0_.refs_1_, bf16[48,2304]{1,0:T(8,128)(2,1)S(1)} %collective-permute-done.53.refs_2_, bf16[48,2304]{1,0:T(8,128)(2,1)S(1)} %collective-permute-done.55.refs_3_, ...), custom_call_target="tpu_custom_call", output_to_operand_aliasing={{}: (10, {})} | custom-call | flops 1000 | bytes 20000000 | tf_op jit(solution)/shard_map/place/pallas_call | solution.py:933
  240.3 2.1 place.8.refs_6_
  242.4 1.8 collective-permute-done.65.refs_2_
  244.6 2.1 place.9
  (143 shorter events, 110.1 us)
Async XLA Ops:
  0.6 12.8 %collective-permute-start.4 = (bf16[768,4608]{1,0:T(8,128)(2,1)}, bf16[768,4608]{1,0:T(8,128)(2,1)}, u32[]{:S(2)}, u32[]{:S(2)}) collective-permute-start(bf16[768,4608]{1,0:T(8,128)(2,1)} %bitcast.12), channel_id=1, source_target_pairs={{0,8},{8,0},{16,24},{24,16},{1,9},{9,1},{17,25},{25,17},{2,10},{10... | collective-permute-start | bytes 21233672 | tf_op jit(solution)/shard_map/ppermute | solution.py:942
  3.6 9.8 %collective-permute-start = (bf16[192,384]{1,0:T(8,128)(2,1)S(1)}, bf16[192,384]{1,0:T(8,128)(2,1)S(1)}, u32[]{:S(2)}, u32[]{:S(2)}) collective-permute-start(bf16[192,384]{1,0:T(8,128)(2,1)S(1)} %get-tuple-element.179), channel_id=1, source_target_pairs={{0,8},{8,0},{16,24},{24,16},{1,9},{9,1},{17,25},{25,17},{2,10},{10... | collective-permute-start | bytes 442376 | tf_op jit(solution)/shard_map/ppermute | solution.py:942
  3.8 9.7 %collective-permute-start.1 = (bf16[192,384]{1,0:T(8,128)(2,1)S(1)}, bf16[192,384]{1,0:T(8,128)(2,1)S(1)}, u32[]{:S(2)}, u32[]{:S(2)}) collective-permute-start(bf16[192,384]{1,0:T(8,128)(2,1)S(1)} %get-tuple-element.180), channel_id=1, source_target_pairs={{0,16},{8,24},{16,0},{24,8},{1,17},{9,25},{17,1},{25,9},{2,18},{10... | collective-permute-start | bytes 442376 | tf_op jit(solution)/shard_map/ppermute | solution.py:1045
  27.3 8.7 %collective-permute-start.5 = (bf16[384,768]{1,0:T(8,128)(2,1)S(1)}, bf16[384,768]{1,0:T(8,128)(2,1)S(1)}, u32[]{:S(2)}, u32[]{:S(2)}) collective-permute-start(bf16[384,768]{1,0:T(8,128)(2,1)S(1)} %get-tuple-element.188.x_two), channel_id=1, source_target_pairs={{0,16},{1,17},{2,18},{3,19},{4,20},{5,21},{6,22},{7,23}} | collective-permute-start | bytes 1769480 | tf_op jit(solution)/shard_map/ppermute | solution.py:1054
  60.1 12.3 %collective-permute-start.7 = (bf16[384,768]{1,0:T(8,128)(2,1)S(1)}, bf16[384,768]{1,0:T(8,128)(2,1)S(1)}, u32[]{:S(2)}, u32[]{:S(2)}) collective-permute-start(bf16[384,768]{1,0:T(8,128)(2,1)S(1)} %get-tuple-element.194), channel_id=1, source_target_pairs={{16,0},{24,8},{17,1},{25,9},{18,2},{26,10},{19,3},{27,11},{20,4},{... | collective-permute-start | bytes 1769480 | tf_op jit(solution)/shard_map/ppermute | solution.py:1059
  72.4 22.7 %collective-permute-start.10 = (bf16[384,3840]{1,0:T(8,128)(2,1)S(1)}, bf16[384,3840]{1,0:T(8,128)(2,1)S(1)}, u32[]{:S(2)}, u32[]{:S(2)}) collective-permute-start(bf16[384,3840]{1,0:T(8,128)(2,1)S(1)} %copy-done.2), channel_id=1, source_target_pairs={{0,8},{8,0},{16,24},{24,16},{1,9},{9,1},{17,25},{25,17},{2,10},{10... | collective-permute-start | bytes 8847368 | tf_op jit(solution)/shard_map/ppermute | solution.py:942
  78.0 17.1 %collective-permute-start.8 = (bf16[384,768]{1,0:T(8,128)(2,1)S(1)}, bf16[384,768]{1,0:T(8,128)(2,1)S(1)}, u32[]{:S(2)}, u32[]{:S(2)}) collective-permute-start(bf16[384,768]{1,0:T(8,128)(2,1)S(1)} %collective-permute-done.7.got), channel_id=1, source_target_pairs={{0,8},{8,0},{16,24},{24,16},{1,9},{9,1},{17,25},{25,17},{2,10},{10... | collective-permute-start | bytes 1769480 | tf_op jit(solution)/shard_map/ppermute | solution.py:942
  78.1 17.1 %collective-permute-start.9 = (bf16[384,768]{1,0:T(8,128)(2,1)S(1)}, bf16[384,768]{1,0:T(8,128)(2,1)S(1)}, u32[]{:S(2)}, u32[]{:S(2)}) collective-permute-start(bf16[384,768]{1,0:T(8,128)(2,1)S(1)} %get-tuple-element.223), channel_id=1, source_target_pairs={{0,8},{8,0},{16,24},{24,16},{1,9},{9,1},{17,25},{25,17},{2,10},{10... | collective-permute-start | bytes 1769480 | tf_op jit(solution)/shard_map/ppermute | solution.py:942
  113.6 8.7 %collective-permute-start.18 = (bf16[48,2432]{1,0:T(8,128)(2,1)S(1)}, bf16[48,2432]{1,0:T(8,128)(2,1)S(1)}, u32[]{:S(2)}, u32[]{:S(2)}) collective-permute-start(bf16[48,2432]{1,0:T(8,128)(2,1)S(1)} %get-tuple-element.248), channel_id=1, source_target_pairs={{0,2},{2,4},{4,6},{6,7},{7,5},{5,3},{3,1},{1,0},{8,10},{10,12},{12... | collective-permute-start | bytes 700424 | tf_op jit(solution)/shard_map/ppermute | solution.py:970
  115.2 8.6 %collective-permute-start.19 = (bf16[48,2432]{1,0:T(8,128)(2,1)S(1)}, bf16[48,2432]{1,0:T(8,128)(2,1)S(1)}, u32[]{:S(2)}, u32[]{:S(2)}) collective-permute-start(bf16[48,2432]{1,0:T(8,128)(2,1)S(1)} %get-tuple-element.249), channel_id=1, source_target_pairs={{0,1},{2,0},{4,2},{6,4},{7,6},{5,7},{3,5},{1,3},{8,9},{10,8},{12,1... | collective-permute-start | bytes 700424 | tf_op jit(solution)/shard_map/ppermute | solution.py:970
  129.2 8.4 %collective-permute-start.20 = (bf16[48,2304]{1,0:T(8,128)(2,1)S(1)}, bf16[48,2304]{1,0:T(8,128)(2,1)S(1)}, u32[]{:S(2)}, u32[]{:S(2)}) collective-permute-start(bf16[48,2304]{1,0:T(8,128)(2,1)S(1)} %get-tuple-element.261), channel_id=1, source_target_pairs={{0,2},{2,4},{4,6},{6,7},{7,5},{5,3},{3,1},{1,0},{8,10},{10,12},{12... | collective-permute-start | bytes 663560 | tf_op jit(solution)/shard_map/ppermute | solution.py:970
  130.7 8.6 %collective-permute-start.21 = (bf16[48,2304]{1,0:T(8,128)(2,1)S(1)}, bf16[48,2304]{1,0:T(8,128)(2,1)S(1)}, u32[]{:S(2)}, u32[]{:S(2)}) collective-permute-start(bf16[48,2304]{1,0:T(8,128)(2,1)S(1)} %get-tuple-element.262), channel_id=1, source_target_pairs={{0,1},{2,0},{4,2},{6,4},{7,6},{5,7},{3,5},{1,3},{8,9},{10,8},{12,1... | collective-permute-start | bytes 663560 | tf_op jit(solution)/shard_map/ppermute | solution.py:970
  172.5 19.2 %collective-permute-start.44 = (bf16[384,768]{1,0:T(8,128)(2,1)S(1)}, bf16[384,768]{1,0:T(8,128)(2,1)S(1)}, u32[]{:S(2)}, u32[]{:S(2)}) collective-permute-start(bf16[384,768]{1,0:T(8,128)(2,1)S(1)} %copy-done.3), channel_id=1, source_target_pairs={{0,8},{8,0},{16,24},{24,16},{1,9},{9,1},{17,25},{25,17},{2,10},{10... | collective-permute-start | bytes 1769480 | tf_op jit(solution)/shard_map/ppermute | solution.py:942
  174.6 8.4 %collective-permute-start.42 = (bf16[48,2304]{1,0:T(8,128)(2,1)S(1)}, bf16[48,2304]{1,0:T(8,128)(2,1)S(1)}, u32[]{:S(2)}, u32[]{:S(2)}) collective-permute-start(bf16[48,2304]{1,0:T(8,128)(2,1)S(1)} %get-tuple-element.297.refs_3_), channel_id=1, source_target_pairs={{0,2},{2,4},{4,6},{6,7},{7,5},{5,3},{3,1},{1,0},{8,10},{10,12},{12... | collective-permute-start | bytes 663560 | tf_op jit(solution)/shard_map/ppermute | solution.py:970
  178.8 8.9 %collective-permute-start.40 = (bf16[48,2304]{1,0:T(8,128)(2,1)S(1)}, bf16[48,2304]{1,0:T(8,128)(2,1)S(1)}, u32[]{:S(2)}, u32[]{:S(2)}) collective-permute-start(bf16[48,2304]{1,0:T(8,128)(2,1)S(1)} %get-tuple-element.301.refs_2_), channel_id=1, source_target_pairs={{0,2},{2,4},{4,6},{6,7},{7,5},{5,3},{3,1},{1,0},{8,10},{10,12},{12... | collective-permute-start | bytes 663560 | tf_op jit(solution)/shard_map/ppermute | solution.py:970
  180.1 9.3 %collective-permute-start.41 = (bf16[48,2304]{1,0:T(8,128)(2,1)S(1)}, bf16[48,2304]{1,0:T(8,128)(2,1)S(1)}, u32[]{:S(2)}, u32[]{:S(2)}) collective-permute-start(bf16[48,2304]{1,0:T(8,128)(2,1)S(1)} %get-tuple-element.302.refs_4_), channel_id=1, source_target_pairs={{0,1},{2,0},{4,2},{6,4},{7,6},{5,7},{3,5},{1,3},{8,9},{10,8},{12,1... | collective-permute-start | bytes 663560 | tf_op jit(solution)/shard_map/ppermute | solution.py:970
  184.6 10.1 %collective-permute-start.47 = (bf16[48,2304]{1,0:T(8,128)(2,1)S(1)}, bf16[48,2304]{1,0:T(8,128)(2,1)S(1)}, u32[]{:S(2)}, u32[]{:S(2)}) collective-permute-start(bf16[48,2304]{1,0:T(8,128)(2,1)S(1)} %collective-permute-done.42.refs_7_), channel_id=1, source_target_pairs={{0,2},{2,4},{4,6},{6,7},{7,5},{5,3},{3,1},{1,0},{8,10},{10,12},{12... | collective-permute-start | bytes 663560 | tf_op jit(solution)/shard_map/ppermute | solution.py:970
  186.0 8.7 %collective-permute-start.48 = (bf16[48,2304]{1,0:T(8,128)(2,1)S(1)}, bf16[48,2304]{1,0:T(8,128)(2,1)S(1)}, u32[]{:S(2)}, u32[]{:S(2)}) collective-permute-start(bf16[48,2304]{1,0:T(8,128)(2,1)S(1)} %collective-permute-done.43.refs_9_), channel_id=1, source_target_pairs={{0,1},{2,0},{4,2},{6,4},{7,6},{5,7},{3,5},{1,3},{8,9},{10,8},{12,1... | collective-permute-start | bytes 663560 | tf_op jit(solution)/shard_map/ppermute | solution.py:970
  189.4 8.6 %collective-permute-start.45 = (bf16[48,2304]{1,0:T(8,128)(2,1)S(1)}, bf16[48,2304]{1,0:T(8,128)(2,1)S(1)}, u32[]{:S(2)}, u32[]{:S(2)}) collective-permute-start(bf16[48,2304]{1,0:T(8,128)(2,1)S(1)} %collective-permute-done.40.refs_6_), channel_id=1, source_target_pairs={{0,2},{2,4},{4,6},{6,7},{7,5},{5,3},{3,1},{1,0},{8,10},{10,12},{12... | collective-permute-start | bytes 663560 | tf_op jit(solution)/shard_map/ppermute | solution.py:970
  194.7 8.4 %collective-permute-start.51 = (bf16[48,2304]{1,0:T(8,128)(2,1)S(1)}, bf16[48,2304]{1,0:T(8,128)(2,1)S(1)}, u32[]{:S(2)}, u32[]{:S(2)}) collective-permute-start(bf16[48,2304]{1,0:T(8,128)(2,1)S(1)} %collective-permute-done.47.refs_3_), channel_id=1, source_target_pairs={{0,2},{2,4},{4,6},{6,7},{7,5},{5,3},{3,1},{1,0},{8,10},{10,12},{12... | collective-permute-start | bytes 663560 | tf_op jit(solution)/shard_map/ppermute | solution.py:970
  199.4 8.5 %collective-permute-start.49 = (bf16[48,2304]{1,0:T(8,128)(2,1)S(1)}, bf16[48,2304]{1,0:T(8,128)(2,1)S(1)}, u32[]{:S(2)}, u32[]{:S(2)}) collective-permute-start(bf16[48,2304]{1,0:T(8,128)(2,1)S(1)} %collective-permute-done.45.refs_2_), channel_id=1, source_target_pairs={{0,2},{2,4},{4,6},{6,7},{7,5},{5,3},{3,1},{1,0},{8,10},{10,12},{12... | collective-permute-start | bytes 663560 | tf_op jit(solution)/shard_map/ppermute | solution.py:970
  200.4 8.9 %collective-permute-start.50 = (bf16[48,2304]{1,0:T(8,128)(2,1)S(1)}, bf16[48,2304]{1,0:T(8,128)(2,1)S(1)}, u32[]{:S(2)}, u32[]{:S(2)}) collective-permute-start(bf16[48,2304]{1,0:T(8,128)(2,1)S(1)} %collective-permute-done.46.refs_4_), channel_id=1, source_target_pairs={{0,1},{2,0},{4,2},{6,4},{7,6},{5,7},{3,5},{1,3},{8,9},{10,8},{12,1... | collective-permute-start | bytes 663560 | tf_op jit(solution)/shard_map/ppermute | solution.py:970
  204.6 10.1 %collective-permute-start.55 = (bf16[48,2304]{1,0:T(8,128)(2,1)S(1)}, bf16[48,2304]{1,0:T(8,128)(2,1)S(1)}, u32[]{:S(2)}, u32[]{:S(2)}) collective-permute-start(bf16[48,2304]{1,0:T(8,128)(2,1)S(1)} %collective-permute-done.51.refs_7_), channel_id=1, source_target_pairs={{0,2},{2,4},{4,6},{6,7},{7,5},{5,3},{3,1},{1,0},{8,10},{10,12},{12... | collective-permute-start | bytes 663560 | tf_op jit(solution)/shard_map/ppermute | solution.py:970
  205.5 9.1 %collective-permute-start.56 = (bf16[48,2304]{1,0:T(8,128)(2,1)S(1)}, bf16[48,2304]{1,0:T(8,128)(2,1)S(1)}, u32[]{:S(2)}, u32[]{:S(2)}) collective-permute-start(bf16[48,2304]{1,0:T(8,128)(2,1)S(1)} %collective-permute-done.52.refs_9_), channel_id=1, source_target_pairs={{0,1},{2,0},{4,2},{6,4},{7,6},{5,7},{3,5},{1,3},{8,9},{10,8},{12,1... | collective-permute-start | bytes 663560 | tf_op jit(solution)/shard_map/ppermute | solution.py:970
  210.3 8.5 %collective-permute-start.54 = (bf16[48,2304]{1,0:T(8,128)(2,1)S(1)}, bf16[48,2304]{1,0:T(8,128)(2,1)S(1)}, u32[]{:S(2)}, u32[]{:S(2)}) collective-permute-start(bf16[48,2304]{1,0:T(8,128)(2,1)S(1)} %collective-permute-done.50.refs_8_), channel_id=1, source_target_pairs={{0,1},{2,0},{4,2},{6,4},{7,6},{5,7},{3,5},{1,3},{8,9},{10,8},{12,1... | collective-permute-start | bytes 663560 | tf_op jit(solution)/shard_map/ppermute | solution.py:970
  218.8 8.8 %collective-permute-start.57 = (bf16[48,2304]{1,0:T(8,128)(2,1)S(1)}, bf16[48,2304]{1,0:T(8,128)(2,1)S(1)}, u32[]{:S(2)}, u32[]{:S(2)}) collective-permute-start(bf16[48,2304]{1,0:T(8,128)(2,1)S(1)} %collective-permute-done.53.refs_2_), channel_id=1, source_target_pairs={{0,2},{2,4},{4,6},{6,7},{7,5},{5,3},{3,1},{1,0},{8,10},{10,12},{12... | collective-permute-start | bytes 663560 | tf_op jit(solution)/shard_map/ppermute | solution.py:970
  219.7 9.0 %collective-permute-start.58 = (bf16[48,2304]{1,0:T(8,128)(2,1)S(1)}, bf16[48,2304]{1,0:T(8,128)(2,1)S(1)}, u32[]{:S(2)}, u32[]{:S(2)}) collective-permute-start(bf16[48,2304]{1,0:T(8,128)(2,1)S(1)} %collective-permute-done.54.refs_4_), channel_id=1, source_target_pairs={{0,1},{2,0},{4,2},{6,4},{7,6},{5,7},{3,5},{1,3},{8,9},{10,8},{12,1... | collective-permute-start | bytes 663560 | tf_op jit(solution)/shard_map/ppermute | solution.py:970
  224.0 9.5 %collective-permute-start.63 = (bf16[48,2304]{1,0:T(8,128)(2,1)S(1)}, bf16[48,2304]{1,0:T(8,128)(2,1)S(1)}, u32[]{:S(2)}, u32[]{:S(2)}) collective-permute-start(bf16[48,2304]{1,0:T(8,128)(2,1)S(1)} %collective-permute-done.59.refs_7_), channel_id=1, source_target_pairs={{0,2},{2,4},{4,6},{6,7},{7,5},{5,3},{3,1},{1,0},{8,10},{10,12},{12... | collective-permute-start | bytes 663560 | tf_op jit(solution)/shard_map/ppermute | solution.py:970
  224.5 9.0 %collective-permute-start.64 = (bf16[48,2304]{1,0:T(8,128)(2,1)S(1)}, bf16[48,2304]{1,0:T(8,128)(2,1)S(1)}, u32[]{:S(2)}, u32[]{:S(2)}) collective-permute-start(bf16[48,2304]{1,0:T(8,128)(2,1)S(1)} %collective-permute-done.60.refs_9_), channel_id=1, source_target_pairs={{0,1},{2,0},{4,2},{6,4},{7,6},{5,7},{3,5},{1,3},{8,9},{10,8},{12,1... | collective-permute-start | bytes 663560 | tf_op jit(solution)/shard_map/ppermute | solution.py:970
  229.2 9.0 %collective-permute-start.62 = (bf16[48,2304]{1,0:T(8,128)(2,1)S(1)}, bf16[48,2304]{1,0:T(8,128)(2,1)S(1)}, u32[]{:S(2)}, u32[]{:S(2)}) collective-permute-start(bf16[48,2304]{1,0:T(8,128)(2,1)S(1)} %collective-permute-done.58.refs_8_), channel_id=1, source_target_pairs={{0,1},{2,0},{4,2},{6,4},{7,6},{5,7},{3,5},{1,3},{8,9},{10,8},{12,1... | collective-permute-start | bytes 663560 | tf_op jit(solution)/shard_map/ppermute | solution.py:970
  233.5 8.9 %collective-permute-start.67 = (bf16[48,2304]{1,0:T(8,128)(2,1)S(1)}, bf16[48,2304]{1,0:T(8,128)(2,1)S(1)}, u32[]{:S(2)}, u32[]{:S(2)}) collective-permute-start(bf16[48,2304]{1,0:T(8,128)(2,1)S(1)} %collective-permute-done.63.refs_3_), channel_id=1, source_target_pairs={{0,2},{2,4},{4,6},{6,7},{7,5},{5,3},{3,1},{1,0},{8,10},{10,12},{12... | collective-permute-start | bytes 663560 | tf_op jit(solution)/shard_map/ppermute | solution.py:970
  234.0 8.4 %collective-permute-start.68 = (bf16[48,2304]{1,0:T(8,128)(2,1)S(1)}, bf16[48,2304]{1,0:T(8,128)(2,1)S(1)}, u32[]{:S(2)}, u32[]{:S(2)}) collective-permute-start(bf16[48,2304]{1,0:T(8,128)(2,1)S(1)} %collective-permute-done.64.refs_5_), channel_id=1, source_target_pairs={{0,1},{2,0},{4,2},{6,4},{7,6},{5,7},{3,5},{1,3},{8,9},{10,8},{12,1... | collective-permute-start | bytes 663560 | tf_op jit(solution)/shard_map/ppermute | solution.py:970
  (41 other events, 306.1 us)

commit v6 on v5

--- a/solution.py
+++ b/solution.py
@@ -673,19 +673,18 @@
     return pl.ds(pl.multiple_of(rows[t, way], 16), r)
 
 
-def add_kernel(t, rows, up, down, *refs, count, vector):
-    parts, outs, vectors = refs[:count], refs[count : count + 2], refs[count + 2 :]
-    for k, (got, out) in enumerate(zip((up, down), outs)):
-        here = own_rows(rows, t, k, got.shape[0])
-        at = 0
-        for part in parts:
-            sl = slice(at, at + part.shape[1])
-            out[:, sl] = (got[:, sl].astype(F32) + part[here, :].astype(F32)).astype(BF)
-            at += part.shape[1]
-        if out.shape[1] > at:
-            out[:, at:] = got[:, at:]
-        if k < vector:
-            vectors[k][...] = got[:, at : at + 128].astype(F32)
+def add_kernel(t, way, rows, got, *refs, count, vector):
+    parts, out = refs[:count], refs[count]
+    here = own_rows(rows, t, way, got.shape[0])
+    at = 0
+    for part in parts:
+        sl = slice(at, at + part.shape[1])
+        out[:, sl] = (got[:, sl].astype(F32) + part[here, :].astype(F32)).astype(BF)
+        at += part.shape[1]
+    if out.shape[1] > at:
+        out[:, at:] = got[:, at:]
+    if vector:
+        refs[count + 1][...] = got[:, at : at + 128].astype(F32)
 
 
 def fold_vector(va, out):
@@ -731,26 +730,24 @@
 
 def place_kernel(spots, whole, flags, rows, *refs):
     count, pair, vectors, into = whole
-    ins, refs = refs[: 2 * count + pair + vectors], refs[2 * count + pair + vectors + into :]
+    ins, refs = refs[: count + pair + vectors], refs[count + pair + vectors + into :]
     out, buf, sems = refs[0], refs[-3], refs[-2]
     copies = []
     if pair:
-        copies += both_rows(flags[0], ins[2 * count], ins[2 * count + 1], refs[1], refs[-1])
+        copies += both_rows(flags[0], ins[count], ins[count + 1], refs[1], refs[-1])
         copies[0].start()
         copies[1].start()
-    r = ins[0].shape[0]
-    for k in range(count):
-        there = pl.ds(r * k, r)
-        buf[there, : 3 * D] = ins[2 * k][...].astype(F32)
-        buf[there, 3 * D :] = ins[2 * k + 1][...].astype(F32)
+    r, w = ins[0].shape
+    for k, (t, way, column) in enumerate(spots):
+        buf[k] = ins[k][...].astype(F32)
         copy = pltpu.make_async_copy(
-            buf.at[there, :], out.at[own_rows(rows, *spots[k], r), :], sems.at[k]
+            buf.at[k], out.at[own_rows(rows, t, way, r), pl.ds(column, w)], sems.at[k]
         )
         copy.start()
         copies.append(copy)
     if vectors:
         outs = refs[1 + pair // 2 : 5 + pair // 2]
-        sum_vectors(rows if vectors > 1 else None, ins[2 * count + pair :], refs[-4], outs)
+        sum_vectors(rows if vectors > 1 else None, ins[count + pair :], refs[-4], outs)
     for copy in copies:
         copy.wait()
 
@@ -829,7 +826,7 @@
         [row(), row_out()] + ANGLES + ATTN_W + MLP_W,
         [row(), VM((D, L), BF), row(3 * D), VM((HEADS, L, L), BF), VM((16, L), F32), row(), VM((D, L), BF),
          VM((D, L), BF), row(), DMA((13,))],
-        int(8e9), int(20e6), 26, out_specs=[VS, HBM] + [VS] * HELD,
+        int(8e9), int(20e6), 24, out_specs=[VS, HBM] + [VS] * HELD,
         aliases={len(a) - 2: 2, len(a) - 1: 3},
     )(*a)
     return results[0], results[1], results[2:]
@@ -849,7 +846,7 @@
         resident + [row(FF // 2), row(FF // 2), row()] + outs,
         HEAD_S + [row(), row(), VM((D, L), BF), VM((D, L), BF), VM((L, D), F32), VM((L, D), F32)]
         + BACK_S + [row(3 * D), DMA((9,))],
-        int(18e9), int(20e6), 26, out_specs=[VS] * (len(resident) + 3) + [HBM] * len(outs),
+        int(18e9), int(20e6), 24, out_specs=[VS] * (len(resident) + 3) + [HBM] * len(outs),
         aliases={len(a) + k: k for k in range(HELD)},
     )(*a, *(in_vmem(x) for x in held))
     n = len(resident)
@@ -859,7 +856,7 @@
 def late_pass(held, *a):
     results = call(
         late_kernel, "late_pass", [SMEM] + [VS] * (len(a) - 1 + len(held)),
-        ANGLES + ATTN_W + MLP_W + SAVED + [sds((L, D))] * 2, [], int(2e9), int(5e6), 26,
+        ANGLES + ATTN_W + MLP_W + SAVED + [sds((L, D))] * 2, [], int(2e9), int(5e6), 24,
         aliases={len(a) + k: k for k in range(len(held))},
     )(*a, *(in_vmem(x) for x in held))
     return results[: len(held)], results[len(held) :]
@@ -873,7 +870,7 @@
         + [row(FF), row(FF), VM((1, FIRST + 6 * D), F32), VM((1, VECTOR), F32), VM((1, VECTOR), F32),
            VM((16, D), BF)]
         + BACK_S + [DMA((5,))],
-        int(10e9), int(15e6), 26, out_specs=[VS] * 4 + [HBM] * 2,
+        int(10e9), int(15e6), 24, out_specs=[VS] * 4 + [HBM] * 2,
     )(*a, *(in_vmem(x) for x in held))
 
 
@@ -903,23 +900,22 @@
     )(rows, *a)[1:]
 
 
-def add(t, rows, up, down, parts, vector, wide):
+def add(t, way, rows, got, parts, vector, wide):
     count = len(parts)
 
     def kernel(*refs):
-        add_kernel(t, *refs, count=count, vector=vector)
+        add_kernel(t, way, *refs, count=count, vector=vector)
 
     width = sum(p.shape[1] for p in parts)
-    out = VM((up.shape[0], width + (128 if wide else 0)), BF)
+    out = VM((got.shape[0], width + (128 if wide else 0)), BF)
     results = call(
-        kernel, "add", [SMEM] + [VS] * (2 + count), [out, out] + [VM(PACKED, F32)] * vector, [], 1000,
-        int(1e6), 4,
-    )(rows, in_vmem(up), in_vmem(down), *(in_vmem(p) for p in parts))
-    return results[:2], results[2:]
+        kernel, "add", [SMEM] + [VS] * (1 + count), [out] + [VM(PACKED, F32)] * vector, [], 1000, int(2e7), 4
+    )(rows, in_vmem(got), *(in_vmem(p) for p in parts))
+    return results[0], results[1:]
 
 
 def place(flags, spots, rows, shards, total, pair=(), vectors=()):
-    r, count = shards[0].shape[0], len(shards) // 2
+    count = len(shards)
     into = [] if total is None else [total]
     whole = count, len(pair), len(vectors), len(into)
 
@@ -932,7 +928,8 @@
     given = len(shards) + len(pair) + len(vectors)
     return call(
         kernel, "place", [SMEM, SMEM] + [VS] * given + [HBM] * len(into), outs,
-        [VM((max(len(vectors), 1),) + PACKED, F32), VM((r * count, 6 * D), F32), DMA((count,)), DMA((2,))], 1000,
+        [VM((max(len(vectors), 1),) + PACKED, F32), VM((count,) + shards[0].shape, F32), DMA((count,)), DMA((2,))],
+        1000,
         int(2e7), 24, out_specs=[HBM] * (2 if pair else 1) + ([VS] * 4 if vectors else []),
         aliases={given + 2: 0} if into else {},
     )(flags, rows, *shards, *pair, *vectors, *into)
@@ -968,15 +965,21 @@
     def step(self, token):
         c = self.cycle
         got = [lax.ppermute(a, "dp", p) for a, p in zip(self.cur, c.pairs)]
-        got = after(got, token)
         self.t += 1
-        if self.t < c.n:
-            t = self.t
-            ways = int(t <= c.n // 2) + int(t <= (c.n - 1) // 2) if self.carries else 0
-            self.cur, came = add(t, c.rows, *got, self.parts, ways, self.carries and t < c.n // 2)
-            self.vectors += came
+        t = self.t
+        if t < c.n:
+            self.cur = []
+            for way in range(2):
+                vector = self.carries and t <= (c.n - way) // 2
+                out, came = add(
+                    t, way, c.rows, after(got[way], token), self.parts, vector, self.carries and t < c.n // 2
+                )
+                self.cur.append(out)
+                self.vectors += came
+                token = out
         else:
-            self.cur = got
+            first = after(got[0], token)
+            self.cur = [first, after(got[1], first)]
         if self.t >= c.n - 1:
             self.shards.append(self.cur)
         return self.cur
@@ -989,32 +992,31 @@
 def summed(flags, rows, main, tail, token, pair, vector):
     if not small_ring():
         chains, vector = lax.psum([main, tail], "dp"), lax.psum(vector, "dp")
-        return place(flags, [(0, 0)], rows, chains, None, pair, [vector])
+        return place(flags, [(0, 0, 0), (0, 0, 3 * D)], rows, chains, None, pair, [vector])
     cycle = main.cycle
     n = cycle.n
-    total, placed = None, 0
-    results = {}
+    total = None
+    waiting, results = [], {}
     while main.t < 2 * n - 2:
-        token = tail.step(token)
-        if total is not None:
-            token = (token, total)
-        token = main.step(token)
-        whole = len(main.shards)
-        if whole > placed and (whole % 2 == 0 or whole == n - 1):
-            spots, shards = [], []
-            for k in range(placed, whole):
-                for way in range(2):
-                    spots.append((cycle.placed(k), way))
-                    shards += [main.shards[k][way], tail.shards[k][way]]
-            now, then = placed == 0, "vectors" not in results and whole >= min(4, n)
-            total, *more = place(
-                flags, spots, cycle.rows, shards, total, pair if now else (), [vector] + tail.vectors if then else ()
-            )
-            if now:
-                results["rows"] = more[0]
-            if then:
-                results["vectors"] = more
-            placed = whole
+        for chain, column in ((tail, 3 * D), (main, 0)):
+            if total is not None:
+                token = (token, total)
+            token = chain.step(token)
+            whole = len(chain.shards)
+            if whole:
+                t = cycle.placed(whole - 1)
+                waiting += [((t, way, column), chain.shards[-1][way]) for way in range(2)]
+            if whole == n or chain is main and whole and whole % 2 == 0:
+                now, then = "rows" not in results, "vectors" not in results and whole >= min(4, n)
+                total, *more = place(
+                    flags, [a for a, _ in waiting], cycle.rows, [b for _, b in waiting], total,
+                    pair if now else (), [vector] + tail.vectors if then else (),
+                )
+                if now:
+                    results["rows"] = more.pop(0)
+                if then:
+                    results["vectors"] = more
+                waiting = []
     return total, results["rows"], *results["vectors"]
 
 

time: 251 us -> 249 us (level)
  waiting for transfers between devices: 72.6 us -> 57.7 us
  Pallas kernels: 98.6 us -> 110 us
    ppermute x56, waiting for transfers between devices: 55.9 us -> 41.1 us  [step(): got = [lax.ppermute(a, 'dp', p) for a, p in zip(self.cur, c.pairs)]]
    pallas_call x14 -> x28, Pallas kernels: 12.5 us -> 23.7 us  [add(): call(kernel, 'add', [SMEM] + [VS] * (1 + count), [out] + [VM(PACKED, F32)...]
  transfers between devices with their start and end apart: 69 -> 69, of which waited for: 48 -> 38; matrix products, arithmetic and copies ran while one was open for 0% -> 0% of each run, Pallas kernels for 23% -> 28%
where the time goes in v6:
time: 249 us; the launch traced here: 244 us
  Pallas kernels  110 us (44%)
  starting transfers between devices  74 us (30%)
  waiting for transfers between devices  57.7 us (23%)
    ppermute x56, starting transfers between devices, step(): got = [lax.ppermute(a, 'dp', p) for a, p in zip(self.cur, c.pairs)]  58.8 us
    ppermute x56, waiting for transfers between devices, step(): got = [lax.ppermute(a, 'dp', p) for a, p in zip(self.cur, c.pairs)]  41.1 us
    pallas_call x1, Pallas kernels, second_pass(): call(second_kernel, 'second_pass', [SMEM] + [VS] * (7 + HELD), resident +...  24 us
    pallas_call x28, Pallas kernels, add(): call(kernel, 'add', [SMEM] + [VS] * (1 + count), [out] + [VM(PACKED, F32)...  23.7 us
    pallas_call x1, Pallas kernels, back_pass(): call(back_kernel, 'back_pass', [SMEM] + [VS] * 5 + [HBM] * 2 + [VS] * len...  16.5 us
    pallas_call x5, Pallas kernels, place(): call(kernel, 'place', [SMEM, SMEM] + [VS] * given + [HBM] * len(into), ou...  13.2 us
    pallas_call x1, Pallas kernels, first_pass(): call(first_kernel, 'first_pass', [SMEM] + [VS] * 8 + [HBM] * 2 + [VS] * 2...  13.2 us
    ppermute x1, waiting for transfers between devices, body(): c_got = lax.ppermute(c_two, 'section', [(2, 0), (3, 1)])  7.92 us
  transfers between devices with their start and end apart: 69, of which 38 were waited for; matrix products, arithmetic and copies ran while one was open for 0% of the time, Pallas kernels for 28%

profile of v6, /device:TPU:0, one launch (start us, length us, event | category | flops | bytes accessed | tf_op | source)
XLA Modules:
  0.0 243.9 jit_solution(7537958889101053216)
XLA Ops:
  3.8 3.0 %collective-permute-start.1 = (bf16[192,384]{1,0:T(8,128)(2,1)S(1)}, bf16[192,384]{1,0:T(8,128)(2,1)S(1)}, u32[]{:S(2)}, u32[]{:S(2)}) collective-permute-start(bf16[192,384]{1,0:T(8,128)(2,1)S(1)} %get-tuple-element.159), channel_id=1, source_target_pairs={{0,16},{8,24},{16,0},{24,8},{1,17},{9,25},{17,1},{25,9},{2,18},{10... | collective-permute-start | bytes 442376 | tf_op jit(solution)/shard_map/ppermute | solution.py:1047
  10.8 2.7 %positions.1 = (f32[384,768]{1,0:T(8,128)S(1)}, f32[384,768]{1,0:T(8,128)S(1)}, f32[384,128]{1,0:T(8,128)}, f32[8,384]{1,0:T(8,128)}) custom-call(s32[3]{0:T(128)} %pad_add_fusion.refs_0_.flags, s32[2,2,2]{2,1,0:T(2,128)} %grid.1, f32[1,5376]{1,0:T(1,128)} %get-tuple-element.161.vown, f32[1,5376]{1,0:T(1,128)} %copy-done.1), custom_call_target="tpu_custom_call" | custom-call | flops 100000000 | bytes 3000000 | tf_op jit(solution)/shard_map/positions/pallas_call | solution.py:816
  13.5 13.2 %first_pass.1 = (bf16[384,768]{1,0:T(8,128)(2,1)S(1)}, bf16[384,768]{1,0:T(8,128)(2,1)}, f32[384,768]{1,0:T(8,128)S(1)}, f32[384,768]{1,0:T(8,128)S(1)}, bf16[4,...) custom-call(s32[3]{0:T(128)} %pad_add_fusion.refs_0_.flags, ...), custom_call_target="tpu_custom_call", output_to_operand_aliasing={{2}: (11, {}), {3}: (12, {})} | custom-call | flops 8000000000 | bytes 20000000 | tf_op jit(solution)/shard_map/first_pass/pallas_call | solution.py:824
  29.1 6.9 %collective-permute-done.5.got = bf16[384,768]{1,0:T(8,128)(2,1)S(1)} collective-permute-done((bf16[384,768]{1,0:T(8,128)(2,1)S(1)}, bf16[384,768]{1,0:T(8,128)(2,1)S(1)}, u32[]{:S(2)}, u32[]{:S(2)}) %collective-permute-start.5) | collective-permute-done | bytes 589856 | tf_op jit(solution)/shard_map/ppermute | solution.py:1056
  36.0 24.0 %second_pass.1 = (f32[384,768]{1,0:T(8,128)S(1)}, f32[384,768]{1,0:T(8,128)S(1)}, bf16[4,768,768]{2,1,0:T(8,128)(2,1)S(1)}, bf16[4,768,768]{2,1,0:T(8,128)(2,1)S...) custom-call(s32[3]{0:T(128)} %pad_add_fusion.refs_0_.flags, ...), custom_call_target="tpu_custom_call", output_to_operand_aliasing={{0}: (8, {}), {1}: (9, {}), {2}: (10, {}), {3}: (11, {}), {... | custom-call | flops 17999998976 | bytes 20000000 | tf_op jit(solution)/shard_map/second_pass/pallas_call | solution.py:844
  61.4 3.1 %late_pass.1 = (f32[384,768]{1,0:T(8,128)S(1)}, f32[384,768]{1,0:T(8,128)S(1)}, bf16[4,768,768]{2,1,0:T(8,128)(2,1)S(1)}, bf16[4,768,768]{2,1,0:T(8,128)(2,1)S(1...) custom-call(s32[3]{0:T(128)} %pad_add_fusion.refs_0_.flags, ...), custom_call_target="tpu_custom_call", output_to_operand_aliasing={{0}: (6, {}), {1}: (7, {}), {2}: (8, {}), {3}: (9, {}), {4}... | custom-call | flops 2000000000 | bytes 5000000 | tf_op jit(solution)/shard_map/late_pass/pallas_call | solution.py:857
  64.4 7.9 %collective-permute-done.7.got = bf16[384,768]{1,0:T(8,128)(2,1)S(1)} collective-permute-done((bf16[384,768]{1,0:T(8,128)(2,1)S(1)}, bf16[384,768]{1,0:T(8,128)(2,1)S(1)}, u32[]{:S(2)}, u32[]{:S(2)}) %collective-permute-start.7) | collective-permute-done | bytes 589856 | tf_op jit(solution)/shard_map/ppermute | solution.py:1061
  72.3 5.6 %collective-permute-start.10 = (bf16[384,3840]{1,0:T(8,128)(2,1)S(1)}, bf16[384,3840]{1,0:T(8,128)(2,1)S(1)}, u32[]{:S(2)}, u32[]{:S(2)}) collective-permute-start(bf16[384,3840]{1,0:T(8,128)(2,1)S(1)} %copy-done.2), channel_id=1, source_target_pairs={{0,8},{8,0},{16,24},{24,16},{1,9},{9,1},{17,25},{25,17},{2,10},{10... | collective-permute-start | bytes 8847368 | tf_op jit(solution)/shard_map/ppermute | solution.py:939
  78.5 16.5 %back_pass.1 = (bf16[384,768]{1,0:T(8,128)(2,1)S(1)}, bf16[384,768]{1,0:T(8,128)(2,1)S(1)}, bf16[384,768]{1,0:T(8,128)(2,1)S(1)}, f32[48,128]{1,0:T(8,128)S(1)},...) custom-call(s32[3]{0:T(128)} %pad_add_fusion.refs_0_.flags, bf16[384,768]{1,0:T(8,128)(2,1)} %get-tuple-element.166.field, ...), custom_call_target="tpu_custom_call" | custom-call | flops 10000000000 | bytes 15000000 | tf_op jit(solution)/shard_map/back_pass/pallas_call | solution.py:866
  95.1 5.8 %gram_down.1 = (bf16[768,1536]{1,0:T(8,128)(2,1)S(1)}, bf16[768,768]{1,0:T(8,128)(2,1)S(1)}, bf16[768,768]{1,0:T(8,128)(2,1)S(1)}, bf16[768,3072]{1,0:T(8,128)(2...) custom-call(s32[3]{0:T(128)} %pad_add_fusion.refs_0_.flags, ...), custom_call_target="tpu_custom_call" | custom-call | flops 2000000000 | bytes 8000000 | tf_op jit(solution)/shard_map/gram_down/pallas_call | solution.py:879
  104.8 3.8 %gram_main.1 = (bf16[768,3072]{1,0:T(8,128)(2,1)S(1)}, bf16[768,2304]{1,0:T(8,128)(2,1)S(1)}, bf16[48,2304]{1,0:T(8,128)(2,1)S(1)}, bf16[48,2304]{1,0:T(8,128)(2,1)S(1)}) custom-call(s32[16,4]{1,0:T(8,128)} %get-tuple-element.212.rows.refs_0_.refs_1_, bf16[400,3072]{1,0:T(8,128)(2,1)S(1)} %collective-permute-done.11.right1, ...), custom_call_target="tpu_custom_call", output_to_operand_aliasing={{0}: (3, {})} | custom-call | flops 6000000000 | bytes 12000000 | tf_op jit(solution)/shard_map/gram_main/pallas_call | solution.py:897
  114.8 2.2 collective-permute-done.14.refs_1_
  117.8 2.0 collective-permute-start.18
  122.8 2.0 collective-permute-start.17
  127.5 2.0 collective-permute-start.22
  132.5 2.0 collective-permute-start.21
  137.3 2.0 collective-permute-start.26
  142.3 2.0 collective-permute-start.25
  170.7 2.0 collective-permute-start.40
  179.1 2.1 collective-permute-start.46
  181.8 2.1 collective-permute-done.42.refs_8_
  186.5 3.1 %place.5 = (f32[768,4608]{1,0:T(8,128)}, bf16[768,768]{1,0:T(8,128)(2,1)}) custom-call(s32[3]{0:T(128)} %pad_add_fusion.refs_0_.flags, s32[16,4]{1,0:T(8,128)} %get-tuple-element.212.rows.refs_0_.refs_1_, bf16[48,2304]{1,0:T(8,128)(2,1)S(1)} %add.67.refs_2_, bf16[48,2304]{1,0:T(8,128)(2,1)S(1)} %add.68.refs_3_, bf16[48,2304]{1,0:T(8,128)(2,1)S(1)} %add.69.refs_4_, ...), custom_call_target="tpu_custom_call" | custom-call | flops 1000 | bytes 20000000 | tf_op jit(solution)/shard_map/place/pallas_call | solution.py:929
  196.0 2.1 collective-permute-done.49.refs_6_
  200.7 2.1 collective-permute-done.48.refs_8_
  205.5 3.3 %place.6 = (f32[768,4608]{1,0:T(8,128)}, f32[1,768]{1,0:T(1,128)}, f32[1,768]{1,0:T(1,128)}, f32[1,3072]{1,0:T(1,128)}, f32[1,768]{1,0:T(1,128)}) custom-call(s32[3]{0:T(128)} %pad_add_fusion.refs_0_.flags, s32[16,4]{1,0:T(8,128)} %get-tuple-element.212.rows.refs_0_.refs_1_, ...), custom_call_target="tpu_custom_call", output_to_operand_aliasing={{0}: (18, {})} | custom-call | flops 1000 | bytes 20000000 | tf_op jit(solution)/shard_map/place/pallas_call | solution.py:929
  215.0 2.3 collective-permute-done.57.refs_6_
  219.7 2.3 collective-permute-done.56.refs_8_
  224.4 2.7 %place.7.refs_8_ = f32[768,4608]{1,0:T(8,128)} custom-call(s32[3]{0:T(128)} %pad_add_fusion.refs_0_.flags, s32[16,4]{1,0:T(8,128)} %get-tuple-element.212.rows.refs_0_.refs_1_, bf16[48,2304]{1,0:T(8,128)(2,1)S(1)} %collective-permute-done.53.refs_2_, bf16[48,2304]{1,0:T(8,128)(2,1)S(1)} %collective-permute-done.55.refs_3_, ...), custom_call_target="tpu_custom_call", output_to_operand_aliasing={{}: (10, {})} | custom-call | flops 1000 | bytes 20000000 | tf_op jit(solution)/shard_map/place/pallas_call | solution.py:929
  229.2 2.2 collective-permute-done.60.refs_4_
  233.9 2.3 collective-permute-done.65.refs_6_
  236.2 2.3 collective-permute-done.67.refs_7_
  238.5 2.4 place.8.refs_4_
  (157 shorter events, 103.1 us)
Async XLA Ops:
  0.6 12.8 %collective-permute-start.4 = (bf16[768,4608]{1,0:T(8,128)(2,1)}, bf16[768,4608]{1,0:T(8,128)(2,1)}, u32[]{:S(2)}, u32[]{:S(2)}) collective-permute-start(bf16[768,4608]{1,0:T(8,128)(2,1)} %bitcast.12), channel_id=1, source_target_pairs={{0,8},{8,0},{16,24},{24,16},{1,9},{9,1},{17,25},{25,17},{2,10},{10... | collective-permute-start | bytes 21233672 | tf_op jit(solution)/shard_map/ppermute | solution.py:939
  3.6 9.8 %collective-permute-start = (bf16[192,384]{1,0:T(8,128)(2,1)S(1)}, bf16[192,384]{1,0:T(8,128)(2,1)S(1)}, u32[]{:S(2)}, u32[]{:S(2)}) collective-permute-start(bf16[192,384]{1,0:T(8,128)(2,1)S(1)} %get-tuple-element.158), channel_id=1, source_target_pairs={{0,8},{8,0},{16,24},{24,16},{1,9},{9,1},{17,25},{25,17},{2,10},{10... | collective-permute-start | bytes 442376 | tf_op jit(solution)/shard_map/ppermute | solution.py:939
  3.8 9.7 %collective-permute-start.1 = (bf16[192,384]{1,0:T(8,128)(2,1)S(1)}, bf16[192,384]{1,0:T(8,128)(2,1)S(1)}, u32[]{:S(2)}, u32[]{:S(2)}) collective-permute-start(bf16[192,384]{1,0:T(8,128)(2,1)S(1)} %get-tuple-element.159), channel_id=1, source_target_pairs={{0,16},{8,24},{16,0},{24,8},{1,17},{9,25},{17,1},{25,9},{2,18},{10... | collective-permute-start | bytes 442376 | tf_op jit(solution)/shard_map/ppermute | solution.py:1047
  60.0 12.3 %collective-permute-start.7 = (bf16[384,768]{1,0:T(8,128)(2,1)S(1)}, bf16[384,768]{1,0:T(8,128)(2,1)S(1)}, u32[]{:S(2)}, u32[]{:S(2)}) collective-permute-start(bf16[384,768]{1,0:T(8,128)(2,1)S(1)} %get-tuple-element.173), channel_id=1, source_target_pairs={{16,0},{24,8},{17,1},{25,9},{18,2},{26,10},{19,3},{27,11},{20,4},{... | collective-permute-start | bytes 1769480 | tf_op jit(solution)/shard_map/ppermute | solution.py:1061
  72.3 22.7 %collective-permute-start.10 = (bf16[384,3840]{1,0:T(8,128)(2,1)S(1)}, bf16[384,3840]{1,0:T(8,128)(2,1)S(1)}, u32[]{:S(2)}, u32[]{:S(2)}) collective-permute-start(bf16[384,3840]{1,0:T(8,128)(2,1)S(1)} %copy-done.2), channel_id=1, source_target_pairs={{0,8},{8,0},{16,24},{24,16},{1,9},{9,1},{17,25},{25,17},{2,10},{10... | collective-permute-start | bytes 8847368 | tf_op jit(solution)/shard_map/ppermute | solution.py:939
  78.0 17.0 %collective-permute-start.8 = (bf16[384,768]{1,0:T(8,128)(2,1)S(1)}, bf16[384,768]{1,0:T(8,128)(2,1)S(1)}, u32[]{:S(2)}, u32[]{:S(2)}) collective-permute-start(bf16[384,768]{1,0:T(8,128)(2,1)S(1)} %collective-permute-done.7.got), channel_id=1, source_target_pairs={{0,8},{8,0},{16,24},{24,16},{1,9},{9,1},{17,25},{25,17},{2,10},{10... | collective-permute-start | bytes 1769480 | tf_op jit(solution)/shard_map/ppermute | solution.py:939
  78.0 17.0 %collective-permute-start.9 = (bf16[384,768]{1,0:T(8,128)(2,1)S(1)}, bf16[384,768]{1,0:T(8,128)(2,1)S(1)}, u32[]{:S(2)}, u32[]{:S(2)}) collective-permute-start(bf16[384,768]{1,0:T(8,128)(2,1)S(1)} %get-tuple-element.202), channel_id=1, source_target_pairs={{0,8},{8,0},{16,24},{24,16},{1,9},{9,1},{17,25},{25,17},{2,10},{10... | collective-permute-start | bytes 1769480 | tf_op jit(solution)/shard_map/ppermute | solution.py:939
  104.7 9.0 %collective-permute-start.15 = (bf16[48,2432]{1,0:T(8,128)(2,1)S(1)}, bf16[48,2432]{1,0:T(8,128)(2,1)S(1)}, u32[]{:S(2)}, u32[]{:S(2)}) collective-permute-start(bf16[48,2432]{1,0:T(8,128)(2,1)S(1)} %get-tuple-element.226), channel_id=1, source_target_pairs={{0,1},{2,0},{4,2},{6,4},{7,6},{5,7},{3,5},{1,3},{8,9},{10,8},{12,1... | collective-permute-start | bytes 700424 | tf_op jit(solution)/shard_map/ppermute | solution.py:967
  110.5 9.2 %collective-permute-start.16 = (bf16[48,2304]{1,0:T(8,128)(2,1)S(1)}, bf16[48,2304]{1,0:T(8,128)(2,1)S(1)}, u32[]{:S(2)}, u32[]{:S(2)}) collective-permute-start(bf16[48,2304]{1,0:T(8,128)(2,1)S(1)} %get-tuple-element.222), channel_id=1, source_target_pairs={{0,1},{2,0},{4,2},{6,4},{7,6},{5,7},{3,5},{1,3},{8,9},{10,8},{12,1... | collective-permute-start | bytes 663560 | tf_op jit(solution)/shard_map/ppermute | solution.py:967
  111.8 10.2 %collective-permute-start.13 = (bf16[48,2432]{1,0:T(8,128)(2,1)S(1)}, bf16[48,2432]{1,0:T(8,128)(2,1)S(1)}, u32[]{:S(2)}, u32[]{:S(2)}) collective-permute-start(bf16[48,2432]{1,0:T(8,128)(2,1)S(1)} %get-tuple-element.225), channel_id=1, source_target_pairs={{0,2},{2,4},{4,6},{6,7},{7,5},{5,3},{3,1},{1,0},{8,10},{10,12},{12... | collective-permute-start | bytes 700424 | tf_op jit(solution)/shard_map/ppermute | solution.py:967
  114.5 10.2 %collective-permute-start.19 = (bf16[48,2432]{1,0:T(8,128)(2,1)S(1)}, bf16[48,2432]{1,0:T(8,128)(2,1)S(1)}, u32[]{:S(2)}, u32[]{:S(2)}) collective-permute-start(bf16[48,2432]{1,0:T(8,128)(2,1)S(1)} %get-tuple-element.228), channel_id=1, source_target_pairs={{0,1},{2,0},{4,2},{6,4},{7,6},{5,7},{3,5},{1,3},{8,9},{10,8},{12,1... | collective-permute-start | bytes 700424 | tf_op jit(solution)/shard_map/ppermute | solution.py:967
  169.0 17.5 %collective-permute-start.44 = (bf16[384,768]{1,0:T(8,128)(2,1)S(1)}, bf16[384,768]{1,0:T(8,128)(2,1)S(1)}, u32[]{:S(2)}, u32[]{:S(2)}) collective-permute-start(bf16[384,768]{1,0:T(8,128)(2,1)S(1)} %copy-done.3), channel_id=1, source_target_pairs={{0,8},{8,0},{16,24},{24,16},{1,9},{9,1},{17,25},{25,17},{2,10},{10... | collective-permute-start | bytes 1769480 | tf_op jit(solution)/shard_map/ppermute | solution.py:939
  179.1 10.5 %collective-permute-start.46 = (bf16[48,2304]{1,0:T(8,128)(2,1)S(1)}, bf16[48,2304]{1,0:T(8,128)(2,1)S(1)}, u32[]{:S(2)}, u32[]{:S(2)}) collective-permute-start(bf16[48,2304]{1,0:T(8,128)(2,1)S(1)} %collective-permute-done.40.refs_6_), channel_id=1, source_target_pairs={{0,2},{2,4},{4,6},{6,7},{7,5},{5,3},{3,1},{1,0},{8,10},{10,12},{12... | collective-permute-start | bytes 663560 | tf_op jit(solution)/shard_map/ppermute | solution.py:967
  181.6 9.9 %collective-permute-start.47 = (bf16[48,2304]{1,0:T(8,128)(2,1)S(1)}, bf16[48,2304]{1,0:T(8,128)(2,1)S(1)}, u32[]{:S(2)}, u32[]{:S(2)}) collective-permute-start(bf16[48,2304]{1,0:T(8,128)(2,1)S(1)} %collective-permute-done.41.refs_7_), channel_id=1, source_target_pairs={{0,1},{2,0},{4,2},{6,4},{7,6},{5,7},{3,5},{1,3},{8,9},{10,8},{12,1... | collective-permute-start | bytes 663560 | tf_op jit(solution)/shard_map/ppermute | solution.py:967
  183.9 9.5 %collective-permute-start.45 = (bf16[48,2304]{1,0:T(8,128)(2,1)S(1)}, bf16[48,2304]{1,0:T(8,128)(2,1)S(1)}, u32[]{:S(2)}, u32[]{:S(2)}) collective-permute-start(bf16[48,2304]{1,0:T(8,128)(2,1)S(1)} %collective-permute-done.42.refs_8_), channel_id=1, source_target_pairs={{0,2},{2,4},{4,6},{6,7},{7,5},{5,3},{3,1},{1,0},{8,10},{10,12},{12... | collective-permute-start | bytes 663560 | tf_op jit(solution)/shard_map/ppermute | solution.py:967
  186.4 9.5 %collective-permute-start.50 = (bf16[48,2304]{1,0:T(8,128)(2,1)S(1)}, bf16[48,2304]{1,0:T(8,128)(2,1)S(1)}, u32[]{:S(2)}, u32[]{:S(2)}) collective-permute-start(bf16[48,2304]{1,0:T(8,128)(2,1)S(1)} %collective-permute-done.43.refs_9_), channel_id=1, source_target_pairs={{0,1},{2,0},{4,2},{6,4},{7,6},{5,7},{3,5},{1,3},{8,9},{10,8},{12,1... | collective-permute-start | bytes 663560 | tf_op jit(solution)/shard_map/ppermute | solution.py:967
  191.6 9.0 %collective-permute-start.51 = (bf16[48,2304]{1,0:T(8,128)(2,1)S(1)}, bf16[48,2304]{1,0:T(8,128)(2,1)S(1)}, u32[]{:S(2)}, u32[]{:S(2)}) collective-permute-start(bf16[48,2304]{1,0:T(8,128)(2,1)S(1)} %collective-permute-done.47.refs_3_), channel_id=1, source_target_pairs={{0,1},{2,0},{4,2},{6,4},{7,6},{5,7},{3,5},{1,3},{8,9},{10,8},{12,1... | collective-permute-start | bytes 663560 | tf_op jit(solution)/shard_map/ppermute | solution.py:967
  193.3 9.5 %collective-permute-start.48 = (bf16[48,2304]{1,0:T(8,128)(2,1)S(1)}, bf16[48,2304]{1,0:T(8,128)(2,1)S(1)}, u32[]{:S(2)}, u32[]{:S(2)}) collective-permute-start(bf16[48,2304]{1,0:T(8,128)(2,1)S(1)} %collective-permute-done.45.refs_4_), channel_id=1, source_target_pairs={{0,2},{2,4},{4,6},{6,7},{7,5},{5,3},{3,1},{1,0},{8,10},{10,12},{12... | collective-permute-start | bytes 663560 | tf_op jit(solution)/shard_map/ppermute | solution.py:967
  195.9 9.5 %collective-permute-start.54 = (bf16[48,2304]{1,0:T(8,128)(2,1)S(1)}, bf16[48,2304]{1,0:T(8,128)(2,1)S(1)}, u32[]{:S(2)}, u32[]{:S(2)}) collective-permute-start(bf16[48,2304]{1,0:T(8,128)(2,1)S(1)} %collective-permute-done.50.refs_5_), channel_id=1, source_target_pairs={{0,1},{2,0},{4,2},{6,4},{7,6},{5,7},{3,5},{1,3},{8,9},{10,8},{12,1... | collective-permute-start | bytes 663560 | tf_op jit(solution)/shard_map/ppermute | solution.py:967
  198.1 10.7 %collective-permute-start.53 = (bf16[48,2304]{1,0:T(8,128)(2,1)S(1)}, bf16[48,2304]{1,0:T(8,128)(2,1)S(1)}, u32[]{:S(2)}, u32[]{:S(2)}) collective-permute-start(bf16[48,2304]{1,0:T(8,128)(2,1)S(1)} %collective-permute-done.49.refs_6_), channel_id=1, source_target_pairs={{0,2},{2,4},{4,6},{6,7},{7,5},{5,3},{3,1},{1,0},{8,10},{10,12},{12... | collective-permute-start | bytes 663560 | tf_op jit(solution)/shard_map/ppermute | solution.py:967
  200.6 10.1 %collective-permute-start.55 = (bf16[48,2304]{1,0:T(8,128)(2,1)S(1)}, bf16[48,2304]{1,0:T(8,128)(2,1)S(1)}, u32[]{:S(2)}, u32[]{:S(2)}) collective-permute-start(bf16[48,2304]{1,0:T(8,128)(2,1)S(1)} %collective-permute-done.51.refs_7_), channel_id=1, source_target_pairs={{0,1},{2,0},{4,2},{6,4},{7,6},{5,7},{3,5},{1,3},{8,9},{10,8},{12,1... | collective-permute-start | bytes 663560 | tf_op jit(solution)/shard_map/ppermute | solution.py:967
  202.8 9.5 %collective-permute-start.52 = (bf16[48,2304]{1,0:T(8,128)(2,1)S(1)}, bf16[48,2304]{1,0:T(8,128)(2,1)S(1)}, u32[]{:S(2)}, u32[]{:S(2)}) collective-permute-start(bf16[48,2304]{1,0:T(8,128)(2,1)S(1)} %collective-permute-done.48.refs_8_), channel_id=1, source_target_pairs={{0,2},{2,4},{4,6},{6,7},{7,5},{5,3},{3,1},{1,0},{8,10},{10,12},{12... | collective-permute-start | bytes 663560 | tf_op jit(solution)/shard_map/ppermute | solution.py:967
  205.3 9.5 %collective-permute-start.58 = (bf16[48,2304]{1,0:T(8,128)(2,1)S(1)}, bf16[48,2304]{1,0:T(8,128)(2,1)S(1)}, u32[]{:S(2)}, u32[]{:S(2)}) collective-permute-start(bf16[48,2304]{1,0:T(8,128)(2,1)S(1)} %collective-permute-done.54.refs_9_), channel_id=1, source_target_pairs={{0,1},{2,0},{4,2},{6,4},{7,6},{5,7},{3,5},{1,3},{8,9},{10,8},{12,1... | collective-permute-start | bytes 663560 | tf_op jit(solution)/shard_map/ppermute | solution.py:967
  212.3 9.7 %collective-permute-start.56 = (bf16[48,2304]{1,0:T(8,128)(2,1)S(1)}, bf16[48,2304]{1,0:T(8,128)(2,1)S(1)}, u32[]{:S(2)}, u32[]{:S(2)}) collective-permute-start(bf16[48,2304]{1,0:T(8,128)(2,1)S(1)} %collective-permute-done.52.refs_4_), channel_id=1, source_target_pairs={{0,2},{2,4},{4,6},{6,7},{7,5},{5,3},{3,1},{1,0},{8,10},{10,12},{12... | collective-permute-start | bytes 663560 | tf_op jit(solution)/shard_map/ppermute | solution.py:967
  214.8 9.5 %collective-permute-start.62 = (bf16[48,2304]{1,0:T(8,128)(2,1)S(1)}, bf16[48,2304]{1,0:T(8,128)(2,1)S(1)}, u32[]{:S(2)}, u32[]{:S(2)}) collective-permute-start(bf16[48,2304]{1,0:T(8,128)(2,1)S(1)} %collective-permute-done.58.refs_5_), channel_id=1, source_target_pairs={{0,1},{2,0},{4,2},{6,4},{7,6},{5,7},{3,5},{1,3},{8,9},{10,8},{12,1... | collective-permute-start | bytes 663560 | tf_op jit(solution)/shard_map/ppermute | solution.py:967
  217.2 9.9 %collective-permute-start.61 = (bf16[48,2304]{1,0:T(8,128)(2,1)S(1)}, bf16[48,2304]{1,0:T(8,128)(2,1)S(1)}, u32[]{:S(2)}, u32[]{:S(2)}) collective-permute-start(bf16[48,2304]{1,0:T(8,128)(2,1)S(1)} %collective-permute-done.57.refs_6_), channel_id=1, source_target_pairs={{0,2},{2,4},{4,6},{6,7},{7,5},{5,3},{3,1},{1,0},{8,10},{10,12},{12... | collective-permute-start | bytes 663560 | tf_op jit(solution)/shard_map/ppermute | solution.py:967
  219.6 9.5 %collective-permute-start.63 = (bf16[48,2304]{1,0:T(8,128)(2,1)S(1)}, bf16[48,2304]{1,0:T(8,128)(2,1)S(1)}, u32[]{:S(2)}, u32[]{:S(2)}) collective-permute-start(bf16[48,2304]{1,0:T(8,128)(2,1)S(1)} %collective-permute-done.59.refs_7_), channel_id=1, source_target_pairs={{0,1},{2,0},{4,2},{6,4},{7,6},{5,7},{3,5},{1,3},{8,9},{10,8},{12,1... | collective-permute-start | bytes 663560 | tf_op jit(solution)/shard_map/ppermute | solution.py:967
  222.0 9.5 %collective-permute-start.60 = (bf16[48,2304]{1,0:T(8,128)(2,1)S(1)}, bf16[48,2304]{1,0:T(8,128)(2,1)S(1)}, u32[]{:S(2)}, u32[]{:S(2)}) collective-permute-start(bf16[48,2304]{1,0:T(8,128)(2,1)S(1)} %collective-permute-done.56.refs_8_), channel_id=1, source_target_pairs={{0,2},{2,4},{4,6},{6,7},{7,5},{5,3},{3,1},{1,0},{8,10},{10,12},{12... | collective-permute-start | bytes 663560 | tf_op jit(solution)/shard_map/ppermute | solution.py:967
  224.3 9.5 %collective-permute-start.66 = (bf16[48,2304]{1,0:T(8,128)(2,1)S(1)}, bf16[48,2304]{1,0:T(8,128)(2,1)S(1)}, u32[]{:S(2)}, u32[]{:S(2)}) collective-permute-start(bf16[48,2304]{1,0:T(8,128)(2,1)S(1)} %collective-permute-done.62.refs_9_), channel_id=1, source_target_pairs={{0,1},{2,0},{4,2},{6,4},{7,6},{5,7},{3,5},{1,3},{8,9},{10,8},{12,1... | collective-permute-start | bytes 663560 | tf_op jit(solution)/shard_map/ppermute | solution.py:967
  227.2 9.0 %collective-permute-start.65 = (bf16[48,2304]{1,0:T(8,128)(2,1)S(1)}, bf16[48,2304]{1,0:T(8,128)(2,1)S(1)}, u32[]{:S(2)}, u32[]{:S(2)}) collective-permute-start(bf16[48,2304]{1,0:T(8,128)(2,1)S(1)} %collective-permute-done.61.refs_2_), channel_id=1, source_target_pairs={{0,2},{2,4},{4,6},{6,7},{7,5},{5,3},{3,1},{1,0},{8,10},{10,12},{12... | collective-permute-start | bytes 663560 | tf_op jit(solution)/shard_map/ppermute | solution.py:967
  229.1 9.4 %collective-permute-start.67 = (bf16[48,2304]{1,0:T(8,128)(2,1)S(1)}, bf16[48,2304]{1,0:T(8,128)(2,1)S(1)}, u32[]{:S(2)}, u32[]{:S(2)}) collective-permute-start(bf16[48,2304]{1,0:T(8,128)(2,1)S(1)} %collective-permute-done.63.refs_3_), channel_id=1, source_target_pairs={{0,1},{2,0},{4,2},{6,4},{7,6},{5,7},{3,5},{1,3},{8,9},{10,8},{12,1... | collective-permute-start | bytes 663560 | tf_op jit(solution)/shard_map/ppermute | solution.py:967
  231.5 9.5 %collective-permute-start.64 = (bf16[48,2304]{1,0:T(8,128)(2,1)S(1)}, bf16[48,2304]{1,0:T(8,128)(2,1)S(1)}, u32[]{:S(2)}, u32[]{:S(2)}) collective-permute-start(bf16[48,2304]{1,0:T(8,128)(2,1)S(1)} %collective-permute-done.60.refs_4_), channel_id=1, source_target_pairs={{0,2},{2,4},{4,6},{6,7},{7,5},{5,3},{3,1},{1,0},{8,10},{10,12},{12... | collective-permute-start | bytes 663560 | tf_op jit(solution)/shard_map/ppermute | solution.py:967
  (41 other events, 328.8 us)

commit v7 on v6

--- a/solution.py
+++ b/solution.py
@@ -23,6 +23,7 @@
 GAIN, SHIFT = slice(0, D), slice(D, 2 * D)
 FIRST, SECOND = 2 * D, 2 * D + FF
 VECTOR = 3 * D + FF
+LONGEST = 16
 PACKED = (48, 128)
 
 
@@ -323,6 +324,9 @@
     core, layer, where = flags[0], flags[1], flags[2]
     for t in range(table.shape[0]):
         for way, d in ((0, 1), (1, -1)):
+            if n > LONGEST:
+                table[t, way], table[t, 2 + way] = 0, 0
+                continue
             at = lax.rem(where - d * (t % n) + 2 * n, n)
             table[t, way] = at * (D // (2 * n)) + way * HALF
             table[t, 2 + way] = jnp.where(2 * at < n, 2 * at, 2 * (n - at) - 1)
@@ -804,7 +808,7 @@
     def kernel(*refs):
         prepare_kernel(*refs, n)
 
-    table = pltpu.HBM((2 * n if n <= 16 else 1, 4), I32)
+    table = pltpu.HBM((2 * n if n <= LONGEST else 1, 4), I32)
     return call(
         kernel, "prepare", [SMEM] + [VS] * 6, [out] * 4 + [pltpu.HBM((1, VECTOR), F32), table], [], 1000,
         int(1e6), 8, out_specs=[VS] * 5 + [SMEM],
@@ -986,7 +990,7 @@
 
 
 def small_ring():
-    return lax.axis_size("dp") <= 16
+    return lax.axis_size("dp") <= LONGEST
 
 
 def summed(flags, rows, main, tail, token, pair, vector):

time: 249 us -> 249 us (level)
  no operation moved by 1% of the time
where the time goes in v7:
time: 249 us; the launch traced here: 244 us
  Pallas kernels  110 us (44%)
  starting transfers between devices  74 us (30%)
  waiting for transfers between devices  57.7 us (23%)
    ppermute x56, starting transfers between devices, step(): got = [lax.ppermute(a, 'dp', p) for a, p in zip(self.cur, c.pairs)]  58.8 us
    ppermute x56, waiting for transfers between devices, step(): got = [lax.ppermute(a, 'dp', p) for a, p in zip(self.cur, c.pairs)]  41.1 us
    pallas_call x1, Pallas kernels, second_pass(): call(second_kernel, 'second_pass', [SMEM] + [VS] * (7 + HELD), resident +...  24 us
    pallas_call x28, Pallas kernels, add(): call(kernel, 'add', [SMEM] + [VS] * (1 + count), [out] + [VM(PACKED, F32)...  23.7 us
    pallas_call x1, Pallas kernels, back_pass(): call(back_kernel, 'back_pass', [SMEM] + [VS] * 5 + [HBM] * 2 + [VS] * len...  16.5 us
    pallas_call x5, Pallas kernels, place(): call(kernel, 'place', [SMEM, SMEM] + [VS] * given + [HBM] * len(into), ou...  13.2 us
    pallas_call x1, Pallas kernels, first_pass(): call(first_kernel, 'first_pass', [SMEM] + [VS] * 8 + [HBM] * 2 + [VS] * 2...  13.2 us
    ppermute x1, waiting for transfers between devices, body(): c_got = lax.ppermute(c_two, 'section', [(2, 0), (3, 1)])  7.92 us
  transfers between devices with their start and end apart: 69, of which 38 were waited for; matrix products, arithmetic and copies ran while one was open for 0% of the time, Pallas kernels for 28%

profile of v7, /device:TPU:0, one launch (start us, length us, event | category | flops | bytes accessed | tf_op | source)
XLA Modules:
  0.0 243.9 jit_solution(7537958889101053216)
XLA Ops:
  3.8 3.0 %collective-permute-start.1 = (bf16[192,384]{1,0:T(8,128)(2,1)S(1)}, bf16[192,384]{1,0:T(8,128)(2,1)S(1)}, u32[]{:S(2)}, u32[]{:S(2)}) collective-permute-start(bf16[192,384]{1,0:T(8,128)(2,1)S(1)} %get-tuple-element.159), channel_id=1, source_target_pairs={{0,16},{8,24},{16,0},{24,8},{1,17},{9,25},{17,1},{25,9},{2,18},{10... | collective-permute-start | bytes 442376 | tf_op jit(solution)/shard_map/ppermute | solution.py:1051
  10.8 2.7 %positions.1 = (f32[384,768]{1,0:T(8,128)S(1)}, f32[384,768]{1,0:T(8,128)S(1)}, f32[384,128]{1,0:T(8,128)}, f32[8,384]{1,0:T(8,128)}) custom-call(s32[3]{0:T(128)} %pad_add_fusion.refs_0_.flags, s32[2,2,2]{2,1,0:T(2,128)} %grid.1, f32[1,5376]{1,0:T(1,128)} %get-tuple-element.161.vown, f32[1,5376]{1,0:T(1,128)} %copy-done.1), custom_call_target="tpu_custom_call" | custom-call | flops 100000000 | bytes 3000000 | tf_op jit(solution)/shard_map/positions/pallas_call | solution.py:820
  13.5 13.2 %first_pass.1 = (bf16[384,768]{1,0:T(8,128)(2,1)S(1)}, bf16[384,768]{1,0:T(8,128)(2,1)}, f32[384,768]{1,0:T(8,128)S(1)}, f32[384,768]{1,0:T(8,128)S(1)}, bf16[4,...) custom-call(s32[3]{0:T(128)} %pad_add_fusion.refs_0_.flags, ...), custom_call_target="tpu_custom_call", output_to_operand_aliasing={{2}: (11, {}), {3}: (12, {})} | custom-call | flops 8000000000 | bytes 20000000 | tf_op jit(solution)/shard_map/first_pass/pallas_call | solution.py:828
  29.1 6.9 %collective-permute-done.5.got = bf16[384,768]{1,0:T(8,128)(2,1)S(1)} collective-permute-done((bf16[384,768]{1,0:T(8,128)(2,1)S(1)}, bf16[384,768]{1,0:T(8,128)(2,1)S(1)}, u32[]{:S(2)}, u32[]{:S(2)}) %collective-permute-start.5) | collective-permute-done | bytes 589856 | tf_op jit(solution)/shard_map/ppermute | solution.py:1060
  36.0 24.0 %second_pass.1 = (f32[384,768]{1,0:T(8,128)S(1)}, f32[384,768]{1,0:T(8,128)S(1)}, bf16[4,768,768]{2,1,0:T(8,128)(2,1)S(1)}, bf16[4,768,768]{2,1,0:T(8,128)(2,1)S...) custom-call(s32[3]{0:T(128)} %pad_add_fusion.refs_0_.flags, ...), custom_call_target="tpu_custom_call", output_to_operand_aliasing={{0}: (8, {}), {1}: (9, {}), {2}: (10, {}), {3}: (11, {}), {... | custom-call | flops 17999998976 | bytes 20000000 | tf_op jit(solution)/shard_map/second_pass/pallas_call | solution.py:848
  61.4 3.1 %late_pass.1 = (f32[384,768]{1,0:T(8,128)S(1)}, f32[384,768]{1,0:T(8,128)S(1)}, bf16[4,768,768]{2,1,0:T(8,128)(2,1)S(1)}, bf16[4,768,768]{2,1,0:T(8,128)(2,1)S(1...) custom-call(s32[3]{0:T(128)} %pad_add_fusion.refs_0_.flags, ...), custom_call_target="tpu_custom_call", output_to_operand_aliasing={{0}: (6, {}), {1}: (7, {}), {2}: (8, {}), {3}: (9, {}), {4}... | custom-call | flops 2000000000 | bytes 5000000 | tf_op jit(solution)/shard_map/late_pass/pallas_call | solution.py:861
  64.4 7.9 %collective-permute-done.7.got = bf16[384,768]{1,0:T(8,128)(2,1)S(1)} collective-permute-done((bf16[384,768]{1,0:T(8,128)(2,1)S(1)}, bf16[384,768]{1,0:T(8,128)(2,1)S(1)}, u32[]{:S(2)}, u32[]{:S(2)}) %collective-permute-start.7) | collective-permute-done | bytes 589856 | tf_op jit(solution)/shard_map/ppermute | solution.py:1065
  72.3 5.6 %collective-permute-start.10 = (bf16[384,3840]{1,0:T(8,128)(2,1)S(1)}, bf16[384,3840]{1,0:T(8,128)(2,1)S(1)}, u32[]{:S(2)}, u32[]{:S(2)}) collective-permute-start(bf16[384,3840]{1,0:T(8,128)(2,1)S(1)} %copy-done.2), channel_id=1, source_target_pairs={{0,8},{8,0},{16,24},{24,16},{1,9},{9,1},{17,25},{25,17},{2,10},{10... | collective-permute-start | bytes 8847368 | tf_op jit(solution)/shard_map/ppermute | solution.py:943
  78.5 16.5 %back_pass.1 = (bf16[384,768]{1,0:T(8,128)(2,1)S(1)}, bf16[384,768]{1,0:T(8,128)(2,1)S(1)}, bf16[384,768]{1,0:T(8,128)(2,1)S(1)}, f32[48,128]{1,0:T(8,128)S(1)},...) custom-call(s32[3]{0:T(128)} %pad_add_fusion.refs_0_.flags, bf16[384,768]{1,0:T(8,128)(2,1)} %get-tuple-element.166.field, ...), custom_call_target="tpu_custom_call" | custom-call | flops 10000000000 | bytes 15000000 | tf_op jit(solution)/shard_map/back_pass/pallas_call | solution.py:870
  95.1 5.8 %gram_down.1 = (bf16[768,1536]{1,0:T(8,128)(2,1)S(1)}, bf16[768,768]{1,0:T(8,128)(2,1)S(1)}, bf16[768,768]{1,0:T(8,128)(2,1)S(1)}, bf16[768,3072]{1,0:T(8,128)(2...) custom-call(s32[3]{0:T(128)} %pad_add_fusion.refs_0_.flags, ...), custom_call_target="tpu_custom_call" | custom-call | flops 2000000000 | bytes 8000000 | tf_op jit(solution)/shard_map/gram_down/pallas_call | solution.py:883
  104.8 3.8 %gram_main.1 = (bf16[768,3072]{1,0:T(8,128)(2,1)S(1)}, bf16[768,2304]{1,0:T(8,128)(2,1)S(1)}, bf16[48,2304]{1,0:T(8,128)(2,1)S(1)}, bf16[48,2304]{1,0:T(8,128)(2,1)S(1)}) custom-call(s32[16,4]{1,0:T(8,128)} %get-tuple-element.212.rows.refs_0_.refs_1_, bf16[400,3072]{1,0:T(8,128)(2,1)S(1)} %collective-permute-done.11.right1, ...), custom_call_target="tpu_custom_call", output_to_operand_aliasing={{0}: (3, {})} | custom-call | flops 6000000000 | bytes 12000000 | tf_op jit(solution)/shard_map/gram_main/pallas_call | solution.py:901
  114.8 2.2 collective-permute-done.14.refs_1_
  117.8 2.0 collective-permute-start.18
  122.8 2.0 collective-permute-start.17
  127.5 2.0 collective-permute-start.22
  132.5 2.0 collective-permute-start.21
  137.3 2.0 collective-permute-start.26
  142.3 2.0 collective-permute-start.25
  170.7 2.0 collective-permute-start.40
  179.1 2.1 collective-permute-start.46
  181.8 2.1 collective-permute-done.42.refs_8_
  186.5 3.1 %place.5 = (f32[768,4608]{1,0:T(8,128)}, bf16[768,768]{1,0:T(8,128)(2,1)}) custom-call(s32[3]{0:T(128)} %pad_add_fusion.refs_0_.flags, s32[16,4]{1,0:T(8,128)} %get-tuple-element.212.rows.refs_0_.refs_1_, bf16[48,2304]{1,0:T(8,128)(2,1)S(1)} %add.67.refs_2_, bf16[48,2304]{1,0:T(8,128)(2,1)S(1)} %add.68.refs_3_, bf16[48,2304]{1,0:T(8,128)(2,1)S(1)} %add.69.refs_4_, ...), custom_call_target="tpu_custom_call" | custom-call | flops 1000 | bytes 20000000 | tf_op jit(solution)/shard_map/place/pallas_call | solution.py:933
  196.0 2.1 collective-permute-done.49.refs_6_
  200.7 2.1 collective-permute-done.48.refs_8_
  205.5 3.3 %place.6 = (f32[768,4608]{1,0:T(8,128)}, f32[1,768]{1,0:T(1,128)}, f32[1,768]{1,0:T(1,128)}, f32[1,3072]{1,0:T(1,128)}, f32[1,768]{1,0:T(1,128)}) custom-call(s32[3]{0:T(128)} %pad_add_fusion.refs_0_.flags, s32[16,4]{1,0:T(8,128)} %get-tuple-element.212.rows.refs_0_.refs_1_, ...), custom_call_target="tpu_custom_call", output_to_operand_aliasing={{0}: (18, {})} | custom-call | flops 1000 | bytes 20000000 | tf_op jit(solution)/shard_map/place/pallas_call | solution.py:933
  215.0 2.3 collective-permute-done.57.refs_6_
  219.7 2.3 collective-permute-done.56.refs_8_
  224.4 2.7 %place.7.refs_8_ = f32[768,4608]{1,0:T(8,128)} custom-call(s32[3]{0:T(128)} %pad_add_fusion.refs_0_.flags, s32[16,4]{1,0:T(8,128)} %get-tuple-element.212.rows.refs_0_.refs_1_, bf16[48,2304]{1,0:T(8,128)(2,1)S(1)} %collective-permute-done.53.refs_2_, bf16[48,2304]{1,0:T(8,128)(2,1)S(1)} %collective-permute-done.55.refs_3_, ...), custom_call_target="tpu_custom_call", output_to_operand_aliasing={{}: (10, {})} | custom-call | flops 1000 | bytes 20000000 | tf_op jit(solution)/shard_map/place/pallas_call | solution.py:933
  229.2 2.2 collective-permute-done.60.refs_4_
  233.9 2.3 collective-permute-done.65.refs_6_
  236.2 2.3 collective-permute-done.67.refs_7_
  238.5 2.4 place.8.refs_4_
  (157 shorter events, 103.1 us)
Async XLA Ops:
  0.6 12.8 %collective-permute-start.4 = (bf16[768,4608]{1,0:T(8,128)(2,1)}, bf16[768,4608]{1,0:T(8,128)(2,1)}, u32[]{:S(2)}, u32[]{:S(2)}) collective-permute-start(bf16[768,4608]{1,0:T(8,128)(2,1)} %bitcast.12), channel_id=1, source_target_pairs={{0,8},{8,0},{16,24},{24,16},{1,9},{9,1},{17,25},{25,17},{2,10},{10... | collective-permute-start | bytes 21233672 | tf_op jit(solution)/shard_map/ppermute | solution.py:943
  3.6 9.8 %collective-permute-start = (bf16[192,384]{1,0:T(8,128)(2,1)S(1)}, bf16[192,384]{1,0:T(8,128)(2,1)S(1)}, u32[]{:S(2)}, u32[]{:S(2)}) collective-permute-start(bf16[192,384]{1,0:T(8,128)(2,1)S(1)} %get-tuple-element.158), channel_id=1, source_target_pairs={{0,8},{8,0},{16,24},{24,16},{1,9},{9,1},{17,25},{25,17},{2,10},{10... | collective-permute-start | bytes 442376 | tf_op jit(solution)/shard_map/ppermute | solution.py:943
  3.8 9.7 %collective-permute-start.1 = (bf16[192,384]{1,0:T(8,128)(2,1)S(1)}, bf16[192,384]{1,0:T(8,128)(2,1)S(1)}, u32[]{:S(2)}, u32[]{:S(2)}) collective-permute-start(bf16[192,384]{1,0:T(8,128)(2,1)S(1)} %get-tuple-element.159), channel_id=1, source_target_pairs={{0,16},{8,24},{16,0},{24,8},{1,17},{9,25},{17,1},{25,9},{2,18},{10... | collective-permute-start | bytes 442376 | tf_op jit(solution)/shard_map/ppermute | solution.py:1051
  60.0 12.3 %collective-permute-start.7 = (bf16[384,768]{1,0:T(8,128)(2,1)S(1)}, bf16[384,768]{1,0:T(8,128)(2,1)S(1)}, u32[]{:S(2)}, u32[]{:S(2)}) collective-permute-start(bf16[384,768]{1,0:T(8,128)(2,1)S(1)} %get-tuple-element.173), channel_id=1, source_target_pairs={{16,0},{24,8},{17,1},{25,9},{18,2},{26,10},{19,3},{27,11},{20,4},{... | collective-permute-start | bytes 1769480 | tf_op jit(solution)/shard_map/ppermute | solution.py:1065
  72.3 22.7 %collective-permute-start.10 = (bf16[384,3840]{1,0:T(8,128)(2,1)S(1)}, bf16[384,3840]{1,0:T(8,128)(2,1)S(1)}, u32[]{:S(2)}, u32[]{:S(2)}) collective-permute-start(bf16[384,3840]{1,0:T(8,128)(2,1)S(1)} %copy-done.2), channel_id=1, source_target_pairs={{0,8},{8,0},{16,24},{24,16},{1,9},{9,1},{17,25},{25,17},{2,10},{10... | collective-permute-start | bytes 8847368 | tf_op jit(solution)/shard_map/ppermute | solution.py:943
  78.0 17.0 %collective-permute-start.8 = (bf16[384,768]{1,0:T(8,128)(2,1)S(1)}, bf16[384,768]{1,0:T(8,128)(2,1)S(1)}, u32[]{:S(2)}, u32[]{:S(2)}) collective-permute-start(bf16[384,768]{1,0:T(8,128)(2,1)S(1)} %collective-permute-done.7.got), channel_id=1, source_target_pairs={{0,8},{8,0},{16,24},{24,16},{1,9},{9,1},{17,25},{25,17},{2,10},{10... | collective-permute-start | bytes 1769480 | tf_op jit(solution)/shard_map/ppermute | solution.py:943
  78.0 17.0 %collective-permute-start.9 = (bf16[384,768]{1,0:T(8,128)(2,1)S(1)}, bf16[384,768]{1,0:T(8,128)(2,1)S(1)}, u32[]{:S(2)}, u32[]{:S(2)}) collective-permute-start(bf16[384,768]{1,0:T(8,128)(2,1)S(1)} %get-tuple-element.202), channel_id=1, source_target_pairs={{0,8},{8,0},{16,24},{24,16},{1,9},{9,1},{17,25},{25,17},{2,10},{10... | collective-permute-start | bytes 1769480 | tf_op jit(solution)/shard_map/ppermute | solution.py:943
  104.7 9.0 %collective-permute-start.15 = (bf16[48,2432]{1,0:T(8,128)(2,1)S(1)}, bf16[48,2432]{1,0:T(8,128)(2,1)S(1)}, u32[]{:S(2)}, u32[]{:S(2)}) collective-permute-start(bf16[48,2432]{1,0:T(8,128)(2,1)S(1)} %get-tuple-element.226), channel_id=1, source_target_pairs={{0,1},{2,0},{4,2},{6,4},{7,6},{5,7},{3,5},{1,3},{8,9},{10,8},{12,1... | collective-permute-start | bytes 700424 | tf_op jit(solution)/shard_map/ppermute | solution.py:971
  110.5 9.2 %collective-permute-start.16 = (bf16[48,2304]{1,0:T(8,128)(2,1)S(1)}, bf16[48,2304]{1,0:T(8,128)(2,1)S(1)}, u32[]{:S(2)}, u32[]{:S(2)}) collective-permute-start(bf16[48,2304]{1,0:T(8,128)(2,1)S(1)} %get-tuple-element.222), channel_id=1, source_target_pairs={{0,1},{2,0},{4,2},{6,4},{7,6},{5,7},{3,5},{1,3},{8,9},{10,8},{12,1... | collective-permute-start | bytes 663560 | tf_op jit(solution)/shard_map/ppermute | solution.py:971
  111.8 10.2 %collective-permute-start.13 = (bf16[48,2432]{1,0:T(8,128)(2,1)S(1)}, bf16[48,2432]{1,0:T(8,128)(2,1)S(1)}, u32[]{:S(2)}, u32[]{:S(2)}) collective-permute-start(bf16[48,2432]{1,0:T(8,128)(2,1)S(1)} %get-tuple-element.225), channel_id=1, source_target_pairs={{0,2},{2,4},{4,6},{6,7},{7,5},{5,3},{3,1},{1,0},{8,10},{10,12},{12... | collective-permute-start | bytes 700424 | tf_op jit(solution)/shard_map/ppermute | solution.py:971
  114.5 10.2 %collective-permute-start.19 = (bf16[48,2432]{1,0:T(8,128)(2,1)S(1)}, bf16[48,2432]{1,0:T(8,128)(2,1)S(1)}, u32[]{:S(2)}, u32[]{:S(2)}) collective-permute-start(bf16[48,2432]{1,0:T(8,128)(2,1)S(1)} %get-tuple-element.228), channel_id=1, source_target_pairs={{0,1},{2,0},{4,2},{6,4},{7,6},{5,7},{3,5},{1,3},{8,9},{10,8},{12,1... | collective-permute-start | bytes 700424 | tf_op jit(solution)/shard_map/ppermute | solution.py:971
  169.0 17.5 %collective-permute-start.44 = (bf16[384,768]{1,0:T(8,128)(2,1)S(1)}, bf16[384,768]{1,0:T(8,128)(2,1)S(1)}, u32[]{:S(2)}, u32[]{:S(2)}) collective-permute-start(bf16[384,768]{1,0:T(8,128)(2,1)S(1)} %copy-done.3), channel_id=1, source_target_pairs={{0,8},{8,0},{16,24},{24,16},{1,9},{9,1},{17,25},{25,17},{2,10},{10... | collective-permute-start | bytes 1769480 | tf_op jit(solution)/shard_map/ppermute | solution.py:943
  179.1 10.5 %collective-permute-start.46 = (bf16[48,2304]{1,0:T(8,128)(2,1)S(1)}, bf16[48,2304]{1,0:T(8,128)(2,1)S(1)}, u32[]{:S(2)}, u32[]{:S(2)}) collective-permute-start(bf16[48,2304]{1,0:T(8,128)(2,1)S(1)} %collective-permute-done.40.refs_6_), channel_id=1, source_target_pairs={{0,2},{2,4},{4,6},{6,7},{7,5},{5,3},{3,1},{1,0},{8,10},{10,12},{12... | collective-permute-start | bytes 663560 | tf_op jit(solution)/shard_map/ppermute | solution.py:971
  181.6 9.9 %collective-permute-start.47 = (bf16[48,2304]{1,0:T(8,128)(2,1)S(1)}, bf16[48,2304]{1,0:T(8,128)(2,1)S(1)}, u32[]{:S(2)}, u32[]{:S(2)}) collective-permute-start(bf16[48,2304]{1,0:T(8,128)(2,1)S(1)} %collective-permute-done.41.refs_7_), channel_id=1, source_target_pairs={{0,1},{2,0},{4,2},{6,4},{7,6},{5,7},{3,5},{1,3},{8,9},{10,8},{12,1... | collective-permute-start | bytes 663560 | tf_op jit(solution)/shard_map/ppermute | solution.py:971
  183.9 9.5 %collective-permute-start.45 = (bf16[48,2304]{1,0:T(8,128)(2,1)S(1)}, bf16[48,2304]{1,0:T(8,128)(2,1)S(1)}, u32[]{:S(2)}, u32[]{:S(2)}) collective-permute-start(bf16[48,2304]{1,0:T(8,128)(2,1)S(1)} %collective-permute-done.42.refs_8_), channel_id=1, source_target_pairs={{0,2},{2,4},{4,6},{6,7},{7,5},{5,3},{3,1},{1,0},{8,10},{10,12},{12... | collective-permute-start | bytes 663560 | tf_op jit(solution)/shard_map/ppermute | solution.py:971
  186.4 9.5 %collective-permute-start.50 = (bf16[48,2304]{1,0:T(8,128)(2,1)S(1)}, bf16[48,2304]{1,0:T(8,128)(2,1)S(1)}, u32[]{:S(2)}, u32[]{:S(2)}) collective-permute-start(bf16[48,2304]{1,0:T(8,128)(2,1)S(1)} %collective-permute-done.43.refs_9_), channel_id=1, source_target_pairs={{0,1},{2,0},{4,2},{6,4},{7,6},{5,7},{3,5},{1,3},{8,9},{10,8},{12,1... | collective-permute-start | bytes 663560 | tf_op jit(solution)/shard_map/ppermute | solution.py:971
  191.6 9.0 %collective-permute-start.51 = (bf16[48,2304]{1,0:T(8,128)(2,1)S(1)}, bf16[48,2304]{1,0:T(8,128)(2,1)S(1)}, u32[]{:S(2)}, u32[]{:S(2)}) collective-permute-start(bf16[48,2304]{1,0:T(8,128)(2,1)S(1)} %collective-permute-done.47.refs_3_), channel_id=1, source_target_pairs={{0,1},{2,0},{4,2},{6,4},{7,6},{5,7},{3,5},{1,3},{8,9},{10,8},{12,1... | collective-permute-start | bytes 663560 | tf_op jit(solution)/shard_map/ppermute | solution.py:971
  193.3 9.5 %collective-permute-start.48 = (bf16[48,2304]{1,0:T(8,128)(2,1)S(1)}, bf16[48,2304]{1,0:T(8,128)(2,1)S(1)}, u32[]{:S(2)}, u32[]{:S(2)}) collective-permute-start(bf16[48,2304]{1,0:T(8,128)(2,1)S(1)} %collective-permute-done.45.refs_4_), channel_id=1, source_target_pairs={{0,2},{2,4},{4,6},{6,7},{7,5},{5,3},{3,1},{1,0},{8,10},{10,12},{12... | collective-permute-start | bytes 663560 | tf_op jit(solution)/shard_map/ppermute | solution.py:971
  195.9 9.5 %collective-permute-start.54 = (bf16[48,2304]{1,0:T(8,128)(2,1)S(1)}, bf16[48,2304]{1,0:T(8,128)(2,1)S(1)}, u32[]{:S(2)}, u32[]{:S(2)}) collective-permute-start(bf16[48,2304]{1,0:T(8,128)(2,1)S(1)} %collective-permute-done.50.refs_5_), channel_id=1, source_target_pairs={{0,1},{2,0},{4,2},{6,4},{7,6},{5,7},{3,5},{1,3},{8,9},{10,8},{12,1... | collective-permute-start | bytes 663560 | tf_op jit(solution)/shard_map/ppermute | solution.py:971
  198.1 10.7 %collective-permute-start.53 = (bf16[48,2304]{1,0:T(8,128)(2,1)S(1)}, bf16[48,2304]{1,0:T(8,128)(2,1)S(1)}, u32[]{:S(2)}, u32[]{:S(2)}) collective-permute-start(bf16[48,2304]{1,0:T(8,128)(2,1)S(1)} %collective-permute-done.49.refs_6_), channel_id=1, source_target_pairs={{0,2},{2,4},{4,6},{6,7},{7,5},{5,3},{3,1},{1,0},{8,10},{10,12},{12... | collective-permute-start | bytes 663560 | tf_op jit(solution)/shard_map/ppermute | solution.py:971
  200.6 10.1 %collective-permute-start.55 = (bf16[48,2304]{1,0:T(8,128)(2,1)S(1)}, bf16[48,2304]{1,0:T(8,128)(2,1)S(1)}, u32[]{:S(2)}, u32[]{:S(2)}) collective-permute-start(bf16[48,2304]{1,0:T(8,128)(2,1)S(1)} %collective-permute-done.51.refs_7_), channel_id=1, source_target_pairs={{0,1},{2,0},{4,2},{6,4},{7,6},{5,7},{3,5},{1,3},{8,9},{10,8},{12,1... | collective-permute-start | bytes 663560 | tf_op jit(solution)/shard_map/ppermute | solution.py:971
  202.8 9.5 %collective-permute-start.52 = (bf16[48,2304]{1,0:T(8,128)(2,1)S(1)}, bf16[48,2304]{1,0:T(8,128)(2,1)S(1)}, u32[]{:S(2)}, u32[]{:S(2)}) collective-permute-start(bf16[48,2304]{1,0:T(8,128)(2,1)S(1)} %collective-permute-done.48.refs_8_), channel_id=1, source_target_pairs={{0,2},{2,4},{4,6},{6,7},{7,5},{5,3},{3,1},{1,0},{8,10},{10,12},{12... | collective-permute-start | bytes 663560 | tf_op jit(solution)/shard_map/ppermute | solution.py:971
  205.3 9.5 %collective-permute-start.58 = (bf16[48,2304]{1,0:T(8,128)(2,1)S(1)}, bf16[48,2304]{1,0:T(8,128)(2,1)S(1)}, u32[]{:S(2)}, u32[]{:S(2)}) collective-permute-start(bf16[48,2304]{1,0:T(8,128)(2,1)S(1)} %collective-permute-done.54.refs_9_), channel_id=1, source_target_pairs={{0,1},{2,0},{4,2},{6,4},{7,6},{5,7},{3,5},{1,3},{8,9},{10,8},{12,1... | collective-permute-start | bytes 663560 | tf_op jit(solution)/shard_map/ppermute | solution.py:971
  212.3 9.7 %collective-permute-start.56 = (bf16[48,2304]{1,0:T(8,128)(2,1)S(1)}, bf16[48,2304]{1,0:T(8,128)(2,1)S(1)}, u32[]{:S(2)}, u32[]{:S(2)}) collective-permute-start(bf16[48,2304]{1,0:T(8,128)(2,1)S(1)} %collective-permute-done.52.refs_4_), channel_id=1, source_target_pairs={{0,2},{2,4},{4,6},{6,7},{7,5},{5,3},{3,1},{1,0},{8,10},{10,12},{12... | collective-permute-start | bytes 663560 | tf_op jit(solution)/shard_map/ppermute | solution.py:971
  214.8 9.5 %collective-permute-start.62 = (bf16[48,2304]{1,0:T(8,128)(2,1)S(1)}, bf16[48,2304]{1,0:T(8,128)(2,1)S(1)}, u32[]{:S(2)}, u32[]{:S(2)}) collective-permute-start(bf16[48,2304]{1,0:T(8,128)(2,1)S(1)} %collective-permute-done.58.refs_5_), channel_id=1, source_target_pairs={{0,1},{2,0},{4,2},{6,4},{7,6},{5,7},{3,5},{1,3},{8,9},{10,8},{12,1... | collective-permute-start | bytes 663560 | tf_op jit(solution)/shard_map/ppermute | solution.py:971
  217.2 9.9 %collective-permute-start.61 = (bf16[48,2304]{1,0:T(8,128)(2,1)S(1)}, bf16[48,2304]{1,0:T(8,128)(2,1)S(1)}, u32[]{:S(2)}, u32[]{:S(2)}) collective-permute-start(bf16[48,2304]{1,0:T(8,128)(2,1)S(1)} %collective-permute-done.57.refs_6_), channel_id=1, source_target_pairs={{0,2},{2,4},{4,6},{6,7},{7,5},{5,3},{3,1},{1,0},{8,10},{10,12},{12... | collective-permute-start | bytes 663560 | tf_op jit(solution)/shard_map/ppermute | solution.py:971
  219.6 9.5 %collective-permute-start.63 = (bf16[48,2304]{1,0:T(8,128)(2,1)S(1)}, bf16[48,2304]{1,0:T(8,128)(2,1)S(1)}, u32[]{:S(2)}, u32[]{:S(2)}) collective-permute-start(bf16[48,2304]{1,0:T(8,128)(2,1)S(1)} %collective-permute-done.59.refs_7_), channel_id=1, source_target_pairs={{0,1},{2,0},{4,2},{6,4},{7,6},{5,7},{3,5},{1,3},{8,9},{10,8},{12,1... | collective-permute-start | bytes 663560 | tf_op jit(solution)/shard_map/ppermute | solution.py:971
  222.0 9.5 %collective-permute-start.60 = (bf16[48,2304]{1,0:T(8,128)(2,1)S(1)}, bf16[48,2304]{1,0:T(8,128)(2,1)S(1)}, u32[]{:S(2)}, u32[]{:S(2)}) collective-permute-start(bf16[48,2304]{1,0:T(8,128)(2,1)S(1)} %collective-permute-done.56.refs_8_), channel_id=1, source_target_pairs={{0,2},{2,4},{4,6},{6,7},{7,5},{5,3},{3,1},{1,0},{8,10},{10,12},{12... | collective-permute-start | bytes 663560 | tf_op jit(solution)/shard_map/ppermute | solution.py:971
  224.3 9.5 %collective-permute-start.66 = (bf16[48,2304]{1,0:T(8,128)(2,1)S(1)}, bf16[48,2304]{1,0:T(8,128)(2,1)S(1)}, u32[]{:S(2)}, u32[]{:S(2)}) collective-permute-start(bf16[48,2304]{1,0:T(8,128)(2,1)S(1)} %collective-permute-done.62.refs_9_), channel_id=1, source_target_pairs={{0,1},{2,0},{4,2},{6,4},{7,6},{5,7},{3,5},{1,3},{8,9},{10,8},{12,1... | collective-permute-start | bytes 663560 | tf_op jit(solution)/shard_map/ppermute | solution.py:971
  227.2 9.0 %collective-permute-start.65 = (bf16[48,2304]{1,0:T(8,128)(2,1)S(1)}, bf16[48,2304]{1,0:T(8,128)(2,1)S(1)}, u32[]{:S(2)}, u32[]{:S(2)}) collective-permute-start(bf16[48,2304]{1,0:T(8,128)(2,1)S(1)} %collective-permute-done.61.refs_2_), channel_id=1, source_target_pairs={{0,2},{2,4},{4,6},{6,7},{7,5},{5,3},{3,1},{1,0},{8,10},{10,12},{12... | collective-permute-start | bytes 663560 | tf_op jit(solution)/shard_map/ppermute | solution.py:971
  229.1 9.4 %collective-permute-start.67 = (bf16[48,2304]{1,0:T(8,128)(2,1)S(1)}, bf16[48,2304]{1,0:T(8,128)(2,1)S(1)}, u32[]{:S(2)}, u32[]{:S(2)}) collective-permute-start(bf16[48,2304]{1,0:T(8,128)(2,1)S(1)} %collective-permute-done.63.refs_3_), channel_id=1, source_target_pairs={{0,1},{2,0},{4,2},{6,4},{7,6},{5,7},{3,5},{1,3},{8,9},{10,8},{12,1... | collective-permute-start | bytes 663560 | tf_op jit(solution)/shard_map/ppermute | solution.py:971
  231.5 9.5 %collective-permute-start.64 = (bf16[48,2304]{1,0:T(8,128)(2,1)S(1)}, bf16[48,2304]{1,0:T(8,128)(2,1)S(1)}, u32[]{:S(2)}, u32[]{:S(2)}) collective-permute-start(bf16[48,2304]{1,0:T(8,128)(2,1)S(1)} %collective-permute-done.60.refs_4_), channel_id=1, source_target_pairs={{0,2},{2,4},{4,6},{6,7},{7,5},{5,3},{3,1},{1,0},{8,10},{10,12},{12... | collective-permute-start | bytes 663560 | tf_op jit(solution)/shard_map/ppermute | solution.py:971
  (41 other events, 328.8 us)

commit v8 on v7

--- a/solution.py
+++ b/solution.py
@@ -271,9 +271,10 @@
             )
 
 
-def positions_kernel(flags, grid, vown, voth, cosf, sinf, pos, segr):
+def positions_kernel(flags, grid, vown, voth, cosf, sinf, pos, segr, kept):
     core = flags[0]
     vec = vectors(core, vown, voth)[0]
+    kept[...] = voth[...]
     h0, w0, h1, w1 = (grid[core, k // 2, k % 2] for k in range(4))
     e1 = h0 * w0
     e2 = e1 + h1 * w1
@@ -819,7 +820,8 @@
     hbm = pltpu.HBM
     return call(
         positions_kernel, "positions", [SMEM, SMEM, VS, VS],
-        [VM((L, D), F32), VM((L, D), F32), hbm((L, 128), F32), hbm((8, L), F32)],
+        [VM((L, D), F32), VM((L, D), F32), hbm((L, 128), F32), hbm((8, L), F32),
+         hbm((1, VECTOR), F32)],
         [], int(1e8), int(3e6), 56,
     )(flags, grid, own, oth)
 
@@ -1045,7 +1047,7 @@
     else:
         voth = core_swap(vown)
     r = D // (2 * n) if small_ring() else PACKED[0]
-    cosf, sinf, pos, segr = positions(flags, grid_sizes, in_hbm(vown), voth)
+    cosf, sinf, pos, segr, voth = positions(flags, grid_sizes, in_hbm(vown), in_vmem(voth))
     vown, voth, rows, pos, segr = (in_hbm(a) for a in (vown, voth, rows, pos, segr))
     got = core_swap(send)
     away = lax.ppermute(away, "section", [(0, 2), (1, 3), (2, 0), (3, 1)])

time: 249 us -> 249 us (level)
  transfers between devices with their start and end apart: 69 -> 69, of which waited for: 38 -> 39; matrix products, arithmetic and copies ran while one was open for 0% -> 0% of each run, Pallas kernels for 28% -> 28%
where the time goes in v8:
time: 249 us; the launch traced here: 244 us
  Pallas kernels  110 us (44%)
  starting transfers between devices  74.5 us (30%)
  waiting for transfers between devices  57.9 us (23%)
    ppermute x56, starting transfers between devices, step(): got = [lax.ppermute(a, 'dp', p) for a, p in zip(self.cur, c.pairs)]  59.3 us
    ppermute x56, waiting for transfers between devices, step(): got = [lax.ppermute(a, 'dp', p) for a, p in zip(self.cur, c.pairs)]  40.6 us
    pallas_call x1, Pallas kernels, second_pass(): call(second_kernel, 'second_pass', [SMEM] + [VS] * (7 + HELD), resident +...  24.1 us
    pallas_call x28, Pallas kernels, add(): call(kernel, 'add', [SMEM] + [VS] * (1 + count), [out] + [VM(PACKED, F32)...  23.7 us
    pallas_call x1, Pallas kernels, back_pass(): call(back_kernel, 'back_pass', [SMEM] + [VS] * 5 + [HBM] * 2 + [VS] * len...  16.6 us
    pallas_call x5, Pallas kernels, place(): call(kernel, 'place', [SMEM, SMEM] + [VS] * given + [HBM] * len(into), ou...  13.2 us
    pallas_call x1, Pallas kernels, first_pass(): call(first_kernel, 'first_pass', [SMEM] + [VS] * 8 + [HBM] * 2 + [VS] * 2...  13.1 us
    ppermute x1, waiting for transfers between devices, body(): c_got = lax.ppermute(c_two, 'section', [(2, 0), (3, 1)])  8 us
  transfers between devices with their start and end apart: 69, of which 39 were waited for; matrix products, arithmetic and copies ran while one was open for 0% of the time, Pallas kernels for 28%

profile of v8, /device:TPU:0, one launch (start us, length us, event | category | flops | bytes accessed | tf_op | source)
XLA Modules:
  0.0 244.1 jit_solution(276146455415405952)
XLA Ops:
  3.8 3.0 %collective-permute-start.1 = (bf16[192,384]{1,0:T(8,128)(2,1)S(1)}, bf16[192,384]{1,0:T(8,128)(2,1)S(1)}, u32[]{:S(2)}, u32[]{:S(2)}) collective-permute-start(bf16[192,384]{1,0:T(8,128)(2,1)S(1)} %get-tuple-element.160), channel_id=1, source_target_pairs={{0,16},{8,24},{16,0},{24,8},{1,17},{9,25},{17,1},{25,9},{2,18},{10... | collective-permute-start | bytes 442376 | tf_op jit(solution)/shard_map/ppermute | solution.py:1053
  10.2 2.6 %positions.1 = (f32[384,768]{1,0:T(8,128)S(1)}, f32[384,768]{1,0:T(8,128)S(1)}, f32[384,128]{1,0:T(8,128)}, f32[8,384]{1,0:T(8,128)}, f32[1,5376]{1,0:T(1,128)}) custom-call(s32[3]{0:T(128)} %pad_add_fusion.refs_0_.flags, s32[2,2,2]{2,1,0:T(2,128)} %grid.1, f32[1,5376]{1,0:T(1,128)} %get-tuple-element.162.vown, f32[1,5376]{1,0:T(1,128)S(1)} %collective-permute-done.3.voth), custom_call_target="tpu_custom_call" | custom-call | flops 100000000 | bytes 3000000 | tf_op jit(solution)/shard_map/positions/pallas_call | solution.py:821
  13.4 13.1 %first_pass.1 = (bf16[384,768]{1,0:T(8,128)(2,1)S(1)}, bf16[384,768]{1,0:T(8,128)(2,1)}, f32[384,768]{1,0:T(8,128)S(1)}, f32[384,768]{1,0:T(8,128)S(1)}, bf16[4,...) custom-call(s32[3]{0:T(128)} %pad_add_fusion.refs_0_.flags, ...), custom_call_target="tpu_custom_call", output_to_operand_aliasing={{2}: (11, {}), {3}: (12, {})} | custom-call | flops 8000000000 | bytes 20000000 | tf_op jit(solution)/shard_map/first_pass/pallas_call | solution.py:830
  29.0 6.9 %collective-permute-done.5.got = bf16[384,768]{1,0:T(8,128)(2,1)S(1)} collective-permute-done((bf16[384,768]{1,0:T(8,128)(2,1)S(1)}, bf16[384,768]{1,0:T(8,128)(2,1)S(1)}, u32[]{:S(2)}, u32[]{:S(2)}) %collective-permute-start.5) | collective-permute-done | bytes 589856 | tf_op jit(solution)/shard_map/ppermute | solution.py:1062
  36.0 24.1 %second_pass.1 = (f32[384,768]{1,0:T(8,128)S(1)}, f32[384,768]{1,0:T(8,128)S(1)}, bf16[4,768,768]{2,1,0:T(8,128)(2,1)S(1)}, bf16[4,768,768]{2,1,0:T(8,128)(2,1)S...) custom-call(s32[3]{0:T(128)} %pad_add_fusion.refs_0_.flags, ...), custom_call_target="tpu_custom_call", output_to_operand_aliasing={{0}: (8, {}), {1}: (9, {}), {2}: (10, {}), {3}: (11, {}), {... | custom-call | flops 17999998976 | bytes 20000000 | tf_op jit(solution)/shard_map/second_pass/pallas_call | solution.py:850
  61.4 3.1 %late_pass.1 = (f32[384,768]{1,0:T(8,128)S(1)}, f32[384,768]{1,0:T(8,128)S(1)}, bf16[4,768,768]{2,1,0:T(8,128)(2,1)S(1)}, bf16[4,768,768]{2,1,0:T(8,128)(2,1)S(1...) custom-call(s32[3]{0:T(128)} %pad_add_fusion.refs_0_.flags, ...), custom_call_target="tpu_custom_call", output_to_operand_aliasing={{0}: (6, {}), {1}: (7, {}), {2}: (8, {}), {3}: (9, {}), {4}... | custom-call | flops 2000000000 | bytes 5000000 | tf_op jit(solution)/shard_map/late_pass/pallas_call | solution.py:863
  64.5 8.0 %collective-permute-done.7.got = bf16[384,768]{1,0:T(8,128)(2,1)S(1)} collective-permute-done((bf16[384,768]{1,0:T(8,128)(2,1)S(1)}, bf16[384,768]{1,0:T(8,128)(2,1)S(1)}, u32[]{:S(2)}, u32[]{:S(2)}) %collective-permute-start.7) | collective-permute-done | bytes 589856 | tf_op jit(solution)/shard_map/ppermute | solution.py:1067
  72.5 5.5 %collective-permute-start.10 = (bf16[384,3840]{1,0:T(8,128)(2,1)S(1)}, bf16[384,3840]{1,0:T(8,128)(2,1)S(1)}, u32[]{:S(2)}, u32[]{:S(2)}) collective-permute-start(bf16[384,3840]{1,0:T(8,128)(2,1)S(1)} %copy-done.1), channel_id=1, source_target_pairs={{0,8},{8,0},{16,24},{24,16},{1,9},{9,1},{17,25},{25,17},{2,10},{10... | collective-permute-start | bytes 8847368 | tf_op jit(solution)/shard_map/ppermute | solution.py:945
  78.5 16.6 %back_pass.1 = (bf16[384,768]{1,0:T(8,128)(2,1)S(1)}, bf16[384,768]{1,0:T(8,128)(2,1)S(1)}, bf16[384,768]{1,0:T(8,128)(2,1)S(1)}, f32[48,128]{1,0:T(8,128)S(1)},...) custom-call(s32[3]{0:T(128)} %pad_add_fusion.refs_0_.flags, bf16[384,768]{1,0:T(8,128)(2,1)} %get-tuple-element.168.field, ...), custom_call_target="tpu_custom_call" | custom-call | flops 10000000000 | bytes 15000000 | tf_op jit(solution)/shard_map/back_pass/pallas_call | solution.py:872
  95.2 5.8 %gram_down.1 = (bf16[768,1536]{1,0:T(8,128)(2,1)S(1)}, bf16[768,768]{1,0:T(8,128)(2,1)S(1)}, bf16[768,768]{1,0:T(8,128)(2,1)S(1)}, bf16[768,3072]{1,0:T(8,128)(2...) custom-call(s32[3]{0:T(128)} %pad_add_fusion.refs_0_.flags, ...), custom_call_target="tpu_custom_call" | custom-call | flops 2000000000 | bytes 8000000 | tf_op jit(solution)/shard_map/gram_down/pallas_call | solution.py:885
  105.0 3.8 %gram_main.1 = (bf16[768,3072]{1,0:T(8,128)(2,1)S(1)}, bf16[768,2304]{1,0:T(8,128)(2,1)S(1)}, bf16[48,2304]{1,0:T(8,128)(2,1)S(1)}, bf16[48,2304]{1,0:T(8,128)(2,1)S(1)}) custom-call(s32[16,4]{1,0:T(8,128)} %get-tuple-element.214.rows.refs_0_.refs_1_, bf16[400,3072]{1,0:T(8,128)(2,1)S(1)} %collective-permute-done.11.right1, ...), custom_call_target="tpu_custom_call", output_to_operand_aliasing={{0}: (3, {})} | custom-call | flops 6000000000 | bytes 12000000 | tf_op jit(solution)/shard_map/gram_main/pallas_call | solution.py:903
  114.9 2.1 collective-permute-done.14.refs_1_
  117.9 2.0 collective-permute-start.18
  127.7 2.0 collective-permute-start.22
  142.4 2.0 collective-permute-start.25
  151.9 2.0 collective-permute-start.29
  156.6 2.0 collective-permute-start.34
  161.4 2.0 collective-permute-start.33
  166.1 2.0 collective-permute-start.38
  170.9 2.0 collective-permute-start.40
  179.3 2.2 collective-permute-start.46
  186.8 3.1 %place.5 = (f32[768,4608]{1,0:T(8,128)}, bf16[768,768]{1,0:T(8,128)(2,1)}) custom-call(s32[3]{0:T(128)} %pad_add_fusion.refs_0_.flags, s32[16,4]{1,0:T(8,128)} %get-tuple-element.214.rows.refs_0_.refs_1_, bf16[48,2304]{1,0:T(8,128)(2,1)S(1)} %add.67.refs_2_, bf16[48,2304]{1,0:T(8,128)(2,1)S(1)} %add.68.refs_3_, bf16[48,2304]{1,0:T(8,128)(2,1)S(1)} %add.69.refs_4_, ...), custom_call_target="tpu_custom_call" | custom-call | flops 1000 | bytes 20000000 | tf_op jit(solution)/shard_map/place/pallas_call | solution.py:935
  196.3 2.0 collective-permute-done.49.refs_6_
  201.0 2.0 collective-permute-done.48.refs_8_
  205.8 3.3 %place.6 = (f32[768,4608]{1,0:T(8,128)}, f32[1,768]{1,0:T(1,128)}, f32[1,768]{1,0:T(1,128)}, f32[1,3072]{1,0:T(1,128)}, f32[1,768]{1,0:T(1,128)}) custom-call(s32[3]{0:T(128)} %pad_add_fusion.refs_0_.flags, s32[16,4]{1,0:T(8,128)} %get-tuple-element.214.rows.refs_0_.refs_1_, ...), custom_call_target="tpu_custom_call", output_to_operand_aliasing={{0}: (18, {})} | custom-call | flops 1000 | bytes 20000000 | tf_op jit(solution)/shard_map/place/pallas_call | solution.py:935
  215.2 2.3 collective-permute-done.57.refs_6_
  220.0 2.3 collective-permute-done.56.refs_8_
  224.7 2.7 %place.7.refs_8_ = f32[768,4608]{1,0:T(8,128)} custom-call(s32[3]{0:T(128)} %pad_add_fusion.refs_0_.flags, s32[16,4]{1,0:T(8,128)} %get-tuple-element.214.rows.refs_0_.refs_1_, bf16[48,2304]{1,0:T(8,128)(2,1)S(1)} %collective-permute-done.53.refs_2_, bf16[48,2304]{1,0:T(8,128)(2,1)S(1)} %collective-permute-done.55.refs_3_, ...), custom_call_target="tpu_custom_call", output_to_operand_aliasing={{}: (10, {})} | custom-call | flops 1000 | bytes 20000000 | tf_op jit(solution)/shard_map/place/pallas_call | solution.py:935
  229.5 2.2 collective-permute-done.60.refs_4_
  234.2 2.3 collective-permute-done.65.refs_6_
  236.5 2.2 collective-permute-done.67.refs_7_
  238.7 2.4 place.8.refs_4_
  (155 shorter events, 103.2 us)
Async XLA Ops:
  0.6 12.8 %collective-permute-start.4 = (bf16[768,4608]{1,0:T(8,128)(2,1)}, bf16[768,4608]{1,0:T(8,128)(2,1)}, u32[]{:S(2)}, u32[]{:S(2)}) collective-permute-start(bf16[768,4608]{1,0:T(8,128)(2,1)} %bitcast.12), channel_id=1, source_target_pairs={{0,8},{8,0},{16,24},{24,16},{1,9},{9,1},{17,25},{25,17},{2,10},{10... | collective-permute-start | bytes 21233672 | tf_op jit(solution)/shard_map/ppermute | solution.py:945
  3.6 9.2 %collective-permute-start = (bf16[192,384]{1,0:T(8,128)(2,1)S(1)}, bf16[192,384]{1,0:T(8,128)(2,1)S(1)}, u32[]{:S(2)}, u32[]{:S(2)}) collective-permute-start(bf16[192,384]{1,0:T(8,128)(2,1)S(1)} %get-tuple-element.159), channel_id=1, source_target_pairs={{0,8},{8,0},{16,24},{24,16},{1,9},{9,1},{17,25},{25,17},{2,10},{10... | collective-permute-start | bytes 442376 | tf_op jit(solution)/shard_map/ppermute | solution.py:945
  3.8 9.1 %collective-permute-start.1 = (bf16[192,384]{1,0:T(8,128)(2,1)S(1)}, bf16[192,384]{1,0:T(8,128)(2,1)S(1)}, u32[]{:S(2)}, u32[]{:S(2)}) collective-permute-start(bf16[192,384]{1,0:T(8,128)(2,1)S(1)} %get-tuple-element.160), channel_id=1, source_target_pairs={{0,16},{8,24},{16,0},{24,8},{1,17},{9,25},{17,1},{25,9},{2,18},{10... | collective-permute-start | bytes 442376 | tf_op jit(solution)/shard_map/ppermute | solution.py:1053
  60.1 12.4 %collective-permute-start.7 = (bf16[384,768]{1,0:T(8,128)(2,1)S(1)}, bf16[384,768]{1,0:T(8,128)(2,1)S(1)}, u32[]{:S(2)}, u32[]{:S(2)}) collective-permute-start(bf16[384,768]{1,0:T(8,128)(2,1)S(1)} %get-tuple-element.175), channel_id=1, source_target_pairs={{16,0},{24,8},{17,1},{25,9},{18,2},{26,10},{19,3},{27,11},{20,4},{... | collective-permute-start | bytes 1769480 | tf_op jit(solution)/shard_map/ppermute | solution.py:1067
  72.5 22.6 %collective-permute-start.10 = (bf16[384,3840]{1,0:T(8,128)(2,1)S(1)}, bf16[384,3840]{1,0:T(8,128)(2,1)S(1)}, u32[]{:S(2)}, u32[]{:S(2)}) collective-permute-start(bf16[384,3840]{1,0:T(8,128)(2,1)S(1)} %copy-done.1), channel_id=1, source_target_pairs={{0,8},{8,0},{16,24},{24,16},{1,9},{9,1},{17,25},{25,17},{2,10},{10... | collective-permute-start | bytes 8847368 | tf_op jit(solution)/shard_map/ppermute | solution.py:945
  78.0 17.1 %collective-permute-start.8 = (bf16[384,768]{1,0:T(8,128)(2,1)S(1)}, bf16[384,768]{1,0:T(8,128)(2,1)S(1)}, u32[]{:S(2)}, u32[]{:S(2)}) collective-permute-start(bf16[384,768]{1,0:T(8,128)(2,1)S(1)} %collective-permute-done.7.got), channel_id=1, source_target_pairs={{0,8},{8,0},{16,24},{24,16},{1,9},{9,1},{17,25},{25,17},{2,10},{10... | collective-permute-start | bytes 1769480 | tf_op jit(solution)/shard_map/ppermute | solution.py:945
  78.0 17.1 %collective-permute-start.9 = (bf16[384,768]{1,0:T(8,128)(2,1)S(1)}, bf16[384,768]{1,0:T(8,128)(2,1)S(1)}, u32[]{:S(2)}, u32[]{:S(2)}) collective-permute-start(bf16[384,768]{1,0:T(8,128)(2,1)S(1)} %get-tuple-element.204), channel_id=1, source_target_pairs={{0,8},{8,0},{16,24},{24,16},{1,9},{9,1},{17,25},{25,17},{2,10},{10... | collective-permute-start | bytes 1769480 | tf_op jit(solution)/shard_map/ppermute | solution.py:945
  104.8 9.0 %collective-permute-start.15 = (bf16[48,2432]{1,0:T(8,128)(2,1)S(1)}, bf16[48,2432]{1,0:T(8,128)(2,1)S(1)}, u32[]{:S(2)}, u32[]{:S(2)}) collective-permute-start(bf16[48,2432]{1,0:T(8,128)(2,1)S(1)} %get-tuple-element.228), channel_id=1, source_target_pairs={{0,1},{2,0},{4,2},{6,4},{7,6},{5,7},{3,5},{1,3},{8,9},{10,8},{12,1... | collective-permute-start | bytes 700424 | tf_op jit(solution)/shard_map/ppermute | solution.py:973
  110.7 9.2 %collective-permute-start.16 = (bf16[48,2304]{1,0:T(8,128)(2,1)S(1)}, bf16[48,2304]{1,0:T(8,128)(2,1)S(1)}, u32[]{:S(2)}, u32[]{:S(2)}) collective-permute-start(bf16[48,2304]{1,0:T(8,128)(2,1)S(1)} %get-tuple-element.224), channel_id=1, source_target_pairs={{0,1},{2,0},{4,2},{6,4},{7,6},{5,7},{3,5},{1,3},{8,9},{10,8},{12,1... | collective-permute-start | bytes 663560 | tf_op jit(solution)/shard_map/ppermute | solution.py:973
  112.0 10.1 %collective-permute-start.13 = (bf16[48,2432]{1,0:T(8,128)(2,1)S(1)}, bf16[48,2432]{1,0:T(8,128)(2,1)S(1)}, u32[]{:S(2)}, u32[]{:S(2)}) collective-permute-start(bf16[48,2432]{1,0:T(8,128)(2,1)S(1)} %get-tuple-element.227), channel_id=1, source_target_pairs={{0,2},{2,4},{4,6},{6,7},{7,5},{5,3},{3,1},{1,0},{8,10},{10,12},{12... | collective-permute-start | bytes 700424 | tf_op jit(solution)/shard_map/ppermute | solution.py:973
  114.7 10.2 %collective-permute-start.19 = (bf16[48,2432]{1,0:T(8,128)(2,1)S(1)}, bf16[48,2432]{1,0:T(8,128)(2,1)S(1)}, u32[]{:S(2)}, u32[]{:S(2)}) collective-permute-start(bf16[48,2432]{1,0:T(8,128)(2,1)S(1)} %get-tuple-element.230), channel_id=1, source_target_pairs={{0,1},{2,0},{4,2},{6,4},{7,6},{5,7},{3,5},{1,3},{8,9},{10,8},{12,1... | collective-permute-start | bytes 700424 | tf_op jit(solution)/shard_map/ppermute | solution.py:973
  169.1 17.7 %collective-permute-start.44 = (bf16[384,768]{1,0:T(8,128)(2,1)S(1)}, bf16[384,768]{1,0:T(8,128)(2,1)S(1)}, u32[]{:S(2)}, u32[]{:S(2)}) collective-permute-start(bf16[384,768]{1,0:T(8,128)(2,1)S(1)} %copy-done.2), channel_id=1, source_target_pairs={{0,8},{8,0},{16,24},{24,16},{1,9},{9,1},{17,25},{25,17},{2,10},{10... | collective-permute-start | bytes 1769480 | tf_op jit(solution)/shard_map/ppermute | solution.py:945
  179.3 10.6 %collective-permute-start.46 = (bf16[48,2304]{1,0:T(8,128)(2,1)S(1)}, bf16[48,2304]{1,0:T(8,128)(2,1)S(1)}, u32[]{:S(2)}, u32[]{:S(2)}) collective-permute-start(bf16[48,2304]{1,0:T(8,128)(2,1)S(1)} %collective-permute-done.40.refs_6_), channel_id=1, source_target_pairs={{0,2},{2,4},{4,6},{6,7},{7,5},{5,3},{3,1},{1,0},{8,10},{10,12},{12... | collective-permute-start | bytes 663560 | tf_op jit(solution)/shard_map/ppermute | solution.py:973
  181.8 9.9 %collective-permute-start.47 = (bf16[48,2304]{1,0:T(8,128)(2,1)S(1)}, bf16[48,2304]{1,0:T(8,128)(2,1)S(1)}, u32[]{:S(2)}, u32[]{:S(2)}) collective-permute-start(bf16[48,2304]{1,0:T(8,128)(2,1)S(1)} %collective-permute-done.41.refs_7_), channel_id=1, source_target_pairs={{0,1},{2,0},{4,2},{6,4},{7,6},{5,7},{3,5},{1,3},{8,9},{10,8},{12,1... | collective-permute-start | bytes 663560 | tf_op jit(solution)/shard_map/ppermute | solution.py:973
  184.0 9.5 %collective-permute-start.45 = (bf16[48,2304]{1,0:T(8,128)(2,1)S(1)}, bf16[48,2304]{1,0:T(8,128)(2,1)S(1)}, u32[]{:S(2)}, u32[]{:S(2)}) collective-permute-start(bf16[48,2304]{1,0:T(8,128)(2,1)S(1)} %collective-permute-done.42.refs_8_), channel_id=1, source_target_pairs={{0,2},{2,4},{4,6},{6,7},{7,5},{5,3},{3,1},{1,0},{8,10},{10,12},{12... | collective-permute-start | bytes 663560 | tf_op jit(solution)/shard_map/ppermute | solution.py:973
  186.6 9.5 %collective-permute-start.50 = (bf16[48,2304]{1,0:T(8,128)(2,1)S(1)}, bf16[48,2304]{1,0:T(8,128)(2,1)S(1)}, u32[]{:S(2)}, u32[]{:S(2)}) collective-permute-start(bf16[48,2304]{1,0:T(8,128)(2,1)S(1)} %collective-permute-done.43.refs_9_), channel_id=1, source_target_pairs={{0,1},{2,0},{4,2},{6,4},{7,6},{5,7},{3,5},{1,3},{8,9},{10,8},{12,1... | collective-permute-start | bytes 663560 | tf_op jit(solution)/shard_map/ppermute | solution.py:973
  191.7 9.0 %collective-permute-start.51 = (bf16[48,2304]{1,0:T(8,128)(2,1)S(1)}, bf16[48,2304]{1,0:T(8,128)(2,1)S(1)}, u32[]{:S(2)}, u32[]{:S(2)}) collective-permute-start(bf16[48,2304]{1,0:T(8,128)(2,1)S(1)} %collective-permute-done.47.refs_3_), channel_id=1, source_target_pairs={{0,1},{2,0},{4,2},{6,4},{7,6},{5,7},{3,5},{1,3},{8,9},{10,8},{12,1... | collective-permute-start | bytes 663560 | tf_op jit(solution)/shard_map/ppermute | solution.py:973
  193.5 9.6 %collective-permute-start.48 = (bf16[48,2304]{1,0:T(8,128)(2,1)S(1)}, bf16[48,2304]{1,0:T(8,128)(2,1)S(1)}, u32[]{:S(2)}, u32[]{:S(2)}) collective-permute-start(bf16[48,2304]{1,0:T(8,128)(2,1)S(1)} %collective-permute-done.45.refs_4_), channel_id=1, source_target_pairs={{0,2},{2,4},{4,6},{6,7},{7,5},{5,3},{3,1},{1,0},{8,10},{10,12},{12... | collective-permute-start | bytes 663560 | tf_op jit(solution)/shard_map/ppermute | solution.py:973
  196.0 9.5 %collective-permute-start.54 = (bf16[48,2304]{1,0:T(8,128)(2,1)S(1)}, bf16[48,2304]{1,0:T(8,128)(2,1)S(1)}, u32[]{:S(2)}, u32[]{:S(2)}) collective-permute-start(bf16[48,2304]{1,0:T(8,128)(2,1)S(1)} %collective-permute-done.50.refs_5_), channel_id=1, source_target_pairs={{0,1},{2,0},{4,2},{6,4},{7,6},{5,7},{3,5},{1,3},{8,9},{10,8},{12,1... | collective-permute-start | bytes 663560 | tf_op jit(solution)/shard_map/ppermute | solution.py:973
  198.3 10.8 %collective-permute-start.53 = (bf16[48,2304]{1,0:T(8,128)(2,1)S(1)}, bf16[48,2304]{1,0:T(8,128)(2,1)S(1)}, u32[]{:S(2)}, u32[]{:S(2)}) collective-permute-start(bf16[48,2304]{1,0:T(8,128)(2,1)S(1)} %collective-permute-done.49.refs_6_), channel_id=1, source_target_pairs={{0,2},{2,4},{4,6},{6,7},{7,5},{5,3},{3,1},{1,0},{8,10},{10,12},{12... | collective-permute-start | bytes 663560 | tf_op jit(solution)/shard_map/ppermute | solution.py:973
  200.8 10.1 %collective-permute-start.55 = (bf16[48,2304]{1,0:T(8,128)(2,1)S(1)}, bf16[48,2304]{1,0:T(8,128)(2,1)S(1)}, u32[]{:S(2)}, u32[]{:S(2)}) collective-permute-start(bf16[48,2304]{1,0:T(8,128)(2,1)S(1)} %collective-permute-done.51.refs_7_), channel_id=1, source_target_pairs={{0,1},{2,0},{4,2},{6,4},{7,6},{5,7},{3,5},{1,3},{8,9},{10,8},{12,1... | collective-permute-start | bytes 663560 | tf_op jit(solution)/shard_map/ppermute | solution.py:973
  203.1 9.5 %collective-permute-start.52 = (bf16[48,2304]{1,0:T(8,128)(2,1)S(1)}, bf16[48,2304]{1,0:T(8,128)(2,1)S(1)}, u32[]{:S(2)}, u32[]{:S(2)}) collective-permute-start(bf16[48,2304]{1,0:T(8,128)(2,1)S(1)} %collective-permute-done.48.refs_8_), channel_id=1, source_target_pairs={{0,2},{2,4},{4,6},{6,7},{7,5},{5,3},{3,1},{1,0},{8,10},{10,12},{12... | collective-permute-start | bytes 663560 | tf_op jit(solution)/shard_map/ppermute | solution.py:973
  205.5 9.5 %collective-permute-start.58 = (bf16[48,2304]{1,0:T(8,128)(2,1)S(1)}, bf16[48,2304]{1,0:T(8,128)(2,1)S(1)}, u32[]{:S(2)}, u32[]{:S(2)}) collective-permute-start(bf16[48,2304]{1,0:T(8,128)(2,1)S(1)} %collective-permute-done.54.refs_9_), channel_id=1, source_target_pairs={{0,1},{2,0},{4,2},{6,4},{7,6},{5,7},{3,5},{1,3},{8,9},{10,8},{12,1... | collective-permute-start | bytes 663560 | tf_op jit(solution)/shard_map/ppermute | solution.py:973
  212.5 9.7 %collective-permute-start.56 = (bf16[48,2304]{1,0:T(8,128)(2,1)S(1)}, bf16[48,2304]{1,0:T(8,128)(2,1)S(1)}, u32[]{:S(2)}, u32[]{:S(2)}) collective-permute-start(bf16[48,2304]{1,0:T(8,128)(2,1)S(1)} %collective-permute-done.52.refs_4_), channel_id=1, source_target_pairs={{0,2},{2,4},{4,6},{6,7},{7,5},{5,3},{3,1},{1,0},{8,10},{10,12},{12... | collective-permute-start | bytes 663560 | tf_op jit(solution)/shard_map/ppermute | solution.py:973
  215.0 9.5 %collective-permute-start.62 = (bf16[48,2304]{1,0:T(8,128)(2,1)S(1)}, bf16[48,2304]{1,0:T(8,128)(2,1)S(1)}, u32[]{:S(2)}, u32[]{:S(2)}) collective-permute-start(bf16[48,2304]{1,0:T(8,128)(2,1)S(1)} %collective-permute-done.58.refs_5_), channel_id=1, source_target_pairs={{0,1},{2,0},{4,2},{6,4},{7,6},{5,7},{3,5},{1,3},{8,9},{10,8},{12,1... | collective-permute-start | bytes 663560 | tf_op jit(solution)/shard_map/ppermute | solution.py:973
  217.5 9.9 %collective-permute-start.61 = (bf16[48,2304]{1,0:T(8,128)(2,1)S(1)}, bf16[48,2304]{1,0:T(8,128)(2,1)S(1)}, u32[]{:S(2)}, u32[]{:S(2)}) collective-permute-start(bf16[48,2304]{1,0:T(8,128)(2,1)S(1)} %collective-permute-done.57.refs_6_), channel_id=1, source_target_pairs={{0,2},{2,4},{4,6},{6,7},{7,5},{5,3},{3,1},{1,0},{8,10},{10,12},{12... | collective-permute-start | bytes 663560 | tf_op jit(solution)/shard_map/ppermute | solution.py:973
  219.7 9.5 %collective-permute-start.63 = (bf16[48,2304]{1,0:T(8,128)(2,1)S(1)}, bf16[48,2304]{1,0:T(8,128)(2,1)S(1)}, u32[]{:S(2)}, u32[]{:S(2)}) collective-permute-start(bf16[48,2304]{1,0:T(8,128)(2,1)S(1)} %collective-permute-done.59.refs_7_), channel_id=1, source_target_pairs={{0,1},{2,0},{4,2},{6,4},{7,6},{5,7},{3,5},{1,3},{8,9},{10,8},{12,1... | collective-permute-start | bytes 663560 | tf_op jit(solution)/shard_map/ppermute | solution.py:973
  222.2 9.5 %collective-permute-start.60 = (bf16[48,2304]{1,0:T(8,128)(2,1)S(1)}, bf16[48,2304]{1,0:T(8,128)(2,1)S(1)}, u32[]{:S(2)}, u32[]{:S(2)}) collective-permute-start(bf16[48,2304]{1,0:T(8,128)(2,1)S(1)} %collective-permute-done.56.refs_8_), channel_id=1, source_target_pairs={{0,2},{2,4},{4,6},{6,7},{7,5},{5,3},{3,1},{1,0},{8,10},{10,12},{12... | collective-permute-start | bytes 663560 | tf_op jit(solution)/shard_map/ppermute | solution.py:973
  224.5 9.5 %collective-permute-start.66 = (bf16[48,2304]{1,0:T(8,128)(2,1)S(1)}, bf16[48,2304]{1,0:T(8,128)(2,1)S(1)}, u32[]{:S(2)}, u32[]{:S(2)}) collective-permute-start(bf16[48,2304]{1,0:T(8,128)(2,1)S(1)} %collective-permute-done.62.refs_9_), channel_id=1, source_target_pairs={{0,1},{2,0},{4,2},{6,4},{7,6},{5,7},{3,5},{1,3},{8,9},{10,8},{12,1... | collective-permute-start | bytes 663560 | tf_op jit(solution)/shard_map/ppermute | solution.py:973
  227.4 9.0 %collective-permute-start.65 = (bf16[48,2304]{1,0:T(8,128)(2,1)S(1)}, bf16[48,2304]{1,0:T(8,128)(2,1)S(1)}, u32[]{:S(2)}, u32[]{:S(2)}) collective-permute-start(bf16[48,2304]{1,0:T(8,128)(2,1)S(1)} %collective-permute-done.61.refs_2_), channel_id=1, source_target_pairs={{0,2},{2,4},{4,6},{6,7},{7,5},{5,3},{3,1},{1,0},{8,10},{10,12},{12... | collective-permute-start | bytes 663560 | tf_op jit(solution)/shard_map/ppermute | solution.py:973
  229.3 9.4 %collective-permute-start.67 = (bf16[48,2304]{1,0:T(8,128)(2,1)S(1)}, bf16[48,2304]{1,0:T(8,128)(2,1)S(1)}, u32[]{:S(2)}, u32[]{:S(2)}) collective-permute-start(bf16[48,2304]{1,0:T(8,128)(2,1)S(1)} %collective-permute-done.63.refs_3_), channel_id=1, source_target_pairs={{0,1},{2,0},{4,2},{6,4},{7,6},{5,7},{3,5},{1,3},{8,9},{10,8},{12,1... | collective-permute-start | bytes 663560 | tf_op jit(solution)/shard_map/ppermute | solution.py:973
  231.7 9.4 %collective-permute-start.64 = (bf16[48,2304]{1,0:T(8,128)(2,1)S(1)}, bf16[48,2304]{1,0:T(8,128)(2,1)S(1)}, u32[]{:S(2)}, u32[]{:S(2)}) collective-permute-start(bf16[48,2304]{1,0:T(8,128)(2,1)S(1)} %collective-permute-done.60.refs_4_), channel_id=1, source_target_pairs={{0,2},{2,4},{4,6},{6,7},{7,5},{5,3},{3,1},{1,0},{8,10},{10,12},{12... | collective-permute-start | bytes 663560 | tf_op jit(solution)/shard_map/ppermute | solution.py:973
  (40 other events, 328.4 us)
